TPU v7x, 32 devices: a whole 2x2x4 slice. The times are simulated.
32 devices in a mesh: img: 8 (over y, x, core), cap: 4 (over z).
Axes of the slice: x: 2, y: 2, z: 4, core: 2. Of those that a mesh axis runs over, the one named last changes fastest.
Arguments:
- image_student: bfloat16 [2560, 1024], P(('img', 'cap')), may hold values from -64 to 64
- caption_student: bfloat16 [2560, 1024], P(('cap', 'img')), may hold values from -64 to 64
- image_teacher: bfloat16 [2560, 768], P(('img', 'cap')), may hold values from -64 to 64
- caption_teacher: bfloat16 [2560, 768], P(('cap', 'img')), may hold values from -64 to 64
Outputs:
- image_grad: float32 [2560, 1024], P(('img', 'cap'))
- caption_grad: float32 [2560, 1024], P(('cap', 'img'))
All inputs are finite; a program needn't handle non-finite values.
Results may differ from a plain program's by a relative error of at most 0.004.
Values may be sent and summed in bfloat16 or wider, within the bound.
No kernel may reach another device: no remote copies, remote signals or barrier semaphores. Data moves between devices by JAX's collectives and lax.ppermute only.
A program may use at most 64 MiB of HBM per device.

v0:
```python
import math

import jax
import jax.numpy as jnp
from jax import lax
from jax.sharding import PartitionSpec as P

logit_gain = 3.0


def scores(left, right, factor):
    return factor * lax.dot_general(
        left, right, (((1,), (1,)), ((), ())), preferred_element_type=jnp.float32
    )


def partials(student, teacher, reduce_dim):
    result = []
    for matrix in (student, teacher):
        peak = jnp.max(matrix, axis=reduce_dim)
        total = jnp.sum(jnp.exp(matrix - jnp.expand_dims(peak, reduce_dim)), axis=reduce_dim)
        result.append(peak)
        result.append(total)
    return tuple(result)


def row_pool(parts):
    peak_s, peak_t = lax.pmax((parts[0], parts[2]), "cap")
    total_s, total_t = lax.psum(
        (parts[1] * jnp.exp(parts[0] - peak_s), parts[3] * jnp.exp(parts[2] - peak_t)), "cap"
    )
    return (peak_s + jnp.log(total_s), peak_t + jnp.log(total_t))


def column_pool(parts):
    peak_s, peak_t = lax.pmax((parts[0], parts[2]), "img")
    total_s, total_t = lax.psum(
        (parts[1] * jnp.exp(parts[0] - peak_s), parts[3] * jnp.exp(parts[2] - peak_t)), "img"
    )
    return (peak_s + jnp.log(total_s), peak_t + jnp.log(total_t))


def diagonal(row_offset, col_offset, row_count, col_count):
    row_ids = row_offset + jnp.arange(row_count, dtype=jnp.int32)
    col_ids = col_offset + jnp.arange(col_count, dtype=jnp.int32)
    return (row_ids[:, None] == col_ids[None, :]).astype(jnp.float32)


def grad_tile(student, teacher, row_student, row_teacher, col_student, col_teacher, diag_mask):
    tile_grad = 0.5 * (
        jnp.exp(student - row_student[:, None]) + jnp.exp(student - col_student[None, :])
    )
    tile_grad = tile_grad - 0.25 * (
        jnp.exp(teacher - row_teacher[:, None]) + jnp.exp(teacher - col_teacher[None, :])
    )
    return (tile_grad - 0.5 * diag_mask).astype(jnp.bfloat16)


def local(image_student, caption_student, image_teacher, caption_teacher):
    img_student, img_teacher = (
        lax.all_gather(image_student, "cap", axis=0, tiled=True),
        lax.all_gather(image_teacher, "cap", axis=0, tiled=True),
    )
    row_count = img_student.shape[0]
    width = img_student.shape[1]
    student_gain = logit_gain / math.sqrt(width)
    teacher_gain = logit_gain / math.sqrt(img_teacher.shape[1])
    row_offset = lax.axis_index("img") * row_count
    cap_student, cap_teacher = (
        lax.all_gather(caption_student, "img", axis=0, tiled=True),
        lax.all_gather(caption_teacher, "img", axis=0, tiled=True),
    )
    col_count = cap_student.shape[0]
    col_offset = lax.axis_index("cap") * col_count
    student = scores(img_student, cap_student, student_gain)
    teacher = scores(img_teacher, cap_teacher, teacher_gain)
    row_student, row_teacher = row_pool(partials(student, teacher, 1))
    col_student, col_teacher = column_pool(partials(student, teacher, 0))
    diag_mask = diagonal(row_offset, col_offset, row_count, col_count)
    tile_grad = grad_tile(
        student, teacher, row_student, row_teacher, col_student, col_teacher, diag_mask
    )
    portion = tile_grad
    image_grad = lax.psum_scatter(
        jnp.dot(portion, cap_student, preferred_element_type=jnp.float32),
        "cap",
        scatter_dimension=0,
        tiled=True,
    )
    portion = tile_grad
    caption_grad = lax.psum_scatter(
        lax.dot_general(
            portion, img_student, (((0,), (0,)), ((), ())), preferred_element_type=jnp.float32
        ),
        "img",
        scatter_dimension=0,
        tiled=True,
    )
    return (image_grad, caption_grad)


def solution(mesh):
    return jax.shard_map(
        local,
        mesh=mesh,
        in_specs=(
            P(("img", "cap"), None),
            P(("cap", "img"), None),
            P(("img", "cap"), None),
            P(("cap", "img"), None),
        ),
        out_specs=(P(("img", "cap"), None), P(("cap", "img"), None)),
        check_vma=False,
    )
```

profile of v0, /device:TPU:0, one launch (start us, length us, event | category | flops | bytes accessed | tf_op | source)
XLA Modules:
  0.0 190.1 jit_solution(1331497277987987971)
XLA Ops:
  7.2 0.0 all-gather.2.cloned.1.call-start
  7.2 0.7 all-gather.2.cloned.1.call-update
  7.9 0.0 reduce-scatter.3.cloned.1.call-start
  8.0 17.2 %all_gather.14 = bf16[320,768]{1,0:T(8,128)(2,1)S(1)} all-gather(bf16[80,768]{1,0:T(8,128)(2,1)} %param.6), channel_id=1, replica_groups=mesh['img'=8,'cap'=4] {'cap'}, dimensions={0}, use_global_device_ids=true | all-gather | bytes 614400 | tf_op jit(solution)/shard_map/all_gather | solution.py:62
  25.2 14.0 %all_gather.15 = bf16[640,768]{1,0:T(8,128)(2,1)S(1)} all-gather(bf16[80,768]{1,0:T(8,128)(2,1)} %param.7), channel_id=1, replica_groups=mesh['img'=8,'cap'=4] {'img'}, dimensions={0}, use_global_device_ids=true | all-gather | bytes 1105920 | tf_op jit(solution)/shard_map/all_gather | solution.py:71
  39.2 0.0 copy-start.1
  39.2 0.7 fusion.1
  39.9 0.3 exponential_reduce_fusion.1
  40.2 0.0 copy-done.1
  40.2 18.4 %all_gather.12 = bf16[320,1024]{1,0:T(8,128)(2,1)S(1)} all-gather(bf16[80,1024]{1,0:T(8,128)(2,1)S(1)} %copy-done.1), channel_id=1, replica_groups=mesh['img'=8,'cap'=4] {'cap'}, dimensions={0}, use_global_device_ids=true | all-gather | bytes 819200 | tf_op jit(solution)/shard_map/all_gather | solution.py:61
  58.6 0.0 all-gather.2.cloned.1.call-done
  58.6 2.1 %fusion = (f32[320]{0:T(512)S(1)}, f32[640]{0:T(1024)S(1)}, f32[320,640]{1,0:T(8,128)S(1)}) fusion(bf16[320,1024]{1,0:T(8,128)(2,1)S(1)} %all_gather.12, bf16[640,1024]{1,0:T(8,128)(2,1)} %all-gather.2.cloned.1.call-done), kind=kOutput, calls=%fused_computation.17 | convolution fusion | flops 420043840 | bytes 2789120 | tf_op jit(solution)/shard_map/dot_general | solution.py:12
  60.7 12.0 %all-reduce.1 = (f32[640]{0:T(1024)S(1)}, f32[640]{0:T(1024)S(1)}) all-reduce(f32[640]{0:T(1024)S(1)} %get-tuple-element.9, f32[640]{0:T(1024)S(1)} %get-tuple-element.5), channel_id=1, replica_groups=mesh['img'=8,'cap'=4] {'img'}, use_global_device_ids=true, to_apply=%region_13.0 | all-reduce | flops 1280 | bytes 10240 | tf_op jit(solution)/shard_map/pmax | solution.py:36
  72.8 10.8 %all-reduce.3 = (f32[320]{0:T(512)S(1)}, f32[320]{0:T(512)S(1)}) all-reduce(f32[320]{0:T(512)S(1)} %get-tuple-element.8, f32[320]{0:T(512)S(1)} %get-tuple-element.4), channel_id=1, replica_groups=mesh['img'=8,'cap'=4] {'cap'}, use_global_device_ids=true, to_apply=%region_9.0 | all-reduce | flops 640 | bytes 5120 | tf_op jit(solution)/shard_map/pmax | solution.py:28
  83.6 0.3 exponential_reduce_fusion.3
  84.0 12.0 %all-reduce = (f32[640]{0:T(1024)S(1)}, f32[640]{0:T(1024)S(1)}) all-reduce(f32[640]{0:T(1024)S(1)} %exponential_multiply_fusion, f32[640]{0:T(1024)S(1)} %exponential_multiply_fusion.1), channel_id=1, replica_groups=mesh['img'=8,'cap'=4] {'img'}, use_global_device_ids=true, to_apply=%region_15.0 | all-reduce | flops 1280 | bytes 10240 | tf_op jit(solution)/shard_map/psum | solution.py:37
  96.1 8.4 %all-reduce.2 = (f32[320]{0:T(512)S(1)}, f32[320]{0:T(512)S(1)}) all-reduce(f32[320]{0:T(512)S(1)} %exponential_multiply_fusion.2, f32[320]{0:T(512)S(1)} %exponential_multiply_fusion.3), channel_id=1, replica_groups=mesh['img'=8,'cap'=4] {'cap'}, use_global_device_ids=true, to_apply=%region_11.0 | all-reduce | flops 640 | bytes 5120 | tf_op jit(solution)/shard_map/psum | solution.py:29
  104.5 0.0 copy-start
  104.5 0.7 subtract_convert_fusion
  105.1 0.6 copy-done
  105.8 1.8 fusion.2
  107.5 0.0 reduce-scatter.3.cloned.1.call-update
  107.6 0.0 reduce-scatter.5.cloned.1.call-start
  107.6 2.4 %fusion.3 = f32[640,1024]{1,0:T(8,128)} fusion(bf16[320,640]{1,0:T(8,128)(2,1)S(1)} %subtract_convert_fusion, bf16[320,1024]{1,0:T(8,128)(2,1)S(1)} %all_gather.12), kind=kOutput, calls=%fused_computation.20 | convolution fusion | flops 419430400 | bytes 3686400 | tf_op jit(solution)/shard_map/dot_general | solution.py:92
  110.0 0.0 reduce-scatter.5.cloned.1.call-update
  110.0 27.2 %reduce-scatter.3.cloned.1.call-done = f32[80,1024]{1,0:T(8,128)} async-done(((f32[320,1024]{1,0:T(8,128)}), f32[80,1024]{1,0:T(8,128)}) %reduce-scatter.3.cloned.1.call-update) | async-done | bytes 327696 | tf_op jit(solution)/shard_map/reduce_scatter | solution.py:84
  137.2 46.4 %reduce-scatter.5.cloned.1.call-done = f32[80,1024]{1,0:T(8,128)} async-done(((f32[640,1024]{1,0:T(8,128)}), f32[80,1024]{1,0:T(8,128)}) %reduce-scatter.5.cloned.1.call-update) | async-done | bytes 327696 | tf_op jit(solution)/shard_map/reduce_scatter | solution.py:91
  (8 shorter events, 0.1 us)
Async XLA Ops:
  7.2 51.4 %all-gather.2.cloned.1.call-start = ((), (), s32[]{:S(2)}) async-start(), calls=%async_computation.2 | async-start | bytes 1474560 | tf_op jit(solution)/shard_map/all_gather | solution.py:70
  7.9 129.3 %reduce-scatter.3.cloned.1.call-start = ((), (), s32[]{:S(2)}) async-start(), calls=%async_computation.3 | async-start | bytes 1638400 | tf_op jit(solution)/shard_map/reduce_scatter | solution.py:84
  39.2 1.0 copy-start.1
  104.5 1.3 copy-start
  107.6 76.0 %reduce-scatter.5.cloned.1.call-start = ((), (), s32[]{:S(2)}) async-start(), calls=%async_computation.4 | async-start | bytes 2949120 | tf_op jit(solution)/shard_map/reduce_scatter | solution.py:91
Sparse Core Ops, SparseCore 0:
  9.9 29.7 all-gather.1
  107.7 29.4 reduce-scatter.2
  141.1 42.4 reduce-scatter.4
where the time goes:
time: 190 us
  blocking collectives  92.9 us (49%)
  waiting for transfers between devices  74.3 us (39%)
  between operations  13.8 us (7%)
  matrix products  6.95 us (4%)
    reduce_scatter x1, waiting for transfers between devices, local(): lax.psum_scatter(lax.dot_general(portion, img_student, (((0,), (0,)), (()...  46.4 us
    reduce_scatter x1, waiting for transfers between devices, local(): lax.psum_scatter(jnp.dot(portion, cap_student, preferred_element_type=jnp...  27.2 us
    all_gather x1, blocking collectives, local(): lax.all_gather(image_student, 'cap', axis=0, tiled=True)  18.4 us
    all_gather x1, blocking collectives, local(): lax.all_gather(image_teacher, 'cap', axis=0, tiled=True)  17.2 us
    all_gather x1, blocking collectives, local(): lax.all_gather(caption_teacher, 'img', axis=0, tiled=True)  14 us
    psum x1, blocking collectives, column_pool(): lax.psum((parts[1] * jnp.exp(parts[0] - peak_s), parts[3] * jnp.exp(parts...  12 us
    pmax x1, blocking collectives, column_pool(): peak_s, peak_t = lax.pmax((parts[0], parts[2]), 'img')  12 us
    pmax x1, blocking collectives, row_pool(): peak_s, peak_t = lax.pmax((parts[0], parts[2]), 'cap')  10.8 us
  transfers between devices with their start and end apart: 3, of which 2 were waited for; matrix products, arithmetic and copies ran while one was open for 2% of the time, Pallas kernels for 0%

commit v1 on v0

v1 whole, which is shorter than its diff:
```python
import math

import jax
import jax.numpy as jnp
from jax import lax
from jax.sharding import Mesh, PartitionSpec as P

logit_gain = 3.0
ROW_AXES = ("ilo", "clo")
COL_AXES = ("ihi", "chi", "core")


def swap(value, axis, mask):
    size = lax.axis_size(axis)
    return lax.ppermute(value, axis, [(j, j ^ mask) for j in range(size)])


def flip(value, axes, first):
    for d, axis in enumerate(axes):
        bit = 1
        while bit < lax.axis_size(axis):
            size = lax.axis_size(axis)
            swapped = jnp.stack([lax.index_in_dim(value, s ^ bit, first + d, False) for s in range(size)], first + d)
            value = jnp.where((lax.axis_index(axis) & bit) != 0, swapped, value)
            bit *= 2
    return value


def scores(left, right, factor):
    return factor * lax.dot_general(
        left, right, (((1,), (1,)), ((), ())), preferred_element_type=jnp.float32
    )


def partial(matrix, dim):
    peak = jnp.max(matrix, axis=dim)
    total = jnp.sum(jnp.exp(matrix - jnp.expand_dims(peak, dim)), axis=dim)
    return peak, total


def pool(stats, axes, rows):
    shape = tuple(lax.axis_size(a) for a in axes)
    count = math.prod(shape)
    mine = flip(stats.reshape((4,) + shape + (rows,)), axes, 1).reshape(4, count * rows)
    every = lax.all_to_all(
        jnp.broadcast_to(mine[None], (count,) + mine.shape), axes, split_axis=0, concat_axis=0, tiled=True
    )
    result = []
    for k in (0, 2):
        peak = jnp.max(every[:, k], axis=0)
        total = jnp.sum(every[:, k + 1] * jnp.exp(every[:, k] - peak[None]), axis=0)
        result.append(peak + jnp.log(total))
    return flip(jnp.stack(result).reshape((2,) + shape + (rows,)), axes, 1).reshape(2, count * rows)


def owners(shape, axes):
    result = []
    for d, axis in enumerate(axes):
        index = lax.axis_index(axis) ^ jnp.arange(shape[d], dtype=jnp.int32)
        result.append(index.reshape([-1 if e == d else 1 for e in range(len(axes))]))
    return result


def local(image_student, caption_student, image_teacher, caption_teacher):
    ilo, clo, ihi, chi, core = (lax.axis_size(a) for a in ROW_AXES + COL_AXES)
    n_img, n_cap = ihi * ilo * core, chi * clo
    my = {a: lax.axis_index(a) for a in ROW_AXES + COL_AXES}
    rows, width = image_student.shape
    student_gain = logit_gain / math.sqrt(width)
    teacher_gain = logit_gain / math.sqrt(image_teacher.shape[1])

    image = jnp.concatenate([image_student, image_teacher], axis=1)
    caption = jnp.concatenate([caption_student, caption_teacher], axis=1)
    image_far = [image] + [swap(image, "clo", m) for m in range(1, clo)]
    caption_far = [caption] + [swap(caption, "chi", m) for m in range(1, chi)]
    image_slots = image_far + [swap(part, "ilo", m) for m in range(1, ilo) for part in image_far]
    caption_even = caption_far + [swap(part, "ihi", m) for m in range(1, ihi) for part in caption_far]
    caption_slots = [s for part in caption_even for s in (part, swap(part, "core", 1))]
    images = jnp.concatenate(image_slots, axis=0)
    captions = jnp.concatenate(caption_slots, axis=0)
    img_s, img_t = images[:, :width], images[:, width:]
    cap_s, cap_t = captions[:, :width], captions[:, width:]

    student = scores(img_s, cap_s, student_gain)
    teacher = scores(img_t, cap_t, teacher_gain)
    row_s, row_t = pool(jnp.stack(partial(student, 1) + partial(teacher, 1)), ROW_AXES, rows)
    col_s, col_t = pool(jnp.stack(partial(student, 0) + partial(teacher, 0)), COL_AXES, rows)

    inner = jnp.arange(rows, dtype=jnp.int32)
    oi, oc = owners((ilo, clo), ROW_AXES)
    row_owner = (((my["ihi"] * ilo + oi) * core + my["core"]) * chi + my["chi"]) * clo + oc
    oh, oc, ok = owners((ihi, chi, core), COL_AXES)
    col_owner = (((oc * clo + my["clo"]) * ihi + oh) * ilo + my["ilo"]) * core + ok
    row_ids = (row_owner.reshape(-1, 1) * rows + inner[None, :]).reshape(-1)
    col_ids = (col_owner.reshape(-1, 1) * rows + inner[None, :]).reshape(-1)
    diag = (row_ids[:, None] == col_ids[None, :]).astype(jnp.float32)

    tile = 0.5 * (jnp.exp(student - row_s[:, None]) + jnp.exp(student - col_s[None, :]))
    tile = tile - 0.25 * (jnp.exp(teacher - row_t[:, None]) + jnp.exp(teacher - col_t[None, :]))
    tile = (tile - 0.5 * diag).astype(jnp.bfloat16)

    def collect(part, near, far):
        sent = part.astype(jnp.bfloat16)
        held = [part[0, m] for m in range(part.shape[1])]
        for f in reversed(range(part.shape[1])):
            for m in range(1, part.shape[0]):
                held[f] = held[f] + swap(sent[m, f], near, m).astype(jnp.float32)
        total = held[0]
        for f in range(1, part.shape[1]):
            total = total + swap(held[f].astype(jnp.bfloat16), far, f).astype(jnp.float32)
        return total

    caption_part = lax.dot_general(
        tile, img_s, (((0,), (0,)), ((), ())), preferred_element_type=jnp.float32
    ).reshape(ihi, chi, 2, rows, width)
    pair = caption_part[:, :, 0] + swap(caption_part[:, :, 1].astype(jnp.bfloat16), "core", 1).astype(jnp.float32)
    image_part = jnp.dot(tile, cap_s, preferred_element_type=jnp.float32).reshape(ilo, clo, rows, width)
    return (collect(image_part, "ilo", "clo"), collect(pair, "ihi", "chi"))


def split(count):
    low = 1 << ((count.bit_length() - 1) // 2)
    return count // low, low


def solution(mesh):
    ihi, ilo = split(mesh.shape["img"] // 2)
    chi, clo = split(mesh.shape["cap"])
    fine = Mesh(mesh.devices.reshape(ihi, ilo, 2, chi, clo), ("ihi", "ilo", "core", "chi", "clo"))
    by_image = P(("ihi", "ilo", "core", "chi", "clo"), None)
    by_caption = P(("chi", "clo", "ihi", "ilo", "core"), None)
    return jax.shard_map(
        local,
        mesh=fine,
        in_specs=(by_image, by_caption, by_image, by_caption),
        out_specs=(by_image, by_caption),
        check_vma=False,
    )
```

time: 190 us -> 84.6 us (0.45)
  blocking collectives: 92.9 us -> 0 us
  waiting for transfers between devices: 74.3 us -> 34.2 us
  starting transfers between devices: 0.12 us -> 24.9 us
  local copies, waits for them, and re-layouts: 0.64 us -> 14.1 us
  between operations: 13.8 us -> 1.07 us
  other arithmetic: 1.39 us -> 3.54 us
    reduce_scatter x2 -> x0, waiting for transfers between devices: 73.5 us -> none  [the longest x1 46.4 us: local(): lax.psum_scatter(lax.dot_general(portion, img_student, (((0,), (0,)), (()...]
    all_gather x3 -> x0, blocking collectives: 49.6 us -> none  [the longest x1 18.4 us: local(): lax.all_gather(image_student, 'cap', axis=0, tiled=True)]
    ppermute x0 -> x17, waiting for transfers between devices: none -> 23.3 us  [swap(): return lax.ppermute(value, axis, [(j, j ^ mask) for j in range(size)])]
    pmax x2 -> x0, blocking collectives: 22.9 us -> none  [the longest x1 12 us: column_pool(): peak_s, peak_t = lax.pmax((parts[0], parts[2]), 'img')]
    psum x2 -> x0, blocking collectives: 20.4 us -> none  [the longest x1 12 us: column_pool(): lax.psum((parts[1] * jnp.exp(parts[0] - peak_s), parts[3] * jnp.exp(parts...]
    ppermute x0 -> x17, starting transfers between devices: none -> 16.4 us  [swap(): return lax.ppermute(value, axis, [(j, j ^ mask) for j in range(size)])]
    all_to_all x0 -> x2, waiting for transfers between devices: none -> 10.9 us  [pool(): lax.all_to_all(jnp.broadcast_to(mine[None], (count,) + mine.shape), axes,...]
    all_to_all x0 -> x2, starting transfers between devices: none -> 8.55 us  [pool(): lax.all_to_all(jnp.broadcast_to(mine[None], (count,) + mine.shape), axes,...]
  transfers between devices with their start and end apart: 3 -> 19, of which waited for: 2 -> 10; matrix products, arithmetic and copies ran while one was open for 2% -> 12% of each run, Pallas kernels for 0% -> 0%
where the time goes in v1:
time: 84.6 us; the launch traced here: 84.2 us
  waiting for transfers between devices  34.2 us (40%)
  starting transfers between devices  24.9 us (29%)
  local copies, waits for them, and re-layouts  14.1 us (17%)
  matrix products  6.33 us (7%)
  other arithmetic  3.54 us (4%)
  between operations  1.07 us (1%)
    ppermute x17, waiting for transfers between devices, swap(): return lax.ppermute(value, axis, [(j, j ^ mask) for j in range(size)])  23.3 us
    ppermute x17, starting transfers between devices, swap(): return lax.ppermute(value, axis, [(j, j ^ mask) for j in range(size)])  16.4 us
    all_to_all x2, waiting for transfers between devices, pool(): lax.all_to_all(jnp.broadcast_to(mine[None], (count,) + mine.shape), axes,...  10.9 us
    all_to_all x2, starting transfers between devices, pool(): lax.all_to_all(jnp.broadcast_to(mine[None], (count,) + mine.shape), axes,...  8.55 us
    unnamed x18, local copies, waits for them, and re-layouts  7.23 us
    dot_general x2, matrix products, scores(): lax.dot_general(left, right, (((1,), (1,)), ((), ())), preferred_element_...  4 us
  transfers between devices with their start and end apart: 19, of which 10 were waited for; matrix products, arithmetic and copies ran while one was open for 12% of the time, Pallas kernels for 0%

profile of v1, /device:TPU:0, one launch (start us, length us, event | category | flops | bytes accessed | tf_op | source)
XLA Modules:
  0.0 84.2 jit_solution(1377246404976336016)
XLA Ops:
  0.6 1.6 %constant_dynamic-update-slice_fusion.3 = (bf16[80,1792]{1,0:T(8,128)(2,1)S(1)}, bf16[640,1792]{1,0:T(8,128)(2,1)}) fusion(bf16[80,1024]{1,0:T(8,128)(2,1)} %param.5), kind=kLoop, calls=%fused_computation.45 | loop fusion | bytes 491520
  2.3 1.6 %constant_dynamic-update-slice_fusion.2 = (bf16[80,1792]{1,0:T(8,128)(2,1)S(1)}, bf16[640,1792]{1,0:T(8,128)(2,1)}) fusion(bf16[80,1792]{1,0:T(8,128)(2,1)S(1)} %get-tuple-element.20, bf16[80,768]{1,0:T(8,128)(2,1)} %param.7, bf16[640,1792]{1,0:T(8,128)(2,1)} %get-tuple-element.21), kind=kLoop, calls=%fused_computation.44 | loop fusion | bytes 368640 | tf_op jit(solution)/shard_map/concatenate | solution.py:73
  4.3 3.6 %collective-permute-start.4 = (bf16[80,1792]{1,0:T(8,128)(2,1)S(1)}, bf16[80,1792]{1,0:T(8,128)(2,1)S(1)}, u32[]{:S(2)}, u32[]{:S(2)}) collective-permute-start(bf16[80,1792]{1,0:T(8,128)(2,1)S(1)} %get-tuple-element.22), channel_id=1, source_target_pairs={{0,2},{2,0},{1,3},{3,1},{4,6},{6,4},{5,7},{7,5},{8,10},{10,8},{9,1... | collective-permute-start | bytes 860168 | tf_op jit(solution)/shard_map/ppermute | solution.py:15
  7.9 1.5 %collective-permute-start.6 = (bf16[80,1792]{1,0:T(8,128)(2,1)S(1)}, bf16[80,1792]{1,0:T(8,128)(2,1)S(1)}, u32[]{:S(2)}, u32[]{:S(2)}) collective-permute-start(bf16[80,1792]{1,0:T(8,128)(2,1)S(1)} %get-tuple-element.22), channel_id=1, source_target_pairs={{0,16},{16,0},{1,17},{17,1},{2,18},{18,2},{3,19},{19,3},{4,20},{20... | collective-permute-start | bytes 860168 | tf_op jit(solution)/shard_map/ppermute | solution.py:15
  9.4 0.9 %constant_dynamic-update-slice_fusion.1 = bf16[80,1792]{1,0:T(8,128)(2,1)S(1)} fusion(bf16[80,1024]{1,0:T(8,128)(2,1)} %param.4), kind=kLoop, calls=%fused_computation.43 | loop fusion | bytes 327680
  10.3 0.9 %constant_dynamic-update-slice_fusion = bf16[80,1792]{1,0:T(8,128)(2,1)S(1)} fusion(bf16[80,1792]{1,0:T(8,128)(2,1)S(1)} %constant_dynamic-update-slice_fusion.1, bf16[80,768]{1,0:T(8,128)(2,1)} %param.6), kind=kLoop, calls=%fused_computation.42 | loop fusion | bytes 245760 | tf_op jit(solution)/shard_map/concatenate | solution.py:72
  11.2 1.6 %collective-permute-start = (bf16[80,1792]{1,0:T(8,128)(2,1)S(1)}, bf16[80,1792]{1,0:T(8,128)(2,1)S(1)}, u32[]{:S(2)}, u32[]{:S(2)}) collective-permute-start(bf16[80,1792]{1,0:T(8,128)(2,1)S(1)} %constant_dynamic-update-slice_fusion), channel_id=1, source_target_pairs={{0,1},{1,0},{2,3},{3,2},{4,5},{5,4},{6,7},{7,6},{8,9},{9,8},{10,11... | collective-permute-start | bytes 860168 | tf_op jit(solution)/shard_map/ppermute | solution.py:15
  12.9 1.5 %collective-permute-start.1 = (bf16[80,1792]{1,0:T(8,128)(2,1)S(1)}, bf16[80,1792]{1,0:T(8,128)(2,1)S(1)}, u32[]{:S(2)}, u32[]{:S(2)}) collective-permute-start(bf16[80,1792]{1,0:T(8,128)(2,1)S(1)} %constant_dynamic-update-slice_fusion), channel_id=1, source_target_pairs={{0,8},{8,0},{1,9},{9,1},{2,10},{10,2},{3,11},{11,3},{4,12},{12,4},... | collective-permute-start | bytes 860168 | tf_op jit(solution)/shard_map/ppermute | solution.py:15
  15.1 6.5 %collective-permute-done.4 = bf16[80,1792]{1,0:T(8,128)(2,1)S(1)} collective-permute-done((bf16[80,1792]{1,0:T(8,128)(2,1)S(1)}, bf16[80,1792]{1,0:T(8,128)(2,1)S(1)}, u32[]{:S(2)}, u32[]{:S(2)}) %collective-permute-start.4) | collective-permute-done | bytes 286752 | tf_op jit(solution)/shard_map/ppermute | solution.py:15
  21.6 1.6 %collective-permute-start.8 = (bf16[80,1792]{1,0:T(8,128)(2,1)S(1)}, bf16[80,1792]{1,0:T(8,128)(2,1)S(1)}, u32[]{:S(2)}, u32[]{:S(2)}) collective-permute-start(bf16[80,1792]{1,0:T(8,128)(2,1)S(1)} %collective-permute-done.4), channel_id=1, source_target_pairs={{0,16},{16,0},{1,17},{17,1},{2,18},{18,2},{3,19},{19,3},{4,20},{20... | collective-permute-start | bytes 860168 | tf_op jit(solution)/shard_map/ppermute | solution.py:15
  23.4 1.5 %collective-permute-done = bf16[80,1792]{1,0:T(8,128)(2,1)S(1)} collective-permute-done((bf16[80,1792]{1,0:T(8,128)(2,1)S(1)}, bf16[80,1792]{1,0:T(8,128)(2,1)S(1)}, u32[]{:S(2)}, u32[]{:S(2)}) %collective-permute-start) | collective-permute-done | bytes 286752 | tf_op jit(solution)/shard_map/ppermute | solution.py:15
  25.0 1.5 %collective-permute-start.2 = (bf16[80,1792]{1,0:T(8,128)(2,1)S(1)}, bf16[80,1792]{1,0:T(8,128)(2,1)S(1)}, u32[]{:S(2)}, u32[]{:S(2)}) collective-permute-start(bf16[80,1792]{1,0:T(8,128)(2,1)S(1)} %collective-permute-done), channel_id=1, source_target_pairs={{0,8},{8,0},{1,9},{9,1},{2,10},{10,2},{3,11},{11,3},{4,12},{12,4},... | collective-permute-start | bytes 860168 | tf_op jit(solution)/shard_map/ppermute | solution.py:15
  28.0 2.9 %collective-permute-done.8 = bf16[80,1792]{1,0:T(8,128)(2,1)S(1)} collective-permute-done((bf16[80,1792]{1,0:T(8,128)(2,1)S(1)}, bf16[80,1792]{1,0:T(8,128)(2,1)S(1)}, u32[]{:S(2)}, u32[]{:S(2)}) %collective-permute-start.8) | collective-permute-done | bytes 286752 | tf_op jit(solution)/shard_map/ppermute | solution.py:15
  31.6 0.8 constant_dynamic-update-slice_fusion.7
  33.1 0.7 constant_dynamic-update-slice_fusion.5
  33.9 0.8 constant_dynamic-update-slice_fusion.4
  34.7 1.9 %fusion.44 = (f32[320]{0:T(512)S(1)}, f32[640]{0:T(1024)S(1)}, f32[320,640]{1,0:T(8,128)S(1)}) fusion(bf16[640,1792]{1,0:T(8,128)(2,1)} %constant_dynamic-update-slice_fusion.4, bf16[80,1792]{1,0:T(8,128)(2,1)S(1)} %collective-permute-done.2, bf16[80,1792]{1,0:T(8,128)(2,1)S(1)} %collective-permute-done.1, bf16[80,1792]{1,0:T(8,128)(2,1)S(1)} %collective-permute-done, ...), kind=kOutput, calls=%fused_computation.124 | convolution fusion | flops 317152320 | bytes 2952960 | tf_op jit(solution)/shard_map/dot_general | solution.py:30
  37.1 2.1 %fusion.45 = (f32[320]{0:T(512)S(1)}, f32[640]{0:T(1024)S(1)}, f32[320,640]{1,0:T(8,128)S(1)}) fusion(bf16[640,1792]{1,0:T(8,128)(2,1)} %constant_dynamic-update-slice_fusion.4, bf16[320,1792]{1,0:T(8,128)(2,1)S(1)} %pad_maximum_fusion), kind=kOutput, calls=%fused_computation.125 | convolution fusion | flops 420043840 | bytes 2789120 | tf_op jit(solution)/shard_map/dot_general | solution.py:30
  41.5 3.3 %all-to-all-start = ((f32[4,4,320]{2,1,0:T(4,128)}), f32[4,4,320]{2,1,0:T(4,128)S(1)}, u32[]{:S(2)}, u32[]{:S(2)}) async-start(f32[4,4,320]{2,1,0:T(4,128)} %broadcast_in_dim.4), calls=%async_computation | async-start | bytes 49152 | tf_op jit(solution)/shard_map/all_to_all | solution.py:45
  44.8 4.7 %all-to-all-done = f32[4,4,320]{2,1,0:T(4,128)S(1)} async-done(((f32[4,4,320]{2,1,0:T(4,128)}), f32[4,4,320]{2,1,0:T(4,128)S(1)}, u32[]{:S(2)}, u32[]{:S(2)}) %all-to-all-start) | async-done | bytes 20512 | tf_op jit(solution)/shard_map/all_to_all | solution.py:45
  50.1 5.3 %all-to-all-start.1 = ((f32[8,4,640]{2,1,0:T(4,128)}), f32[8,4,640]{2,1,0:T(4,128)S(1)}, u32[]{:S(2)}, u32[]{:S(2)}) async-start(f32[8,4,640]{2,1,0:T(4,128)} %broadcast_in_dim.5), calls=%async_computation.1 | async-start | bytes 163840 | tf_op jit(solution)/shard_map/all_to_all | solution.py:45
  55.9 6.3 %all-to-all-done.1 = f32[8,4,640]{2,1,0:T(4,128)S(1)} async-done(((f32[8,4,640]{2,1,0:T(4,128)}), f32[8,4,640]{2,1,0:T(4,128)S(1)}, u32[]{:S(2)}, u32[]{:S(2)}) %all-to-all-start.1) | async-done | bytes 81952 | tf_op jit(solution)/shard_map/all_to_all | solution.py:45
  62.8 1.3 %fusion.6 = f32[640,1024]{1,0:T(8,128)S(1)} fusion(bf16[320,1792]{1,0:T(8,128)(2,1)S(1)} %pad_maximum_fusion, f32[320,640]{1,0:T(8,128)S(1)} %get-tuple-element.63, f32[320,640]{1,0:T(8,128)S(1)} %get-tuple-element.62, s32[640]{0:T(1024)S(1)} %add.267, f32[640]{0:T(1024)S(1)} %sub.135, f32[320]{0:T(512)S(1)} %sub.132, f32[640]{0:T(1024)S(1)} %sub.129, ...), kind=kOutput, calls=%fused_computation.16 | convolution fusion | flops 422092800 | bytes 4933632 | tf_op jit(solution)/shard_map/dot_general | solution.py:113
  64.4 1.1 %fusion.1 = f32[320,1024]{1,0:T(8,128)S(1)} fusion(bf16[640,1792]{1,0:T(8,128)(2,1)S(1)} %copy-done, f32[320,640]{1,0:T(8,128)S(1)} %get-tuple-element.63, f32[320,640]{1,0:T(8,128)S(1)} %get-tuple-element.62, s32[640]{0:T(1024)S(1)} %add.267, f32[640]{0:T(1024)S(1)} %sub.135, f32[320]{0:T(512)S(1)} %sub.132, f32[640]{0:T(1024)S(1)} %sub.129, ...), kind=kOutput, calls=%fused_computation.5 | convolution fusion | flops 422092800 | bytes 4278272 | tf_op jit(solution)/shard_map/dot_general | solution.py:117
  66.3 1.5 %collective-permute-start.10 = (bf16[80,1024]{1,0:T(8,128)(2,1)S(1)}, bf16[80,1024]{1,0:T(8,128)(2,1)S(1)}, u32[]{:S(2)}, u32[]{:S(2)}) collective-permute-start(bf16[80,1024]{1,0:T(8,128)(2,1)S(1)} %get-tuple-element.18), channel_id=1, source_target_pairs={{0,8},{8,0},{1,9},{9,1},{2,10},{10,2},{3,11},{11,3},{4,12},{12,4},... | collective-permute-start | bytes 491528 | tf_op jit(solution)/shard_map/ppermute | solution.py:15
  68.7 4.1 %collective-permute-done.11 = bf16[80,1024]{1,0:T(8,128)(2,1)S(1)} collective-permute-done((bf16[80,1024]{1,0:T(8,128)(2,1)S(1)}, bf16[80,1024]{1,0:T(8,128)(2,1)S(1)}, u32[]{:S(2)}, u32[]{:S(2)}) %collective-permute-start.11) | collective-permute-done | bytes 163872 | tf_op jit(solution)/shard_map/ppermute | solution.py:15
  74.0 0.8 %collective-permute-start.16 = (bf16[80,1024]{1,0:T(8,128)(2,1)S(1)}, bf16[80,1024]{1,0:T(8,128)(2,1)S(1)}, u32[]{:S(2)}, u32[]{:S(2)}) collective-permute-start(bf16[80,1024]{1,0:T(8,128)(2,1)S(1)} %fusion.17), channel_id=1, source_target_pairs={{0,2},{2,0},{1,3},{3,1},{4,6},{6,4},{5,7},{7,5},{8,10},{10,8},{9,1... | collective-permute-start | bytes 491528 | tf_op jit(solution)/shard_map/ppermute | solution.py:15
  74.8 0.8 collective-permute-done.10
  75.6 3.6 %collective-permute-done.12 = bf16[80,1024]{1,0:T(8,128)(2,1)S(1)} collective-permute-done((bf16[80,1024]{1,0:T(8,128)(2,1)S(1)}, bf16[80,1024]{1,0:T(8,128)(2,1)S(1)}, u32[]{:S(2)}, u32[]{:S(2)}) %collective-permute-start.12) | collective-permute-done | bytes 163872 | tf_op jit(solution)/shard_map/ppermute | solution.py:15
  79.3 0.8 fusion.23
  80.0 3.4 %collective-permute-done.16 = bf16[80,1024]{1,0:T(8,128)(2,1)S(1)} collective-permute-done((bf16[80,1024]{1,0:T(8,128)(2,1)S(1)}, bf16[80,1024]{1,0:T(8,128)(2,1)S(1)}, u32[]{:S(2)}, u32[]{:S(2)}) %collective-permute-start.16) | collective-permute-done | bytes 163872 | tf_op jit(solution)/shard_map/ppermute | solution.py:15
  83.4 0.8 fusion.19
  (122 shorter events, 11.9 us)
Async XLA Ops:
  3.8 17.8 %collective-permute-start.3 = (bf16[80,1792]{1,0:T(8,128)(2,1)S(1)}, bf16[80,1792]{1,0:T(8,128)(2,1)S(1)}, u32[]{:S(2)}, u32[]{:S(2)}) collective-permute-start(bf16[80,1792]{1,0:T(8,128)(2,1)S(1)} %get-tuple-element.22), channel_id=1, source_target_pairs={{0,4},{4,0},{1,5},{5,1},{2,6},{6,2},{3,7},{7,3},{8,12},{12,8},{9,1... | collective-permute-start | bytes 860168 | tf_op jit(solution)/shard_map/ppermute | solution.py:15
  4.3 17.3 %collective-permute-start.4 = (bf16[80,1792]{1,0:T(8,128)(2,1)S(1)}, bf16[80,1792]{1,0:T(8,128)(2,1)S(1)}, u32[]{:S(2)}, u32[]{:S(2)}) collective-permute-start(bf16[80,1792]{1,0:T(8,128)(2,1)S(1)} %get-tuple-element.22), channel_id=1, source_target_pairs={{0,2},{2,0},{1,3},{3,1},{4,6},{6,4},{5,7},{7,5},{8,10},{10,8},{9,1... | collective-permute-start | bytes 860168 | tf_op jit(solution)/shard_map/ppermute | solution.py:15
  7.9 15.3 %collective-permute-start.6 = (bf16[80,1792]{1,0:T(8,128)(2,1)S(1)}, bf16[80,1792]{1,0:T(8,128)(2,1)S(1)}, u32[]{:S(2)}, u32[]{:S(2)}) collective-permute-start(bf16[80,1792]{1,0:T(8,128)(2,1)S(1)} %get-tuple-element.22), channel_id=1, source_target_pairs={{0,16},{16,0},{1,17},{17,1},{2,18},{18,2},{3,19},{19,3},{4,20},{20... | collective-permute-start | bytes 860168 | tf_op jit(solution)/shard_map/ppermute | solution.py:15
  11.2 13.7 %collective-permute-start = (bf16[80,1792]{1,0:T(8,128)(2,1)S(1)}, bf16[80,1792]{1,0:T(8,128)(2,1)S(1)}, u32[]{:S(2)}, u32[]{:S(2)}) collective-permute-start(bf16[80,1792]{1,0:T(8,128)(2,1)S(1)} %constant_dynamic-update-slice_fusion), channel_id=1, source_target_pairs={{0,1},{1,0},{2,3},{3,2},{4,5},{5,4},{6,7},{7,6},{8,9},{9,8},{10,11... | collective-permute-start | bytes 860168 | tf_op jit(solution)/shard_map/ppermute | solution.py:15
  12.9 21.0 %collective-permute-start.1 = (bf16[80,1792]{1,0:T(8,128)(2,1)S(1)}, bf16[80,1792]{1,0:T(8,128)(2,1)S(1)}, u32[]{:S(2)}, u32[]{:S(2)}) collective-permute-start(bf16[80,1792]{1,0:T(8,128)(2,1)S(1)} %constant_dynamic-update-slice_fusion), channel_id=1, source_target_pairs={{0,8},{8,0},{1,9},{9,1},{2,10},{10,2},{3,11},{11,3},{4,12},{12,4},... | collective-permute-start | bytes 860168 | tf_op jit(solution)/shard_map/ppermute | solution.py:15
  21.6 9.3 %collective-permute-start.5 = (bf16[80,1792]{1,0:T(8,128)(2,1)S(1)}, bf16[80,1792]{1,0:T(8,128)(2,1)S(1)}, u32[]{:S(2)}, u32[]{:S(2)}) collective-permute-start(bf16[80,1792]{1,0:T(8,128)(2,1)S(1)} %collective-permute-done.4), channel_id=1, source_target_pairs={{0,4},{4,0},{1,5},{5,1},{2,6},{6,2},{3,7},{7,3},{8,12},{12,8},{9,1... | collective-permute-start | bytes 860168 | tf_op jit(solution)/shard_map/ppermute | solution.py:15
  21.6 9.2 %collective-permute-start.8 = (bf16[80,1792]{1,0:T(8,128)(2,1)S(1)}, bf16[80,1792]{1,0:T(8,128)(2,1)S(1)}, u32[]{:S(2)}, u32[]{:S(2)}) collective-permute-start(bf16[80,1792]{1,0:T(8,128)(2,1)S(1)} %collective-permute-done.4), channel_id=1, source_target_pairs={{0,16},{16,0},{1,17},{17,1},{2,18},{18,2},{3,19},{19,3},{4,20},{20... | collective-permute-start | bytes 860168 | tf_op jit(solution)/shard_map/ppermute | solution.py:15
  23.2 9.2 %collective-permute-start.7 = (bf16[80,1792]{1,0:T(8,128)(2,1)S(1)}, bf16[80,1792]{1,0:T(8,128)(2,1)S(1)}, u32[]{:S(2)}, u32[]{:S(2)}) collective-permute-start(bf16[80,1792]{1,0:T(8,128)(2,1)S(1)} %collective-permute-done.6), channel_id=1, source_target_pairs={{0,4},{4,0},{1,5},{5,1},{2,6},{6,2},{3,7},{7,3},{8,12},{12,8},{9,1... | collective-permute-start | bytes 860168 | tf_op jit(solution)/shard_map/ppermute | solution.py:15
  25.0 8.9 %collective-permute-start.2 = (bf16[80,1792]{1,0:T(8,128)(2,1)S(1)}, bf16[80,1792]{1,0:T(8,128)(2,1)S(1)}, u32[]{:S(2)}, u32[]{:S(2)}) collective-permute-start(bf16[80,1792]{1,0:T(8,128)(2,1)S(1)} %collective-permute-done), channel_id=1, source_target_pairs={{0,8},{8,0},{1,9},{9,1},{2,10},{10,2},{3,11},{11,3},{4,12},{12,4},... | collective-permute-start | bytes 860168 | tf_op jit(solution)/shard_map/ppermute | solution.py:15
  30.9 3.1 %collective-permute-start.9 = (bf16[80,1792]{1,0:T(8,128)(2,1)S(1)}, bf16[80,1792]{1,0:T(8,128)(2,1)S(1)}, u32[]{:S(2)}, u32[]{:S(2)}) collective-permute-start(bf16[80,1792]{1,0:T(8,128)(2,1)S(1)} %collective-permute-done.8), channel_id=1, source_target_pairs={{0,4},{4,0},{1,5},{5,1},{2,6},{6,2},{3,7},{7,3},{8,12},{12,8},{9,1... | collective-permute-start | bytes 860168 | tf_op jit(solution)/shard_map/ppermute | solution.py:15
  41.5 8.0 %all-to-all-start = ((f32[4,4,320]{2,1,0:T(4,128)}), f32[4,4,320]{2,1,0:T(4,128)S(1)}, u32[]{:S(2)}, u32[]{:S(2)}) async-start(f32[4,4,320]{2,1,0:T(4,128)} %broadcast_in_dim.4), calls=%async_computation | async-start | bytes 49152 | tf_op jit(solution)/shard_map/all_to_all | solution.py:45
  50.1 12.1 %all-to-all-start.1 = ((f32[8,4,640]{2,1,0:T(4,128)}), f32[8,4,640]{2,1,0:T(4,128)S(1)}, u32[]{:S(2)}, u32[]{:S(2)}) async-start(f32[8,4,640]{2,1,0:T(4,128)} %broadcast_in_dim.5), calls=%async_computation.1 | async-start | bytes 163840 | tf_op jit(solution)/shard_map/all_to_all | solution.py:45
  62.8 1.7 %copy-start = (bf16[640,1792]{1,0:T(8,128)(2,1)S(1)}, bf16[640,1792]{1,0:T(8,128)(2,1)}, u32[]{:S(2)}) copy-start(bf16[640,1792]{1,0:T(8,128)(2,1)} %constant_dynamic-update-slice_fusion.4) | copy-start | bytes 6881284
  64.2 3.6 %collective-permute-start.13 = (bf16[2,2,80,1024]{3,2,1,0:T(8,128)(2,1)S(1)}, bf16[2,2,80,1024]{3,2,1,0:T(8,128)(2,1)S(1)}, u32[]{:S(2)}, u32[]{:S(2)}) collective-permute-start(bf16[2,2,80,1024]{3,2,1,0:T(8,128)(2,1)S(1)} %fusion.5), channel_id=1, source_target_pairs={{0,4},{4,0},{1,5},{5,1},{2,6},{6,2},{3,7},{7,3},{8,12},{12,8},{9,1... | collective-permute-start | bytes 1966088 | tf_op jit(solution)/shard_map/ppermute | solution.py:15
  65.7 7.1 %collective-permute-start.11 = (bf16[80,1024]{1,0:T(8,128)(2,1)S(1)}, bf16[80,1024]{1,0:T(8,128)(2,1)S(1)}, u32[]{:S(2)}, u32[]{:S(2)}) collective-permute-start(bf16[80,1024]{1,0:T(8,128)(2,1)S(1)} %get-tuple-element.19), channel_id=1, source_target_pairs={{0,8},{8,0},{1,9},{9,1},{2,10},{10,2},{3,11},{11,3},{4,12},{12,4},... | collective-permute-start | bytes 491528 | tf_op jit(solution)/shard_map/ppermute | solution.py:15
  66.3 9.3 %collective-permute-start.10 = (bf16[80,1024]{1,0:T(8,128)(2,1)S(1)}, bf16[80,1024]{1,0:T(8,128)(2,1)S(1)}, u32[]{:S(2)}, u32[]{:S(2)}) collective-permute-start(bf16[80,1024]{1,0:T(8,128)(2,1)S(1)} %get-tuple-element.18), channel_id=1, source_target_pairs={{0,8},{8,0},{1,9},{9,1},{2,10},{10,2},{3,11},{11,3},{4,12},{12,4},... | collective-permute-start | bytes 491528 | tf_op jit(solution)/shard_map/ppermute | solution.py:15
  68.1 5.9 %collective-permute-start.15 = (bf16[80,1024]{1,0:T(8,128)(2,1)S(1)}, bf16[80,1024]{1,0:T(8,128)(2,1)S(1)}, u32[]{:S(2)}, u32[]{:S(2)}) collective-permute-start(bf16[80,1024]{1,0:T(8,128)(2,1)S(1)} %get-tuple-element.17), channel_id=1, source_target_pairs={{0,16},{16,0},{1,17},{17,1},{2,18},{18,2},{3,19},{19,3},{4,20},{20... | collective-permute-start | bytes 491528 | tf_op jit(solution)/shard_map/ppermute | solution.py:15
  72.8 6.5 %collective-permute-start.12 = (bf16[80,1024]{1,0:T(8,128)(2,1)S(1)}, bf16[80,1024]{1,0:T(8,128)(2,1)S(1)}, u32[]{:S(2)}, u32[]{:S(2)}) collective-permute-start(bf16[80,1024]{1,0:T(8,128)(2,1)S(1)} %fusion.21), channel_id=1, source_target_pairs={{0,1},{1,0},{2,3},{3,2},{4,5},{5,4},{6,7},{7,6},{8,9},{9,8},{10,11... | collective-permute-start | bytes 491528 | tf_op jit(solution)/shard_map/ppermute | solution.py:15
  72.9 7.2 %collective-permute-start.14 = (bf16[80,1024]{1,0:T(8,128)(2,1)S(1)}, bf16[80,1024]{1,0:T(8,128)(2,1)S(1)}, u32[]{:S(2)}, u32[]{:S(2)}) collective-permute-start(bf16[80,1024]{1,0:T(8,128)(2,1)S(1)} %get-tuple-element.16), channel_id=1, source_target_pairs={{0,16},{16,0},{1,17},{17,1},{2,18},{18,2},{3,19},{19,3},{4,20},{20... | collective-permute-start | bytes 491528 | tf_op jit(solution)/shard_map/ppermute | solution.py:15
  74.0 9.4 %collective-permute-start.16 = (bf16[80,1024]{1,0:T(8,128)(2,1)S(1)}, bf16[80,1024]{1,0:T(8,128)(2,1)S(1)}, u32[]{:S(2)}, u32[]{:S(2)}) collective-permute-start(bf16[80,1024]{1,0:T(8,128)(2,1)S(1)} %fusion.17), channel_id=1, source_target_pairs={{0,2},{2,0},{1,3},{3,1},{4,6},{6,4},{5,7},{7,5},{8,10},{10,8},{9,1... | collective-permute-start | bytes 491528 | tf_op jit(solution)/shard_map/ppermute | solution.py:15

commit v2 on v1

v2 whole, which is shorter than its diff:
```python
import functools
import math

import jax
import jax.numpy as jnp
from jax import lax
from jax.experimental import pallas as pl
from jax.experimental.pallas import tpu as pltpu
from jax.sharding import Mesh, PartitionSpec as P

logit_gain = 3.0
ROW_AXES = ("ilo", "clo")
COL_AXES = ("core", "ihi", "chi")
LANES = 128
PEAK_S, TOTAL_S, PEAK_T, TOTAL_T, INDEX = range(5)


def swap(value, axis, mask):
    size = lax.axis_size(axis)
    return lax.ppermute(value, axis, [(j, j ^ mask) for j in range(size)])


def bits(axis):
    size = lax.axis_size(axis)
    return [1 << b for b in range(size.bit_length() - 1)]


def joined(refs):
    parts = [ref[...] for ref in refs]
    return parts[0] if len(parts) == 1 else jnp.concatenate(parts, axis=0)


def lines_of(columns):
    count = columns[0].shape[0]
    lane = lax.broadcasted_iota(jnp.int32, (count, LANES), 1)
    wide = jnp.zeros((count, LANES), jnp.float32)
    for k, column in enumerate(columns):
        wide = jnp.where(lane == k, column, wide)
    spare = -count % LANES
    if spare:
        wide = jnp.concatenate([wide, jnp.zeros((spare, LANES), jnp.float32)], axis=0)
    return wide.T[:8, :count]


def columns_of(lines):
    count = lines.shape[1]
    spare = -count % LANES
    if spare:
        lines = jnp.concatenate([lines, jnp.zeros((8, spare), jnp.float32)], axis=1)
    tall = jnp.concatenate([lines, jnp.zeros((LANES - 8, count + spare), jnp.float32)], axis=0)
    return tall.T[:count]


def store_slots(ref, lines, rows):
    ref[...] = jnp.zeros_like(ref)
    for s in range(ref.shape[0]):
        ref[s, :, :rows] = lines[:, s * rows : (s + 1) * rows]


def load_slots(ref, rows):
    return jnp.concatenate([ref[s, :, :rows] for s in range(ref.shape[0])], axis=1)


def logits_kernel(counts, rows, *refs):
    groups, start = [], 0
    for count in counts:
        groups.append(refs[start : start + count])
        start += count
    img_s, img_t, cap_s, cap_t = groups
    student_ref, teacher_ref, row_ref, col_ref = refs[start:]
    row_columns, col_lines = [], []
    for left, right, out in ((img_t, cap_t, teacher_ref), (img_s, cap_s, student_ref)):
        left, right = joined(left), joined(right)
        gain = logit_gain / math.sqrt(left.shape[1])
        out[...] = gain * lax.dot_general(
            left, right, (((1,), (1,)), ((), ())), preferred_element_type=jnp.float32
        )
        matrix = out[...]
        peak = jnp.max(matrix, axis=1, keepdims=True)
        row_columns = [peak, jnp.sum(jnp.exp(matrix - peak), axis=1, keepdims=True)] + row_columns
        peak = jnp.max(matrix, axis=0, keepdims=True)
        col_lines = [peak, jnp.sum(jnp.exp(matrix - peak), axis=0, keepdims=True)] + col_lines
    store_slots(row_ref, lines_of(row_columns), rows)
    blank = jnp.zeros((4, col_lines[0].shape[1]), jnp.float32)
    store_slots(col_ref, jnp.concatenate(col_lines + [blank], axis=0), rows)


def tile_kernel(n_img, rows, *refs):
    student_ref, teacher_ref, row_ref, row_id_ref, col_ref, col_id_ref = refs[:6]
    images = refs[6 : 6 + n_img]
    tile_ref, held_ref, sent_ref = refs[6 + n_img :]

    def finish(ref, id_ref):
        lines = load_slots(ref, rows)
        ids = load_slots(id_ref, rows)
        line = lax.broadcasted_iota(jnp.int32, lines.shape, 0)
        lse_s = lines[PEAK_S : PEAK_S + 1] + jnp.log(lines[TOTAL_S : TOTAL_S + 1])
        lse_t = lines[PEAK_T : PEAK_T + 1] + jnp.log(lines[TOTAL_T : TOTAL_T + 1])
        return jnp.where(line == 0, lse_s, jnp.where(line == 1, lse_t, ids))

    across = finish(col_ref, col_id_ref)
    down = columns_of(finish(row_ref, row_id_ref))
    total = student_ref.shape[0]
    step = 64 if total % 64 == 0 else total
    for r in range(0, total, step):
        at = slice(r, r + step)
        s, t = student_ref[at], teacher_ref[at]
        grad = 0.5 * (jnp.exp(s - down[at, 0:1]) + jnp.exp(s - across[0:1]))
        grad = grad - 0.25 * (jnp.exp(t - down[at, 1:2]) + jnp.exp(t - across[1:2]))
        grad = grad - jnp.where(down[at, INDEX : INDEX + 1] == across[INDEX : INDEX + 1], 0.5, 0.0)
        tile_ref[at] = grad.astype(jnp.bfloat16)
    part = lax.dot_general(
        tile_ref[...], joined(images), (((0,), (0,)), ((), ())), preferred_element_type=jnp.float32
    )
    held = held_ref.shape[0]
    held_ref[...] = part[:held]
    sent_ref[...] = part[held:].astype(jnp.bfloat16)


def image_kernel(tile_ref, *refs):
    held_ref, sent_ref = refs[-2:]
    part = jnp.dot(tile_ref[...], joined(refs[:-2]), preferred_element_type=jnp.float32)
    held = held_ref.shape[0]
    held_ref[...] = part[:held]
    sent_ref[...] = part[held:].astype(jnp.bfloat16)


def call(kernel, outs, args, flops):
    moved = sum(math.prod(a.shape) * a.dtype.itemsize for a in list(args) + list(outs))
    return pl.pallas_call(
        kernel,
        out_shape=outs,
        in_specs=[pl.BlockSpec(memory_space=pltpu.VMEM)] * len(args),
        out_specs=[pl.BlockSpec(memory_space=pltpu.VMEM)] * len(outs),
        compiler_params=pltpu.CompilerParams(vmem_limit_bytes=32 * 2**20),
        cost_estimate=pl.CostEstimate(flops=flops, bytes_accessed=moved, transcendentals=0),
    )(*args)


def merge(one, two):
    result = []
    for k in (PEAK_S, PEAK_T):
        peak = jnp.maximum(one[..., k, :], two[..., k, :])
        result.append(peak)
        result.append(
            one[..., k + 1, :] * jnp.exp(one[..., k, :] - peak) + two[..., k + 1, :] * jnp.exp(two[..., k, :] - peak)
        )
    result += [jnp.zeros_like(result[0])] * 4
    return jnp.stack(result, axis=-2)


def pool_step(stats, axes, d, bit):
    shape = tuple(lax.axis_size(a) for a in axes)
    other = swap(stats, axes[d], bit)
    before = math.prod(shape[:d]) * (shape[d] // (2 * bit))
    after = bit * math.prod(shape[d + 1 :])
    other = jnp.flip(other.reshape((before, 2, after) + stats.shape[1:]), axis=1).reshape(stats.shape)
    return merge(stats, other)


def owners(axes):
    result = {}
    for d, axis in enumerate(axes):
        index = lax.axis_index(axis) ^ jnp.arange(lax.axis_size(axis), dtype=jnp.int32)
        result[axis] = index.reshape([-1 if e == d else 1 for e in range(len(axes))])
    return result


def identity_block(axes, order, rows):
    place = {a: lax.axis_index(a) for a in order}
    place.update(owners(axes))
    owner = 0
    for axis in order:
        owner = owner * lax.axis_size(axis) + place[axis]
    index = owner.reshape(-1, 1, 1) * rows + jnp.arange(LANES, dtype=jnp.int32)[None, None, :]
    line = jnp.arange(8, dtype=jnp.int32)[None, :, None]
    return jnp.where(line == INDEX, index, 0).astype(jnp.float32)


def local(image_student, caption_student, image_teacher, caption_teacher):
    ilo, clo, core, ihi, chi = (lax.axis_size(a) for a in ROW_AXES + COL_AXES)
    rows, width = image_student.shape
    assert rows <= LANES and core == 2
    n_img, n_cap = ilo * clo, core * ihi * chi
    total, columns = n_img * rows, n_cap * rows

    def gather_images(own):
        far = [own] + [swap(own, "clo", m) for m in range(1, clo)]
        return far + [swap(part, "ilo", m) for m in range(1, ilo) for part in far]

    def gather_captions(own):
        far = [own] + [swap(own, "chi", m) for m in range(1, chi)]
        far = far + [swap(part, "ihi", m) for m in range(1, ihi) for part in far]
        return far + [swap(part, "core", 1) for part in far]

    def shards(parts):
        return parts if rows % 16 == 0 else [jnp.concatenate(parts, axis=0)]

    img_t, cap_t = shards(gather_images(image_teacher)), shards(gather_captions(caption_teacher))
    img_s, cap_s = shards(gather_images(image_student)), shards(gather_captions(caption_student))

    f32, bf16 = jnp.float32, jnp.bfloat16
    shape = jax.ShapeDtypeStruct
    student, teacher, row_stats, col_stats = call(
        functools.partial(logits_kernel, [len(g) for g in (img_s, img_t, cap_s, cap_t)], rows),
        [
            shape((total, columns), f32),
            shape((total, columns), f32),
            shape((n_img, 8, LANES), f32),
            shape((n_cap, 8, LANES), f32),
        ],
        img_s + img_t + cap_s + cap_t,
        2 * total * columns * (width + image_teacher.shape[1]),
    )
    for d, axis in enumerate(ROW_AXES):
        for bit in bits(axis):
            row_stats = pool_step(row_stats, ROW_AXES, d, bit)
    for d, axis in enumerate(COL_AXES):
        for bit in bits(axis):
            col_stats = pool_step(col_stats, COL_AXES, d, bit)
    row_ids = identity_block(ROW_AXES, ("ihi", "ilo", "core", "chi", "clo"), rows)
    col_ids = identity_block(COL_AXES, ("chi", "clo", "ihi", "ilo", "core"), rows)

    tile, held, sent = call(
        functools.partial(tile_kernel, len(img_s), rows),
        [shape((total, columns), bf16), shape((columns // 2, width), f32), shape((columns // 2, width), bf16)],
        [student, teacher, row_stats, row_ids, col_stats, col_ids] + img_s,
        2 * total * columns * width,
    )
    image_held, image_sent = call(
        image_kernel,
        [shape((total // ilo, width), f32), shape((total - total // ilo, width), bf16)],
        [tile] + cap_s,
        2 * total * columns * width,
    )

    def collect(held, sent, near, far):
        near, far, count = near, far, held.shape[0]
        held = [held[f] for f in range(count)]
        for f in reversed(range(count)):
            for m in range(1, lax.axis_size(near)):
                held[f] = held[f] + swap(sent[m - 1, f], near, m).astype(f32)
        result = held[0]
        for f in range(1, count):
            result = result + swap(held[f].astype(bf16), far, f).astype(f32)
        return result

    pair = (held + swap(sent, "core", 1).astype(f32)).reshape(ihi, chi, rows, width)
    caption_grad = collect(pair[0], pair[1:].astype(bf16), "ihi", "chi")
    image_grad = collect(
        image_held.reshape(clo, rows, width), image_sent.reshape(ilo - 1, clo, rows, width), "ilo", "clo"
    )
    return (image_grad, caption_grad)


def split(count):
    low = 1 << ((count.bit_length() - 1) // 2)
    return count // low, low


def solution(mesh):
    ihi, ilo = split(mesh.shape["img"] // 2)
    chi, clo = split(mesh.shape["cap"])
    fine = Mesh(mesh.devices.reshape(ihi, ilo, 2, chi, clo), ("ihi", "ilo", "core", "chi", "clo"))
    by_image = P(("ihi", "ilo", "core", "chi", "clo"), None)
    by_caption = P(("chi", "clo", "ihi", "ilo", "core"), None)
    return jax.shard_map(
        local,
        mesh=fine,
        in_specs=(by_image, by_caption, by_image, by_caption),
        out_specs=(by_image, by_caption),
        check_vma=False,
    )
```

time: 84.6 us -> 91.4 us (1.080)
  matrix products: 6.33 us -> 0 us
  local copies, waits for them, and re-layouts: 14.1 us -> 20.1 us
  Pallas kernels: 0 us -> 3.88 us
  waiting for transfers between devices: 34.2 us -> 35.7 us
  starting transfers between devices: 24.9 us -> 26.3 us
    ppermute x17 -> x32, waiting for transfers between devices: 23.3 us -> 35.7 us  [swap(): return lax.ppermute(value, axis, [(j, j ^ mask) for j in range(size)])]
    all_to_all x2 -> x0, waiting for transfers between devices: 10.9 us -> none  [pool(): lax.all_to_all(jnp.broadcast_to(mine[None], (count,) + mine.shape), axes,...]
    unnamed x18 -> x60, local copies, waits for them, and re-layouts: 7.23 us -> 17.6 us
    ppermute x17 -> x32, starting transfers between devices: 16.4 us -> 26.3 us  [swap(): return lax.ppermute(value, axis, [(j, j ^ mask) for j in range(size)])]
    all_to_all x2 -> x0, starting transfers between devices: 8.55 us -> none  [pool(): lax.all_to_all(jnp.broadcast_to(mine[None], (count,) + mine.shape), axes,...]
    dot_general x4 -> x0, matrix products: 6.33 us -> none  [the longest x2 4 us: scores(): lax.dot_general(left, right, (((1,), (1,)), ((), ())), preferred_element_...]
    pallas_call x0 -> x3, Pallas kernels: none -> 3.88 us  [call(): pl.pallas_call(kernel, out_shape=outs, in_specs=[pl.BlockSpec(memory_spac...]
    concatenate x3 -> x0, local copies, waits for them, and re-layouts: 3.26 us -> none  [the longest x1 1.57 us: local(): caption = jnp.concatenate([caption_student, caption_teacher], axis=1)]
  transfers between devices with their start and end apart: 19 -> 32, of which waited for: 10 -> 12; matrix products, arithmetic and copies ran while one was open for 12% -> 2% of each run, Pallas kernels for 0% -> 1%
where the time goes in v2:
time: 91.4 us; the launch traced here: 90.8 us
  waiting for transfers between devices  35.7 us (39%)
  starting transfers between devices  26.3 us (29%)
  local copies, waits for them, and re-layouts  20.1 us (22%)
  Pallas kernels  3.88 us (4%)
  other arithmetic  3.81 us (4%)
  between operations  0.97 us (1%)
    ppermute x32, waiting for transfers between devices, swap(): return lax.ppermute(value, axis, [(j, j ^ mask) for j in range(size)])  35.7 us
    ppermute x32, starting transfers between devices, swap(): return lax.ppermute(value, axis, [(j, j ^ mask) for j in range(size)])  26.3 us
    unnamed x60, local copies, waits for them, and re-layouts  17.6 us
    pallas_call x3, Pallas kernels, call(): pl.pallas_call(kernel, out_shape=outs, in_specs=[pl.BlockSpec(memory_spac...  3.88 us
  transfers between devices with their start and end apart: 32, of which 12 were waited for; matrix products, arithmetic and copies ran while one was open for 2% of the time, Pallas kernels for 1%

profile of v2, /device:TPU:0, one launch (start us, length us, event | category | flops | bytes accessed | tf_op | source)
XLA Modules:
  0.0 90.8 jit_solution(17751011523523170388)
XLA Ops:
  0.6 3.1 %collective-permute-start.3 = (bf16[80,768]{1,0:T(8,128)(2,1)}, bf16[80,768]{1,0:T(8,128)(2,1)S(1)}, u32[]{:S(2)}, u32[]{:S(2)}) collective-permute-start(bf16[80,768]{1,0:T(8,128)(2,1)} %refs_4_.1), channel_id=1, source_target_pairs={{0,1},{1,0},{2,3},{3,2},{4,5},{5,4},{6,7},{7,6},{8,9},{9,8},{10,11... | collective-permute-start | bytes 368648 | tf_op jit(solution)/shard_map/ppermute | solution.py:20
  3.7 1.5 %collective-permute-start.4 = (bf16[80,768]{1,0:T(8,128)(2,1)}, bf16[80,768]{1,0:T(8,128)(2,1)S(1)}, u32[]{:S(2)}, u32[]{:S(2)}) collective-permute-start(bf16[80,768]{1,0:T(8,128)(2,1)} %refs_4_.1), channel_id=1, source_target_pairs={{0,8},{8,0},{1,9},{9,1},{2,10},{10,2},{3,11},{11,3},{4,12},{12,4},... | collective-permute-start | bytes 368648 | tf_op jit(solution)/shard_map/ppermute | solution.py:20
  5.2 1.5 %collective-permute-start.14 = (bf16[80,768]{1,0:T(8,128)(2,1)}, bf16[80,768]{1,0:T(8,128)(2,1)S(1)}, u32[]{:S(2)}, u32[]{:S(2)}) collective-permute-start(bf16[80,768]{1,0:T(8,128)(2,1)} %refs_16_.1), channel_id=1, source_target_pairs={{0,16},{16,0},{1,17},{17,1},{2,18},{18,2},{3,19},{19,3},{4,20},{20... | collective-permute-start | bytes 368648 | tf_op jit(solution)/shard_map/ppermute | solution.py:20
  6.7 2.6 %collective-permute-start.13 = (bf16[80,768]{1,0:T(8,128)(2,1)}, bf16[80,768]{1,0:T(8,128)(2,1)S(1)}, u32[]{:S(2)}, u32[]{:S(2)}) collective-permute-start(bf16[80,768]{1,0:T(8,128)(2,1)} %refs_16_.1), channel_id=1, source_target_pairs={{0,2},{2,0},{1,3},{3,1},{4,6},{6,4},{5,7},{7,5},{8,10},{10,8},{9,1... | collective-permute-start | bytes 368648 | tf_op jit(solution)/shard_map/ppermute | solution.py:20
  11.2 3.5 %collective-permute-done.13.refs_17_ = bf16[80,768]{1,0:T(8,128)(2,1)S(1)} collective-permute-done((bf16[80,768]{1,0:T(8,128)(2,1)}, bf16[80,768]{1,0:T(8,128)(2,1)S(1)}, u32[]{:S(2)}, u32[]{:S(2)}) %collective-permute-start.13) | collective-permute-done | bytes 122912 | tf_op jit(solution)/shard_map/ppermute | solution.py:20
  15.9 1.1 %collective-permute-start.6 = (bf16[80,1024]{1,0:T(8,128)(2,1)}, bf16[80,1024]{1,0:T(8,128)(2,1)S(1)}, u32[]{:S(2)}, u32[]{:S(2)}) collective-permute-start(bf16[80,1024]{1,0:T(8,128)(2,1)} %refs_0_.3), channel_id=1, source_target_pairs={{0,2},{2,0},{1,3},{3,1},{4,6},{6,4},{5,7},{7,5},{8,10},{10,8},{9,1... | collective-permute-start | bytes 491528 | tf_op jit(solution)/shard_map/ppermute | solution.py:20
  17.1 1.1 %collective-permute-done.refs_1_.refs_7_ = bf16[80,1024]{1,0:T(8,128)(2,1)S(1)} collective-permute-done((bf16[80,1024]{1,0:T(8,128)(2,1)}, bf16[80,1024]{1,0:T(8,128)(2,1)S(1)}, u32[]{:S(2)}, u32[]{:S(2)}) %collective-permute-start) | collective-permute-done | bytes 163872 | tf_op jit(solution)/shard_map/ppermute | solution.py:20
  21.3 4.0 %collective-permute-done.6.refs_9_.refs_1_ = bf16[80,1024]{1,0:T(8,128)(2,1)S(1)} collective-permute-done((bf16[80,1024]{1,0:T(8,128)(2,1)}, bf16[80,1024]{1,0:T(8,128)(2,1)S(1)}, u32[]{:S(2)}, u32[]{:S(2)}) %collective-permute-start.6) | collective-permute-done | bytes 163872 | tf_op jit(solution)/shard_map/ppermute | solution.py:20
  25.3 1.3 %collective-permute-start.8 = (bf16[80,1024]{1,0:T(8,128)(2,1)S(1)}, bf16[80,1024]{1,0:T(8,128)(2,1)S(1)}, u32[]{:S(2)}, u32[]{:S(2)}) collective-permute-start(bf16[80,1024]{1,0:T(8,128)(2,1)S(1)} %collective-permute-done.6.refs_9_.refs_1_), channel_id=1, source_target_pairs={{0,16},{16,0},{1,17},{17,1},{2,18},{18,2},{3,19},{19,3},{4,20},{20... | collective-permute-start | bytes 491528 | tf_op jit(solution)/shard_map/ppermute | solution.py:20
  31.3 3.4 %collective-permute-done.2.refs_3_.refs_9_ = bf16[80,1024]{1,0:T(8,128)(2,1)S(1)} collective-permute-done((bf16[80,1024]{1,0:T(8,128)(2,1)S(1)}, bf16[80,1024]{1,0:T(8,128)(2,1)S(1)}, u32[]{:S(2)}, u32[]{:S(2)}) %collective-permute-start.2) | collective-permute-done | bytes 163872 | tf_op jit(solution)/shard_map/ppermute | solution.py:20
  34.7 0.9 copy-done
  35.6 0.9 %copy-done.2 = bf16[80,1024]{1,0:T(8,128)(2,1)S(1)} copy-done((bf16[80,1024]{1,0:T(8,128)(2,1)S(1)}, bf16[80,1024]{1,0:T(8,128)(2,1)}, u32[]{:S(2)}) %copy-start.2) | copy-done | bytes 163864
  36.5 0.9 copy-done.6
  37.4 0.9 copy-done.7
  39.2 0.9 copy-done.11
  40.2 0.9 copy-done.13
  41.1 0.9 copy-done.15
  42.9 0.9 copy-done.19
  46.5 1.5 %shard_map.59 = (f32[320,640]{1,0:T(8,128)S(1)}, f32[320,640]{1,0:T(8,128)S(1)}, f32[4,8,128]{2,1,0:T(8,128)S(1)}, f32[8,8,128]{2,1,0:T(8,128)S(1)}) custom-call(bf16[80,1024]{1,0:T(8,128)(2,1)S(1)} %copy-done, bf16[80,1024]{1,0:T(8,128)(2,1)S(1)} %collective-permute-done.refs_1_.refs_7_, bf16[80,1024]{1,0:T(8,128)(2,1)S(1)} %collective-permute-done.1.refs_2_.refs_8_, ...), custom_call_target="tpu_custom_call" | custom-call | flops 734003200 | bytes 5128192 | tf_op jit(solution)/shard_map/pallas_call | solution.py:130
  49.0 2.9 %collective-permute-done.20 = f32[4,8,128]{2,1,0:T(8,128)S(1)} collective-permute-done((f32[4,8,128]{2,1,0:T(8,128)S(1)}, f32[4,8,128]{2,1,0:T(8,128)S(1)}, u32[]{:S(2)}, u32[]{:S(2)}) %collective-permute-start.20) | collective-permute-done | bytes 16416 | tf_op jit(solution)/shard_map/ppermute | solution.py:20
  53.0 2.8 %collective-permute-done.21 = f32[4,8,128]{2,1,0:T(8,128)S(1)} collective-permute-done((f32[4,8,128]{2,1,0:T(8,128)S(1)}, f32[4,8,128]{2,1,0:T(8,128)S(1)}, u32[]{:S(2)}, u32[]{:S(2)}) %collective-permute-start.21) | collective-permute-done | bytes 16416 | tf_op jit(solution)/shard_map/ppermute | solution.py:20
  56.8 2.3 %collective-permute-start.24 = (f32[8,8,128]{2,1,0:T(8,128)}, f32[8,8,128]{2,1,0:T(8,128)}, u32[]{:S(2)}, u32[]{:S(2)}) collective-permute-start(f32[8,8,128]{2,1,0:T(8,128)} %stack.13), channel_id=1, source_target_pairs={{0,2},{2,0},{1,3},{3,1},{4,6},{6,4},{5,7},{7,5},{8,10},{10,8},{9,1... | collective-permute-start | bytes 98312 | tf_op jit(solution)/shard_map/ppermute | solution.py:20
  59.2 2.8 %collective-permute-done.24 = f32[8,8,128]{2,1,0:T(8,128)} collective-permute-done((f32[8,8,128]{2,1,0:T(8,128)}, f32[8,8,128]{2,1,0:T(8,128)}, u32[]{:S(2)}, u32[]{:S(2)}) %collective-permute-start.24) | collective-permute-done | bytes 32800 | tf_op jit(solution)/shard_map/ppermute | solution.py:20
  62.7 1.3 %fusion.2 = (f32[8,1,128]{2,1,0:T(1,128)}, f32[8,1,128]{2,1,0:T(1,128)}, f32[8,1,128]{2,1,0:T(1,128)}, f32[8,1,128]{2,1,0:T(1,128)}) fusion(f32[8,8,128]{2,1,0:T(8,128)S(1)} %bitcast.23, f32[8,1,128]{2,1,0:T(1,128)} %copy-done.26, f32[8,1,128]{2,1,0:T(1,128)} %copy-done.27, f32[8,1,128]{2,1,0:T(1,128)} %copy-done.29, f32[8,1,128]{2,1,0:T(1,128)} %copy-done.28), kind=kLoop, calls=%fused_computation.15 | loop fusion | flops 12288 | bytes 49152 | tf_op jit(solution)/shard_map/add | solution.py:146
  64.8 1.7 %shard_map.60 = (bf16[320,640]{1,0:T(8,128)(2,1)S(1)}, f32[320,1024]{1,0:T(8,128)S(1)}, bf16[320,1024]{1,0:T(8,128)(2,1)S(1)}) custom-call(f32[320,640]{1,0:T(8,128)S(1)} %get-tuple-element.11.refs_0_, f32[320,640]{1,0:T(8,128)S(1)} %get-tuple-element.12.refs_1_, f32[4,8,128]{2,1,0:T(8,128)S(1)} %stack.11.refs_2_, ...), custom_call_target="tpu_custom_call" | custom-call | flops 419430400 | bytes 4767744 | tf_op jit(solution)/shard_map/pallas_call | solution.py:130
  68.2 1.2 %collective-permute-start.26 = (bf16[80,1024]{1,0:T(8,128)(2,1)S(1)}, bf16[80,1024]{1,0:T(8,128)(2,1)S(1)}, u32[]{:S(2)}, u32[]{:S(2)}) collective-permute-start(bf16[80,1024]{1,0:T(8,128)(2,1)S(1)} %get-tuple-element.35), channel_id=1, source_target_pairs={{0,8},{8,0},{1,9},{9,1},{2,10},{10,2},{3,11},{11,3},{4,12},{12,4},... | collective-permute-start | bytes 491528 | tf_op jit(solution)/shard_map/ppermute | solution.py:20
  69.7 1.0 %collective-permute-start.30 = (bf16[80,1024]{1,0:T(8,128)(2,1)S(1)}, bf16[80,1024]{1,0:T(8,128)(2,1)S(1)}, u32[]{:S(2)}, u32[]{:S(2)}) collective-permute-start(bf16[80,1024]{1,0:T(8,128)(2,1)S(1)} %get-tuple-element.33), channel_id=1, source_target_pairs={{0,16},{16,0},{1,17},{17,1},{2,18},{18,2},{3,19},{19,3},{4,20},{20... | collective-permute-start | bytes 491528 | tf_op jit(solution)/shard_map/ppermute | solution.py:20
  70.7 6.8 %collective-permute-done.26 = bf16[80,1024]{1,0:T(8,128)(2,1)S(1)} collective-permute-done((bf16[80,1024]{1,0:T(8,128)(2,1)S(1)}, bf16[80,1024]{1,0:T(8,128)(2,1)S(1)}, u32[]{:S(2)}, u32[]{:S(2)}) %collective-permute-start.26) | collective-permute-done | bytes 163872 | tf_op jit(solution)/shard_map/ppermute | solution.py:20
  77.5 2.1 %collective-permute-start.27 = (bf16[80,1024]{1,0:T(8,128)(2,1)S(1)}, bf16[80,1024]{1,0:T(8,128)(2,1)S(1)}, u32[]{:S(2)}, u32[]{:S(2)}) collective-permute-start(bf16[80,1024]{1,0:T(8,128)(2,1)S(1)} %add_convert_fusion), channel_id=1, source_target_pairs={{0,1},{1,0},{2,3},{3,2},{4,5},{5,4},{6,7},{7,6},{8,9},{9,8},{10,11... | collective-permute-start | bytes 491528 | tf_op jit(solution)/shard_map/ppermute | solution.py:20
  80.3 1.3 %collective-permute-start.31 = (bf16[80,1024]{1,0:T(8,128)(2,1)S(1)}, bf16[80,1024]{1,0:T(8,128)(2,1)S(1)}, u32[]{:S(2)}, u32[]{:S(2)}) collective-permute-start(bf16[80,1024]{1,0:T(8,128)(2,1)S(1)} %fusion), channel_id=1, source_target_pairs={{0,2},{2,0},{1,3},{3,1},{4,6},{6,4},{5,7},{7,5},{8,10},{10,8},{9,1... | collective-permute-start | bytes 491528 | tf_op jit(solution)/shard_map/ppermute | solution.py:20
  81.7 3.4 %collective-permute-done.27 = bf16[80,1024]{1,0:T(8,128)(2,1)S(1)} collective-permute-done((bf16[80,1024]{1,0:T(8,128)(2,1)S(1)}, bf16[80,1024]{1,0:T(8,128)(2,1)S(1)}, u32[]{:S(2)}, u32[]{:S(2)}) %collective-permute-start.27) | collective-permute-done | bytes 163872 | tf_op jit(solution)/shard_map/ppermute | solution.py:20
  85.8 4.2 %collective-permute-done.31 = bf16[80,1024]{1,0:T(8,128)(2,1)S(1)} collective-permute-done((bf16[80,1024]{1,0:T(8,128)(2,1)S(1)}, bf16[80,1024]{1,0:T(8,128)(2,1)S(1)}, u32[]{:S(2)}, u32[]{:S(2)}) %collective-permute-start.31) | collective-permute-done | bytes 163872 | tf_op jit(solution)/shard_map/ppermute | solution.py:20
  (133 shorter events, 24.3 us)
Async XLA Ops:
  0.6 9.0 %collective-permute-start.3 = (bf16[80,768]{1,0:T(8,128)(2,1)}, bf16[80,768]{1,0:T(8,128)(2,1)S(1)}, u32[]{:S(2)}, u32[]{:S(2)}) collective-permute-start(bf16[80,768]{1,0:T(8,128)(2,1)} %refs_4_.1), channel_id=1, source_target_pairs={{0,1},{1,0},{2,3},{3,2},{4,5},{5,4},{6,7},{7,6},{8,9},{9,8},{10,11... | collective-permute-start | bytes 368648 | tf_op jit(solution)/shard_map/ppermute | solution.py:20
  3.7 6.4 %collective-permute-start.4 = (bf16[80,768]{1,0:T(8,128)(2,1)}, bf16[80,768]{1,0:T(8,128)(2,1)S(1)}, u32[]{:S(2)}, u32[]{:S(2)}) collective-permute-start(bf16[80,768]{1,0:T(8,128)(2,1)} %refs_4_.1), channel_id=1, source_target_pairs={{0,8},{8,0},{1,9},{9,1},{2,10},{10,2},{3,11},{11,3},{4,12},{12,4},... | collective-permute-start | bytes 368648 | tf_op jit(solution)/shard_map/ppermute | solution.py:20
  5.2 6.0 %collective-permute-start.14 = (bf16[80,768]{1,0:T(8,128)(2,1)}, bf16[80,768]{1,0:T(8,128)(2,1)S(1)}, u32[]{:S(2)}, u32[]{:S(2)}) collective-permute-start(bf16[80,768]{1,0:T(8,128)(2,1)} %refs_16_.1), channel_id=1, source_target_pairs={{0,16},{16,0},{1,17},{17,1},{2,18},{18,2},{3,19},{19,3},{4,20},{20... | collective-permute-start | bytes 368648 | tf_op jit(solution)/shard_map/ppermute | solution.py:20
  6.7 8.0 %collective-permute-start.13 = (bf16[80,768]{1,0:T(8,128)(2,1)}, bf16[80,768]{1,0:T(8,128)(2,1)S(1)}, u32[]{:S(2)}, u32[]{:S(2)}) collective-permute-start(bf16[80,768]{1,0:T(8,128)(2,1)} %refs_16_.1), channel_id=1, source_target_pairs={{0,2},{2,0},{1,3},{3,1},{4,6},{6,4},{5,7},{7,5},{8,10},{10,8},{9,1... | collective-permute-start | bytes 368648 | tf_op jit(solution)/shard_map/ppermute | solution.py:20
  9.3 5.9 %collective-permute-start.16 = (bf16[80,768]{1,0:T(8,128)(2,1)}, bf16[80,768]{1,0:T(8,128)(2,1)S(1)}, u32[]{:S(2)}, u32[]{:S(2)}) collective-permute-start(bf16[80,768]{1,0:T(8,128)(2,1)} %refs_16_.1), channel_id=1, source_target_pairs={{0,4},{4,0},{1,5},{5,1},{2,6},{6,2},{3,7},{7,3},{8,12},{12,8},{9,1... | collective-permute-start | bytes 368648 | tf_op jit(solution)/shard_map/ppermute | solution.py:20
  9.6 7.5 %collective-permute-start.1 = (bf16[80,1024]{1,0:T(8,128)(2,1)}, bf16[80,1024]{1,0:T(8,128)(2,1)S(1)}, u32[]{:S(2)}, u32[]{:S(2)}) collective-permute-start(bf16[80,1024]{1,0:T(8,128)(2,1)} %refs_6_.1), channel_id=1, source_target_pairs={{0,8},{8,0},{1,9},{9,1},{2,10},{10,2},{3,11},{11,3},{4,12},{12,4},... | collective-permute-start | bytes 491528 | tf_op jit(solution)/shard_map/ppermute | solution.py:20
  10.8 7.4 %collective-permute-start = (bf16[80,1024]{1,0:T(8,128)(2,1)}, bf16[80,1024]{1,0:T(8,128)(2,1)S(1)}, u32[]{:S(2)}, u32[]{:S(2)}) collective-permute-start(bf16[80,1024]{1,0:T(8,128)(2,1)} %refs_6_.1), channel_id=1, source_target_pairs={{0,1},{1,0},{2,3},{3,2},{4,5},{5,4},{6,7},{7,6},{8,9},{9,8},{10,11... | collective-permute-start | bytes 491528 | tf_op jit(solution)/shard_map/ppermute | solution.py:20
  11.2 8.1 %collective-permute-start.9 = (bf16[80,1024]{1,0:T(8,128)(2,1)}, bf16[80,1024]{1,0:T(8,128)(2,1)S(1)}, u32[]{:S(2)}, u32[]{:S(2)}) collective-permute-start(bf16[80,1024]{1,0:T(8,128)(2,1)} %refs_0_.3), channel_id=1, source_target_pairs={{0,4},{4,0},{1,5},{5,1},{2,6},{6,2},{3,7},{7,3},{8,12},{12,8},{9,1... | collective-permute-start | bytes 491528 | tf_op jit(solution)/shard_map/ppermute | solution.py:20
  14.8 5.9 %collective-permute-start.7 = (bf16[80,1024]{1,0:T(8,128)(2,1)}, bf16[80,1024]{1,0:T(8,128)(2,1)S(1)}, u32[]{:S(2)}, u32[]{:S(2)}) collective-permute-start(bf16[80,1024]{1,0:T(8,128)(2,1)} %refs_0_.3), channel_id=1, source_target_pairs={{0,16},{16,0},{1,17},{17,1},{2,18},{18,2},{3,19},{19,3},{4,20},{20... | collective-permute-start | bytes 491528 | tf_op jit(solution)/shard_map/ppermute | solution.py:20
  15.9 9.3 %collective-permute-start.6 = (bf16[80,1024]{1,0:T(8,128)(2,1)}, bf16[80,1024]{1,0:T(8,128)(2,1)S(1)}, u32[]{:S(2)}, u32[]{:S(2)}) collective-permute-start(bf16[80,1024]{1,0:T(8,128)(2,1)} %refs_0_.3), channel_id=1, source_target_pairs={{0,2},{2,0},{1,3},{3,1},{4,6},{6,4},{5,7},{7,5},{8,10},{10,8},{9,1... | collective-permute-start | bytes 491528 | tf_op jit(solution)/shard_map/ppermute | solution.py:20
  17.1 11.7 %collective-permute-start.17 = (bf16[80,768]{1,0:T(8,128)(2,1)S(1)}, bf16[80,768]{1,0:T(8,128)(2,1)S(1)}, u32[]{:S(2)}, u32[]{:S(2)}) collective-permute-start(bf16[80,768]{1,0:T(8,128)(2,1)S(1)} %collective-permute-done.13.refs_17_), channel_id=1, source_target_pairs={{0,4},{4,0},{1,5},{5,1},{2,6},{6,2},{3,7},{7,3},{8,12},{12,8},{9,1... | collective-permute-start | bytes 368648 | tf_op jit(solution)/shard_map/ppermute | solution.py:20
  18.2 11.5 %collective-permute-start.15 = (bf16[80,768]{1,0:T(8,128)(2,1)S(1)}, bf16[80,768]{1,0:T(8,128)(2,1)S(1)}, u32[]{:S(2)}, u32[]{:S(2)}) collective-permute-start(bf16[80,768]{1,0:T(8,128)(2,1)S(1)} %collective-permute-done.13.refs_17_), channel_id=1, source_target_pairs={{0,16},{16,0},{1,17},{17,1},{2,18},{18,2},{3,19},{19,3},{4,20},{20... | collective-permute-start | bytes 368648 | tf_op jit(solution)/shard_map/ppermute | solution.py:20
  19.3 7.4 %collective-permute-start.5 = (bf16[80,768]{1,0:T(8,128)(2,1)S(1)}, bf16[80,768]{1,0:T(8,128)(2,1)S(1)}, u32[]{:S(2)}, u32[]{:S(2)}) collective-permute-start(bf16[80,768]{1,0:T(8,128)(2,1)S(1)} %collective-permute-done.3.refs_5_), channel_id=1, source_target_pairs={{0,8},{8,0},{1,9},{9,1},{2,10},{10,2},{3,11},{11,3},{4,12},{12,4},... | collective-permute-start | bytes 368648 | tf_op jit(solution)/shard_map/ppermute | solution.py:20
  20.6 6.8 %collective-permute-start.18 = (bf16[80,768]{1,0:T(8,128)(2,1)S(1)}, bf16[80,768]{1,0:T(8,128)(2,1)S(1)}, u32[]{:S(2)}, u32[]{:S(2)}) collective-permute-start(bf16[80,768]{1,0:T(8,128)(2,1)S(1)} %collective-permute-done.14.refs_18_), channel_id=1, source_target_pairs={{0,4},{4,0},{1,5},{5,1},{2,6},{6,2},{3,7},{7,3},{8,12},{12,8},{9,1... | collective-permute-start | bytes 368648 | tf_op jit(solution)/shard_map/ppermute | solution.py:20
  25.3 6.0 %collective-permute-start.8 = (bf16[80,1024]{1,0:T(8,128)(2,1)S(1)}, bf16[80,1024]{1,0:T(8,128)(2,1)S(1)}, u32[]{:S(2)}, u32[]{:S(2)}) collective-permute-start(bf16[80,1024]{1,0:T(8,128)(2,1)S(1)} %collective-permute-done.6.refs_9_.refs_1_), channel_id=1, source_target_pairs={{0,16},{16,0},{1,17},{17,1},{2,18},{18,2},{3,19},{19,3},{4,20},{20... | collective-permute-start | bytes 491528 | tf_op jit(solution)/shard_map/ppermute | solution.py:20
  27.4 7.3 %collective-permute-start.10 = (bf16[80,1024]{1,0:T(8,128)(2,1)S(1)}, bf16[80,1024]{1,0:T(8,128)(2,1)S(1)}, u32[]{:S(2)}, u32[]{:S(2)}) collective-permute-start(bf16[80,1024]{1,0:T(8,128)(2,1)S(1)} %collective-permute-done.6.refs_9_.refs_1_), channel_id=1, source_target_pairs={{0,4},{4,0},{1,5},{5,1},{2,6},{6,2},{3,7},{7,3},{8,12},{12,8},{9,1... | collective-permute-start | bytes 491528 | tf_op jit(solution)/shard_map/ppermute | solution.py:20
  28.1 6.6 %collective-permute-start.2 = (bf16[80,1024]{1,0:T(8,128)(2,1)S(1)}, bf16[80,1024]{1,0:T(8,128)(2,1)S(1)}, u32[]{:S(2)}, u32[]{:S(2)}) collective-permute-start(bf16[80,1024]{1,0:T(8,128)(2,1)S(1)} %collective-permute-done.refs_1_.refs_7_), channel_id=1, source_target_pairs={{0,8},{8,0},{1,9},{9,1},{2,10},{10,2},{3,11},{11,3},{4,12},{12,4},... | collective-permute-start | bytes 491528 | tf_op jit(solution)/shard_map/ppermute | solution.py:20
  29.5 5.2 %collective-permute-start.11 = (bf16[80,1024]{1,0:T(8,128)(2,1)S(1)}, bf16[80,1024]{1,0:T(8,128)(2,1)S(1)}, u32[]{:S(2)}, u32[]{:S(2)}) collective-permute-start(bf16[80,1024]{1,0:T(8,128)(2,1)S(1)} %collective-permute-done.7.refs_10_.refs_2_), channel_id=1, source_target_pairs={{0,4},{4,0},{1,5},{5,1},{2,6},{6,2},{3,7},{7,3},{8,12},{12,8},{9,1... | collective-permute-start | bytes 491528 | tf_op jit(solution)/shard_map/ppermute | solution.py:20
  29.7 5.0 %collective-permute-start.19 = (bf16[80,768]{1,0:T(8,128)(2,1)S(1)}, bf16[80,768]{1,0:T(8,128)(2,1)S(1)}, u32[]{:S(2)}, u32[]{:S(2)}) collective-permute-start(bf16[80,768]{1,0:T(8,128)(2,1)S(1)} %collective-permute-done.15.refs_19_), channel_id=1, source_target_pairs={{0,4},{4,0},{1,5},{5,1},{2,6},{6,2},{3,7},{7,3},{8,12},{12,8},{9,1... | collective-permute-start | bytes 368648 | tf_op jit(solution)/shard_map/ppermute | solution.py:20
  31.2 3.5 %collective-permute-start.12 = (bf16[80,1024]{1,0:T(8,128)(2,1)S(1)}, bf16[80,1024]{1,0:T(8,128)(2,1)S(1)}, u32[]{:S(2)}, u32[]{:S(2)}) collective-permute-start(bf16[80,1024]{1,0:T(8,128)(2,1)S(1)} %collective-permute-done.8.refs_11_.refs_3_), channel_id=1, source_target_pairs={{0,4},{4,0},{1,5},{5,1},{2,6},{6,2},{3,7},{7,3},{8,12},{12,8},{9,1... | collective-permute-start | bytes 491528 | tf_op jit(solution)/shard_map/ppermute | solution.py:20
  48.0 3.8 %collective-permute-start.20 = (f32[4,8,128]{2,1,0:T(8,128)S(1)}, f32[4,8,128]{2,1,0:T(8,128)S(1)}, u32[]{:S(2)}, u32[]{:S(2)}) collective-permute-start(f32[4,8,128]{2,1,0:T(8,128)S(1)} %get-tuple-element.13), channel_id=1, source_target_pairs={{0,8},{8,0},{1,9},{9,1},{2,10},{10,2},{3,11},{11,3},{4,12},{12,4},... | collective-permute-start | bytes 49160 | tf_op jit(solution)/shard_map/ppermute | solution.py:20
  49.0 3.0 %collective-permute-start.22 = (f32[8,8,128]{2,1,0:T(8,128)S(1)}, f32[8,8,128]{2,1,0:T(8,128)S(1)}, u32[]{:S(2)}, u32[]{:S(2)}) collective-permute-start(f32[8,8,128]{2,1,0:T(8,128)S(1)} %get-tuple-element.14), channel_id=1, source_target_pairs={{0,4},{4,0},{1,5},{5,1},{2,6},{6,2},{3,7},{7,3},{8,12},{12,8},{9,1... | collective-permute-start | bytes 98312 | tf_op jit(solution)/shard_map/ppermute | solution.py:20
  51.9 3.8 %collective-permute-start.21 = (f32[4,8,128]{2,1,0:T(8,128)S(1)}, f32[4,8,128]{2,1,0:T(8,128)S(1)}, u32[]{:S(2)}, u32[]{:S(2)}) collective-permute-start(f32[4,8,128]{2,1,0:T(8,128)S(1)} %stack.10), channel_id=1, source_target_pairs={{0,1},{1,0},{2,3},{3,2},{4,5},{5,4},{6,7},{7,6},{8,9},{9,8},{10,11... | collective-permute-start | bytes 49160 | tf_op jit(solution)/shard_map/ppermute | solution.py:20
  52.1 4.0 %collective-permute-start.23 = (f32[8,8,128]{2,1,0:T(8,128)S(1)}, f32[8,8,128]{2,1,0:T(8,128)S(1)}, u32[]{:S(2)}, u32[]{:S(2)}) collective-permute-start(f32[8,8,128]{2,1,0:T(8,128)S(1)} %stack.12), channel_id=1, source_target_pairs={{0,16},{16,0},{1,17},{17,1},{2,18},{18,2},{3,19},{19,3},{4,20},{20... | collective-permute-start | bytes 98312 | tf_op jit(solution)/shard_map/ppermute | solution.py:20
  56.8 5.1 %collective-permute-start.24 = (f32[8,8,128]{2,1,0:T(8,128)}, f32[8,8,128]{2,1,0:T(8,128)}, u32[]{:S(2)}, u32[]{:S(2)}) collective-permute-start(f32[8,8,128]{2,1,0:T(8,128)} %stack.13), channel_id=1, source_target_pairs={{0,2},{2,0},{1,3},{3,1},{4,6},{6,4},{5,7},{7,5},{8,10},{10,8},{9,1... | collective-permute-start | bytes 98312 | tf_op jit(solution)/shard_map/ppermute | solution.py:20
  66.5 2.9 %collective-permute-start.28 = (bf16[320,1024]{1,0:T(8,128)(2,1)S(1)}, bf16[320,1024]{1,0:T(8,128)(2,1)S(1)}, u32[]{:S(2)}, u32[]{:S(2)}) collective-permute-start(bf16[320,1024]{1,0:T(8,128)(2,1)S(1)} %get-tuple-element.19), channel_id=1, source_target_pairs={{0,4},{4,0},{1,5},{5,1},{2,6},{6,2},{3,7},{7,3},{8,12},{12,8},{9,1... | collective-permute-start | bytes 1966088 | tf_op jit(solution)/shard_map/ppermute | solution.py:20
  67.3 14.3 %collective-permute-start.25 = (bf16[80,1024]{1,0:T(8,128)(2,1)S(1)}, bf16[80,1024]{1,0:T(8,128)(2,1)S(1)}, u32[]{:S(2)}, u32[]{:S(2)}) collective-permute-start(bf16[80,1024]{1,0:T(8,128)(2,1)S(1)} %get-tuple-element.34), channel_id=1, source_target_pairs={{0,8},{8,0},{1,9},{9,1},{2,10},{10,2},{3,11},{11,3},{4,12},{12,4},... | collective-permute-start | bytes 491528 | tf_op jit(solution)/shard_map/ppermute | solution.py:20
  68.2 9.3 %collective-permute-start.26 = (bf16[80,1024]{1,0:T(8,128)(2,1)S(1)}, bf16[80,1024]{1,0:T(8,128)(2,1)S(1)}, u32[]{:S(2)}, u32[]{:S(2)}) collective-permute-start(bf16[80,1024]{1,0:T(8,128)(2,1)S(1)} %get-tuple-element.35), channel_id=1, source_target_pairs={{0,8},{8,0},{1,9},{9,1},{2,10},{10,2},{3,11},{11,3},{4,12},{12,4},... | collective-permute-start | bytes 491528 | tf_op jit(solution)/shard_map/ppermute | solution.py:20
  69.7 10.6 %collective-permute-start.30 = (bf16[80,1024]{1,0:T(8,128)(2,1)S(1)}, bf16[80,1024]{1,0:T(8,128)(2,1)S(1)}, u32[]{:S(2)}, u32[]{:S(2)}) collective-permute-start(bf16[80,1024]{1,0:T(8,128)(2,1)S(1)} %get-tuple-element.33), channel_id=1, source_target_pairs={{0,16},{16,0},{1,17},{17,1},{2,18},{18,2},{3,19},{19,3},{4,20},{20... | collective-permute-start | bytes 491528 | tf_op jit(solution)/shard_map/ppermute | solution.py:20
  77.5 7.5 %collective-permute-start.27 = (bf16[80,1024]{1,0:T(8,128)(2,1)S(1)}, bf16[80,1024]{1,0:T(8,128)(2,1)S(1)}, u32[]{:S(2)}, u32[]{:S(2)}) collective-permute-start(bf16[80,1024]{1,0:T(8,128)(2,1)S(1)} %add_convert_fusion), channel_id=1, source_target_pairs={{0,1},{1,0},{2,3},{3,2},{4,5},{5,4},{6,7},{7,6},{8,9},{9,8},{10,11... | collective-permute-start | bytes 491528 | tf_op jit(solution)/shard_map/ppermute | solution.py:20
  79.6 6.2 %collective-permute-start.29 = (bf16[80,1024]{1,0:T(8,128)(2,1)S(1)}, bf16[80,1024]{1,0:T(8,128)(2,1)S(1)}, u32[]{:S(2)}, u32[]{:S(2)}) collective-permute-start(bf16[80,1024]{1,0:T(8,128)(2,1)S(1)} %get-tuple-element.32), channel_id=1, source_target_pairs={{0,16},{16,0},{1,17},{17,1},{2,18},{18,2},{3,19},{19,3},{4,20},{20... | collective-permute-start | bytes 491528 | tf_op jit(solution)/shard_map/ppermute | solution.py:20
  80.3 9.7 %collective-permute-start.31 = (bf16[80,1024]{1,0:T(8,128)(2,1)S(1)}, bf16[80,1024]{1,0:T(8,128)(2,1)S(1)}, u32[]{:S(2)}, u32[]{:S(2)}) collective-permute-start(bf16[80,1024]{1,0:T(8,128)(2,1)S(1)} %fusion), channel_id=1, source_target_pairs={{0,2},{2,0},{1,3},{3,1},{4,6},{6,4},{5,7},{7,5},{8,10},{10,8},{9,1... | collective-permute-start | bytes 491528 | tf_op jit(solution)/shard_map/ppermute | solution.py:20
  (30 other events, 58.6 us)

commit v3 on v2

v3 whole, which is shorter than its diff:
```python
import functools
import math

import jax
import jax.numpy as jnp
from jax import lax
from jax.experimental import pallas as pl
from jax.experimental.pallas import tpu as pltpu
from jax.sharding import Mesh, PartitionSpec as P

logit_gain = 3.0
ROW_AXES = ("ilo", "chi")
COL_AXES = ("core", "ihi", "clo")
LANES = 128
PEAK_S, TOTAL_S, PEAK_T, TOTAL_T, INDEX = range(5)


def swap(value, axis, mask):
    size = lax.axis_size(axis)
    return lax.ppermute(value, axis, [(j, j ^ mask) for j in range(size)])


def bits(axis):
    size = lax.axis_size(axis)
    return [1 << b for b in range(size.bit_length() - 1)]


def lines_of(columns):
    count = columns[0].shape[0]
    lane = lax.broadcasted_iota(jnp.int32, (count, LANES), 1)
    wide = jnp.zeros((count, LANES), jnp.float32)
    for k, column in enumerate(columns):
        wide = jnp.where(lane == k, column, wide)
    spare = -count % LANES
    if spare:
        wide = jnp.concatenate([wide, jnp.zeros((spare, LANES), jnp.float32)], axis=0)
    return wide.T[:8, :count]


def columns_of(lines):
    count = lines.shape[1]
    spare = -count % LANES
    if spare:
        lines = jnp.concatenate([lines, jnp.zeros((8, spare), jnp.float32)], axis=1)
    tall = jnp.concatenate([lines, jnp.zeros((LANES - 8, count + spare), jnp.float32)], axis=0)
    return tall.T[:count]


def store_slots(ref, lines, rows):
    ref[...] = jnp.zeros_like(ref)
    for s in range(ref.shape[0]):
        ref[s, :, :rows] = lines[:, s * rows : (s + 1) * rows]


def load_slots(ref, rows):
    return jnp.concatenate([ref[s, :, :rows] for s in range(ref.shape[0])], axis=1)


def pack_kernel(left, right, out, sem):
    width = left.shape[1]
    copies = [
        pltpu.make_async_copy(left, out.at[:, :width], sem.at[0]),
        pltpu.make_async_copy(right, out.at[:, width:], sem.at[1]),
    ]
    for copy in copies:
        copy.start()
    for copy in copies:
        copy.wait()


def place(pieces, sems):
    copies = [pltpu.make_async_copy(src, dst, sem) for (src, dst), sem in zip(pieces, sems)]
    for copy in copies:
        copy.start()
    return copies


def logits_kernel(n_img, n_cap, rows, width, *refs):
    img_s_parts, refs = refs[:n_img], refs[n_img:]
    img_t_parts, refs = refs[:n_img], refs[n_img:]
    cap_parts, refs = refs[:n_cap], refs[n_cap:]
    student_ref, teacher_ref, row_ref, col_ref, img_s, cap_s, img_t, cap_t, sems = refs

    def pieces(parts, out, columns):
        each = out.shape[0] // len(parts)
        return [(part.at[:, columns], out.at[k * each : (k + 1) * each]) for k, part in enumerate(parts)]

    front, back = slice(0, width), slice(width, width + cap_t.shape[1])
    everything = (
        pieces(cap_parts, cap_t, back)
        + pieces(img_t_parts, img_t, slice(None))
        + pieces(cap_parts, cap_s, front)
        + pieces(img_s_parts, img_s, slice(None))
    )
    copies = place(everything, [sems.at[k] for k in range(len(everything))])
    half = n_img + n_cap
    row_columns, col_lines = [], []
    for wait, left, right, out in (
        (copies[:half], img_t, cap_t, teacher_ref),
        (copies[half:], img_s, cap_s, student_ref),
    ):
        for copy in wait:
            copy.wait()
        gain = logit_gain / math.sqrt(left.shape[1])
        out[...] = gain * lax.dot_general(
            left[...], right[...], (((1,), (1,)), ((), ())), preferred_element_type=jnp.float32
        )
        matrix = out[...]
        peak = jnp.max(matrix, axis=1, keepdims=True)
        row_columns = [peak, jnp.sum(jnp.exp(matrix - peak), axis=1, keepdims=True)] + row_columns
        peak = jnp.max(matrix, axis=0, keepdims=True)
        col_lines = [peak, jnp.sum(jnp.exp(matrix - peak), axis=0, keepdims=True)] + col_lines
    store_slots(row_ref, lines_of(row_columns), rows)
    blank = jnp.zeros((4, col_lines[0].shape[1]), jnp.float32)
    store_slots(col_ref, jnp.concatenate(col_lines + [blank], axis=0), rows)


def tile_kernel(rows, student_ref, teacher_ref, row_ref, row_id_ref, col_ref, col_id_ref, cap_s, tile_ref, *outs):
    def finish(ref, id_ref):
        lines = load_slots(ref, rows)
        ids = load_slots(id_ref, rows)
        line = lax.broadcasted_iota(jnp.int32, lines.shape, 0)
        lse_s = lines[PEAK_S : PEAK_S + 1] + jnp.log(lines[TOTAL_S : TOTAL_S + 1])
        lse_t = lines[PEAK_T : PEAK_T + 1] + jnp.log(lines[TOTAL_T : TOTAL_T + 1])
        return jnp.where(line == 0, lse_s, jnp.where(line == 1, lse_t, ids))

    across = finish(col_ref, col_id_ref)
    down = columns_of(finish(row_ref, row_id_ref))
    total = student_ref.shape[0]
    step = 64 if total % 64 == 0 else total
    for r in range(0, total, step):
        at = slice(r, r + step)
        s, t = student_ref[at], teacher_ref[at]
        grad = 0.5 * (jnp.exp(s - down[at, 0:1]) + jnp.exp(s - across[0:1]))
        grad = grad - 0.25 * (jnp.exp(t - down[at, 1:2]) + jnp.exp(t - across[1:2]))
        grad = grad - jnp.where(down[at, INDEX : INDEX + 1] == across[INDEX : INDEX + 1], 0.5, 0.0)
        tile_ref[at] = grad.astype(jnp.bfloat16)
    spread(jnp.dot(tile_ref[...], cap_s[...], preferred_element_type=jnp.float32), outs)


def caption_kernel(tile_ref, img_s, *outs):
    part = lax.dot_general(
        tile_ref[...], img_s[...], (((0,), (0,)), ((), ())), preferred_element_type=jnp.float32
    )
    spread(part, outs)


def spread(part, outs):
    start = 0
    for out in outs:
        out[...] = part[start : start + out.shape[0]].astype(out.dtype)
        start += out.shape[0]


def merge_kernel(order, one, two, out):
    for s, o in enumerate(order):
        x, y = one[s], two[o]
        peak_s = jnp.maximum(x[PEAK_S : PEAK_S + 1], y[PEAK_S : PEAK_S + 1])
        peak_t = jnp.maximum(x[PEAK_T : PEAK_T + 1], y[PEAK_T : PEAK_T + 1])
        line = lax.broadcasted_iota(jnp.int32, x.shape, 0)
        peak = jnp.where(line <= TOTAL_S, peak_s, peak_t)
        x_peak = jnp.where(line <= TOTAL_S, x[PEAK_S : PEAK_S + 1], x[PEAK_T : PEAK_T + 1])
        y_peak = jnp.where(line <= TOTAL_S, y[PEAK_S : PEAK_S + 1], y[PEAK_T : PEAK_T + 1])
        total = x * jnp.exp(x_peak - peak) + y * jnp.exp(y_peak - peak)
        merged = jnp.where((line == PEAK_S) | (line == PEAK_T), peak, total)
        out[s] = jnp.where(line < INDEX, merged, 0.0)


VMEM, ANY = pltpu.VMEM, pl.ANY


def call(kernel, outs, args, flops=0, scratch=(), space=VMEM, out_space=VMEM):
    moved = sum(math.prod(a.shape) * a.dtype.itemsize for a in list(args) + list(outs))
    return pl.pallas_call(
        kernel,
        out_shape=outs,
        in_specs=[pl.BlockSpec(memory_space=space)] * len(args),
        out_specs=[pl.BlockSpec(memory_space=out_space)] * len(outs),
        scratch_shapes=scratch,
        compiler_params=pltpu.CompilerParams(vmem_limit_bytes=16 * 2**20),
        cost_estimate=pl.CostEstimate(flops=flops, bytes_accessed=moved, transcendentals=0),
    )(*args)


def pool_step(stats, axes, d, bit):
    stride = math.prod(lax.axis_size(a) for a in axes[d + 1 :]) * bit
    order = [s ^ stride for s in range(stats.shape[0])]
    other = swap(stats, axes[d], bit)
    return call(
        functools.partial(merge_kernel, order), [jax.ShapeDtypeStruct(stats.shape, stats.dtype)], [stats, other]
    )[0]


def owners(axes):
    result = {}
    for d, axis in enumerate(axes):
        index = lax.axis_index(axis) ^ jnp.arange(lax.axis_size(axis), dtype=jnp.int32)
        result[axis] = index.reshape([-1 if e == d else 1 for e in range(len(axes))])
    return result


def identity_block(axes, order, rows):
    place = {a: lax.axis_index(a) for a in order}
    place.update(owners(axes))
    owner = 0
    for axis in order:
        owner = owner * lax.axis_size(axis) + place[axis]
    index = owner.reshape(-1, 1, 1) * rows + jnp.arange(LANES, dtype=jnp.int32)[None, None, :]
    line = jnp.arange(8, dtype=jnp.int32)[None, :, None]
    return jnp.where(line == INDEX, index, 0).astype(jnp.float32)


def after(value, other):
    return lax.optimization_barrier((value, other))[0]


def local(image_student, caption_student, image_teacher, caption_teacher):
    ilo, chi, core, ihi, clo = (lax.axis_size(a) for a in ROW_AXES + COL_AXES)
    rows, width = image_student.shape
    depth = image_teacher.shape[1]
    assert rows <= LANES and core == 2
    n_img, n_cap = ilo * chi, core * ihi * clo
    total, columns = n_img * rows, n_cap * rows
    f32, bf16 = jnp.float32, jnp.bfloat16
    shape = jax.ShapeDtypeStruct

    def gather_images(own):
        far = [own] + [swap(own, "chi", m) for m in range(1, chi)]
        return far + [swap(part, "ilo", m) for m in range(1, ilo) for part in far]

    def gather_captions(own):
        far = [own] + [swap(own, "clo", m) for m in range(1, clo)]
        far = far + [swap(part, "ihi", m) for m in range(1, ihi) for part in far]
        return far + [swap(part, "core", 1) for part in far]

    def shards(parts):
        return parts if rows % 16 == 0 else [jnp.concatenate(parts, axis=0)]

    if rows % 16 == 0:
        caption = call(
            pack_kernel,
            [shape((rows, width + depth), bf16)],
            [caption_student, caption_teacher],
            scratch=[pltpu.SemaphoreType.DMA((2,))],
            space=ANY,
            out_space=ANY,
        )[0]
    else:
        caption = jnp.concatenate([caption_student, caption_teacher], axis=1)
    img_t, img_s = shards(gather_images(image_teacher)), shards(gather_images(image_student))
    cap = shards(gather_captions(caption))

    student, teacher, row_stats, col_stats, images, captions = call(
        functools.partial(logits_kernel, len(img_s), len(cap), rows, width),
        [
            shape((total, columns), f32),
            shape((total, columns), f32),
            shape((n_img, 8, LANES), f32),
            shape((n_cap, 8, LANES), f32),
            shape((total, width), bf16),
            shape((columns, width), bf16),
        ],
        img_s + img_t + cap,
        2 * total * columns * (width + depth),
        scratch=[
            pltpu.VMEM((total, depth), bf16),
            pltpu.VMEM((columns, depth), bf16),
            pltpu.SemaphoreType.DMA((2 * (len(img_s) + len(cap)),)),
        ],
        space=ANY,
    )
    for d, axis in enumerate(ROW_AXES):
        for bit in bits(axis):
            row_stats = pool_step(row_stats, ROW_AXES, d, bit)
    for d, axis in enumerate(COL_AXES):
        for bit in bits(axis):
            col_stats = pool_step(col_stats, COL_AXES, d, bit)
    row_ids = identity_block(ROW_AXES, ("ihi", "ilo", "core", "chi", "clo"), rows)
    col_ids = identity_block(COL_AXES, ("chi", "clo", "ihi", "ilo", "core"), rows)

    def outs(count, near, far):
        piece = count // (near * far)
        own = [shape((piece, width), f32)] * far
        return own + [shape((piece, width), bf16)] * ((near - 1) * far)

    tile, *image_parts = call(
        functools.partial(tile_kernel, rows),
        [shape((total, columns), bf16)] + outs(total, ilo, chi),
        [student, teacher, row_stats, row_ids, col_stats, col_ids, captions],
        2 * total * columns * width,
    )
    held, sent = call(
        caption_kernel,
        [shape((columns // 2, width), f32), shape((columns // 2, width), bf16)],
        [tile, images],
        2 * total * columns * width,
    )

    def collect(held, sent, near, far):
        count = lax.axis_size(far)
        held = list(held)
        arrived = None
        for f in reversed(range(count)):
            for m in range(1, lax.axis_size(near)):
                term = sent[m - 1][f]
                if f == 0 and arrived is not None:
                    term = after(term, arrived)
                arrived = swap(term, near, m)
                held[f] = held[f] + arrived.astype(f32)
        result = held[0]
        for f in range(1, count):
            result = result + swap(held[f].astype(bf16), far, f).astype(f32)
        return result

    image_sent = [image_parts[m * chi : (m + 1) * chi] for m in range(1, ilo)]
    image_grad = collect(image_parts[:chi], image_sent, "ilo", "chi")
    pair = (held + swap(sent, "core", 1).astype(f32)).reshape(ihi, clo, rows, width)
    caption_grad = collect(pair[0], pair[1:].astype(bf16), "ihi", "clo")
    return (image_grad, caption_grad)


def split(count):
    low = 1 << ((count.bit_length() - 1) // 2)
    return count // low, low


def solution(mesh):
    ihi, ilo = split(mesh.shape["img"] // 2)
    chi, clo = split(mesh.shape["cap"])
    fine = Mesh(mesh.devices.reshape(ihi, ilo, 2, chi, clo), ("ihi", "ilo", "core", "chi", "clo"))
    by_image = P(("ihi", "ilo", "core", "chi", "clo"), None)
    by_caption = P(("chi", "clo", "ihi", "ilo", "core"), None)
    return jax.shard_map(
        local,
        mesh=fine,
        in_specs=(by_image, by_caption, by_image, by_caption),
        out_specs=(by_image, by_caption),
        check_vma=False,
    )
```

time: 91.4 us -> 79.4 us (0.87)
  waiting for transfers between devices: 35.7 us -> 22.5 us
  local copies, waits for them, and re-layouts: 20.1 us -> 12.4 us
  Pallas kernels: 3.88 us -> 8.15 us
  starting transfers between devices: 26.3 us -> 30.3 us
  other arithmetic: 3.81 us -> 4.82 us
    ppermute x32 -> x25, waiting for transfers between devices: 35.7 us -> 22.5 us  [swap(): return lax.ppermute(value, axis, [(j, j ^ mask) for j in range(size)])]
    unnamed x60 -> x34, local copies, waits for them, and re-layouts: 17.6 us -> 12.1 us
    pallas_call x3 -> x9, Pallas kernels: 3.88 us -> 8.15 us  [call(): pl.pallas_call(kernel, out_shape=outs, in_specs=[pl.BlockSpec(memory_spac...]
    ppermute x32 -> x25, starting transfers between devices: 26.3 us -> 30.3 us  [swap(): return lax.ppermute(value, axis, [(j, j ^ mask) for j in range(size)])]
    another operation x7 -> x0, local copies, waits for them, and re-layouts: 1.5 us -> none  [the longest x5 1.5 us: merge(): return jnp.stack(result, axis=-2)]
    add x5 -> x0, other arithmetic: 1.46 us -> none  [merge(): one[..., k + 1, :] * jnp.exp(one[..., k, :] - peak)]
    convert_element_type x2, other arithmetic: 0.14 us -> 1.48 us  [identity_block(): return jnp.where(line == INDEX, index, 0).astype(jnp.float32)]
  transfers between devices with their start and end apart: 32 -> 25, of which waited for: 12 -> 10; matrix products, arithmetic and copies ran while one was open for 2% -> 5% of each run, Pallas kernels for 1% -> 1%
where the time goes in v3:
time: 79.4 us; the launch traced here: 78.9 us
  starting transfers between devices  30.3 us (38%)
  waiting for transfers between devices  22.5 us (28%)
  local copies, waits for them, and re-layouts  12.4 us (16%)
  Pallas kernels  8.15 us (10%)
  other arithmetic  4.82 us (6%)
  between operations  0.81 us (1%)
    ppermute x25, starting transfers between devices, swap(): return lax.ppermute(value, axis, [(j, j ^ mask) for j in range(size)])  30.3 us
    ppermute x25, waiting for transfers between devices, swap(): return lax.ppermute(value, axis, [(j, j ^ mask) for j in range(size)])  22.5 us
    unnamed x34, local copies, waits for them, and re-layouts  12.1 us
    pallas_call x9, Pallas kernels, call(): pl.pallas_call(kernel, out_shape=outs, in_specs=[pl.BlockSpec(memory_spac...  8.15 us
  transfers between devices with their start and end apart: 25, of which 10 were waited for; matrix products, arithmetic and copies ran while one was open for 5% of the time, Pallas kernels for 1%

profile of v3, /device:TPU:0, one launch (start us, length us, event | category | flops | bytes accessed | tf_op | source)
XLA Modules:
  0.0 78.9 jit_solution(7146610562467493643)
XLA Ops:
  0.6 0.9 %copy-done.2 = bf16[80,1024]{1,0:T(8,128)(2,1)S(1)} copy-done((bf16[80,1024]{1,0:T(8,128)(2,1)S(1)}, bf16[80,1024]{1,0:T(8,128)(2,1)}, u32[]{:S(2)}) %copy-start.2) | copy-done | bytes 163864
  2.5 3.1 %collective-permute-start.6 = (bf16[80,1792]{1,0:T(8,128)(2,1)S(1)}, bf16[80,1792]{1,0:T(8,128)(2,1)S(1)}, u32[]{:S(2)}, u32[]{:S(2)}) collective-permute-start(bf16[80,1792]{1,0:T(8,128)(2,1)S(1)} %shard_map.59.refs_8_), channel_id=1, source_target_pairs={{0,1},{1,0},{2,3},{3,2},{4,5},{5,4},{6,7},{7,6},{8,9},{9,8},{10,11... | collective-permute-start | bytes 860168 | tf_op jit(solution)/shard_map/ppermute | solution.py:20
  5.6 1.5 %collective-permute-start.7 = (bf16[80,1792]{1,0:T(8,128)(2,1)S(1)}, bf16[80,1792]{1,0:T(8,128)(2,1)S(1)}, u32[]{:S(2)}, u32[]{:S(2)}) collective-permute-start(bf16[80,1792]{1,0:T(8,128)(2,1)S(1)} %shard_map.59.refs_8_), channel_id=1, source_target_pairs={{0,16},{16,0},{1,17},{17,1},{2,18},{18,2},{3,19},{19,3},{4,20},{20... | collective-permute-start | bytes 860168 | tf_op jit(solution)/shard_map/ppermute | solution.py:20
  7.1 2.6 %collective-permute-start.3 = (bf16[80,768]{1,0:T(8,128)(2,1)}, bf16[80,768]{1,0:T(8,128)(2,1)S(1)}, u32[]{:S(2)}, u32[]{:S(2)}) collective-permute-start(bf16[80,768]{1,0:T(8,128)(2,1)} %refs_4_.1), channel_id=1, source_target_pairs={{0,2},{2,0},{1,3},{3,1},{4,6},{6,4},{5,7},{7,5},{8,10},{10,8},{9,1... | collective-permute-start | bytes 368648 | tf_op jit(solution)/shard_map/ppermute | solution.py:20
  9.7 1.5 %collective-permute-start.4 = (bf16[80,768]{1,0:T(8,128)(2,1)}, bf16[80,768]{1,0:T(8,128)(2,1)S(1)}, u32[]{:S(2)}, u32[]{:S(2)}) collective-permute-start(bf16[80,768]{1,0:T(8,128)(2,1)} %refs_4_.1), channel_id=1, source_target_pairs={{0,8},{8,0},{1,9},{9,1},{2,10},{10,2},{3,11},{11,3},{4,12},{12,4},... | collective-permute-start | bytes 368648 | tf_op jit(solution)/shard_map/ppermute | solution.py:20
  12.3 3.3 %collective-permute-done.3.refs_5_ = bf16[80,768]{1,0:T(8,128)(2,1)S(1)} collective-permute-done((bf16[80,768]{1,0:T(8,128)(2,1)}, bf16[80,768]{1,0:T(8,128)(2,1)S(1)}, u32[]{:S(2)}, u32[]{:S(2)}) %collective-permute-start.3) | collective-permute-done | bytes 122912 | tf_op jit(solution)/shard_map/ppermute | solution.py:20
  15.6 1.5 %collective-permute-start.1 = (bf16[80,1024]{1,0:T(8,128)(2,1)}, bf16[80,1024]{1,0:T(8,128)(2,1)S(1)}, u32[]{:S(2)}, u32[]{:S(2)}) collective-permute-start(bf16[80,1024]{1,0:T(8,128)(2,1)} %refs_0_.1), channel_id=1, source_target_pairs={{0,8},{8,0},{1,9},{9,1},{2,10},{10,2},{3,11},{11,3},{4,12},{12,4},... | collective-permute-start | bytes 491528 | tf_op jit(solution)/shard_map/ppermute | solution.py:20
  19.0 1.5 %collective-permute-start.8 = (bf16[80,1792]{1,0:T(8,128)(2,1)S(1)}, bf16[80,1792]{1,0:T(8,128)(2,1)S(1)}, u32[]{:S(2)}, u32[]{:S(2)}) collective-permute-start(bf16[80,1792]{1,0:T(8,128)(2,1)S(1)} %collective-permute-done.6.refs_9_), channel_id=1, source_target_pairs={{0,16},{16,0},{1,17},{17,1},{2,18},{18,2},{3,19},{19,3},{4,20},{20... | collective-permute-start | bytes 860168 | tf_op jit(solution)/shard_map/ppermute | solution.py:20
  21.1 2.1 %collective-permute-done.refs_1_ = bf16[80,1024]{1,0:T(8,128)(2,1)S(1)} collective-permute-done((bf16[80,1024]{1,0:T(8,128)(2,1)}, bf16[80,1024]{1,0:T(8,128)(2,1)S(1)}, u32[]{:S(2)}, u32[]{:S(2)}) %collective-permute-start) | collective-permute-done | bytes 163872 | tf_op jit(solution)/shard_map/ppermute | solution.py:20
  23.2 1.1 %collective-permute-start.2 = (bf16[80,1024]{1,0:T(8,128)(2,1)S(1)}, bf16[80,1024]{1,0:T(8,128)(2,1)S(1)}, u32[]{:S(2)}, u32[]{:S(2)}) collective-permute-start(bf16[80,1024]{1,0:T(8,128)(2,1)S(1)} %collective-permute-done.refs_1_), channel_id=1, source_target_pairs={{0,8},{8,0},{1,9},{9,1},{2,10},{10,2},{3,11},{11,3},{4,12},{12,4},... | collective-permute-start | bytes 491528 | tf_op jit(solution)/shard_map/ppermute | solution.py:20
  27.1 2.7 %collective-permute-done.2.refs_3_ = bf16[80,1024]{1,0:T(8,128)(2,1)S(1)} collective-permute-done((bf16[80,1024]{1,0:T(8,128)(2,1)S(1)}, bf16[80,1024]{1,0:T(8,128)(2,1)S(1)}, u32[]{:S(2)}, u32[]{:S(2)}) %collective-permute-start.2) | collective-permute-done | bytes 163872 | tf_op jit(solution)/shard_map/ppermute | solution.py:20
  29.9 0.9 %copy-done.1 = bf16[80,1792]{1,0:T(8,128)(2,1)S(1)} copy-done((bf16[80,1792]{1,0:T(8,128)(2,1)S(1)}, bf16[80,1792]{1,0:T(8,128)(2,1)}, u32[]{:S(2)}) %copy-start.1) | copy-done | bytes 286744
  30.8 0.9 %copy-done.3 = bf16[80,1024]{1,0:T(8,128)(2,1)S(1)} copy-done((bf16[80,1024]{1,0:T(8,128)(2,1)S(1)}, bf16[80,1024]{1,0:T(8,128)(2,1)}, u32[]{:S(2)}) %copy-start.3) | copy-done | bytes 163864
  31.7 0.9 %copy-done.5 = bf16[80,1024]{1,0:T(8,128)(2,1)S(1)} copy-done((bf16[80,1024]{1,0:T(8,128)(2,1)S(1)}, bf16[80,1024]{1,0:T(8,128)(2,1)}, u32[]{:S(2)}) %copy-start.5) | copy-done | bytes 163864
  32.6 0.9 %copy-done.7 = bf16[80,768]{1,0:T(8,128)(2,1)S(1)} copy-done((bf16[80,768]{1,0:T(8,128)(2,1)S(1)}, bf16[80,768]{1,0:T(8,128)(2,1)}, u32[]{:S(2)}) %copy-start.7) | copy-done | bytes 122904
  35.3 5.0 %shard_map.60 = (f32[320,640]{1,0:T(8,128)S(1)}, f32[320,640]{1,0:T(8,128)S(1)}, f32[4,8,128]{2,1,0:T(8,128)S(1)}, f32[8,8,128]{2,1,0:T(8,128)}, bf16[320,1024]{...) custom-call(bf16[80,1024]{1,0:T(8,128)(2,1)S(1)} %copy-done.3, bf16[80,1024]{1,0:T(8,128)(2,1)S(1)} %copy-done.5, ...), custom_call_target="tpu_custom_call" | custom-call | flops 734003200 | bytes 7094272 | tf_op jit(solution)/shard_map/pallas_call | solution.py:174
  41.9 1.1 %collective-permute-start.13 = (f32[4,8,128]{2,1,0:T(8,128)}, f32[4,8,128]{2,1,0:T(8,128)S(1)}, u32[]{:S(2)}, u32[]{:S(2)}) collective-permute-start(f32[4,8,128]{2,1,0:T(8,128)} %copy-done.12), channel_id=1, source_target_pairs={{0,8},{8,0},{1,9},{9,1},{2,10},{10,2},{3,11},{11,3},{4,12},{12,4},... | collective-permute-start | bytes 49160 | tf_op jit(solution)/shard_map/ppermute | solution.py:20
  44.7 1.2 %collective-permute-done.13.two = f32[4,8,128]{2,1,0:T(8,128)S(1)} collective-permute-done((f32[4,8,128]{2,1,0:T(8,128)}, f32[4,8,128]{2,1,0:T(8,128)S(1)}, u32[]{:S(2)}, u32[]{:S(2)}) %collective-permute-start.13) | collective-permute-done | bytes 16416 | tf_op jit(solution)/shard_map/ppermute | solution.py:20
  46.6 1.3 %collective-permute-start.14 = (f32[4,8,128]{2,1,0:T(8,128)S(1)}, f32[4,8,128]{2,1,0:T(8,128)S(1)}, u32[]{:S(2)}, u32[]{:S(2)}) collective-permute-start(f32[4,8,128]{2,1,0:T(8,128)S(1)} %shard_map.61.one), channel_id=1, source_target_pairs={{0,2},{2,0},{1,3},{3,1},{4,6},{6,4},{5,7},{7,5},{8,10},{10,8},{9,1... | collective-permute-start | bytes 49160 | tf_op jit(solution)/shard_map/ppermute | solution.py:20
  48.0 4.3 %collective-permute-start.17 = (f32[8,8,128]{2,1,0:T(8,128)S(1)}, f32[8,8,128]{2,1,0:T(8,128)S(1)}, u32[]{:S(2)}, u32[]{:S(2)}) collective-permute-start(f32[8,8,128]{2,1,0:T(8,128)S(1)} %shard_map.64.one), channel_id=1, source_target_pairs={{0,1},{1,0},{2,3},{3,2},{4,5},{5,4},{6,7},{7,6},{8,9},{9,8},{10,11... | collective-permute-start | bytes 98312 | tf_op jit(solution)/shard_map/ppermute | solution.py:20
  53.1 1.1 %collective-permute-done.17.two = f32[8,8,128]{2,1,0:T(8,128)S(1)} collective-permute-done((f32[8,8,128]{2,1,0:T(8,128)S(1)}, f32[8,8,128]{2,1,0:T(8,128)S(1)}, u32[]{:S(2)}, u32[]{:S(2)}) %collective-permute-start.17) | collective-permute-done | bytes 32800 | tf_op jit(solution)/shard_map/ppermute | solution.py:20
  54.3 1.4 %shard_map.66 = (bf16[320,640]{1,0:T(8,128)(2,1)S(1)}, f32[80,1024]{1,0:T(8,128)S(1)}, f32[80,1024]{1,0:T(8,128)S(1)}, bf16[80,1024]{1,0:T(8,128)(2,1)S(1)}, bf16[80,1024]{1,0:T(8,128)(2,1)S(1)}) custom-call(f32[320,640]{1,0:T(8,128)S(1)} %get-tuple-element.17.student_ref, f32[320,640]{1,0:T(8,128)S(1)} %get-tuple-element.18.teacher_ref, ...), custom_call_target="tpu_custom_call" | custom-call | flops 419430400 | bytes 4440064 | tf_op jit(solution)/shard_map/pallas_call | solution.py:174
  56.6 1.6 %collective-permute-start.18 = (bf16[80,1024]{1,0:T(8,128)(2,1)S(1)}, bf16[80,1024]{1,0:T(8,128)(2,1)S(1)}, u32[]{:S(2)}, u32[]{:S(2)}) collective-permute-start(bf16[80,1024]{1,0:T(8,128)(2,1)S(1)} %get-tuple-element.24), channel_id=1, source_target_pairs={{0,8},{8,0},{1,9},{9,1},{2,10},{10,2},{3,11},{11,3},{4,12},{12,4},... | collective-permute-start | bytes 491528 | tf_op jit(solution)/shard_map/ppermute | solution.py:20
  58.2 5.1 %collective-permute-done.18 = bf16[80,1024]{1,0:T(8,128)(2,1)S(1)} collective-permute-done((bf16[80,1024]{1,0:T(8,128)(2,1)S(1)}, bf16[80,1024]{1,0:T(8,128)(2,1)S(1)}, u32[]{:S(2)}, u32[]{:S(2)}) %collective-permute-start.18) | collective-permute-done | bytes 163872 | tf_op jit(solution)/shard_map/ppermute | solution.py:20
  63.2 1.5 %collective-permute-start.19 = (bf16[80,1024]{1,0:T(8,128)(2,1)S(1)}, bf16[80,1024]{1,0:T(8,128)(2,1)S(1)}, u32[]{:S(2)}, u32[]{:S(2)}) collective-permute-start(bf16[80,1024]{1,0:T(8,128)(2,1)S(1)} %get-tuple-element.25), channel_id=1, source_target_pairs={{0,8},{8,0},{1,9},{9,1},{2,10},{10,2},{3,11},{11,3},{4,12},{12,4},... | collective-permute-start | bytes 491528 | tf_op jit(solution)/shard_map/ppermute | solution.py:20
  65.0 1.0 %collective-permute-start.22 = (bf16[80,1024]{1,0:T(8,128)(2,1)S(1)}, bf16[80,1024]{1,0:T(8,128)(2,1)S(1)}, u32[]{:S(2)}, u32[]{:S(2)}) collective-permute-start(bf16[80,1024]{1,0:T(8,128)(2,1)S(1)} %get-tuple-element.33), channel_id=1, source_target_pairs={{0,16},{16,0},{1,17},{17,1},{2,18},{18,2},{3,19},{19,3},{4,20},{20... | collective-permute-start | bytes 491528 | tf_op jit(solution)/shard_map/ppermute | solution.py:20
  66.1 1.3 %collective-permute-start.20 = (bf16[80,1024]{1,0:T(8,128)(2,1)S(1)}, bf16[80,1024]{1,0:T(8,128)(2,1)S(1)}, u32[]{:S(2)}, u32[]{:S(2)}) collective-permute-start(bf16[80,1024]{1,0:T(8,128)(2,1)S(1)} %add_convert_fusion), channel_id=1, source_target_pairs={{0,2},{2,0},{1,3},{3,1},{4,6},{6,4},{5,7},{7,5},{8,10},{10,8},{9,1... | collective-permute-start | bytes 491528 | tf_op jit(solution)/shard_map/ppermute | solution.py:20
  67.4 3.1 %collective-permute-done.22 = bf16[80,1024]{1,0:T(8,128)(2,1)S(1)} collective-permute-done((bf16[80,1024]{1,0:T(8,128)(2,1)S(1)}, bf16[80,1024]{1,0:T(8,128)(2,1)S(1)}, u32[]{:S(2)}, u32[]{:S(2)}) %collective-permute-start.22) | collective-permute-done | bytes 163872 | tf_op jit(solution)/shard_map/ppermute | solution.py:20
  70.6 1.0 %collective-permute-start.23 = (bf16[80,1024]{1,0:T(8,128)(2,1)S(1)}, bf16[80,1024]{1,0:T(8,128)(2,1)S(1)}, u32[]{:S(2)}, u32[]{:S(2)}) collective-permute-start(bf16[80,1024]{1,0:T(8,128)(2,1)S(1)} %get-tuple-element.31), channel_id=1, source_target_pairs={{0,16},{16,0},{1,17},{17,1},{2,18},{18,2},{3,19},{19,3},{4,20},{20... | collective-permute-start | bytes 491528 | tf_op jit(solution)/shard_map/ppermute | solution.py:20
  71.6 2.1 %collective-permute-start.24 = (bf16[80,1024]{1,0:T(8,128)(2,1)S(1)}, bf16[80,1024]{1,0:T(8,128)(2,1)S(1)}, u32[]{:S(2)}, u32[]{:S(2)}) collective-permute-start(bf16[80,1024]{1,0:T(8,128)(2,1)S(1)} %fusion), channel_id=1, source_target_pairs={{0,1},{1,0},{2,3},{3,2},{4,5},{5,4},{6,7},{7,6},{8,9},{9,8},{10,11... | collective-permute-start | bytes 491528 | tf_op jit(solution)/shard_map/ppermute | solution.py:20
  73.7 2.2 %collective-permute-done.20 = bf16[80,1024]{1,0:T(8,128)(2,1)S(1)} collective-permute-done((bf16[80,1024]{1,0:T(8,128)(2,1)S(1)}, bf16[80,1024]{1,0:T(8,128)(2,1)S(1)}, u32[]{:S(2)}, u32[]{:S(2)}) %collective-permute-start.20) | collective-permute-done | bytes 163872 | tf_op jit(solution)/shard_map/ppermute | solution.py:20
  76.7 1.5 %collective-permute-done.24 = bf16[80,1024]{1,0:T(8,128)(2,1)S(1)} collective-permute-done((bf16[80,1024]{1,0:T(8,128)(2,1)S(1)}, bf16[80,1024]{1,0:T(8,128)(2,1)S(1)}, u32[]{:S(2)}, u32[]{:S(2)}) %collective-permute-start.24) | collective-permute-done | bytes 163872 | tf_op jit(solution)/shard_map/ppermute | solution.py:20
  (81 shorter events, 17.0 us)
Async XLA Ops:
  0.6 0.9 %copy-start.2 = (bf16[80,1024]{1,0:T(8,128)(2,1)S(1)}, bf16[80,1024]{1,0:T(8,128)(2,1)}, u32[]{:S(2)}) copy-start(bf16[80,1024]{1,0:T(8,128)(2,1)} %left.1) | copy-start | bytes 491524
  1.5 0.9 %copy-start.6 = (bf16[80,768]{1,0:T(8,128)(2,1)S(1)}, bf16[80,768]{1,0:T(8,128)(2,1)}, u32[]{:S(2)}) copy-start(bf16[80,768]{1,0:T(8,128)(2,1)} %right.1) | copy-start | bytes 368644
  2.5 16.5 %collective-permute-start.6 = (bf16[80,1792]{1,0:T(8,128)(2,1)S(1)}, bf16[80,1792]{1,0:T(8,128)(2,1)S(1)}, u32[]{:S(2)}, u32[]{:S(2)}) collective-permute-start(bf16[80,1792]{1,0:T(8,128)(2,1)S(1)} %shard_map.59.refs_8_), channel_id=1, source_target_pairs={{0,1},{1,0},{2,3},{3,2},{4,5},{5,4},{6,7},{7,6},{8,9},{9,8},{10,11... | collective-permute-start | bytes 860168 | tf_op jit(solution)/shard_map/ppermute | solution.py:20
  5.6 19.6 %collective-permute-start.7 = (bf16[80,1792]{1,0:T(8,128)(2,1)S(1)}, bf16[80,1792]{1,0:T(8,128)(2,1)S(1)}, u32[]{:S(2)}, u32[]{:S(2)}) collective-permute-start(bf16[80,1792]{1,0:T(8,128)(2,1)S(1)} %shard_map.59.refs_8_), channel_id=1, source_target_pairs={{0,16},{16,0},{1,17},{17,1},{2,18},{18,2},{3,19},{19,3},{4,20},{20... | collective-permute-start | bytes 860168 | tf_op jit(solution)/shard_map/ppermute | solution.py:20
  7.1 8.5 %collective-permute-start.3 = (bf16[80,768]{1,0:T(8,128)(2,1)}, bf16[80,768]{1,0:T(8,128)(2,1)S(1)}, u32[]{:S(2)}, u32[]{:S(2)}) collective-permute-start(bf16[80,768]{1,0:T(8,128)(2,1)} %refs_4_.1), channel_id=1, source_target_pairs={{0,2},{2,0},{1,3},{3,1},{4,6},{6,4},{5,7},{7,5},{8,10},{10,8},{9,1... | collective-permute-start | bytes 368648 | tf_op jit(solution)/shard_map/ppermute | solution.py:20
  9.7 7.4 %collective-permute-start.4 = (bf16[80,768]{1,0:T(8,128)(2,1)}, bf16[80,768]{1,0:T(8,128)(2,1)S(1)}, u32[]{:S(2)}, u32[]{:S(2)}) collective-permute-start(bf16[80,768]{1,0:T(8,128)(2,1)} %refs_4_.1), channel_id=1, source_target_pairs={{0,8},{8,0},{1,9},{9,1},{2,10},{10,2},{3,11},{11,3},{4,12},{12,4},... | collective-permute-start | bytes 368648 | tf_op jit(solution)/shard_map/ppermute | solution.py:20
  11.2 12.0 %collective-permute-start = (bf16[80,1024]{1,0:T(8,128)(2,1)}, bf16[80,1024]{1,0:T(8,128)(2,1)S(1)}, u32[]{:S(2)}, u32[]{:S(2)}) collective-permute-start(bf16[80,1024]{1,0:T(8,128)(2,1)} %refs_0_.1), channel_id=1, source_target_pairs={{0,2},{2,0},{1,3},{3,1},{4,6},{6,4},{5,7},{7,5},{8,10},{10,8},{9,1... | collective-permute-start | bytes 491528 | tf_op jit(solution)/shard_map/ppermute | solution.py:20
  15.6 7.6 %collective-permute-start.1 = (bf16[80,1024]{1,0:T(8,128)(2,1)}, bf16[80,1024]{1,0:T(8,128)(2,1)S(1)}, u32[]{:S(2)}, u32[]{:S(2)}) collective-permute-start(bf16[80,1024]{1,0:T(8,128)(2,1)} %refs_0_.1), channel_id=1, source_target_pairs={{0,8},{8,0},{1,9},{9,1},{2,10},{10,2},{3,11},{11,3},{4,12},{12,4},... | collective-permute-start | bytes 491528 | tf_op jit(solution)/shard_map/ppermute | solution.py:20
  17.8 7.2 %collective-permute-start.5 = (bf16[80,768]{1,0:T(8,128)(2,1)S(1)}, bf16[80,768]{1,0:T(8,128)(2,1)S(1)}, u32[]{:S(2)}, u32[]{:S(2)}) collective-permute-start(bf16[80,768]{1,0:T(8,128)(2,1)S(1)} %collective-permute-done.3.refs_5_), channel_id=1, source_target_pairs={{0,8},{8,0},{1,9},{9,1},{2,10},{10,2},{3,11},{11,3},{4,12},{12,4},... | collective-permute-start | bytes 368648 | tf_op jit(solution)/shard_map/ppermute | solution.py:20
  19.0 7.2 %collective-permute-start.8 = (bf16[80,1792]{1,0:T(8,128)(2,1)S(1)}, bf16[80,1792]{1,0:T(8,128)(2,1)S(1)}, u32[]{:S(2)}, u32[]{:S(2)}) collective-permute-start(bf16[80,1792]{1,0:T(8,128)(2,1)S(1)} %collective-permute-done.6.refs_9_), channel_id=1, source_target_pairs={{0,16},{16,0},{1,17},{17,1},{2,18},{18,2},{3,19},{19,3},{4,20},{20... | collective-permute-start | bytes 860168 | tf_op jit(solution)/shard_map/ppermute | solution.py:20
  23.2 3.9 %collective-permute-start.9 = (bf16[80,1792]{1,0:T(8,128)(2,1)S(1)}, bf16[80,1792]{1,0:T(8,128)(2,1)S(1)}, u32[]{:S(2)}, u32[]{:S(2)}) collective-permute-start(bf16[80,1792]{1,0:T(8,128)(2,1)S(1)} %shard_map.59.refs_8_), channel_id=1, source_target_pairs={{0,4},{4,0},{1,5},{5,1},{2,6},{6,2},{3,7},{7,3},{8,12},{12,8},{9,1... | collective-permute-start | bytes 860168 | tf_op jit(solution)/shard_map/ppermute | solution.py:20
  23.2 6.6 %collective-permute-start.2 = (bf16[80,1024]{1,0:T(8,128)(2,1)S(1)}, bf16[80,1024]{1,0:T(8,128)(2,1)S(1)}, u32[]{:S(2)}, u32[]{:S(2)}) collective-permute-start(bf16[80,1024]{1,0:T(8,128)(2,1)S(1)} %collective-permute-done.refs_1_), channel_id=1, source_target_pairs={{0,8},{8,0},{1,9},{9,1},{2,10},{10,2},{3,11},{11,3},{4,12},{12,4},... | collective-permute-start | bytes 491528 | tf_op jit(solution)/shard_map/ppermute | solution.py:20
  24.9 4.9 %collective-permute-start.10 = (bf16[80,1792]{1,0:T(8,128)(2,1)S(1)}, bf16[80,1792]{1,0:T(8,128)(2,1)S(1)}, u32[]{:S(2)}, u32[]{:S(2)}) collective-permute-start(bf16[80,1792]{1,0:T(8,128)(2,1)S(1)} %collective-permute-done.6.refs_9_), channel_id=1, source_target_pairs={{0,4},{4,0},{1,5},{5,1},{2,6},{6,2},{3,7},{7,3},{8,12},{12,8},{9,1... | collective-permute-start | bytes 860168 | tf_op jit(solution)/shard_map/ppermute | solution.py:20
  25.2 4.7 %collective-permute-start.11 = (bf16[80,1792]{1,0:T(8,128)(2,1)S(1)}, bf16[80,1792]{1,0:T(8,128)(2,1)S(1)}, u32[]{:S(2)}, u32[]{:S(2)}) collective-permute-start(bf16[80,1792]{1,0:T(8,128)(2,1)S(1)} %collective-permute-done.7.refs_10_), channel_id=1, source_target_pairs={{0,4},{4,0},{1,5},{5,1},{2,6},{6,2},{3,7},{7,3},{8,12},{12,8},{9,1... | collective-permute-start | bytes 860168 | tf_op jit(solution)/shard_map/ppermute | solution.py:20
  26.2 3.7 %collective-permute-start.12 = (bf16[80,1792]{1,0:T(8,128)(2,1)S(1)}, bf16[80,1792]{1,0:T(8,128)(2,1)S(1)}, u32[]{:S(2)}, u32[]{:S(2)}) collective-permute-start(bf16[80,1792]{1,0:T(8,128)(2,1)S(1)} %collective-permute-done.8.refs_11_), channel_id=1, source_target_pairs={{0,4},{4,0},{1,5},{5,1},{2,6},{6,2},{3,7},{7,3},{8,12},{12,8},{9,1... | collective-permute-start | bytes 860168 | tf_op jit(solution)/shard_map/ppermute | solution.py:20
  27.1 14.6 %copy-start.16 = (s32[2]{0:T(128)S(1)}, s32[2]{0:T(128)}, u32[]{:S(2)}) copy-start(s32[2]{0:T(128)} %get-tuple-element.35) | copy-start | bytes 28
  29.8 1.0 %copy-start.1 = (bf16[80,1792]{1,0:T(8,128)(2,1)S(1)}, bf16[80,1792]{1,0:T(8,128)(2,1)}, u32[]{:S(2)}) copy-start(bf16[80,1792]{1,0:T(8,128)(2,1)} %copy-done) | copy-start | bytes 860164
  30.8 0.9 %copy-start.3 = (bf16[80,1024]{1,0:T(8,128)(2,1)S(1)}, bf16[80,1024]{1,0:T(8,128)(2,1)}, u32[]{:S(2)}) copy-start(bf16[80,1024]{1,0:T(8,128)(2,1)} %refs_0_.1) | copy-start | bytes 491524
  31.7 0.9 %copy-start.5 = (bf16[80,1024]{1,0:T(8,128)(2,1)S(1)}, bf16[80,1024]{1,0:T(8,128)(2,1)}, u32[]{:S(2)}) copy-start(bf16[80,1024]{1,0:T(8,128)(2,1)} %copy-done.4) | copy-start | bytes 491524
  41.8 1.4 %collective-permute-start.15 = (f32[8,8,128]{2,1,0:T(8,128)}, f32[8,8,128]{2,1,0:T(8,128)S(1)}, u32[]{:S(2)}, u32[]{:S(2)}) collective-permute-start(f32[8,8,128]{2,1,0:T(8,128)} %get-tuple-element.20.one), channel_id=1, source_target_pairs={{0,4},{4,0},{1,5},{5,1},{2,6},{6,2},{3,7},{7,3},{8,12},{12,8},{9,1... | collective-permute-start | bytes 98312 | tf_op jit(solution)/shard_map/ppermute | solution.py:20
  41.9 4.0 %collective-permute-start.13 = (f32[4,8,128]{2,1,0:T(8,128)}, f32[4,8,128]{2,1,0:T(8,128)S(1)}, u32[]{:S(2)}, u32[]{:S(2)}) collective-permute-start(f32[4,8,128]{2,1,0:T(8,128)} %copy-done.12), channel_id=1, source_target_pairs={{0,8},{8,0},{1,9},{9,1},{2,10},{10,2},{3,11},{11,3},{4,12},{12,4},... | collective-permute-start | bytes 49160 | tf_op jit(solution)/shard_map/ppermute | solution.py:20
  44.0 4.0 %collective-permute-start.16 = (f32[8,8,128]{2,1,0:T(8,128)S(1)}, f32[8,8,128]{2,1,0:T(8,128)S(1)}, u32[]{:S(2)}, u32[]{:S(2)}) collective-permute-start(f32[8,8,128]{2,1,0:T(8,128)S(1)} %shard_map.63.one), channel_id=1, source_target_pairs={{0,16},{16,0},{1,17},{17,1},{2,18},{18,2},{3,19},{19,3},{4,20},{20... | collective-permute-start | bytes 98312 | tf_op jit(solution)/shard_map/ppermute | solution.py:20
  46.6 6.5 %collective-permute-start.14 = (f32[4,8,128]{2,1,0:T(8,128)S(1)}, f32[4,8,128]{2,1,0:T(8,128)S(1)}, u32[]{:S(2)}, u32[]{:S(2)}) collective-permute-start(f32[4,8,128]{2,1,0:T(8,128)S(1)} %shard_map.61.one), channel_id=1, source_target_pairs={{0,2},{2,0},{1,3},{3,1},{4,6},{6,4},{5,7},{7,5},{8,10},{10,8},{9,1... | collective-permute-start | bytes 49160 | tf_op jit(solution)/shard_map/ppermute | solution.py:20
  48.0 6.2 %collective-permute-start.17 = (f32[8,8,128]{2,1,0:T(8,128)S(1)}, f32[8,8,128]{2,1,0:T(8,128)S(1)}, u32[]{:S(2)}, u32[]{:S(2)}) collective-permute-start(f32[8,8,128]{2,1,0:T(8,128)S(1)} %shard_map.64.one), channel_id=1, source_target_pairs={{0,1},{1,0},{2,3},{3,2},{4,5},{5,4},{6,7},{7,6},{8,9},{9,8},{10,11... | collective-permute-start | bytes 98312 | tf_op jit(solution)/shard_map/ppermute | solution.py:20
  54.3 1.4 %copy-start.15 = (bf16[320,1024]{1,0:T(8,128)(2,1)S(1)}, bf16[320,1024]{1,0:T(8,128)(2,1)}, u32[]{:S(2)}) copy-start(bf16[320,1024]{1,0:T(8,128)(2,1)} %copy-done.14) | copy-start | bytes 1966084
  56.5 8.2 %collective-permute-start.21 = (bf16[320,1024]{1,0:T(8,128)(2,1)S(1)}, bf16[320,1024]{1,0:T(8,128)(2,1)S(1)}, u32[]{:S(2)}, u32[]{:S(2)}) collective-permute-start(bf16[320,1024]{1,0:T(8,128)(2,1)S(1)} %get-tuple-element.30), channel_id=1, source_target_pairs={{0,4},{4,0},{1,5},{5,1},{2,6},{6,2},{3,7},{7,3},{8,12},{12,8},{9,1... | collective-permute-start | bytes 1966088 | tf_op jit(solution)/shard_map/ppermute | solution.py:20
  56.6 6.6 %collective-permute-start.18 = (bf16[80,1024]{1,0:T(8,128)(2,1)S(1)}, bf16[80,1024]{1,0:T(8,128)(2,1)S(1)}, u32[]{:S(2)}, u32[]{:S(2)}) collective-permute-start(bf16[80,1024]{1,0:T(8,128)(2,1)S(1)} %get-tuple-element.24), channel_id=1, source_target_pairs={{0,8},{8,0},{1,9},{9,1},{2,10},{10,2},{3,11},{11,3},{4,12},{12,4},... | collective-permute-start | bytes 491528 | tf_op jit(solution)/shard_map/ppermute | solution.py:20
  63.2 10.4 %collective-permute-start.19 = (bf16[80,1024]{1,0:T(8,128)(2,1)S(1)}, bf16[80,1024]{1,0:T(8,128)(2,1)S(1)}, u32[]{:S(2)}, u32[]{:S(2)}) collective-permute-start(bf16[80,1024]{1,0:T(8,128)(2,1)S(1)} %get-tuple-element.25), channel_id=1, source_target_pairs={{0,8},{8,0},{1,9},{9,1},{2,10},{10,2},{3,11},{11,3},{4,12},{12,4},... | collective-permute-start | bytes 491528 | tf_op jit(solution)/shard_map/ppermute | solution.py:20
  65.0 5.5 %collective-permute-start.22 = (bf16[80,1024]{1,0:T(8,128)(2,1)S(1)}, bf16[80,1024]{1,0:T(8,128)(2,1)S(1)}, u32[]{:S(2)}, u32[]{:S(2)}) collective-permute-start(bf16[80,1024]{1,0:T(8,128)(2,1)S(1)} %get-tuple-element.33), channel_id=1, source_target_pairs={{0,16},{16,0},{1,17},{17,1},{2,18},{18,2},{3,19},{19,3},{4,20},{20... | collective-permute-start | bytes 491528 | tf_op jit(solution)/shard_map/ppermute | solution.py:20
  66.1 9.8 %collective-permute-start.20 = (bf16[80,1024]{1,0:T(8,128)(2,1)S(1)}, bf16[80,1024]{1,0:T(8,128)(2,1)S(1)}, u32[]{:S(2)}, u32[]{:S(2)}) collective-permute-start(bf16[80,1024]{1,0:T(8,128)(2,1)S(1)} %add_convert_fusion), channel_id=1, source_target_pairs={{0,2},{2,0},{1,3},{3,1},{4,6},{6,4},{5,7},{7,5},{8,10},{10,8},{9,1... | collective-permute-start | bytes 491528 | tf_op jit(solution)/shard_map/ppermute | solution.py:20
  70.6 6.1 %collective-permute-start.23 = (bf16[80,1024]{1,0:T(8,128)(2,1)S(1)}, bf16[80,1024]{1,0:T(8,128)(2,1)S(1)}, u32[]{:S(2)}, u32[]{:S(2)}) collective-permute-start(bf16[80,1024]{1,0:T(8,128)(2,1)S(1)} %get-tuple-element.31), channel_id=1, source_target_pairs={{0,16},{16,0},{1,17},{17,1},{2,18},{18,2},{3,19},{19,3},{4,20},{20... | collective-permute-start | bytes 491528 | tf_op jit(solution)/shard_map/ppermute | solution.py:20
  71.6 6.6 %collective-permute-start.24 = (bf16[80,1024]{1,0:T(8,128)(2,1)S(1)}, bf16[80,1024]{1,0:T(8,128)(2,1)S(1)}, u32[]{:S(2)}, u32[]{:S(2)}) collective-permute-start(bf16[80,1024]{1,0:T(8,128)(2,1)S(1)} %fusion), channel_id=1, source_target_pairs={{0,1},{1,0},{2,3},{3,2},{4,5},{5,4},{6,7},{7,6},{8,9},{9,8},{10,11... | collective-permute-start | bytes 491528 | tf_op jit(solution)/shard_map/ppermute | solution.py:20
  (10 other events, 7.6 us)

commit v4 on v1

v4 whole, which is shorter than its diff:
```python
import functools
import math

import jax
import jax.numpy as jnp
from jax import lax
from jax.experimental import pallas as pl
from jax.experimental.pallas import tpu as pltpu
from jax.sharding import Mesh, PartitionSpec as P

logit_gain = 3.0
ROW_AXES = ("ilo", "chi")
COL_AXES = ("core", "ihi", "clo")
ROW_STEPS = ("ilo", "chi")
COL_STEPS = ("ihi", "clo", "core")
ROW_ORDER = ("ihi", "ilo", "core", "chi", "clo")
COL_ORDER = ("chi", "clo", "ihi", "ilo", "core")
LANES = 128
PEAK_S, TOTAL_S, PEAK_T, TOTAL_T, INDEX = range(5)


def swap(value, axis, mask):
    size = lax.axis_size(axis)
    return lax.ppermute(value, axis, [(j, j ^ mask) for j in range(size)])


def bits(axis):
    size = lax.axis_size(axis)
    return [1 << b for b in range(size.bit_length() - 1)]


def lines_of(columns):
    count = columns[0].shape[0]
    lane = lax.broadcasted_iota(jnp.int32, (count, LANES), 1)
    wide = jnp.zeros((count, LANES), jnp.float32)
    for k, column in enumerate(columns):
        wide = jnp.where(lane == k, column, wide)
    spare = -count % LANES
    if spare:
        wide = jnp.concatenate([wide, jnp.zeros((spare, LANES), jnp.float32)], axis=0)
    return wide.T[:8, :count]


def columns_of(lines):
    count = lines.shape[1]
    spare = -count % LANES
    if spare:
        lines = jnp.concatenate([lines, jnp.zeros((8, spare), jnp.float32)], axis=1)
    tall = jnp.concatenate([lines, jnp.zeros((LANES - 8, count + spare), jnp.float32)], axis=0)
    return tall.T[:count]


def load_slots(blocks, rows):
    return jnp.concatenate([block[:, :rows] for block in blocks], axis=1)


def owners(axes, order):
    sizes = [lax.axis_size(a) for a in axes]
    result = []
    for s in range(math.prod(sizes)):
        place = {a: lax.axis_index(a) for a in order}
        for axis, size in zip(reversed(axes), reversed(sizes)):
            place[axis] = place[axis] ^ (s % size)
            s //= size
        owner = 0
        for axis in order:
            owner = owner * lax.axis_size(axis) + place[axis]
        result.append(owner)
    return result


def joined(refs, columns=slice(None)):
    values = [ref[:, columns] for ref in refs]
    return values[0] if len(values) == 1 else jnp.concatenate(values, axis=0)


def copy_all(pairs, sems):
    copies = [pltpu.make_async_copy(src, dst, sems.at[k]) for k, (src, dst) in enumerate(pairs)]
    for copy in copies:
        copy.start()
    for copy in copies:
        copy.wait()


def pack_kernel(image_s, image_t, caption_s, caption_t, image, caption, sems):
    width = image_s.shape[1]
    copy_all(
        [
            (image_s, image.at[:, :width]),
            (image_t, image.at[:, width:]),
            (caption_s, caption.at[:, :width]),
            (caption_t, caption.at[:, width:]),
        ],
        sems,
    )


def assemble_kernel(*refs):
    refs[-1][...] = joined(refs[:-1])


def logits(left, right, out):
    gain = logit_gain / math.sqrt(left.shape[1])
    out[...] = gain * lax.dot_general(left, right, (((1,), (1,)), ((), ())), preferred_element_type=jnp.float32)
    matrix = out[...]
    peak = jnp.max(matrix, axis=1, keepdims=True)
    columns = [peak, jnp.sum(jnp.exp(matrix - peak), axis=1, keepdims=True)]
    peak = jnp.max(matrix, axis=0, keepdims=True)
    return columns, [peak, jnp.sum(jnp.exp(matrix - peak), axis=0, keepdims=True)]


def logits_kernel(n_img, rows, width, *refs):
    img_parts, cap_parts = refs[:n_img], refs[n_img:-5]
    student_ref, teacher_ref, row_ref, col_ref, images = refs[-5:]
    columns, lines = [], []
    for part, out in ((slice(0, width), student_ref), (slice(width, None), teacher_ref)):
        left = joined(img_parts, part)
        if out is student_ref:
            images[...] = left
        more = logits(left, joined(cap_parts, part), out)
        columns, lines = columns + more[0], lines + more[1]
    lines.append(jnp.zeros((4, lines[0].shape[1]), jnp.float32))
    row = lax.broadcasted_iota(jnp.int32, (8, LANES), 0)
    lane = lax.broadcasted_iota(jnp.int32, (8, LANES), 1)
    for ref, values, axes, order in (
        (row_ref, lines_of(columns), ROW_AXES, ROW_ORDER),
        (col_ref, jnp.concatenate(lines, axis=0), COL_AXES, COL_ORDER),
    ):
        for s, owner in enumerate(owners(axes, order)):
            ref[s] = jnp.zeros((8, LANES), jnp.float32)
            ref[s, :, :rows] = values[:, s * rows : (s + 1) * rows]
            index = (owner * rows + lane).astype(jnp.float32)
            ref[s] = jnp.where(row == INDEX, index, ref[s])


def merged(x, y):
    line = lax.broadcasted_iota(jnp.int32, x.shape, 0)
    student = line <= TOTAL_S
    x_peak = jnp.where(student, x[PEAK_S : PEAK_S + 1], x[PEAK_T : PEAK_T + 1])
    y_peak = jnp.where(student, y[PEAK_S : PEAK_S + 1], y[PEAK_T : PEAK_T + 1])
    peak = jnp.maximum(x_peak, y_peak)
    total = x * jnp.exp(x_peak - peak) + y * jnp.exp(y_peak - peak)
    both = jnp.where((line == PEAK_S) | (line == PEAK_T), peak, total)
    return jnp.where(line < INDEX, both, x)


def merged_blocks(mine, other, distance):
    return [merged(mine[s], other[s ^ distance]) for s in range(mine.shape[0])]


def merge_kernel(distances, *refs):
    n = len(distances)
    for k, distance in enumerate(distances):
        for s, block in enumerate(merged_blocks(refs[2 * k], refs[2 * k + 1], distance)):
            refs[2 * n + k][s] = block


def tile_kernel(distances, rows, student_ref, teacher_ref, *refs):
    refs = list(refs)
    blocks = []
    for distance in distances:
        mine = refs.pop(0)
        if distance is None:
            blocks.append([mine[s] for s in range(mine.shape[0])])
        else:
            blocks.append(merged_blocks(mine, refs.pop(0), distance))
    tile_ref, send_ref = refs
    total, count = teacher_ref.shape

    def finish(blocks):
        lines = load_slots(blocks, rows)
        line = lax.broadcasted_iota(jnp.int32, lines.shape, 0)
        lse_s = lines[PEAK_S : PEAK_S + 1] + jnp.log(lines[TOTAL_S : TOTAL_S + 1])
        lse_t = lines[PEAK_T : PEAK_T + 1] + jnp.log(lines[TOTAL_T : TOTAL_T + 1])
        return jnp.where(line == 0, lse_s, jnp.where(line == 1, lse_t, lines))

    down, across = columns_of(finish(blocks[0])), finish(blocks[1])
    step = 64 if total % 64 == 0 else total
    for r in range(0, total, step):
        at = slice(r, r + step)
        s, t = student_ref[at], teacher_ref[at]
        grad = 0.5 * (jnp.exp(s - down[at, 0:1]) + jnp.exp(s - across[0:1]))
        grad = grad - 0.25 * (jnp.exp(t - down[at, 1:2]) + jnp.exp(t - across[1:2]))
        grad = grad - jnp.where(down[at, INDEX : INDEX + 1] == across[INDEX : INDEX + 1], 0.5, 0.0)
        tile_ref[at] = grad.astype(jnp.bfloat16)
    send_ref[...] = tile_ref[:, count // 2 :]


def spread(part, outs):
    start = 0
    for out in outs:
        out[...] = part[start : start + out.shape[0]].astype(out.dtype)
        start += out.shape[0]


def image_kernel(width, tile_ref, *refs):
    parts = [ref for ref in refs if ref.dtype == jnp.bfloat16 and ref.shape[1] > width]
    right = joined(parts, slice(0, width))
    spread(jnp.dot(tile_ref[...], right, preferred_element_type=jnp.float32), refs[len(parts) :])


def caption_kernel(tile_ref, tile_other, images, images_other, *outs):
    half = tile_other.shape[1]
    part = 0.0
    for tile, rows in ((tile_ref[:, :half], images[...]), (tile_other[...], images_other[...])):
        part = part + lax.dot_general(tile, rows, (((0,), (0,)), ((), ())), preferred_element_type=jnp.float32)
    spread(part, outs)


def sum_kernel(counts, *refs):
    refs = list(refs)
    terms = [[refs.pop(0) for _ in range(count)] for count in counts]
    outs, held, sems = refs[: len(counts)], refs[len(counts) : -1], refs[-1]
    copies = []
    for k, (group, out, here) in enumerate(zip(terms, outs, held)):
        total = group[0][...]
        for term in group[1:]:
            total = total + term[...].astype(jnp.float32)
        here[...] = total
        copies.append(pltpu.make_async_copy(here, out, sems.at[k]))
        copies[-1].start()
    for copy in copies:
        copy.wait()


VMEM, HBM = pltpu.VMEM, pltpu.HBM


def call(kernel, outs, args, flops=0, scratch=(), in_hbm=0, out_space=VMEM):
    moved = sum(math.prod(a.shape) * a.dtype.itemsize for a in list(args) + list(outs))
    spaces = [HBM] * in_hbm + [VMEM] * (len(args) - in_hbm)
    return pl.pallas_call(
        kernel,
        out_shape=[out_space(out.shape, out.dtype) for out in outs],
        in_specs=[pl.BlockSpec(memory_space=space) for space in spaces],
        out_specs=[pl.BlockSpec(memory_space=out_space)] * len(outs),
        scratch_shapes=scratch,
        compiler_params=pltpu.CompilerParams(vmem_limit_bytes=16 * 2**20),
        cost_estimate=pl.CostEstimate(flops=flops, bytes_accessed=moved, transcendentals=0),
    )(*(pltpu.with_memory_space_constraint(arg, space) for arg, space in zip(args, spaces)))


def steps_of(names, axes):
    result = []
    for name in names:
        stride = math.prod(lax.axis_size(a) for a in axes[axes.index(name) + 1 :])
        result += [(name, bit, stride * bit) for bit in bits(name)]
    return result


def after(value, *others):
    return lax.optimization_barrier((value, others))[0]


def local(image_student, caption_student, image_teacher, caption_teacher):
    ilo, chi, core, ihi, clo = (lax.axis_size(a) for a in ROW_AXES + COL_AXES)
    rows, width = image_student.shape
    depth = image_teacher.shape[1]
    assert rows <= LANES and core == 2 and chi > 1 and clo > 1
    n_img, n_cap = ilo * chi, core * ihi * clo
    total, columns = n_img * rows, n_cap * rows
    f32, bf16 = jnp.float32, jnp.bfloat16
    shape = jax.ShapeDtypeStruct
    dma = pltpu.SemaphoreType.DMA

    aligned = rows % 16 == 0
    if aligned:
        image, caption = call(
            pack_kernel,
            [shape((rows, width + depth), bf16)] * 2,
            [image_student, image_teacher, caption_student, caption_teacher],
            scratch=[dma((4,))],
            in_hbm=4,
        )
    else:
        image = jnp.concatenate([image_student, image_teacher], axis=1)
        caption = jnp.concatenate([caption_student, caption_teacher], axis=1)

    def assemble(parts):
        if not aligned:
            return jnp.concatenate(parts, axis=0)
        return call(assemble_kernel, [shape((len(parts) * rows, width + depth), bf16)], parts)[0]

    def gather(own, far_axis, near_axis):
        near = {m: swap(own, near_axis, m) for m in range(1, lax.axis_size(near_axis))}
        far = [swap(own, far_axis, m) for m in range(1, lax.axis_size(far_axis))]
        return [own] + far + [p for m in near for p in [near[m]] + [swap(part, near_axis, m) for part in far]]

    img, cap = gather(image, "chi", "ilo"), gather(caption, "clo", "ihi")
    cap = [assemble([after(cap[0], *img[1 : chi + 1])] + cap[1:-1]), cap[-1]]
    cap = cap + [swap(part, "core", 1) for part in cap]
    if not aligned:
        img, cap = [assemble(img)], [assemble(cap)]

    row_shape, col_shape = shape((n_img, 8, LANES), f32), shape((n_cap, 8, LANES), f32)
    student, teacher, row_stats, col_stats, images = call(
        functools.partial(logits_kernel, len(img), rows, width),
        [shape((total, columns), f32)] * 2 + [row_shape, col_shape, shape((total, width), bf16)],
        img + cap,
        2 * total * columns * (width + depth),
    )

    stats = [row_stats, col_stats]
    steps = [steps_of(ROW_STEPS, ROW_AXES), steps_of(COL_STEPS, COL_AXES)]
    count = max(map(len, steps))
    for k in range(count):
        active = [d for d in range(2) if k < len(steps[d])]
        arrived = {d: swap(stats[d], steps[d][k][0], steps[d][k][1]) for d in active}
        if k == count - 1:
            break
        results = call(
            functools.partial(merge_kernel, [steps[d][k][2] for d in active]),
            [shape(stats[d].shape, f32) for d in active],
            [block for d in active for block in (stats[d], arrived[d])],
        )
        for d, result in zip(active, results):
            stats[d] = result

    images_other = swap(after(images, stats[1]), "core", 1)
    tile, tile_send = call(
        functools.partial(tile_kernel, [steps[d][k][2] if d in active else None for d in range(2)], rows),
        [shape((total, columns), bf16), shape((total, columns // 2), bf16)],
        [student, teacher] + [b for d in range(2) for b in ([stats[d], arrived[d]] if d in active else [stats[d]])],
        10 * total * columns,
    )
    tile_other = swap(tile_send, "core", 1)

    def outs_of(count, near, far):
        piece = count // (near * far)
        return [shape((piece, width), f32)] * far + [shape((piece, width), bf16)] * ((near - 1) * far)

    image_parts = call(
        functools.partial(image_kernel, width),
        outs_of(total, ilo, chi),
        [tile] + cap,
        2 * total * columns * width,
    )
    caption_parts = call(
        caption_kernel,
        outs_of(columns // 2, ihi, clo),
        [tile, tile_other, images, images_other],
        2 * total * columns * width,
    )

    def hop(parts, near, far, f, *gate):
        size = lax.axis_size(far)
        sent = [(m, parts[m * size + f]) for m in range(1, lax.axis_size(near))]
        return [parts[f]] + [swap(after(term, *gate) if gate else term, near, m) for m, term in sent]

    def rounded(terms):
        total = terms[0]
        for term in terms[1:]:
            total = total + term.astype(f32)
        return total.astype(bf16)

    image_far = [rounded(hop(image_parts, "ilo", "chi", f)) for f in range(1, chi)]
    caption_far = [rounded(hop(caption_parts, "ihi", "clo", f)) for f in range(1, clo)]
    image_terms = hop(image_parts, "ilo", "chi", 0, image_far[0], caption_far[0])
    caption_terms = hop(caption_parts, "ihi", "clo", 0, image_far[0], caption_far[0])
    image_terms += [swap(image_far[f - 1], "chi", f) for f in range(1, chi)]
    caption_terms += [swap(caption_far[f - 1], "clo", f) for f in range(1, clo)]
    out = shape((rows, width), f32)
    return tuple(
        call(
            functools.partial(sum_kernel, (len(image_terms), len(caption_terms))),
            [out, out],
            image_terms + caption_terms,
            scratch=[pltpu.VMEM((rows, width), f32)] * 2 + [dma((2,))],
            out_space=HBM,
        )
    )


def split(count):
    low = 1 << ((count.bit_length() - 1) // 2)
    return count // low, low


def solution(mesh):
    ihi, ilo = split(mesh.shape["img"] // 2)
    chi, clo = split(mesh.shape["cap"])
    fine = Mesh(mesh.devices.reshape(ihi, ilo, 2, chi, clo), ("ihi", "ilo", "core", "chi", "clo"))
    by_image = P(("ihi", "ilo", "core", "chi", "clo"), None)
    by_caption = P(("chi", "clo", "ihi", "ilo", "core"), None)
    return jax.shard_map(
        local,
        mesh=fine,
        in_specs=(by_image, by_caption, by_image, by_caption),
        out_specs=(by_image, by_caption),
        check_vma=False,
    )
```

time: 84.6 us -> 68.1 us (0.80)
  local copies, waits for them, and re-layouts: 14.1 us -> 0 us
  matrix products: 6.33 us -> 0 us
  Pallas kernels: 0 us -> 6.2 us
  waiting for transfers between devices: 34.2 us -> 39.4 us
  other arithmetic: 3.54 us -> 0.06 us
  starting transfers between devices: 24.9 us -> 21.6 us
    ppermute x17 -> x21, waiting for transfers between devices: 23.3 us -> 39.4 us  [swap(): return lax.ppermute(value, axis, [(j, j ^ mask) for j in range(size)])]
    all_to_all x2 -> x0, waiting for transfers between devices: 10.9 us -> none  [pool(): lax.all_to_all(jnp.broadcast_to(mine[None], (count,) + mine.shape), axes,...]
    all_to_all x2 -> x0, starting transfers between devices: 8.55 us -> none  [pool(): lax.all_to_all(jnp.broadcast_to(mine[None], (count,) + mine.shape), axes,...]
    unnamed x18 -> x0, local copies, waits for them, and re-layouts: 7.23 us -> none
    dot_general x4 -> x0, matrix products: 6.33 us -> none  [the longest x2 4 us: scores(): lax.dot_general(left, right, (((1,), (1,)), ((), ())), preferred_element_...]
    pallas_call x0 -> x9, Pallas kernels: none -> 6.2 us  [call(): pl.pallas_call(kernel, out_shape=[out_space(out.shape, out.dtype) for out...]
    ppermute x17 -> x21, starting transfers between devices: 16.4 us -> 21.6 us  [swap(): return lax.ppermute(value, axis, [(j, j ^ mask) for j in range(size)])]
    concatenate x3 -> x0, local copies, waits for them, and re-layouts: 3.26 us -> none  [the longest x1 1.57 us: local(): caption = jnp.concatenate([caption_student, caption_teacher], axis=1)]
  transfers between devices with their start and end apart: 19 -> 21, of which waited for: 10 -> 13; matrix products, arithmetic and copies ran while one was open for 12% -> 0% of each run, Pallas kernels for 0% -> 4%
where the time goes in v4:
time: 68.1 us; the launch traced here: 68 us
  waiting for transfers between devices  39.4 us (58%)
  starting transfers between devices  21.6 us (32%)
  Pallas kernels  6.2 us (9%)
  between operations  0.72 us (1%)
    ppermute x21, waiting for transfers between devices, swap(): return lax.ppermute(value, axis, [(j, j ^ mask) for j in range(size)])  39.4 us
    ppermute x21, starting transfers between devices, swap(): return lax.ppermute(value, axis, [(j, j ^ mask) for j in range(size)])  21.6 us
    pallas_call x9, Pallas kernels, call(): pl.pallas_call(kernel, out_shape=[out_space(out.shape, out.dtype) for out...  6.2 us
  transfers between devices with their start and end apart: 21, of which 13 were waited for; matrix products, arithmetic and copies ran while one was open for 0% of the time, Pallas kernels for 4%

profile of v4, /device:TPU:0, one launch (start us, length us, event | category | flops | bytes accessed | tf_op | source)
XLA Modules:
  0.0 68.0 jit_solution(2916504979014566586)
XLA Ops:
  0.6 1.2 %shard_map.59 = (bf16[80,1792]{1,0:T(8,128)(2,1)S(1)}, bf16[80,1792]{1,0:T(8,128)(2,1)S(1)}) custom-call(bf16[80,1024]{1,0:T(8,128)(2,1)} %image_s.1, bf16[80,768]{1,0:T(8,128)(2,1)} %image_t.1, bf16[80,1024]{1,0:T(8,128)(2,1)} %caption_s.1, bf16[80,768]{1,0:T(8,128)(2,1)} %caption_t.1), custom_call_target="tpu_custom_call" | custom-call | bytes 1146880 | tf_op jit(solution)/shard_map/pallas_call | solution.py:232
  1.8 3.0 %collective-permute-start.1 = (bf16[80,1792]{1,0:T(8,128)(2,1)S(1)}, bf16[80,1792]{1,0:T(8,128)(2,1)S(1)}, u32[]{:S(2)}, u32[]{:S(2)}) collective-permute-start(bf16[80,1792]{1,0:T(8,128)(2,1)S(1)} %get-tuple-element.27.refs_0_), channel_id=1, source_target_pairs={{0,8},{8,0},{1,9},{9,1},{2,10},{10,2},{3,11},{11,3},{4,12},{12,4},... | collective-permute-start | bytes 860168 | tf_op jit(solution)/shard_map/ppermute | solution.py:24
  4.8 2.6 %collective-permute-start = (bf16[80,1792]{1,0:T(8,128)(2,1)S(1)}, bf16[80,1792]{1,0:T(8,128)(2,1)S(1)}, u32[]{:S(2)}, u32[]{:S(2)}) collective-permute-start(bf16[80,1792]{1,0:T(8,128)(2,1)S(1)} %get-tuple-element.27.refs_0_), channel_id=1, source_target_pairs={{0,2},{2,0},{1,3},{3,1},{4,6},{6,4},{5,7},{7,5},{8,10},{10,8},{9,1... | collective-permute-start | bytes 860168 | tf_op jit(solution)/shard_map/ppermute | solution.py:24
  7.4 1.5 %collective-permute-start.4 = (bf16[80,1792]{1,0:T(8,128)(2,1)S(1)}, bf16[80,1792]{1,0:T(8,128)(2,1)S(1)}, u32[]{:S(2)}, u32[]{:S(2)}) collective-permute-start(bf16[80,1792]{1,0:T(8,128)(2,1)S(1)} %get-tuple-element.29.refs_0_), channel_id=1, source_target_pairs={{0,16},{16,0},{1,17},{17,1},{2,18},{18,2},{3,19},{19,3},{4,20},{20... | collective-permute-start | bytes 860168 | tf_op jit(solution)/shard_map/ppermute | solution.py:24
  8.9 1.6 %collective-permute-start.3 = (bf16[80,1792]{1,0:T(8,128)(2,1)S(1)}, bf16[80,1792]{1,0:T(8,128)(2,1)S(1)}, u32[]{:S(2)}, u32[]{:S(2)}) collective-permute-start(bf16[80,1792]{1,0:T(8,128)(2,1)S(1)} %get-tuple-element.29.refs_0_), channel_id=1, source_target_pairs={{0,1},{1,0},{2,3},{3,2},{4,5},{5,4},{6,7},{7,6},{8,9},{9,8},{10,11... | collective-permute-start | bytes 860168 | tf_op jit(solution)/shard_map/ppermute | solution.py:24
  10.5 1.1 %collective-permute-done.1.refs_2_ = bf16[80,1792]{1,0:T(8,128)(2,1)S(1)} collective-permute-done((bf16[80,1792]{1,0:T(8,128)(2,1)S(1)}, bf16[80,1792]{1,0:T(8,128)(2,1)S(1)}, u32[]{:S(2)}, u32[]{:S(2)}) %collective-permute-start.1) | collective-permute-done | bytes 286752 | tf_op jit(solution)/shard_map/ppermute | solution.py:24
  11.6 8.6 %collective-permute-done.refs_1_ = bf16[80,1792]{1,0:T(8,128)(2,1)S(1)} collective-permute-done((bf16[80,1792]{1,0:T(8,128)(2,1)S(1)}, bf16[80,1792]{1,0:T(8,128)(2,1)S(1)}, u32[]{:S(2)}, u32[]{:S(2)}) %collective-permute-start) | collective-permute-done | bytes 286752 | tf_op jit(solution)/shard_map/ppermute | solution.py:24
  20.2 1.4 %collective-permute-done.3.refs_1_ = bf16[80,1792]{1,0:T(8,128)(2,1)S(1)} collective-permute-done((bf16[80,1792]{1,0:T(8,128)(2,1)S(1)}, bf16[80,1792]{1,0:T(8,128)(2,1)S(1)}, u32[]{:S(2)}, u32[]{:S(2)}) %collective-permute-start.3) | collective-permute-done | bytes 286752 | tf_op jit(solution)/shard_map/ppermute | solution.py:24
  21.8 0.6 collective-permute-start.5
  22.4 0.5 collective-permute-start.2
  22.9 8.1 %collective-permute-done.5.refs_5_.refs_1_ = bf16[80,1792]{1,0:T(8,128)(2,1)S(1)} collective-permute-done((bf16[80,1792]{1,0:T(8,128)(2,1)S(1)}, bf16[80,1792]{1,0:T(8,128)(2,1)S(1)}, u32[]{:S(2)}, u32[]{:S(2)}) %collective-permute-start.5) | collective-permute-done | bytes 286752 | tf_op jit(solution)/shard_map/ppermute | solution.py:24
  31.3 1.3 %collective-permute-done.7.refs_7_.refs_3_ = bf16[80,1792]{1,0:T(8,128)(2,1)S(1)} collective-permute-done((bf16[80,1792]{1,0:T(8,128)(2,1)S(1)}, bf16[80,1792]{1,0:T(8,128)(2,1)S(1)}, u32[]{:S(2)}, u32[]{:S(2)}) %collective-permute-start.7) | collective-permute-done | bytes 286752 | tf_op jit(solution)/shard_map/ppermute | solution.py:24
  32.6 1.6 %shard_map.61 = (f32[320,640]{1,0:T(8,128)S(1)}, f32[320,640]{1,0:T(8,128)S(1)}, f32[4,8,128]{2,1,0:T(8,128)S(1)}, f32[8,8,128]{2,1,0:T(8,128)S(1)}, bf16[320,1024]{1,0:T(8,128)(2,1)S(1)}) custom-call(bf16[80,1792]{1,0:T(8,128)(2,1)S(1)} %get-tuple-element.27.refs_0_, bf16[80,1792]{1,0:T(8,128)(2,1)S(1)} %collective-permute-done.refs_1_, ...), custom_call_target="tpu_custom_call" | custom-call | flops 734003200 | bytes 5783552 | tf_op jit(solution)/shard_map/pallas_call | solution.py:232
  34.2 0.6 collective-permute-start.9
  35.3 3.2 %collective-permute-done.8.refs_1_ = f32[4,8,128]{2,1,0:T(8,128)S(1)} collective-permute-done((f32[4,8,128]{2,1,0:T(8,128)S(1)}, f32[4,8,128]{2,1,0:T(8,128)S(1)}, u32[]{:S(2)}, u32[]{:S(2)}) %collective-permute-start.8) | collective-permute-done | bytes 16416 | tf_op jit(solution)/shard_map/ppermute | solution.py:24
  38.6 1.3 %collective-permute-start.11 = (f32[8,8,128]{2,1,0:T(8,128)S(1)}, f32[8,8,128]{2,1,0:T(8,128)S(1)}, u32[]{:S(2)}, u32[]{:S(2)}) collective-permute-start(f32[8,8,128]{2,1,0:T(8,128)S(1)} %get-tuple-element.35.refs_2_), channel_id=1, source_target_pairs={{0,1},{1,0},{2,3},{3,2},{4,5},{5,4},{6,7},{7,6},{8,9},{9,8},{10,11... | collective-permute-start | bytes 98312 | tf_op jit(solution)/shard_map/ppermute | solution.py:24
  39.9 2.3 %collective-permute-start.10 = (f32[4,8,128]{2,1,0:T(8,128)S(1)}, f32[4,8,128]{2,1,0:T(8,128)S(1)}, u32[]{:S(2)}, u32[]{:S(2)}) collective-permute-start(f32[4,8,128]{2,1,0:T(8,128)S(1)} %get-tuple-element.34.refs_0_), channel_id=1, source_target_pairs={{0,2},{2,0},{1,3},{3,1},{4,6},{6,4},{5,7},{7,5},{8,10},{10,8},{9,1... | collective-permute-start | bytes 49160 | tf_op jit(solution)/shard_map/ppermute | solution.py:24
  42.2 2.3 %collective-permute-done.10.refs_1_ = f32[4,8,128]{2,1,0:T(8,128)S(1)} collective-permute-done((f32[4,8,128]{2,1,0:T(8,128)S(1)}, f32[4,8,128]{2,1,0:T(8,128)S(1)}, u32[]{:S(2)}, u32[]{:S(2)}) %collective-permute-start.10) | collective-permute-done | bytes 16416 | tf_op jit(solution)/shard_map/ppermute | solution.py:24
  45.1 1.6 %collective-permute-done.12.refs_2_ = f32[8,8,128]{2,1,0:T(8,128)S(1)} collective-permute-done((f32[8,8,128]{2,1,0:T(8,128)S(1)}, f32[8,8,128]{2,1,0:T(8,128)S(1)}, u32[]{:S(2)}, u32[]{:S(2)}) %collective-permute-start.12) | collective-permute-done | bytes 32800 | tf_op jit(solution)/shard_map/ppermute | solution.py:24
  46.8 0.9 %shard_map.64 = (bf16[320,640]{1,0:T(8,128)(2,1)S(1)}, bf16[320,320]{1,0:T(8,128)(2,1)S(1)}) custom-call(f32[320,640]{1,0:T(8,128)S(1)} %get-tuple-element.30.student_ref, f32[320,640]{1,0:T(8,128)S(1)} %get-tuple-element.31.teacher_ref, f32[4,8,128]{2,1,0:T(8,128)S(1)} %get-tuple-element.36.refs_0_, f32[8,8,128]{2,1,0:T(8,128)S(1)} %get-tuple-element.37.refs_1_, ...), custom_call_target="tpu_custom_call" | custom-call | flops 2048000 | bytes 2334720 | tf_op jit(solution)/shard_map/pallas_call | solution.py:232
  47.9 0.7 shard_map.65
  48.5 0.6 collective-permute-start.13
  49.2 0.9 %shard_map.66 = (f32[80,1024]{1,0:T(8,128)S(1)}, f32[80,1024]{1,0:T(8,128)S(1)}, bf16[80,1024]{1,0:T(8,128)(2,1)S(1)}, bf16[80,1024]{1,0:T(8,128)(2,1)S(1)}) custom-call(bf16[320,640]{1,0:T(8,128)(2,1)S(1)} %get-tuple-element.38.tile_ref, bf16[320,320]{1,0:T(8,128)(2,1)S(1)} %collective-permute-done.14.tile_other, ...), custom_call_target="tpu_custom_call" | custom-call | flops 419430400 | bytes 2908160 | tf_op jit(solution)/shard_map/pallas_call | solution.py:232
  50.1 0.6 collective-permute-start.16
  50.7 4.4 %collective-permute-done.13 = bf16[80,1024]{1,0:T(8,128)(2,1)S(1)} collective-permute-done((bf16[80,1024]{1,0:T(8,128)(2,1)S(1)}, bf16[80,1024]{1,0:T(8,128)(2,1)S(1)}, u32[]{:S(2)}, u32[]{:S(2)}) %collective-permute-start.13) | collective-permute-done | bytes 163872 | tf_op jit(solution)/shard_map/ppermute | solution.py:24
  55.1 2.4 %collective-permute-start.18 = (bf16[80,1024]{1,0:T(8,128)(2,1)S(1)}, bf16[80,1024]{1,0:T(8,128)(2,1)S(1)}, u32[]{:S(2)}, u32[]{:S(2)}) collective-permute-start(bf16[80,1024]{1,0:T(8,128)(2,1)S(1)} %add_convert_fusion.1), channel_id=1, source_target_pairs={{0,2},{2,0},{1,3},{3,1},{4,6},{6,4},{5,7},{7,5},{8,10},{10,8},{9,1... | collective-permute-start | bytes 491528 | tf_op jit(solution)/shard_map/ppermute | solution.py:24
  57.6 0.6 collective-permute-start.17
  58.2 1.0 %collective-permute-start.19 = (bf16[80,1024]{1,0:T(8,128)(2,1)S(1)}, bf16[80,1024]{1,0:T(8,128)(2,1)S(1)}, u32[]{:S(2)}, u32[]{:S(2)}) collective-permute-start(bf16[80,1024]{1,0:T(8,128)(2,1)S(1)} %get-tuple-element.51), channel_id=1, source_target_pairs={{0,16},{16,0},{1,17},{17,1},{2,18},{18,2},{3,19},{19,3},{4,20},{20... | collective-permute-start | bytes 491528 | tf_op jit(solution)/shard_map/ppermute | solution.py:24
  59.1 1.1 %collective-permute-start.20 = (bf16[80,1024]{1,0:T(8,128)(2,1)S(1)}, bf16[80,1024]{1,0:T(8,128)(2,1)S(1)}, u32[]{:S(2)}, u32[]{:S(2)}) collective-permute-start(bf16[80,1024]{1,0:T(8,128)(2,1)S(1)} %add_convert_fusion), channel_id=1, source_target_pairs={{0,1},{1,0},{2,3},{3,2},{4,5},{5,4},{6,7},{7,6},{8,9},{9,8},{10,11... | collective-permute-start | bytes 491528 | tf_op jit(solution)/shard_map/ppermute | solution.py:24
  60.2 5.2 %collective-permute-done.18.refs_2_ = bf16[80,1024]{1,0:T(8,128)(2,1)S(1)} collective-permute-done((bf16[80,1024]{1,0:T(8,128)(2,1)S(1)}, bf16[80,1024]{1,0:T(8,128)(2,1)S(1)}, u32[]{:S(2)}, u32[]{:S(2)}) %collective-permute-start.18) | collective-permute-done | bytes 163872 | tf_op jit(solution)/shard_map/ppermute | solution.py:24
  65.4 1.7 %collective-permute-done.20.refs_5_ = bf16[80,1024]{1,0:T(8,128)(2,1)S(1)} collective-permute-done((bf16[80,1024]{1,0:T(8,128)(2,1)S(1)}, bf16[80,1024]{1,0:T(8,128)(2,1)S(1)}, u32[]{:S(2)}, u32[]{:S(2)}) %collective-permute-start.20) | collective-permute-done | bytes 163872 | tf_op jit(solution)/shard_map/ppermute | solution.py:24
  67.1 0.9 %shard_map.67 = (f32[80,1024]{1,0:T(8,128)}, f32[80,1024]{1,0:T(8,128)}) custom-call(f32[80,1024]{1,0:T(8,128)S(1)} %get-tuple-element.39.refs_0_, bf16[80,1024]{1,0:T(8,128)(2,1)S(1)} %collective-permute-done.17.refs_1_, bf16[80,1024]{1,0:T(8,128)(2,1)S(1)} %collective-permute-done.18.refs_2_, f32[80,1024]{1,0:T(8,128)S(1)} %get-tuple-element.49.refs_3_, ...), custom_call_target="tpu_custom_call" | custom-call | bytes 1966080 | tf_op jit(solution)/shard_map/pallas_call | solution.py:232
  (21 shorter events, 1.9 us)
Async XLA Ops:
  1.8 9.8 %collective-permute-start.1 = (bf16[80,1792]{1,0:T(8,128)(2,1)S(1)}, bf16[80,1792]{1,0:T(8,128)(2,1)S(1)}, u32[]{:S(2)}, u32[]{:S(2)}) collective-permute-start(bf16[80,1792]{1,0:T(8,128)(2,1)S(1)} %get-tuple-element.27.refs_0_), channel_id=1, source_target_pairs={{0,8},{8,0},{1,9},{9,1},{2,10},{10,2},{3,11},{11,3},{4,12},{12,4},... | collective-permute-start | bytes 860168 | tf_op jit(solution)/shard_map/ppermute | solution.py:24
  4.8 15.4 %collective-permute-start = (bf16[80,1792]{1,0:T(8,128)(2,1)S(1)}, bf16[80,1792]{1,0:T(8,128)(2,1)S(1)}, u32[]{:S(2)}, u32[]{:S(2)}) collective-permute-start(bf16[80,1792]{1,0:T(8,128)(2,1)S(1)} %get-tuple-element.27.refs_0_), channel_id=1, source_target_pairs={{0,2},{2,0},{1,3},{3,1},{4,6},{6,4},{5,7},{7,5},{8,10},{10,8},{9,1... | collective-permute-start | bytes 860168 | tf_op jit(solution)/shard_map/ppermute | solution.py:24
  7.4 12.9 %collective-permute-start.4 = (bf16[80,1792]{1,0:T(8,128)(2,1)S(1)}, bf16[80,1792]{1,0:T(8,128)(2,1)S(1)}, u32[]{:S(2)}, u32[]{:S(2)}) collective-permute-start(bf16[80,1792]{1,0:T(8,128)(2,1)S(1)} %get-tuple-element.29.refs_0_), channel_id=1, source_target_pairs={{0,16},{16,0},{1,17},{17,1},{2,18},{18,2},{3,19},{19,3},{4,20},{20... | collective-permute-start | bytes 860168 | tf_op jit(solution)/shard_map/ppermute | solution.py:24
  8.9 12.8 %collective-permute-start.3 = (bf16[80,1792]{1,0:T(8,128)(2,1)S(1)}, bf16[80,1792]{1,0:T(8,128)(2,1)S(1)}, u32[]{:S(2)}, u32[]{:S(2)}) collective-permute-start(bf16[80,1792]{1,0:T(8,128)(2,1)S(1)} %get-tuple-element.29.refs_0_), channel_id=1, source_target_pairs={{0,1},{1,0},{2,3},{3,2},{4,5},{5,4},{6,7},{7,6},{8,9},{9,8},{10,11... | collective-permute-start | bytes 860168 | tf_op jit(solution)/shard_map/ppermute | solution.py:24
  21.7 10.9 %collective-permute-start.6 = (bf16[240,1792]{1,0:T(8,128)(2,1)S(1)}, bf16[240,1792]{1,0:T(8,128)(2,1)S(1)}, u32[]{:S(2)}, u32[]{:S(2)}) collective-permute-start(bf16[240,1792]{1,0:T(8,128)(2,1)S(1)} %shard_map.60.refs_4_.refs_0_), channel_id=1, source_target_pairs={{0,4},{4,0},{1,5},{5,1},{2,6},{6,2},{3,7},{7,3},{8,12},{12,8},{9,1... | collective-permute-start | bytes 2580488 | tf_op jit(solution)/shard_map/ppermute | solution.py:24
  21.8 9.2 %collective-permute-start.5 = (bf16[80,1792]{1,0:T(8,128)(2,1)S(1)}, bf16[80,1792]{1,0:T(8,128)(2,1)S(1)}, u32[]{:S(2)}, u32[]{:S(2)}) collective-permute-start(bf16[80,1792]{1,0:T(8,128)(2,1)S(1)} %collective-permute-done.3.refs_1_), channel_id=1, source_target_pairs={{0,16},{16,0},{1,17},{17,1},{2,18},{18,2},{3,19},{19,3},{4,20},{20... | collective-permute-start | bytes 860168 | tf_op jit(solution)/shard_map/ppermute | solution.py:24
  22.4 8.9 %collective-permute-start.2 = (bf16[80,1792]{1,0:T(8,128)(2,1)S(1)}, bf16[80,1792]{1,0:T(8,128)(2,1)S(1)}, u32[]{:S(2)}, u32[]{:S(2)}) collective-permute-start(bf16[80,1792]{1,0:T(8,128)(2,1)S(1)} %collective-permute-done.refs_1_), channel_id=1, source_target_pairs={{0,8},{8,0},{1,9},{9,1},{2,10},{10,2},{3,11},{11,3},{4,12},{12,4},... | collective-permute-start | bytes 860168 | tf_op jit(solution)/shard_map/ppermute | solution.py:24
  31.1 1.6 %collective-permute-start.7 = (bf16[80,1792]{1,0:T(8,128)(2,1)S(1)}, bf16[80,1792]{1,0:T(8,128)(2,1)S(1)}, u32[]{:S(2)}, u32[]{:S(2)}) collective-permute-start(bf16[80,1792]{1,0:T(8,128)(2,1)S(1)} %collective-permute-done.5.refs_5_.refs_1_), channel_id=1, source_target_pairs={{0,4},{4,0},{1,5},{5,1},{2,6},{6,2},{3,7},{7,3},{8,12},{12,8},{9,1... | collective-permute-start | bytes 860168 | tf_op jit(solution)/shard_map/ppermute | solution.py:24
  34.2 4.3 %collective-permute-start.9 = (f32[8,8,128]{2,1,0:T(8,128)S(1)}, f32[8,8,128]{2,1,0:T(8,128)S(1)}, u32[]{:S(2)}, u32[]{:S(2)}) collective-permute-start(f32[8,8,128]{2,1,0:T(8,128)S(1)} %get-tuple-element.33.refs_2_), channel_id=1, source_target_pairs={{0,16},{16,0},{1,17},{17,1},{2,18},{18,2},{3,19},{19,3},{4,20},{20... | collective-permute-start | bytes 98312 | tf_op jit(solution)/shard_map/ppermute | solution.py:24
  34.8 3.7 %collective-permute-start.8 = (f32[4,8,128]{2,1,0:T(8,128)S(1)}, f32[4,8,128]{2,1,0:T(8,128)S(1)}, u32[]{:S(2)}, u32[]{:S(2)}) collective-permute-start(f32[4,8,128]{2,1,0:T(8,128)S(1)} %get-tuple-element.32.refs_0_), channel_id=1, source_target_pairs={{0,8},{8,0},{1,9},{9,1},{2,10},{10,2},{3,11},{11,3},{4,12},{12,4},... | collective-permute-start | bytes 49160 | tf_op jit(solution)/shard_map/ppermute | solution.py:24
  38.6 5.9 %collective-permute-start.11 = (f32[8,8,128]{2,1,0:T(8,128)S(1)}, f32[8,8,128]{2,1,0:T(8,128)S(1)}, u32[]{:S(2)}, u32[]{:S(2)}) collective-permute-start(f32[8,8,128]{2,1,0:T(8,128)S(1)} %get-tuple-element.35.refs_2_), channel_id=1, source_target_pairs={{0,1},{1,0},{2,3},{3,2},{4,5},{5,4},{6,7},{7,6},{8,9},{9,8},{10,11... | collective-permute-start | bytes 98312 | tf_op jit(solution)/shard_map/ppermute | solution.py:24
  39.9 4.6 %collective-permute-start.10 = (f32[4,8,128]{2,1,0:T(8,128)S(1)}, f32[4,8,128]{2,1,0:T(8,128)S(1)}, u32[]{:S(2)}, u32[]{:S(2)}) collective-permute-start(f32[4,8,128]{2,1,0:T(8,128)S(1)} %get-tuple-element.34.refs_0_), channel_id=1, source_target_pairs={{0,2},{2,0},{1,3},{3,1},{4,6},{6,4},{5,7},{7,5},{8,10},{10,8},{9,1... | collective-permute-start | bytes 49160 | tf_op jit(solution)/shard_map/ppermute | solution.py:24
  44.5 4.7 %collective-permute-start.15 = (bf16[320,1024]{1,0:T(8,128)(2,1)S(1)}, bf16[320,1024]{1,0:T(8,128)(2,1)S(1)}, u32[]{:S(2)}, u32[]{:S(2)}) collective-permute-start(bf16[320,1024]{1,0:T(8,128)(2,1)S(1)} %get-tuple-element.45.images), channel_id=1, source_target_pairs={{0,4},{4,0},{1,5},{5,1},{2,6},{6,2},{3,7},{7,3},{8,12},{12,8},{9,1... | collective-permute-start | bytes 1966088 | tf_op jit(solution)/shard_map/ppermute | solution.py:24
  44.6 2.1 %collective-permute-start.12 = (f32[8,8,128]{2,1,0:T(8,128)S(1)}, f32[8,8,128]{2,1,0:T(8,128)S(1)}, u32[]{:S(2)}, u32[]{:S(2)}) collective-permute-start(f32[8,8,128]{2,1,0:T(8,128)S(1)} %get-tuple-element.37.refs_1_), channel_id=1, source_target_pairs={{0,4},{4,0},{1,5},{5,1},{2,6},{6,2},{3,7},{7,3},{8,12},{12,8},{9,1... | collective-permute-start | bytes 98312 | tf_op jit(solution)/shard_map/ppermute | solution.py:24
  47.7 1.6 %collective-permute-start.14 = (bf16[320,320]{1,0:T(8,128)(2,1)S(1)}, bf16[320,320]{1,0:T(8,128)(2,1)S(1)}, u32[]{:S(2)}, u32[]{:S(2)}) collective-permute-start(bf16[320,320]{1,0:T(8,128)(2,1)S(1)} %get-tuple-element.43), channel_id=1, source_target_pairs={{0,4},{4,0},{1,5},{5,1},{2,6},{6,2},{3,7},{7,3},{8,12},{12,8},{9,1... | collective-permute-start | bytes 614408 | tf_op jit(solution)/shard_map/ppermute | solution.py:24
  48.5 6.5 %collective-permute-start.13 = (bf16[80,1024]{1,0:T(8,128)(2,1)S(1)}, bf16[80,1024]{1,0:T(8,128)(2,1)S(1)}, u32[]{:S(2)}, u32[]{:S(2)}) collective-permute-start(bf16[80,1024]{1,0:T(8,128)(2,1)S(1)} %get-tuple-element.42), channel_id=1, source_target_pairs={{0,8},{8,0},{1,9},{9,1},{2,10},{10,2},{3,11},{11,3},{4,12},{12,4},... | collective-permute-start | bytes 491528 | tf_op jit(solution)/shard_map/ppermute | solution.py:24
  50.1 7.4 %collective-permute-start.16 = (bf16[80,1024]{1,0:T(8,128)(2,1)S(1)}, bf16[80,1024]{1,0:T(8,128)(2,1)S(1)}, u32[]{:S(2)}, u32[]{:S(2)}) collective-permute-start(bf16[80,1024]{1,0:T(8,128)(2,1)S(1)} %get-tuple-element.47), channel_id=1, source_target_pairs={{0,16},{16,0},{1,17},{17,1},{2,18},{18,2},{3,19},{19,3},{4,20},{20... | collective-permute-start | bytes 491528 | tf_op jit(solution)/shard_map/ppermute | solution.py:24
  55.1 10.2 %collective-permute-start.18 = (bf16[80,1024]{1,0:T(8,128)(2,1)S(1)}, bf16[80,1024]{1,0:T(8,128)(2,1)S(1)}, u32[]{:S(2)}, u32[]{:S(2)}) collective-permute-start(bf16[80,1024]{1,0:T(8,128)(2,1)S(1)} %add_convert_fusion.1), channel_id=1, source_target_pairs={{0,2},{2,0},{1,3},{3,1},{4,6},{6,4},{5,7},{7,5},{8,10},{10,8},{9,1... | collective-permute-start | bytes 491528 | tf_op jit(solution)/shard_map/ppermute | solution.py:24
  57.6 7.8 %collective-permute-start.17 = (bf16[80,1024]{1,0:T(8,128)(2,1)S(1)}, bf16[80,1024]{1,0:T(8,128)(2,1)S(1)}, u32[]{:S(2)}, u32[]{:S(2)}) collective-permute-start(bf16[80,1024]{1,0:T(8,128)(2,1)S(1)} %get-tuple-element.48), channel_id=1, source_target_pairs={{0,8},{8,0},{1,9},{9,1},{2,10},{10,2},{3,11},{11,3},{4,12},{12,4},... | collective-permute-start | bytes 491528 | tf_op jit(solution)/shard_map/ppermute | solution.py:24
  58.2 7.2 %collective-permute-start.19 = (bf16[80,1024]{1,0:T(8,128)(2,1)S(1)}, bf16[80,1024]{1,0:T(8,128)(2,1)S(1)}, u32[]{:S(2)}, u32[]{:S(2)}) collective-permute-start(bf16[80,1024]{1,0:T(8,128)(2,1)S(1)} %get-tuple-element.51), channel_id=1, source_target_pairs={{0,16},{16,0},{1,17},{17,1},{2,18},{18,2},{3,19},{19,3},{4,20},{20... | collective-permute-start | bytes 491528 | tf_op jit(solution)/shard_map/ppermute | solution.py:24
  59.1 8.0 %collective-permute-start.20 = (bf16[80,1024]{1,0:T(8,128)(2,1)S(1)}, bf16[80,1024]{1,0:T(8,128)(2,1)S(1)}, u32[]{:S(2)}, u32[]{:S(2)}) collective-permute-start(bf16[80,1024]{1,0:T(8,128)(2,1)S(1)} %add_convert_fusion), channel_id=1, source_target_pairs={{0,1},{1,0},{2,3},{3,2},{4,5},{5,4},{6,7},{7,6},{8,9},{9,8},{10,11... | collective-permute-start | bytes 491528 | tf_op jit(solution)/shard_map/ppermute | solution.py:24

commit v5 on v4

--- a/solution.py
+++ b/solution.py
@@ -11,8 +11,8 @@
 logit_gain = 3.0
 ROW_AXES = ("ilo", "chi")
 COL_AXES = ("core", "ihi", "clo")
-ROW_STEPS = ("ilo", "chi")
-COL_STEPS = ("ihi", "clo", "core")
+ROW_STAGES = (("ilo",), ("chi",))
+COL_STAGES = (("ihi", "clo"), ("core",))
 ROW_ORDER = ("ihi", "ilo", "core", "chi", "clo")
 COL_ORDER = ("chi", "clo", "ihi", "ilo", "core")
 LANES = 128
@@ -24,9 +24,17 @@
     return lax.ppermute(value, axis, [(j, j ^ mask) for j in range(size)])
 
 
-def bits(axis):
-    size = lax.axis_size(axis)
-    return [1 << b for b in range(size.bit_length() - 1)]
+def partners(names, axes):
+    sizes = [lax.axis_size(a) for a in names]
+    strides = [math.prod(lax.axis_size(a) for a in axes[axes.index(name) + 1 :]) for name in names]
+    result = []
+    for mask in range(1, math.prod(sizes)):
+        distance, rest = 0, mask
+        for size, stride in zip(reversed(sizes), reversed(strides)):
+            distance += rest % size * stride
+            rest //= size
+        result.append((mask, distance))
+    return result
 
 
 def lines_of(columns):
@@ -93,6 +101,11 @@
         ],
         sems,
     )
+
+
+def duplicate_kernel(image, caption, image_out, caption_out):
+    image_out[...] = image[...]
+    caption_out[...] = caption[...]
 
 
 def assemble_kernel(*refs):
@@ -144,26 +157,33 @@
     return jnp.where(line < INDEX, both, x)
 
 
-def merged_blocks(mine, other, distance):
-    return [merged(mine[s], other[s ^ distance]) for s in range(mine.shape[0])]
-
-
-def merge_kernel(distances, *refs):
-    n = len(distances)
-    for k, distance in enumerate(distances):
-        for s, block in enumerate(merged_blocks(refs[2 * k], refs[2 * k + 1], distance)):
-            refs[2 * n + k][s] = block
-
-
-def tile_kernel(distances, rows, student_ref, teacher_ref, *refs):
+def merged_blocks(mine, others, distances):
+    blocks = [mine[s] for s in range(mine.shape[0])]
+    for other, distance in zip(others, distances):
+        blocks = [merged(block, other[s ^ distance]) for s, block in enumerate(blocks)]
+    return blocks
+
+
+def take(refs, plan):
+    result = []
+    for distances in plan:
+        mine, others = refs[0], refs[1 : 1 + len(distances)]
+        del refs[: 1 + len(distances)]
+        result.append(merged_blocks(mine, others, distances))
+    return result
+
+
+def merge_kernel(plan, *refs):
     refs = list(refs)
-    blocks = []
-    for distance in distances:
-        mine = refs.pop(0)
-        if distance is None:
-            blocks.append([mine[s] for s in range(mine.shape[0])])
-        else:
-            blocks.append(merged_blocks(mine, refs.pop(0), distance))
+    results = take(refs, plan)
+    for out, blocks in zip(refs, results):
+        for s, block in enumerate(blocks):
+            out[s] = block
+
+
+def tile_kernel(plan, rows, student_ref, teacher_ref, *refs):
+    refs = list(refs)
+    blocks = take(refs, plan)
     tile_ref, send_ref = refs
     total, count = teacher_ref.shape
 
@@ -240,14 +260,6 @@
     )(*(pltpu.with_memory_space_constraint(arg, space) for arg, space in zip(args, spaces)))
 
 
-def steps_of(names, axes):
-    result = []
-    for name in names:
-        stride = math.prod(lax.axis_size(a) for a in axes[axes.index(name) + 1 :])
-        result += [(name, bit, stride * bit) for bit in bits(name)]
-    return result
-
-
 def after(value, *others):
     return lax.optimization_barrier((value, others))[0]
 
@@ -281,12 +293,21 @@
             return jnp.concatenate(parts, axis=0)
         return call(assemble_kernel, [shape((len(parts) * rows, width + depth), bf16)], parts)[0]
 
-    def gather(own, far_axis, near_axis):
-        near = {m: swap(own, near_axis, m) for m in range(1, lax.axis_size(near_axis))}
+    if aligned:
+        image_near, caption_near = call(
+            duplicate_kernel, [shape((rows, width + depth), bf16)] * 2, [image, caption]
+        )
+    else:
+        image_near, caption_near = image, caption
+
+    def gather(own, own_near, far_axis, near_axis):
         far = [swap(own, far_axis, m) for m in range(1, lax.axis_size(far_axis))]
-        return [own] + far + [p for m in near for p in [near[m]] + [swap(part, near_axis, m) for part in far]]
-
-    img, cap = gather(image, "chi", "ilo"), gather(caption, "clo", "ihi")
+        parts = [own] + far
+        for m in range(1, lax.axis_size(near_axis)):
+            parts += [swap(part, near_axis, m) for part in [own_near] + far]
+        return parts
+
+    img, cap = gather(image, image_near, "chi", "ilo"), gather(caption, caption_near, "clo", "ihi")
     cap = [assemble([after(cap[0], *img[1 : chi + 1])] + cap[1:-1]), cap[-1]]
     cap = cap + [swap(part, "core", 1) for part in cap]
     if not aligned:
@@ -300,27 +321,22 @@
         2 * total * columns * (width + depth),
     )
 
+    images_other = swap(images, "core", 1)
     stats = [row_stats, col_stats]
-    steps = [steps_of(ROW_STEPS, ROW_AXES), steps_of(COL_STEPS, COL_AXES)]
-    count = max(map(len, steps))
-    for k in range(count):
-        active = [d for d in range(2) if k < len(steps[d])]
-        arrived = {d: swap(stats[d], steps[d][k][0], steps[d][k][1]) for d in active}
-        if k == count - 1:
-            break
-        results = call(
-            functools.partial(merge_kernel, [steps[d][k][2] for d in active]),
-            [shape(stats[d].shape, f32) for d in active],
-            [block for d in active for block in (stats[d], arrived[d])],
-        )
-        for d, result in zip(active, results):
-            stats[d] = result
-
-    images_other = swap(after(images, stats[1]), "core", 1)
+    for row_names, col_names in zip(ROW_STAGES, COL_STAGES):
+        plan, blocks = [], []
+        for block, names, axes in zip(stats, (row_names, col_names), (ROW_AXES, COL_AXES)):
+            others = partners(names, axes)
+            plan.append([distance for _, distance in others])
+            blocks += [block] + [swap(block, names, mask) for mask, _ in others]
+        if row_names != ROW_STAGES[-1]:
+            blocks[0] = after(blocks[0], images_other)
+            stats = call(functools.partial(merge_kernel, plan), [row_shape, col_shape], blocks)
+
     tile, tile_send = call(
-        functools.partial(tile_kernel, [steps[d][k][2] if d in active else None for d in range(2)], rows),
+        functools.partial(tile_kernel, plan, rows),
         [shape((total, columns), bf16), shape((total, columns // 2), bf16)],
-        [student, teacher] + [b for d in range(2) for b in ([stats[d], arrived[d]] if d in active else [stats[d]])],
+        [student, teacher] + blocks,
         10 * total * columns,
     )
     tile_other = swap(tile_send, "core", 1)

time: 68.1 us -> 67.4 us (0.990)
  waiting for transfers between devices: 39.4 us -> 35.6 us
  starting transfers between devices: 21.6 us -> 24.7 us
    ppermute x21 -> x22, waiting for transfers between devices: 39.4 us -> 35.6 us  [swap(): return lax.ppermute(value, axis, [(j, j ^ mask) for j in range(size)])]
    ppermute x21 -> x22, starting transfers between devices: 21.6 us -> 24.7 us  [swap(): return lax.ppermute(value, axis, [(j, j ^ mask) for j in range(size)])]
  transfers between devices with their start and end apart: 21 -> 22, of which waited for: 13 -> 11; matrix products, arithmetic and copies ran while one was open for 0% -> 0% of each run, Pallas kernels for 4% -> 2%
where the time goes in v5:
time: 67.4 us; the launch traced here: 67.3 us
  waiting for transfers between devices  35.6 us (53%)
  starting transfers between devices  24.7 us (37%)
  Pallas kernels  6.22 us (9%)
  between operations  0.73 us (1%)
    ppermute x22, waiting for transfers between devices, swap(): return lax.ppermute(value, axis, [(j, j ^ mask) for j in range(size)])  35.6 us
    ppermute x22, starting transfers between devices, swap(): return lax.ppermute(value, axis, [(j, j ^ mask) for j in range(size)])  24.7 us
    pallas_call x9, Pallas kernels, call(): pl.pallas_call(kernel, out_shape=[out_space(out.shape, out.dtype) for out...  6.22 us
  transfers between devices with their start and end apart: 22, of which 11 were waited for; matrix products, arithmetic and copies ran while one was open for 0% of the time, Pallas kernels for 2%

profile of v5, /device:TPU:0, one launch (start us, length us, event | category | flops | bytes accessed | tf_op | source)
XLA Modules:
  0.0 67.3 jit_solution(1425865112224721414)
XLA Ops:
  0.6 1.2 %shard_map.59 = (bf16[80,1792]{1,0:T(8,128)(2,1)S(1)}, bf16[80,1792]{1,0:T(8,128)(2,1)S(1)}) custom-call(bf16[80,1024]{1,0:T(8,128)(2,1)} %image_s.1, bf16[80,768]{1,0:T(8,128)(2,1)} %image_t.1, bf16[80,1024]{1,0:T(8,128)(2,1)} %caption_s.1, bf16[80,768]{1,0:T(8,128)(2,1)} %caption_t.1), custom_call_target="tpu_custom_call" | custom-call | bytes 1146880 | tf_op jit(solution)/shard_map/pallas_call | solution.py:252
  1.8 4.1 %collective-permute-start = (bf16[80,1792]{1,0:T(8,128)(2,1)S(1)}, bf16[80,1792]{1,0:T(8,128)(2,1)S(1)}, u32[]{:S(2)}, u32[]{:S(2)}) collective-permute-start(bf16[80,1792]{1,0:T(8,128)(2,1)S(1)} %get-tuple-element.27.image.refs_0_), channel_id=1, source_target_pairs={{0,2},{2,0},{1,3},{3,1},{4,6},{6,4},{5,7},{7,5},{8,10},{10,8},{9,1... | collective-permute-start | bytes 860168 | tf_op jit(solution)/shard_map/ppermute | solution.py:24
  5.9 1.6 %collective-permute-start.1 = (bf16[80,1792]{1,0:T(8,128)(2,1)S(1)}, bf16[80,1792]{1,0:T(8,128)(2,1)S(1)}, u32[]{:S(2)}, u32[]{:S(2)}) collective-permute-start(bf16[80,1792]{1,0:T(8,128)(2,1)S(1)} %get-tuple-element.29), channel_id=1, source_target_pairs={{0,8},{8,0},{1,9},{9,1},{2,10},{10,2},{3,11},{11,3},{4,12},{12,4},... | collective-permute-start | bytes 860168 | tf_op jit(solution)/shard_map/ppermute | solution.py:24
  7.5 1.6 %collective-permute-start.3 = (bf16[80,1792]{1,0:T(8,128)(2,1)S(1)}, bf16[80,1792]{1,0:T(8,128)(2,1)S(1)}, u32[]{:S(2)}, u32[]{:S(2)}) collective-permute-start(bf16[80,1792]{1,0:T(8,128)(2,1)S(1)} %get-tuple-element.30.caption.refs_0_), channel_id=1, source_target_pairs={{0,1},{1,0},{2,3},{3,2},{4,5},{5,4},{6,7},{7,6},{8,9},{9,8},{10,11... | collective-permute-start | bytes 860168 | tf_op jit(solution)/shard_map/ppermute | solution.py:24
  9.1 1.5 %collective-permute-start.4 = (bf16[80,1792]{1,0:T(8,128)(2,1)S(1)}, bf16[80,1792]{1,0:T(8,128)(2,1)S(1)}, u32[]{:S(2)}, u32[]{:S(2)}) collective-permute-start(bf16[80,1792]{1,0:T(8,128)(2,1)S(1)} %get-tuple-element.31), channel_id=1, source_target_pairs={{0,16},{16,0},{1,17},{17,1},{2,18},{18,2},{3,19},{19,3},{4,20},{20... | collective-permute-start | bytes 860168 | tf_op jit(solution)/shard_map/ppermute | solution.py:24
  10.6 8.4 %collective-permute-done.refs_1_ = bf16[80,1792]{1,0:T(8,128)(2,1)S(1)} collective-permute-done((bf16[80,1792]{1,0:T(8,128)(2,1)S(1)}, bf16[80,1792]{1,0:T(8,128)(2,1)S(1)}, u32[]{:S(2)}, u32[]{:S(2)}) %collective-permute-start) | collective-permute-done | bytes 286752 | tf_op jit(solution)/shard_map/ppermute | solution.py:24
  19.0 1.5 %collective-permute-done.3.refs_1_ = bf16[80,1792]{1,0:T(8,128)(2,1)S(1)} collective-permute-done((bf16[80,1792]{1,0:T(8,128)(2,1)S(1)}, bf16[80,1792]{1,0:T(8,128)(2,1)S(1)}, u32[]{:S(2)}, u32[]{:S(2)}) %collective-permute-start.3) | collective-permute-done | bytes 286752 | tf_op jit(solution)/shard_map/ppermute | solution.py:24
  20.6 1.6 %collective-permute-start.5 = (bf16[80,1792]{1,0:T(8,128)(2,1)S(1)}, bf16[80,1792]{1,0:T(8,128)(2,1)S(1)}, u32[]{:S(2)}, u32[]{:S(2)}) collective-permute-start(bf16[80,1792]{1,0:T(8,128)(2,1)S(1)} %collective-permute-done.3.refs_1_), channel_id=1, source_target_pairs={{0,16},{16,0},{1,17},{17,1},{2,18},{18,2},{3,19},{19,3},{4,20},{20... | collective-permute-start | bytes 860168 | tf_op jit(solution)/shard_map/ppermute | solution.py:24
  22.3 0.5 collective-permute-start.2
  22.8 7.1 %collective-permute-done.5.refs_5_.refs_1_ = bf16[80,1792]{1,0:T(8,128)(2,1)S(1)} collective-permute-done((bf16[80,1792]{1,0:T(8,128)(2,1)S(1)}, bf16[80,1792]{1,0:T(8,128)(2,1)S(1)}, u32[]{:S(2)}, u32[]{:S(2)}) %collective-permute-start.5) | collective-permute-done | bytes 286752 | tf_op jit(solution)/shard_map/ppermute | solution.py:24
  29.9 1.3 %collective-permute-done.2.refs_3_ = bf16[80,1792]{1,0:T(8,128)(2,1)S(1)} collective-permute-done((bf16[80,1792]{1,0:T(8,128)(2,1)S(1)}, bf16[80,1792]{1,0:T(8,128)(2,1)S(1)}, u32[]{:S(2)}, u32[]{:S(2)}) %collective-permute-start.2) | collective-permute-done | bytes 286752 | tf_op jit(solution)/shard_map/ppermute | solution.py:24
  31.5 1.6 %shard_map.62 = (f32[320,640]{1,0:T(8,128)S(1)}, f32[320,640]{1,0:T(8,128)S(1)}, f32[4,8,128]{2,1,0:T(8,128)S(1)}, f32[8,8,128]{2,1,0:T(8,128)S(1)}, bf16[320,1024]{1,0:T(8,128)(2,1)S(1)}) custom-call(bf16[80,1792]{1,0:T(8,128)(2,1)S(1)} %get-tuple-element.27.image.refs_0_, bf16[80,1792]{1,0:T(8,128)(2,1)S(1)} %collective-permute-done.refs_1_, ...), custom_call_target="tpu_custom_call" | custom-call | flops 734003200 | bytes 5783552 | tf_op jit(solution)/shard_map/pallas_call | solution.py:252
  33.3 1.1 %collective-permute-start.12 = (f32[8,8,128]{2,1,0:T(8,128)S(1)}, f32[8,8,128]{2,1,0:T(8,128)S(1)}, u32[]{:S(2)}, u32[]{:S(2)}) collective-permute-start(f32[8,8,128]{2,1,0:T(8,128)S(1)} %get-tuple-element.37.refs_2_), channel_id=1, source_target_pairs={{0,17},{1,16},{16,1},{17,0},{2,19},{3,18},{18,3},{19,2},{4,21},{5,... | collective-permute-start | bytes 98312 | tf_op jit(solution)/shard_map/ppermute | solution.py:24
  34.4 0.5 collective-permute-start.11
  34.9 1.9 %collective-permute-start.10 = (f32[8,8,128]{2,1,0:T(8,128)S(1)}, f32[8,8,128]{2,1,0:T(8,128)S(1)}, u32[]{:S(2)}, u32[]{:S(2)}) collective-permute-start(f32[8,8,128]{2,1,0:T(8,128)S(1)} %get-tuple-element.37.refs_2_), channel_id=1, source_target_pairs={{0,1},{1,0},{16,17},{17,16},{2,3},{3,2},{18,19},{19,18},{4,5},{5,4... | collective-permute-start | bytes 98312 | tf_op jit(solution)/shard_map/ppermute | solution.py:24
  36.8 0.6 collective-permute-start.9
  37.4 3.1 %collective-permute-done.9.refs_1_ = f32[4,8,128]{2,1,0:T(8,128)S(1)} collective-permute-done((f32[4,8,128]{2,1,0:T(8,128)S(1)}, f32[4,8,128]{2,1,0:T(8,128)S(1)}, u32[]{:S(2)}, u32[]{:S(2)}) %collective-permute-start.9) | collective-permute-done | bytes 16416 | tf_op jit(solution)/shard_map/ppermute | solution.py:24
  40.7 1.2 %collective-permute-start.13 = (f32[4,8,128]{2,1,0:T(8,128)S(1)}, f32[4,8,128]{2,1,0:T(8,128)S(1)}, u32[]{:S(2)}, u32[]{:S(2)}) collective-permute-start(f32[4,8,128]{2,1,0:T(8,128)S(1)} %get-tuple-element.38.refs_0_), channel_id=1, source_target_pairs={{0,2},{2,0},{1,3},{3,1},{4,6},{6,4},{5,7},{7,5},{8,10},{10,8},{9,1... | collective-permute-start | bytes 49160 | tf_op jit(solution)/shard_map/ppermute | solution.py:24
  41.9 3.5 %collective-permute-done.13.refs_1_ = f32[4,8,128]{2,1,0:T(8,128)S(1)} collective-permute-done((f32[4,8,128]{2,1,0:T(8,128)S(1)}, f32[4,8,128]{2,1,0:T(8,128)S(1)}, u32[]{:S(2)}, u32[]{:S(2)}) %collective-permute-start.13) | collective-permute-done | bytes 16416 | tf_op jit(solution)/shard_map/ppermute | solution.py:24
  45.4 0.8 %shard_map.64 = (bf16[320,640]{1,0:T(8,128)(2,1)S(1)}, bf16[320,320]{1,0:T(8,128)(2,1)S(1)}) custom-call(f32[320,640]{1,0:T(8,128)S(1)} %get-tuple-element.32.student_ref, f32[320,640]{1,0:T(8,128)S(1)} %get-tuple-element.33.teacher_ref, f32[4,8,128]{2,1,0:T(8,128)S(1)} %get-tuple-element.38.refs_0_, f32[4,8,128]{2,1,0:T(8,128)S(1)} %collective-permute-done.13.refs_1_, ...), custom_call_target="tpu_custom_call" | custom-call | flops 2048000 | bytes 2351104 | tf_op jit(solution)/shard_map/pallas_call | solution.py:252
  46.3 0.7 %shard_map.65 = (f32[80,1024]{1,0:T(8,128)S(1)}, f32[80,1024]{1,0:T(8,128)S(1)}, bf16[80,1024]{1,0:T(8,128)(2,1)S(1)}, bf16[80,1024]{1,0:T(8,128)(2,1)S(1)}) custom-call(bf16[320,640]{1,0:T(8,128)(2,1)S(1)} %get-tuple-element.40.tile_ref, bf16[240,1792]{1,0:T(8,128)(2,1)S(1)} %shard_map.61.refs_4_.refs_0_, ...), custom_call_target="tpu_custom_call" | custom-call | flops 419430400 | bytes 3686400 | tf_op jit(solution)/shard_map/pallas_call | solution.py:252
  47.0 0.8 %collective-permute-start.15 = (bf16[80,1024]{1,0:T(8,128)(2,1)S(1)}, bf16[80,1024]{1,0:T(8,128)(2,1)S(1)}, u32[]{:S(2)}, u32[]{:S(2)}) collective-permute-start(bf16[80,1024]{1,0:T(8,128)(2,1)S(1)} %get-tuple-element.44), channel_id=1, source_target_pairs={{0,8},{8,0},{1,9},{9,1},{2,10},{10,2},{3,11},{11,3},{4,12},{12,4},... | collective-permute-start | bytes 491528 | tf_op jit(solution)/shard_map/ppermute | solution.py:24
  47.8 0.9 %shard_map.66 = (f32[80,1024]{1,0:T(8,128)S(1)}, f32[80,1024]{1,0:T(8,128)S(1)}, bf16[80,1024]{1,0:T(8,128)(2,1)S(1)}, bf16[80,1024]{1,0:T(8,128)(2,1)S(1)}) custom-call(bf16[320,640]{1,0:T(8,128)(2,1)S(1)} %get-tuple-element.40.tile_ref, bf16[320,320]{1,0:T(8,128)(2,1)S(1)} %collective-permute-done.16.tile_other, ...), custom_call_target="tpu_custom_call" | custom-call | flops 419430400 | bytes 2908160 | tf_op jit(solution)/shard_map/pallas_call | solution.py:252
  48.7 1.6 %collective-permute-start.17 = (bf16[80,1024]{1,0:T(8,128)(2,1)S(1)}, bf16[80,1024]{1,0:T(8,128)(2,1)S(1)}, u32[]{:S(2)}, u32[]{:S(2)}) collective-permute-start(bf16[80,1024]{1,0:T(8,128)(2,1)S(1)} %get-tuple-element.47), channel_id=1, source_target_pairs={{0,16},{16,0},{1,17},{17,1},{2,18},{18,2},{3,19},{19,3},{4,20},{20... | collective-permute-start | bytes 491528 | tf_op jit(solution)/shard_map/ppermute | solution.py:24
  50.3 3.4 %collective-permute-done.15 = bf16[80,1024]{1,0:T(8,128)(2,1)S(1)} collective-permute-done((bf16[80,1024]{1,0:T(8,128)(2,1)S(1)}, bf16[80,1024]{1,0:T(8,128)(2,1)S(1)}, u32[]{:S(2)}, u32[]{:S(2)}) %collective-permute-start.15) | collective-permute-done | bytes 163872 | tf_op jit(solution)/shard_map/ppermute | solution.py:24
  53.7 1.3 %collective-permute-start.19 = (bf16[80,1024]{1,0:T(8,128)(2,1)S(1)}, bf16[80,1024]{1,0:T(8,128)(2,1)S(1)}, u32[]{:S(2)}, u32[]{:S(2)}) collective-permute-start(bf16[80,1024]{1,0:T(8,128)(2,1)S(1)} %add_convert_fusion.1), channel_id=1, source_target_pairs={{0,2},{2,0},{1,3},{3,1},{4,6},{6,4},{5,7},{7,5},{8,10},{10,8},{9,1... | collective-permute-start | bytes 491528 | tf_op jit(solution)/shard_map/ppermute | solution.py:24
  55.1 1.3 %collective-permute-start.18 = (bf16[80,1024]{1,0:T(8,128)(2,1)S(1)}, bf16[80,1024]{1,0:T(8,128)(2,1)S(1)}, u32[]{:S(2)}, u32[]{:S(2)}) collective-permute-start(bf16[80,1024]{1,0:T(8,128)(2,1)S(1)} %get-tuple-element.48), channel_id=1, source_target_pairs={{0,8},{8,0},{1,9},{9,1},{2,10},{10,2},{3,11},{11,3},{4,12},{12,4},... | collective-permute-start | bytes 491528 | tf_op jit(solution)/shard_map/ppermute | solution.py:24
  56.5 1.6 %collective-permute-start.20 = (bf16[80,1024]{1,0:T(8,128)(2,1)S(1)}, bf16[80,1024]{1,0:T(8,128)(2,1)S(1)}, u32[]{:S(2)}, u32[]{:S(2)}) collective-permute-start(bf16[80,1024]{1,0:T(8,128)(2,1)S(1)} %get-tuple-element.51), channel_id=1, source_target_pairs={{0,16},{16,0},{1,17},{17,1},{2,18},{18,2},{3,19},{19,3},{4,20},{20... | collective-permute-start | bytes 491528 | tf_op jit(solution)/shard_map/ppermute | solution.py:24
  58.0 1.4 %collective-permute-start.21 = (bf16[80,1024]{1,0:T(8,128)(2,1)S(1)}, bf16[80,1024]{1,0:T(8,128)(2,1)S(1)}, u32[]{:S(2)}, u32[]{:S(2)}) collective-permute-start(bf16[80,1024]{1,0:T(8,128)(2,1)S(1)} %add_convert_fusion), channel_id=1, source_target_pairs={{0,1},{1,0},{2,3},{3,2},{4,5},{5,4},{6,7},{7,6},{8,9},{9,8},{10,11... | collective-permute-start | bytes 491528 | tf_op jit(solution)/shard_map/ppermute | solution.py:24
  59.4 4.5 %collective-permute-done.19.refs_2_ = bf16[80,1024]{1,0:T(8,128)(2,1)S(1)} collective-permute-done((bf16[80,1024]{1,0:T(8,128)(2,1)S(1)}, bf16[80,1024]{1,0:T(8,128)(2,1)S(1)}, u32[]{:S(2)}, u32[]{:S(2)}) %collective-permute-start.19) | collective-permute-done | bytes 163872 | tf_op jit(solution)/shard_map/ppermute | solution.py:24
  64.0 2.4 %collective-permute-done.21.refs_5_ = bf16[80,1024]{1,0:T(8,128)(2,1)S(1)} collective-permute-done((bf16[80,1024]{1,0:T(8,128)(2,1)S(1)}, bf16[80,1024]{1,0:T(8,128)(2,1)S(1)}, u32[]{:S(2)}, u32[]{:S(2)}) %collective-permute-start.21) | collective-permute-done | bytes 163872 | tf_op jit(solution)/shard_map/ppermute | solution.py:24
  66.4 0.9 %shard_map.67 = (f32[80,1024]{1,0:T(8,128)}, f32[80,1024]{1,0:T(8,128)}) custom-call(f32[80,1024]{1,0:T(8,128)S(1)} %get-tuple-element.41.refs_0_, bf16[80,1024]{1,0:T(8,128)(2,1)S(1)} %collective-permute-done.18.refs_1_, bf16[80,1024]{1,0:T(8,128)(2,1)S(1)} %collective-permute-done.19.refs_2_, f32[80,1024]{1,0:T(8,128)S(1)} %get-tuple-element.49.refs_3_, ...), custom_call_target="tpu_custom_call" | custom-call | bytes 1966080 | tf_op jit(solution)/shard_map/pallas_call | solution.py:252
  (23 shorter events, 1.1 us)
Async XLA Ops:
  1.8 17.2 %collective-permute-start = (bf16[80,1792]{1,0:T(8,128)(2,1)S(1)}, bf16[80,1792]{1,0:T(8,128)(2,1)S(1)}, u32[]{:S(2)}, u32[]{:S(2)}) collective-permute-start(bf16[80,1792]{1,0:T(8,128)(2,1)S(1)} %get-tuple-element.27.image.refs_0_), channel_id=1, source_target_pairs={{0,2},{2,0},{1,3},{3,1},{4,6},{6,4},{5,7},{7,5},{8,10},{10,8},{9,1... | collective-permute-start | bytes 860168 | tf_op jit(solution)/shard_map/ppermute | solution.py:24
  5.9 13.0 %collective-permute-start.1 = (bf16[80,1792]{1,0:T(8,128)(2,1)S(1)}, bf16[80,1792]{1,0:T(8,128)(2,1)S(1)}, u32[]{:S(2)}, u32[]{:S(2)}) collective-permute-start(bf16[80,1792]{1,0:T(8,128)(2,1)S(1)} %get-tuple-element.29), channel_id=1, source_target_pairs={{0,8},{8,0},{1,9},{9,1},{2,10},{10,2},{3,11},{11,3},{4,12},{12,4},... | collective-permute-start | bytes 860168 | tf_op jit(solution)/shard_map/ppermute | solution.py:24
  7.5 13.0 %collective-permute-start.3 = (bf16[80,1792]{1,0:T(8,128)(2,1)S(1)}, bf16[80,1792]{1,0:T(8,128)(2,1)S(1)}, u32[]{:S(2)}, u32[]{:S(2)}) collective-permute-start(bf16[80,1792]{1,0:T(8,128)(2,1)S(1)} %get-tuple-element.30.caption.refs_0_), channel_id=1, source_target_pairs={{0,1},{1,0},{2,3},{3,2},{4,5},{5,4},{6,7},{7,6},{8,9},{9,8},{10,11... | collective-permute-start | bytes 860168 | tf_op jit(solution)/shard_map/ppermute | solution.py:24
  9.1 11.4 %collective-permute-start.4 = (bf16[80,1792]{1,0:T(8,128)(2,1)S(1)}, bf16[80,1792]{1,0:T(8,128)(2,1)S(1)}, u32[]{:S(2)}, u32[]{:S(2)}) collective-permute-start(bf16[80,1792]{1,0:T(8,128)(2,1)S(1)} %get-tuple-element.31), channel_id=1, source_target_pairs={{0,16},{16,0},{1,17},{17,1},{2,18},{18,2},{3,19},{19,3},{4,20},{20... | collective-permute-start | bytes 860168 | tf_op jit(solution)/shard_map/ppermute | solution.py:24
  20.6 10.9 %collective-permute-start.6 = (bf16[240,1792]{1,0:T(8,128)(2,1)S(1)}, bf16[240,1792]{1,0:T(8,128)(2,1)S(1)}, u32[]{:S(2)}, u32[]{:S(2)}) collective-permute-start(bf16[240,1792]{1,0:T(8,128)(2,1)S(1)} %shard_map.61.refs_4_.refs_0_), channel_id=1, source_target_pairs={{0,4},{4,0},{1,5},{5,1},{2,6},{6,2},{3,7},{7,3},{8,12},{12,8},{9,1... | collective-permute-start | bytes 2580488 | tf_op jit(solution)/shard_map/ppermute | solution.py:24
  20.6 9.2 %collective-permute-start.5 = (bf16[80,1792]{1,0:T(8,128)(2,1)S(1)}, bf16[80,1792]{1,0:T(8,128)(2,1)S(1)}, u32[]{:S(2)}, u32[]{:S(2)}) collective-permute-start(bf16[80,1792]{1,0:T(8,128)(2,1)S(1)} %collective-permute-done.3.refs_1_), channel_id=1, source_target_pairs={{0,16},{16,0},{1,17},{17,1},{2,18},{18,2},{3,19},{19,3},{4,20},{20... | collective-permute-start | bytes 860168 | tf_op jit(solution)/shard_map/ppermute | solution.py:24
  22.3 8.9 %collective-permute-start.2 = (bf16[80,1792]{1,0:T(8,128)(2,1)S(1)}, bf16[80,1792]{1,0:T(8,128)(2,1)S(1)}, u32[]{:S(2)}, u32[]{:S(2)}) collective-permute-start(bf16[80,1792]{1,0:T(8,128)(2,1)S(1)} %collective-permute-done.refs_1_), channel_id=1, source_target_pairs={{0,8},{8,0},{1,9},{9,1},{2,10},{10,2},{3,11},{11,3},{4,12},{12,4},... | collective-permute-start | bytes 860168 | tf_op jit(solution)/shard_map/ppermute | solution.py:24
  29.9 1.6 %collective-permute-start.7 = (bf16[80,1792]{1,0:T(8,128)(2,1)S(1)}, bf16[80,1792]{1,0:T(8,128)(2,1)S(1)}, u32[]{:S(2)}, u32[]{:S(2)}) collective-permute-start(bf16[80,1792]{1,0:T(8,128)(2,1)S(1)} %collective-permute-done.5.refs_5_.refs_1_), channel_id=1, source_target_pairs={{0,4},{4,0},{1,5},{5,1},{2,6},{6,2},{3,7},{7,3},{8,12},{12,8},{9,1... | collective-permute-start | bytes 860168 | tf_op jit(solution)/shard_map/ppermute | solution.py:24
  33.1 4.3 %collective-permute-start.8 = (bf16[320,1024]{1,0:T(8,128)(2,1)S(1)}, bf16[320,1024]{1,0:T(8,128)(2,1)S(1)}, u32[]{:S(2)}, u32[]{:S(2)}) collective-permute-start(bf16[320,1024]{1,0:T(8,128)(2,1)S(1)} %get-tuple-element.35.images), channel_id=1, source_target_pairs={{0,4},{4,0},{1,5},{5,1},{2,6},{6,2},{3,7},{7,3},{8,12},{12,8},{9,1... | collective-permute-start | bytes 1966088 | tf_op jit(solution)/shard_map/ppermute | solution.py:24
  33.3 7.2 %collective-permute-start.12 = (f32[8,8,128]{2,1,0:T(8,128)S(1)}, f32[8,8,128]{2,1,0:T(8,128)S(1)}, u32[]{:S(2)}, u32[]{:S(2)}) collective-permute-start(f32[8,8,128]{2,1,0:T(8,128)S(1)} %get-tuple-element.37.refs_2_), channel_id=1, source_target_pairs={{0,17},{1,16},{16,1},{17,0},{2,19},{3,18},{18,3},{19,2},{4,21},{5,... | collective-permute-start | bytes 98312 | tf_op jit(solution)/shard_map/ppermute | solution.py:24
  34.4 6.1 %collective-permute-start.11 = (f32[8,8,128]{2,1,0:T(8,128)S(1)}, f32[8,8,128]{2,1,0:T(8,128)S(1)}, u32[]{:S(2)}, u32[]{:S(2)}) collective-permute-start(f32[8,8,128]{2,1,0:T(8,128)S(1)} %get-tuple-element.37.refs_2_), channel_id=1, source_target_pairs={{0,16},{1,17},{16,0},{17,1},{2,18},{3,19},{18,2},{19,3},{4,20},{5,... | collective-permute-start | bytes 98312 | tf_op jit(solution)/shard_map/ppermute | solution.py:24
  34.9 5.6 %collective-permute-start.10 = (f32[8,8,128]{2,1,0:T(8,128)S(1)}, f32[8,8,128]{2,1,0:T(8,128)S(1)}, u32[]{:S(2)}, u32[]{:S(2)}) collective-permute-start(f32[8,8,128]{2,1,0:T(8,128)S(1)} %get-tuple-element.37.refs_2_), channel_id=1, source_target_pairs={{0,1},{1,0},{16,17},{17,16},{2,3},{3,2},{18,19},{19,18},{4,5},{5,4... | collective-permute-start | bytes 98312 | tf_op jit(solution)/shard_map/ppermute | solution.py:24
  36.8 3.7 %collective-permute-start.9 = (f32[4,8,128]{2,1,0:T(8,128)S(1)}, f32[4,8,128]{2,1,0:T(8,128)S(1)}, u32[]{:S(2)}, u32[]{:S(2)}) collective-permute-start(f32[4,8,128]{2,1,0:T(8,128)S(1)} %get-tuple-element.36.refs_0_), channel_id=1, source_target_pairs={{0,8},{8,0},{1,9},{9,1},{2,10},{10,2},{3,11},{11,3},{4,12},{12,4},... | collective-permute-start | bytes 49160 | tf_op jit(solution)/shard_map/ppermute | solution.py:24
  40.6 4.8 %collective-permute-start.14 = (f32[8,8,128]{2,1,0:T(8,128)S(1)}, f32[8,8,128]{2,1,0:T(8,128)S(1)}, u32[]{:S(2)}, u32[]{:S(2)}) collective-permute-start(f32[8,8,128]{2,1,0:T(8,128)S(1)} %get-tuple-element.39.refs_2_), channel_id=1, source_target_pairs={{0,4},{4,0},{1,5},{5,1},{2,6},{6,2},{3,7},{7,3},{8,12},{12,8},{9,1... | collective-permute-start | bytes 98312 | tf_op jit(solution)/shard_map/ppermute | solution.py:24
  40.7 4.7 %collective-permute-start.13 = (f32[4,8,128]{2,1,0:T(8,128)S(1)}, f32[4,8,128]{2,1,0:T(8,128)S(1)}, u32[]{:S(2)}, u32[]{:S(2)}) collective-permute-start(f32[4,8,128]{2,1,0:T(8,128)S(1)} %get-tuple-element.38.refs_0_), channel_id=1, source_target_pairs={{0,2},{2,0},{1,3},{3,1},{4,6},{6,4},{5,7},{7,5},{8,10},{10,8},{9,1... | collective-permute-start | bytes 49160 | tf_op jit(solution)/shard_map/ppermute | solution.py:24
  46.2 1.6 %collective-permute-start.16 = (bf16[320,320]{1,0:T(8,128)(2,1)S(1)}, bf16[320,320]{1,0:T(8,128)(2,1)S(1)}, u32[]{:S(2)}, u32[]{:S(2)}) collective-permute-start(bf16[320,320]{1,0:T(8,128)(2,1)S(1)} %get-tuple-element.45), channel_id=1, source_target_pairs={{0,4},{4,0},{1,5},{5,1},{2,6},{6,2},{3,7},{7,3},{8,12},{12,8},{9,1... | collective-permute-start | bytes 614408 | tf_op jit(solution)/shard_map/ppermute | solution.py:24
  47.0 6.7 %collective-permute-start.15 = (bf16[80,1024]{1,0:T(8,128)(2,1)S(1)}, bf16[80,1024]{1,0:T(8,128)(2,1)S(1)}, u32[]{:S(2)}, u32[]{:S(2)}) collective-permute-start(bf16[80,1024]{1,0:T(8,128)(2,1)S(1)} %get-tuple-element.44), channel_id=1, source_target_pairs={{0,8},{8,0},{1,9},{9,1},{2,10},{10,2},{3,11},{11,3},{4,12},{12,4},... | collective-permute-start | bytes 491528 | tf_op jit(solution)/shard_map/ppermute | solution.py:24
  48.7 6.4 %collective-permute-start.17 = (bf16[80,1024]{1,0:T(8,128)(2,1)S(1)}, bf16[80,1024]{1,0:T(8,128)(2,1)S(1)}, u32[]{:S(2)}, u32[]{:S(2)}) collective-permute-start(bf16[80,1024]{1,0:T(8,128)(2,1)S(1)} %get-tuple-element.47), channel_id=1, source_target_pairs={{0,16},{16,0},{1,17},{17,1},{2,18},{18,2},{3,19},{19,3},{4,20},{20... | collective-permute-start | bytes 491528 | tf_op jit(solution)/shard_map/ppermute | solution.py:24
  53.7 10.2 %collective-permute-start.19 = (bf16[80,1024]{1,0:T(8,128)(2,1)S(1)}, bf16[80,1024]{1,0:T(8,128)(2,1)S(1)}, u32[]{:S(2)}, u32[]{:S(2)}) collective-permute-start(bf16[80,1024]{1,0:T(8,128)(2,1)S(1)} %add_convert_fusion.1), channel_id=1, source_target_pairs={{0,2},{2,0},{1,3},{3,1},{4,6},{6,4},{5,7},{7,5},{8,10},{10,8},{9,1... | collective-permute-start | bytes 491528 | tf_op jit(solution)/shard_map/ppermute | solution.py:24
  55.1 8.8 %collective-permute-start.18 = (bf16[80,1024]{1,0:T(8,128)(2,1)S(1)}, bf16[80,1024]{1,0:T(8,128)(2,1)S(1)}, u32[]{:S(2)}, u32[]{:S(2)}) collective-permute-start(bf16[80,1024]{1,0:T(8,128)(2,1)S(1)} %get-tuple-element.48), channel_id=1, source_target_pairs={{0,8},{8,0},{1,9},{9,1},{2,10},{10,2},{3,11},{11,3},{4,12},{12,4},... | collective-permute-start | bytes 491528 | tf_op jit(solution)/shard_map/ppermute | solution.py:24
  56.5 7.5 %collective-permute-start.20 = (bf16[80,1024]{1,0:T(8,128)(2,1)S(1)}, bf16[80,1024]{1,0:T(8,128)(2,1)S(1)}, u32[]{:S(2)}, u32[]{:S(2)}) collective-permute-start(bf16[80,1024]{1,0:T(8,128)(2,1)S(1)} %get-tuple-element.51), channel_id=1, source_target_pairs={{0,16},{16,0},{1,17},{17,1},{2,18},{18,2},{3,19},{19,3},{4,20},{20... | collective-permute-start | bytes 491528 | tf_op jit(solution)/shard_map/ppermute | solution.py:24
  58.0 8.4 %collective-permute-start.21 = (bf16[80,1024]{1,0:T(8,128)(2,1)S(1)}, bf16[80,1024]{1,0:T(8,128)(2,1)S(1)}, u32[]{:S(2)}, u32[]{:S(2)}) collective-permute-start(bf16[80,1024]{1,0:T(8,128)(2,1)S(1)} %add_convert_fusion), channel_id=1, source_target_pairs={{0,1},{1,0},{2,3},{3,2},{4,5},{5,4},{6,7},{7,6},{8,9},{9,8},{10,11... | collective-permute-start | bytes 491528 | tf_op jit(solution)/shard_map/ppermute | solution.py:24

commit v6 on v5

--- a/solution.py
+++ b/solution.py
@@ -103,9 +103,10 @@
     )
 
 
-def duplicate_kernel(image, caption, image_out, caption_out):
-    image_out[...] = image[...]
-    caption_out[...] = caption[...]
+def duplicate_kernel(*refs):
+    count = len(refs) // 2
+    for value, out in zip(refs[:count], refs[count:]):
+        out[...] = value[...]
 
 
 def assemble_kernel(*refs):
@@ -181,10 +182,11 @@
             out[s] = block
 
 
-def tile_kernel(plan, rows, student_ref, teacher_ref, *refs):
+def tile_kernel(plan, n_cap, rows, width, student_ref, teacher_ref, *refs):
     refs = list(refs)
     blocks = take(refs, plan)
-    tile_ref, send_ref = refs
+    captions = [refs.pop(0) for _ in range(n_cap)]
+    tile_ref, send_ref, first_ref = refs
     total, count = teacher_ref.shape
 
     def finish(blocks):
@@ -204,6 +206,9 @@
         grad = grad - jnp.where(down[at, INDEX : INDEX + 1] == across[INDEX : INDEX + 1], 0.5, 0.0)
         tile_ref[at] = grad.astype(jnp.bfloat16)
     send_ref[...] = tile_ref[:, count // 2 :]
+    right = joined(captions, slice(0, width))
+    part = jnp.dot(tile_ref[total - first_ref.shape[0] :], right, preferred_element_type=jnp.float32)
+    first_ref[...] = part.astype(jnp.bfloat16)
 
 
 def spread(part, outs):
@@ -216,7 +221,9 @@
 def image_kernel(width, tile_ref, *refs):
     parts = [ref for ref in refs if ref.dtype == jnp.bfloat16 and ref.shape[1] > width]
     right = joined(parts, slice(0, width))
-    spread(jnp.dot(tile_ref[...], right, preferred_element_type=jnp.float32), refs[len(parts) :])
+    outs = refs[len(parts) :]
+    count = sum(out.shape[0] for out in outs)
+    spread(jnp.dot(tile_ref[:count], right, preferred_element_type=jnp.float32), outs)
 
 
 def caption_kernel(tile_ref, tile_other, images, images_other, *outs):
@@ -333,11 +340,11 @@
             blocks[0] = after(blocks[0], images_other)
             stats = call(functools.partial(merge_kernel, plan), [row_shape, col_shape], blocks)
 
-    tile, tile_send = call(
-        functools.partial(tile_kernel, plan, rows),
-        [shape((total, columns), bf16), shape((total, columns // 2), bf16)],
-        [student, teacher] + blocks,
-        10 * total * columns,
+    tile, tile_send, image_first = call(
+        functools.partial(tile_kernel, plan, len(cap), rows, width),
+        [shape((total, columns), bf16), shape((total, columns // 2), bf16), shape((rows, width), bf16)],
+        [student, teacher] + blocks + cap,
+        2 * rows * columns * width,
     )
     tile_other = swap(tile_send, "core", 1)
 
@@ -347,10 +354,11 @@
 
     image_parts = call(
         functools.partial(image_kernel, width),
-        outs_of(total, ilo, chi),
+        outs_of(total, ilo, chi)[:-1],
         [tile] + cap,
         2 * total * columns * width,
     )
+    image_parts = list(image_parts) + [image_first]
     caption_parts = call(
         caption_kernel,
         outs_of(columns // 2, ihi, clo),
@@ -358,10 +366,9 @@
         2 * total * columns * width,
     )
 
-    def hop(parts, near, far, f, *gate):
+    def hop(parts, near, far, f):
         size = lax.axis_size(far)
-        sent = [(m, parts[m * size + f]) for m in range(1, lax.axis_size(near))]
-        return [parts[f]] + [swap(after(term, *gate) if gate else term, near, m) for m, term in sent]
+        return [parts[f]] + [swap(parts[m * size + f], near, m) for m in range(1, lax.axis_size(near))]
 
     def rounded(terms):
         total = terms[0]
@@ -371,20 +378,20 @@
 
     image_far = [rounded(hop(image_parts, "ilo", "chi", f)) for f in range(1, chi)]
     caption_far = [rounded(hop(caption_parts, "ihi", "clo", f)) for f in range(1, clo)]
-    image_terms = hop(image_parts, "ilo", "chi", 0, image_far[0], caption_far[0])
-    caption_terms = hop(caption_parts, "ihi", "clo", 0, image_far[0], caption_far[0])
+    seconds = [parts[m * far] for parts, near, far in ((image_parts, ilo, chi), (caption_parts, ihi, clo)) for m in range(1, near)]
+    image_terms = [image_parts[0]] + [swap(part, "ilo", m) for m, part in enumerate(seconds[: ilo - 1], 1)]
+    caption_terms = [caption_parts[0]] + [swap(part, "ihi", m) for m, part in enumerate(seconds[ilo - 1 :], 1)]
     image_terms += [swap(image_far[f - 1], "chi", f) for f in range(1, chi)]
     caption_terms += [swap(caption_far[f - 1], "clo", f) for f in range(1, clo)]
     out = shape((rows, width), f32)
-    return tuple(
-        call(
-            functools.partial(sum_kernel, (len(image_terms), len(caption_terms))),
-            [out, out],
-            image_terms + caption_terms,
-            scratch=[pltpu.VMEM((rows, width), f32)] * 2 + [dma((2,))],
-            out_space=HBM,
-        )
-    )
+    caption_grad, image_grad = call(
+        functools.partial(sum_kernel, (len(caption_terms), len(image_terms))),
+        [out, out],
+        caption_terms + image_terms,
+        scratch=[pltpu.VMEM((rows, width), f32)] * 2 + [dma((2,))],
+        out_space=HBM,
+    )
+    return (image_grad, caption_grad)
 
 
 def split(count):

time: 67.4 us -> 65.8 us (0.976)
  waiting for transfers between devices: 35.6 us -> 33.5 us
    ppermute x22, waiting for transfers between devices: 35.6 us -> 33.5 us  [swap(): return lax.ppermute(value, axis, [(j, j ^ mask) for j in range(size)])]
  transfers between devices with their start and end apart: 22 -> 22, of which waited for: 11 -> 10; matrix products, arithmetic and copies ran while one was open for 0% -> 0% of each run, Pallas kernels for 2% -> 2%
where the time goes in v6:
time: 65.8 us; the launch traced here: 65.6 us
  waiting for transfers between devices  33.5 us (51%)
  starting transfers between devices  25.1 us (38%)
  Pallas kernels  6.19 us (9%)
  between operations  0.74 us (1%)
    ppermute x22, waiting for transfers between devices, swap(): return lax.ppermute(value, axis, [(j, j ^ mask) for j in range(size)])  33.5 us
    ppermute x22, starting transfers between devices, swap(): return lax.ppermute(value, axis, [(j, j ^ mask) for j in range(size)])  25.1 us
    pallas_call x9, Pallas kernels, call(): pl.pallas_call(kernel, out_shape=[out_space(out.shape, out.dtype) for out...  6.19 us
  transfers between devices with their start and end apart: 22, of which 10 were waited for; matrix products, arithmetic and copies ran while one was open for 0% of the time, Pallas kernels for 2%

profile of v6, /device:TPU:0, one launch (start us, length us, event | category | flops | bytes accessed | tf_op | source)
XLA Modules:
  0.0 65.6 jit_solution(11875422362068780215)
XLA Ops:
  0.6 1.2 %shard_map.59 = (bf16[80,1792]{1,0:T(8,128)(2,1)S(1)}, bf16[80,1792]{1,0:T(8,128)(2,1)S(1)}) custom-call(bf16[80,1024]{1,0:T(8,128)(2,1)} %image_s.1, bf16[80,768]{1,0:T(8,128)(2,1)} %image_t.1, bf16[80,1024]{1,0:T(8,128)(2,1)} %caption_s.1, bf16[80,768]{1,0:T(8,128)(2,1)} %caption_t.1), custom_call_target="tpu_custom_call" | custom-call | bytes 1146880 | tf_op jit(solution)/shard_map/pallas_call | solution.py:259
  1.8 4.1 %collective-permute-start = (bf16[80,1792]{1,0:T(8,128)(2,1)S(1)}, bf16[80,1792]{1,0:T(8,128)(2,1)S(1)}, u32[]{:S(2)}, u32[]{:S(2)}) collective-permute-start(bf16[80,1792]{1,0:T(8,128)(2,1)S(1)} %get-tuple-element.27.refs_0_), channel_id=1, source_target_pairs={{0,2},{2,0},{1,3},{3,1},{4,6},{6,4},{5,7},{7,5},{8,10},{10,8},{9,1... | collective-permute-start | bytes 860168 | tf_op jit(solution)/shard_map/ppermute | solution.py:24
  5.9 1.6 %collective-permute-start.1 = (bf16[80,1792]{1,0:T(8,128)(2,1)S(1)}, bf16[80,1792]{1,0:T(8,128)(2,1)S(1)}, u32[]{:S(2)}, u32[]{:S(2)}) collective-permute-start(bf16[80,1792]{1,0:T(8,128)(2,1)S(1)} %get-tuple-element.29), channel_id=1, source_target_pairs={{0,8},{8,0},{1,9},{9,1},{2,10},{10,2},{3,11},{11,3},{4,12},{12,4},... | collective-permute-start | bytes 860168 | tf_op jit(solution)/shard_map/ppermute | solution.py:24
  7.5 1.6 %collective-permute-start.3 = (bf16[80,1792]{1,0:T(8,128)(2,1)S(1)}, bf16[80,1792]{1,0:T(8,128)(2,1)S(1)}, u32[]{:S(2)}, u32[]{:S(2)}) collective-permute-start(bf16[80,1792]{1,0:T(8,128)(2,1)S(1)} %get-tuple-element.30.refs_1_.refs_0_), channel_id=1, source_target_pairs={{0,1},{1,0},{2,3},{3,2},{4,5},{5,4},{6,7},{7,6},{8,9},{9,8},{10,11... | collective-permute-start | bytes 860168 | tf_op jit(solution)/shard_map/ppermute | solution.py:24
  9.1 1.5 %collective-permute-start.4 = (bf16[80,1792]{1,0:T(8,128)(2,1)S(1)}, bf16[80,1792]{1,0:T(8,128)(2,1)S(1)}, u32[]{:S(2)}, u32[]{:S(2)}) collective-permute-start(bf16[80,1792]{1,0:T(8,128)(2,1)S(1)} %get-tuple-element.31), channel_id=1, source_target_pairs={{0,16},{16,0},{1,17},{17,1},{2,18},{18,2},{3,19},{19,3},{4,20},{20... | collective-permute-start | bytes 860168 | tf_op jit(solution)/shard_map/ppermute | solution.py:24
  10.6 8.4 %collective-permute-done.refs_1_ = bf16[80,1792]{1,0:T(8,128)(2,1)S(1)} collective-permute-done((bf16[80,1792]{1,0:T(8,128)(2,1)S(1)}, bf16[80,1792]{1,0:T(8,128)(2,1)S(1)}, u32[]{:S(2)}, u32[]{:S(2)}) %collective-permute-start) | collective-permute-done | bytes 286752 | tf_op jit(solution)/shard_map/ppermute | solution.py:24
  19.0 1.5 %collective-permute-done.3.refs_1_ = bf16[80,1792]{1,0:T(8,128)(2,1)S(1)} collective-permute-done((bf16[80,1792]{1,0:T(8,128)(2,1)S(1)}, bf16[80,1792]{1,0:T(8,128)(2,1)S(1)}, u32[]{:S(2)}, u32[]{:S(2)}) %collective-permute-start.3) | collective-permute-done | bytes 286752 | tf_op jit(solution)/shard_map/ppermute | solution.py:24
  20.6 1.6 %collective-permute-start.5 = (bf16[80,1792]{1,0:T(8,128)(2,1)S(1)}, bf16[80,1792]{1,0:T(8,128)(2,1)S(1)}, u32[]{:S(2)}, u32[]{:S(2)}) collective-permute-start(bf16[80,1792]{1,0:T(8,128)(2,1)S(1)} %collective-permute-done.3.refs_1_), channel_id=1, source_target_pairs={{0,16},{16,0},{1,17},{17,1},{2,18},{18,2},{3,19},{19,3},{4,20},{20... | collective-permute-start | bytes 860168 | tf_op jit(solution)/shard_map/ppermute | solution.py:24
  22.3 0.5 collective-permute-start.2
  22.8 7.1 %collective-permute-done.5.refs_5_.refs_1_ = bf16[80,1792]{1,0:T(8,128)(2,1)S(1)} collective-permute-done((bf16[80,1792]{1,0:T(8,128)(2,1)S(1)}, bf16[80,1792]{1,0:T(8,128)(2,1)S(1)}, u32[]{:S(2)}, u32[]{:S(2)}) %collective-permute-start.5) | collective-permute-done | bytes 286752 | tf_op jit(solution)/shard_map/ppermute | solution.py:24
  29.9 1.3 %collective-permute-done.2.refs_3_ = bf16[80,1792]{1,0:T(8,128)(2,1)S(1)} collective-permute-done((bf16[80,1792]{1,0:T(8,128)(2,1)S(1)}, bf16[80,1792]{1,0:T(8,128)(2,1)S(1)}, u32[]{:S(2)}, u32[]{:S(2)}) %collective-permute-start.2) | collective-permute-done | bytes 286752 | tf_op jit(solution)/shard_map/ppermute | solution.py:24
  31.5 1.6 %shard_map.62 = (f32[320,640]{1,0:T(8,128)S(1)}, f32[320,640]{1,0:T(8,128)S(1)}, f32[4,8,128]{2,1,0:T(8,128)S(1)}, f32[8,8,128]{2,1,0:T(8,128)S(1)}, bf16[320,1024]{1,0:T(8,128)(2,1)S(1)}) custom-call(bf16[80,1792]{1,0:T(8,128)(2,1)S(1)} %get-tuple-element.27.refs_0_, bf16[80,1792]{1,0:T(8,128)(2,1)S(1)} %collective-permute-done.refs_1_, ...), custom_call_target="tpu_custom_call" | custom-call | flops 734003200 | bytes 5783552 | tf_op jit(solution)/shard_map/pallas_call | solution.py:259
  33.3 1.1 %collective-permute-start.12 = (f32[8,8,128]{2,1,0:T(8,128)S(1)}, f32[8,8,128]{2,1,0:T(8,128)S(1)}, u32[]{:S(2)}, u32[]{:S(2)}) collective-permute-start(f32[8,8,128]{2,1,0:T(8,128)S(1)} %get-tuple-element.37.refs_2_), channel_id=1, source_target_pairs={{0,17},{1,16},{16,1},{17,0},{2,19},{3,18},{18,3},{19,2},{4,21},{5,... | collective-permute-start | bytes 98312 | tf_op jit(solution)/shard_map/ppermute | solution.py:24
  34.4 0.5 collective-permute-start.11
  34.9 1.9 %collective-permute-start.10 = (f32[8,8,128]{2,1,0:T(8,128)S(1)}, f32[8,8,128]{2,1,0:T(8,128)S(1)}, u32[]{:S(2)}, u32[]{:S(2)}) collective-permute-start(f32[8,8,128]{2,1,0:T(8,128)S(1)} %get-tuple-element.37.refs_2_), channel_id=1, source_target_pairs={{0,1},{1,0},{16,17},{17,16},{2,3},{3,2},{18,19},{19,18},{4,5},{5,4... | collective-permute-start | bytes 98312 | tf_op jit(solution)/shard_map/ppermute | solution.py:24
  36.8 0.6 collective-permute-start.9
  37.3 3.2 %collective-permute-done.9.refs_1_ = f32[4,8,128]{2,1,0:T(8,128)S(1)} collective-permute-done((f32[4,8,128]{2,1,0:T(8,128)S(1)}, f32[4,8,128]{2,1,0:T(8,128)S(1)}, u32[]{:S(2)}, u32[]{:S(2)}) %collective-permute-start.9) | collective-permute-done | bytes 16416 | tf_op jit(solution)/shard_map/ppermute | solution.py:24
  40.7 1.2 %collective-permute-start.13 = (f32[4,8,128]{2,1,0:T(8,128)S(1)}, f32[4,8,128]{2,1,0:T(8,128)S(1)}, u32[]{:S(2)}, u32[]{:S(2)}) collective-permute-start(f32[4,8,128]{2,1,0:T(8,128)S(1)} %get-tuple-element.38.refs_0_), channel_id=1, source_target_pairs={{0,2},{2,0},{1,3},{3,1},{4,6},{6,4},{5,7},{7,5},{8,10},{10,8},{9,1... | collective-permute-start | bytes 49160 | tf_op jit(solution)/shard_map/ppermute | solution.py:24
  41.9 3.5 %collective-permute-done.13.refs_1_ = f32[4,8,128]{2,1,0:T(8,128)S(1)} collective-permute-done((f32[4,8,128]{2,1,0:T(8,128)S(1)}, f32[4,8,128]{2,1,0:T(8,128)S(1)}, u32[]{:S(2)}, u32[]{:S(2)}) %collective-permute-start.13) | collective-permute-done | bytes 16416 | tf_op jit(solution)/shard_map/ppermute | solution.py:24
  45.4 1.0 %shard_map.64 = (bf16[320,640]{1,0:T(8,128)(2,1)S(1)}, bf16[320,320]{1,0:T(8,128)(2,1)S(1)}, bf16[80,1024]{1,0:T(8,128)(2,1)S(1)}) custom-call(f32[320,640]{1,0:T(8,128)S(1)} %get-tuple-element.32.student_ref, f32[320,640]{1,0:T(8,128)S(1)} %get-tuple-element.33.teacher_ref, f32[4,8,128]{2,1,0:T(8,128)S(1)} %get-tuple-element.38.refs_0_, ...), custom_call_target="tpu_custom_call" | custom-call | flops 104857600 | bytes 4808704 | tf_op jit(solution)/shard_map/pallas_call | solution.py:259
  46.4 0.8 %collective-permute-start.20 = (bf16[80,1024]{1,0:T(8,128)(2,1)S(1)}, bf16[80,1024]{1,0:T(8,128)(2,1)S(1)}, u32[]{:S(2)}, u32[]{:S(2)}) collective-permute-start(bf16[80,1024]{1,0:T(8,128)(2,1)S(1)} %get-tuple-element.49), channel_id=1, source_target_pairs={{0,8},{8,0},{1,9},{9,1},{2,10},{10,2},{3,11},{11,3},{4,12},{12,4},... | collective-permute-start | bytes 491528 | tf_op jit(solution)/shard_map/ppermute | solution.py:24
  47.2 0.6 shard_map.66
  47.8 1.3 %collective-permute-start.19 = (bf16[80,1024]{1,0:T(8,128)(2,1)S(1)}, bf16[80,1024]{1,0:T(8,128)(2,1)S(1)}, u32[]{:S(2)}, u32[]{:S(2)}) collective-permute-start(bf16[80,1024]{1,0:T(8,128)(2,1)S(1)} %get-tuple-element.47), channel_id=1, source_target_pairs={{0,8},{8,0},{1,9},{9,1},{2,10},{10,2},{3,11},{11,3},{4,12},{12,4},... | collective-permute-start | bytes 491528 | tf_op jit(solution)/shard_map/ppermute | solution.py:24
  49.2 0.9 %shard_map.65 = (f32[80,1024]{1,0:T(8,128)S(1)}, f32[80,1024]{1,0:T(8,128)S(1)}, bf16[80,1024]{1,0:T(8,128)(2,1)S(1)}, bf16[80,1024]{1,0:T(8,128)(2,1)S(1)}) custom-call(bf16[320,640]{1,0:T(8,128)(2,1)S(1)} %get-tuple-element.40.tile_ref, bf16[320,320]{1,0:T(8,128)(2,1)S(1)} %collective-permute-done.15.tile_other, ...), custom_call_target="tpu_custom_call" | custom-call | flops 419430400 | bytes 2908160 | tf_op jit(solution)/shard_map/pallas_call | solution.py:259
  50.0 1.6 %collective-permute-start.17 = (bf16[80,1024]{1,0:T(8,128)(2,1)S(1)}, bf16[80,1024]{1,0:T(8,128)(2,1)S(1)}, u32[]{:S(2)}, u32[]{:S(2)}) collective-permute-start(bf16[80,1024]{1,0:T(8,128)(2,1)S(1)} %get-tuple-element.45), channel_id=1, source_target_pairs={{0,16},{16,0},{1,17},{17,1},{2,18},{18,2},{3,19},{19,3},{4,20},{20... | collective-permute-start | bytes 491528 | tf_op jit(solution)/shard_map/ppermute | solution.py:24
  51.7 1.8 %collective-permute-done.20 = bf16[80,1024]{1,0:T(8,128)(2,1)S(1)} collective-permute-done((bf16[80,1024]{1,0:T(8,128)(2,1)S(1)}, bf16[80,1024]{1,0:T(8,128)(2,1)S(1)}, u32[]{:S(2)}, u32[]{:S(2)}) %collective-permute-start.20) | collective-permute-done | bytes 163872 | tf_op jit(solution)/shard_map/ppermute | solution.py:24
  53.5 1.3 %collective-permute-start.21 = (bf16[80,1024]{1,0:T(8,128)(2,1)S(1)}, bf16[80,1024]{1,0:T(8,128)(2,1)S(1)}, u32[]{:S(2)}, u32[]{:S(2)}) collective-permute-start(bf16[80,1024]{1,0:T(8,128)(2,1)S(1)} %add_convert_fusion), channel_id=1, source_target_pairs={{0,2},{2,0},{1,3},{3,1},{4,6},{6,4},{5,7},{7,5},{8,10},{10,8},{9,1... | collective-permute-start | bytes 491528 | tf_op jit(solution)/shard_map/ppermute | solution.py:24
  54.8 1.5 %collective-permute-start.16 = (bf16[80,1024]{1,0:T(8,128)(2,1)S(1)}, bf16[80,1024]{1,0:T(8,128)(2,1)S(1)}, u32[]{:S(2)}, u32[]{:S(2)}) collective-permute-start(bf16[80,1024]{1,0:T(8,128)(2,1)S(1)} %get-tuple-element.43), channel_id=1, source_target_pairs={{0,16},{16,0},{1,17},{17,1},{2,18},{18,2},{3,19},{19,3},{4,20},{20... | collective-permute-start | bytes 491528 | tf_op jit(solution)/shard_map/ppermute | solution.py:24
  56.4 1.9 %collective-permute-start.18 = (bf16[80,1024]{1,0:T(8,128)(2,1)S(1)}, bf16[80,1024]{1,0:T(8,128)(2,1)S(1)}, u32[]{:S(2)}, u32[]{:S(2)}) collective-permute-start(bf16[80,1024]{1,0:T(8,128)(2,1)S(1)} %add_convert_fusion.1), channel_id=1, source_target_pairs={{0,1},{1,0},{2,3},{3,2},{4,5},{5,4},{6,7},{7,6},{8,9},{9,8},{10,11... | collective-permute-start | bytes 491528 | tf_op jit(solution)/shard_map/ppermute | solution.py:24
  58.3 5.0 %collective-permute-done.21.refs_5_ = bf16[80,1024]{1,0:T(8,128)(2,1)S(1)} collective-permute-done((bf16[80,1024]{1,0:T(8,128)(2,1)S(1)}, bf16[80,1024]{1,0:T(8,128)(2,1)S(1)}, u32[]{:S(2)}, u32[]{:S(2)}) %collective-permute-start.21) | collective-permute-done | bytes 163872 | tf_op jit(solution)/shard_map/ppermute | solution.py:24
  63.3 1.4 %collective-permute-done.18.refs_2_ = bf16[80,1024]{1,0:T(8,128)(2,1)S(1)} collective-permute-done((bf16[80,1024]{1,0:T(8,128)(2,1)S(1)}, bf16[80,1024]{1,0:T(8,128)(2,1)S(1)}, u32[]{:S(2)}, u32[]{:S(2)}) %collective-permute-start.18) | collective-permute-done | bytes 163872 | tf_op jit(solution)/shard_map/ppermute | solution.py:24
  64.7 0.9 %shard_map.67 = (f32[80,1024]{1,0:T(8,128)}, f32[80,1024]{1,0:T(8,128)}) custom-call(f32[80,1024]{1,0:T(8,128)S(1)} %get-tuple-element.42.refs_0_, bf16[80,1024]{1,0:T(8,128)(2,1)S(1)} %collective-permute-done.16.refs_1_, bf16[80,1024]{1,0:T(8,128)(2,1)S(1)} %collective-permute-done.18.refs_2_, f32[80,1024]{1,0:T(8,128)S(1)} %get-tuple-element.46.refs_3_, ...), custom_call_target="tpu_custom_call" | custom-call | bytes 1966080 | tf_op jit(solution)/shard_map/pallas_call | solution.py:259
  (23 shorter events, 1.0 us)
Async XLA Ops:
  1.8 17.2 %collective-permute-start = (bf16[80,1792]{1,0:T(8,128)(2,1)S(1)}, bf16[80,1792]{1,0:T(8,128)(2,1)S(1)}, u32[]{:S(2)}, u32[]{:S(2)}) collective-permute-start(bf16[80,1792]{1,0:T(8,128)(2,1)S(1)} %get-tuple-element.27.refs_0_), channel_id=1, source_target_pairs={{0,2},{2,0},{1,3},{3,1},{4,6},{6,4},{5,7},{7,5},{8,10},{10,8},{9,1... | collective-permute-start | bytes 860168 | tf_op jit(solution)/shard_map/ppermute | solution.py:24
  5.9 13.0 %collective-permute-start.1 = (bf16[80,1792]{1,0:T(8,128)(2,1)S(1)}, bf16[80,1792]{1,0:T(8,128)(2,1)S(1)}, u32[]{:S(2)}, u32[]{:S(2)}) collective-permute-start(bf16[80,1792]{1,0:T(8,128)(2,1)S(1)} %get-tuple-element.29), channel_id=1, source_target_pairs={{0,8},{8,0},{1,9},{9,1},{2,10},{10,2},{3,11},{11,3},{4,12},{12,4},... | collective-permute-start | bytes 860168 | tf_op jit(solution)/shard_map/ppermute | solution.py:24
  7.5 13.0 %collective-permute-start.3 = (bf16[80,1792]{1,0:T(8,128)(2,1)S(1)}, bf16[80,1792]{1,0:T(8,128)(2,1)S(1)}, u32[]{:S(2)}, u32[]{:S(2)}) collective-permute-start(bf16[80,1792]{1,0:T(8,128)(2,1)S(1)} %get-tuple-element.30.refs_1_.refs_0_), channel_id=1, source_target_pairs={{0,1},{1,0},{2,3},{3,2},{4,5},{5,4},{6,7},{7,6},{8,9},{9,8},{10,11... | collective-permute-start | bytes 860168 | tf_op jit(solution)/shard_map/ppermute | solution.py:24
  9.1 11.4 %collective-permute-start.4 = (bf16[80,1792]{1,0:T(8,128)(2,1)S(1)}, bf16[80,1792]{1,0:T(8,128)(2,1)S(1)}, u32[]{:S(2)}, u32[]{:S(2)}) collective-permute-start(bf16[80,1792]{1,0:T(8,128)(2,1)S(1)} %get-tuple-element.31), channel_id=1, source_target_pairs={{0,16},{16,0},{1,17},{17,1},{2,18},{18,2},{3,19},{19,3},{4,20},{20... | collective-permute-start | bytes 860168 | tf_op jit(solution)/shard_map/ppermute | solution.py:24
  20.6 10.9 %collective-permute-start.6 = (bf16[240,1792]{1,0:T(8,128)(2,1)S(1)}, bf16[240,1792]{1,0:T(8,128)(2,1)S(1)}, u32[]{:S(2)}, u32[]{:S(2)}) collective-permute-start(bf16[240,1792]{1,0:T(8,128)(2,1)S(1)} %shard_map.61.refs_4_.refs_0_), channel_id=1, source_target_pairs={{0,4},{4,0},{1,5},{5,1},{2,6},{6,2},{3,7},{7,3},{8,12},{12,8},{9,1... | collective-permute-start | bytes 2580488 | tf_op jit(solution)/shard_map/ppermute | solution.py:24
  20.6 9.2 %collective-permute-start.5 = (bf16[80,1792]{1,0:T(8,128)(2,1)S(1)}, bf16[80,1792]{1,0:T(8,128)(2,1)S(1)}, u32[]{:S(2)}, u32[]{:S(2)}) collective-permute-start(bf16[80,1792]{1,0:T(8,128)(2,1)S(1)} %collective-permute-done.3.refs_1_), channel_id=1, source_target_pairs={{0,16},{16,0},{1,17},{17,1},{2,18},{18,2},{3,19},{19,3},{4,20},{20... | collective-permute-start | bytes 860168 | tf_op jit(solution)/shard_map/ppermute | solution.py:24
  22.3 8.9 %collective-permute-start.2 = (bf16[80,1792]{1,0:T(8,128)(2,1)S(1)}, bf16[80,1792]{1,0:T(8,128)(2,1)S(1)}, u32[]{:S(2)}, u32[]{:S(2)}) collective-permute-start(bf16[80,1792]{1,0:T(8,128)(2,1)S(1)} %collective-permute-done.refs_1_), channel_id=1, source_target_pairs={{0,8},{8,0},{1,9},{9,1},{2,10},{10,2},{3,11},{11,3},{4,12},{12,4},... | collective-permute-start | bytes 860168 | tf_op jit(solution)/shard_map/ppermute | solution.py:24
  29.9 1.6 %collective-permute-start.7 = (bf16[80,1792]{1,0:T(8,128)(2,1)S(1)}, bf16[80,1792]{1,0:T(8,128)(2,1)S(1)}, u32[]{:S(2)}, u32[]{:S(2)}) collective-permute-start(bf16[80,1792]{1,0:T(8,128)(2,1)S(1)} %collective-permute-done.5.refs_5_.refs_1_), channel_id=1, source_target_pairs={{0,4},{4,0},{1,5},{5,1},{2,6},{6,2},{3,7},{7,3},{8,12},{12,8},{9,1... | collective-permute-start | bytes 860168 | tf_op jit(solution)/shard_map/ppermute | solution.py:24
  33.1 4.3 %collective-permute-start.8 = (bf16[320,1024]{1,0:T(8,128)(2,1)S(1)}, bf16[320,1024]{1,0:T(8,128)(2,1)S(1)}, u32[]{:S(2)}, u32[]{:S(2)}) collective-permute-start(bf16[320,1024]{1,0:T(8,128)(2,1)S(1)} %get-tuple-element.35.images), channel_id=1, source_target_pairs={{0,4},{4,0},{1,5},{5,1},{2,6},{6,2},{3,7},{7,3},{8,12},{12,8},{9,1... | collective-permute-start | bytes 1966088 | tf_op jit(solution)/shard_map/ppermute | solution.py:24
  33.3 7.2 %collective-permute-start.12 = (f32[8,8,128]{2,1,0:T(8,128)S(1)}, f32[8,8,128]{2,1,0:T(8,128)S(1)}, u32[]{:S(2)}, u32[]{:S(2)}) collective-permute-start(f32[8,8,128]{2,1,0:T(8,128)S(1)} %get-tuple-element.37.refs_2_), channel_id=1, source_target_pairs={{0,17},{1,16},{16,1},{17,0},{2,19},{3,18},{18,3},{19,2},{4,21},{5,... | collective-permute-start | bytes 98312 | tf_op jit(solution)/shard_map/ppermute | solution.py:24
  34.4 6.1 %collective-permute-start.11 = (f32[8,8,128]{2,1,0:T(8,128)S(1)}, f32[8,8,128]{2,1,0:T(8,128)S(1)}, u32[]{:S(2)}, u32[]{:S(2)}) collective-permute-start(f32[8,8,128]{2,1,0:T(8,128)S(1)} %get-tuple-element.37.refs_2_), channel_id=1, source_target_pairs={{0,16},{1,17},{16,0},{17,1},{2,18},{3,19},{18,2},{19,3},{4,20},{5,... | collective-permute-start | bytes 98312 | tf_op jit(solution)/shard_map/ppermute | solution.py:24
  34.9 5.6 %collective-permute-start.10 = (f32[8,8,128]{2,1,0:T(8,128)S(1)}, f32[8,8,128]{2,1,0:T(8,128)S(1)}, u32[]{:S(2)}, u32[]{:S(2)}) collective-permute-start(f32[8,8,128]{2,1,0:T(8,128)S(1)} %get-tuple-element.37.refs_2_), channel_id=1, source_target_pairs={{0,1},{1,0},{16,17},{17,16},{2,3},{3,2},{18,19},{19,18},{4,5},{5,4... | collective-permute-start | bytes 98312 | tf_op jit(solution)/shard_map/ppermute | solution.py:24
  36.8 3.7 %collective-permute-start.9 = (f32[4,8,128]{2,1,0:T(8,128)S(1)}, f32[4,8,128]{2,1,0:T(8,128)S(1)}, u32[]{:S(2)}, u32[]{:S(2)}) collective-permute-start(f32[4,8,128]{2,1,0:T(8,128)S(1)} %get-tuple-element.36.refs_0_), channel_id=1, source_target_pairs={{0,8},{8,0},{1,9},{9,1},{2,10},{10,2},{3,11},{11,3},{4,12},{12,4},... | collective-permute-start | bytes 49160 | tf_op jit(solution)/shard_map/ppermute | solution.py:24
  40.6 4.8 %collective-permute-start.14 = (f32[8,8,128]{2,1,0:T(8,128)S(1)}, f32[8,8,128]{2,1,0:T(8,128)S(1)}, u32[]{:S(2)}, u32[]{:S(2)}) collective-permute-start(f32[8,8,128]{2,1,0:T(8,128)S(1)} %get-tuple-element.39.refs_2_), channel_id=1, source_target_pairs={{0,4},{4,0},{1,5},{5,1},{2,6},{6,2},{3,7},{7,3},{8,12},{12,8},{9,1... | collective-permute-start | bytes 98312 | tf_op jit(solution)/shard_map/ppermute | solution.py:24
  40.7 4.7 %collective-permute-start.13 = (f32[4,8,128]{2,1,0:T(8,128)S(1)}, f32[4,8,128]{2,1,0:T(8,128)S(1)}, u32[]{:S(2)}, u32[]{:S(2)}) collective-permute-start(f32[4,8,128]{2,1,0:T(8,128)S(1)} %get-tuple-element.38.refs_0_), channel_id=1, source_target_pairs={{0,2},{2,0},{1,3},{3,1},{4,6},{6,4},{5,7},{7,5},{8,10},{10,8},{9,1... | collective-permute-start | bytes 49160 | tf_op jit(solution)/shard_map/ppermute | solution.py:24
  46.4 2.8 %collective-permute-start.15 = (bf16[320,320]{1,0:T(8,128)(2,1)S(1)}, bf16[320,320]{1,0:T(8,128)(2,1)S(1)}, u32[]{:S(2)}, u32[]{:S(2)}) collective-permute-start(bf16[320,320]{1,0:T(8,128)(2,1)S(1)} %get-tuple-element.41), channel_id=1, source_target_pairs={{0,4},{4,0},{1,5},{5,1},{2,6},{6,2},{3,7},{7,3},{8,12},{12,8},{9,1... | collective-permute-start | bytes 614408 | tf_op jit(solution)/shard_map/ppermute | solution.py:24
  46.4 7.1 %collective-permute-start.20 = (bf16[80,1024]{1,0:T(8,128)(2,1)S(1)}, bf16[80,1024]{1,0:T(8,128)(2,1)S(1)}, u32[]{:S(2)}, u32[]{:S(2)}) collective-permute-start(bf16[80,1024]{1,0:T(8,128)(2,1)S(1)} %get-tuple-element.49), channel_id=1, source_target_pairs={{0,8},{8,0},{1,9},{9,1},{2,10},{10,2},{3,11},{11,3},{4,12},{12,4},... | collective-permute-start | bytes 491528 | tf_op jit(solution)/shard_map/ppermute | solution.py:24
  47.8 10.5 %collective-permute-start.19 = (bf16[80,1024]{1,0:T(8,128)(2,1)S(1)}, bf16[80,1024]{1,0:T(8,128)(2,1)S(1)}, u32[]{:S(2)}, u32[]{:S(2)}) collective-permute-start(bf16[80,1024]{1,0:T(8,128)(2,1)S(1)} %get-tuple-element.47), channel_id=1, source_target_pairs={{0,8},{8,0},{1,9},{9,1},{2,10},{10,2},{3,11},{11,3},{4,12},{12,4},... | collective-permute-start | bytes 491528 | tf_op jit(solution)/shard_map/ppermute | solution.py:24
  50.0 6.3 %collective-permute-start.17 = (bf16[80,1024]{1,0:T(8,128)(2,1)S(1)}, bf16[80,1024]{1,0:T(8,128)(2,1)S(1)}, u32[]{:S(2)}, u32[]{:S(2)}) collective-permute-start(bf16[80,1024]{1,0:T(8,128)(2,1)S(1)} %get-tuple-element.45), channel_id=1, source_target_pairs={{0,16},{16,0},{1,17},{17,1},{2,18},{18,2},{3,19},{19,3},{4,20},{20... | collective-permute-start | bytes 491528 | tf_op jit(solution)/shard_map/ppermute | solution.py:24
  53.5 9.7 %collective-permute-start.21 = (bf16[80,1024]{1,0:T(8,128)(2,1)S(1)}, bf16[80,1024]{1,0:T(8,128)(2,1)S(1)}, u32[]{:S(2)}, u32[]{:S(2)}) collective-permute-start(bf16[80,1024]{1,0:T(8,128)(2,1)S(1)} %add_convert_fusion), channel_id=1, source_target_pairs={{0,2},{2,0},{1,3},{3,1},{4,6},{6,4},{5,7},{7,5},{8,10},{10,8},{9,1... | collective-permute-start | bytes 491528 | tf_op jit(solution)/shard_map/ppermute | solution.py:24
  54.8 8.4 %collective-permute-start.16 = (bf16[80,1024]{1,0:T(8,128)(2,1)S(1)}, bf16[80,1024]{1,0:T(8,128)(2,1)S(1)}, u32[]{:S(2)}, u32[]{:S(2)}) collective-permute-start(bf16[80,1024]{1,0:T(8,128)(2,1)S(1)} %get-tuple-element.43), channel_id=1, source_target_pairs={{0,16},{16,0},{1,17},{17,1},{2,18},{18,2},{3,19},{19,3},{4,20},{20... | collective-permute-start | bytes 491528 | tf_op jit(solution)/shard_map/ppermute | solution.py:24
  56.4 8.3 %collective-permute-start.18 = (bf16[80,1024]{1,0:T(8,128)(2,1)S(1)}, bf16[80,1024]{1,0:T(8,128)(2,1)S(1)}, u32[]{:S(2)}, u32[]{:S(2)}) collective-permute-start(bf16[80,1024]{1,0:T(8,128)(2,1)S(1)} %add_convert_fusion.1), channel_id=1, source_target_pairs={{0,1},{1,0},{2,3},{3,2},{4,5},{5,4},{6,7},{7,6},{8,9},{9,8},{10,11... | collective-permute-start | bytes 491528 | tf_op jit(solution)/shard_map/ppermute | solution.py:24

commit v7 on v6

--- a/solution.py
+++ b/solution.py
@@ -10,7 +10,7 @@
 
 logit_gain = 3.0
 ROW_AXES = ("ilo", "chi")
-COL_AXES = ("core", "ihi", "clo")
+COL_AXES = ("core", "clo", "ihi")
 ROW_STAGES = (("ilo",), ("chi",))
 COL_STAGES = (("ihi", "clo"), ("core",))
 ROW_ORDER = ("ihi", "ilo", "core", "chi", "clo")
@@ -186,7 +186,7 @@
     refs = list(refs)
     blocks = take(refs, plan)
     captions = [refs.pop(0) for _ in range(n_cap)]
-    tile_ref, send_ref, first_ref = refs
+    tile_ref, send_ref, *outs = refs
     total, count = teacher_ref.shape
 
     def finish(blocks):
@@ -207,8 +207,11 @@
         tile_ref[at] = grad.astype(jnp.bfloat16)
     send_ref[...] = tile_ref[:, count // 2 :]
     right = joined(captions, slice(0, width))
-    part = jnp.dot(tile_ref[total - first_ref.shape[0] :], right, preferred_element_type=jnp.float32)
-    first_ref[...] = part.astype(jnp.bfloat16)
+    each = len(outs) * rows // lax.axis_size("ilo")
+    step = each + rows
+    for k in range(lax.axis_size("ilo")):
+        part = jnp.dot(tile_ref[k * step + rows : (k + 1) * step], right, preferred_element_type=jnp.float32)
+        spread(part, outs[k * each // rows : (k + 1) * each // rows])
 
 
 def spread(part, outs):
@@ -218,12 +221,12 @@
         start += out.shape[0]
 
 
-def image_kernel(width, tile_ref, *refs):
+def image_kernel(width, step, tile_ref, *refs):
     parts = [ref for ref in refs if ref.dtype == jnp.bfloat16 and ref.shape[1] > width]
     right = joined(parts, slice(0, width))
-    outs = refs[len(parts) :]
-    count = sum(out.shape[0] for out in outs)
-    spread(jnp.dot(tile_ref[:count], right, preferred_element_type=jnp.float32), outs)
+    for k, out in enumerate(refs[len(parts) :]):
+        start = k * step
+        spread(jnp.dot(tile_ref[start : start + out.shape[0]], right, preferred_element_type=jnp.float32), [out])
 
 
 def caption_kernel(tile_ref, tile_other, images, images_other, *outs):
@@ -272,7 +275,7 @@
 
 
 def local(image_student, caption_student, image_teacher, caption_teacher):
-    ilo, chi, core, ihi, clo = (lax.axis_size(a) for a in ROW_AXES + COL_AXES)
+    ilo, chi, core, clo, ihi = (lax.axis_size(a) for a in ROW_AXES + COL_AXES)
     rows, width = image_student.shape
     depth = image_teacher.shape[1]
     assert rows <= LANES and core == 2 and chi > 1 and clo > 1
@@ -308,15 +311,18 @@
         image_near, caption_near = image, caption
 
     def gather(own, own_near, far_axis, near_axis):
-        far = [swap(own, far_axis, m) for m in range(1, lax.axis_size(far_axis))]
-        parts = [own] + far
-        for m in range(1, lax.axis_size(near_axis)):
-            parts += [swap(part, near_axis, m) for part in [own_near] + far]
+        parts = {(0, c): swap(own, far_axis, c) if c else own for c in range(lax.axis_size(far_axis))}
+        for h in range(1, lax.axis_size(near_axis)):
+            parts.update({(h, c): swap(parts[0, c] if c else own_near, near_axis, h) for c in range(lax.axis_size(far_axis))})
         return parts
 
     img, cap = gather(image, image_near, "chi", "ilo"), gather(caption, caption_near, "clo", "ihi")
-    cap = [assemble([after(cap[0], *img[1 : chi + 1])] + cap[1:-1]), cap[-1]]
-    cap = cap + [swap(part, "core", 1) for part in cap]
+    early = [cap[h, 0] for h in range(ihi)]
+    early = assemble([after(early[0], img[1, 0], img[0, 1])] + early[1:])
+    late = [cap[h, c] for c in range(1, clo) for h in range(ihi)]
+    late = assemble([after(late[0], img[1, 1])] + late[1:])
+    img = [img[h, c] for h in range(ilo) for c in range(chi)]
+    cap = [early, late, swap(early, "core", 1), swap(late, "core", 1)]
     if not aligned:
         img, cap = [assemble(img)], [assemble(cap)]
 
@@ -340,35 +346,32 @@
             blocks[0] = after(blocks[0], images_other)
             stats = call(functools.partial(merge_kernel, plan), [row_shape, col_shape], blocks)
 
-    tile, tile_send, image_first = call(
+    far_blocks = [(h, c) for h in range(ilo) for c in range(1, chi)]
+    near_blocks = [(h, 0) for h in range(ilo)]
+
+    def pieces(blocks):
+        return [shape((rows, width), bf16 if h else f32) for h, _ in blocks]
+
+    tile, tile_send, *image_parts = call(
         functools.partial(tile_kernel, plan, len(cap), rows, width),
-        [shape((total, columns), bf16), shape((total, columns // 2), bf16), shape((rows, width), bf16)],
+        [shape((total, columns), bf16), shape((total, columns // 2), bf16)] + pieces(far_blocks),
         [student, teacher] + blocks + cap,
-        2 * rows * columns * width,
-    )
+        2 * total * columns * width // 2,
+    )
+    image_parts = dict(zip(far_blocks, image_parts))
     tile_other = swap(tile_send, "core", 1)
 
-    def outs_of(count, near, far):
-        piece = count // (near * far)
-        return [shape((piece, width), f32)] * far + [shape((piece, width), bf16)] * ((near - 1) * far)
-
-    image_parts = call(
-        functools.partial(image_kernel, width),
-        outs_of(total, ilo, chi)[:-1],
-        [tile] + cap,
-        2 * total * columns * width,
-    )
-    image_parts = list(image_parts) + [image_first]
+    caption_blocks = [(h, c) for c in range(clo) for h in range(ihi)]
     caption_parts = call(
         caption_kernel,
-        outs_of(columns // 2, ihi, clo),
+        pieces(caption_blocks),
         [tile, tile_other, images, images_other],
         2 * total * columns * width,
     )
-
-    def hop(parts, near, far, f):
-        size = lax.axis_size(far)
-        return [parts[f]] + [swap(parts[m * size + f], near, m) for m in range(1, lax.axis_size(near))]
+    caption_parts = dict(zip(caption_blocks, caption_parts))
+
+    def hop(parts, near, f):
+        return [parts[0, f]] + [swap(parts[h, f], near, h) for h in range(1, lax.axis_size(near))]
 
     def rounded(terms):
         total = terms[0]
@@ -376,11 +379,16 @@
             total = total + term.astype(f32)
         return total.astype(bf16)
 
-    image_far = [rounded(hop(image_parts, "ilo", "chi", f)) for f in range(1, chi)]
-    caption_far = [rounded(hop(caption_parts, "ihi", "clo", f)) for f in range(1, clo)]
-    seconds = [parts[m * far] for parts, near, far in ((image_parts, ilo, chi), (caption_parts, ihi, clo)) for m in range(1, near)]
-    image_terms = [image_parts[0]] + [swap(part, "ilo", m) for m, part in enumerate(seconds[: ilo - 1], 1)]
-    caption_terms = [caption_parts[0]] + [swap(part, "ihi", m) for m, part in enumerate(seconds[ilo - 1 :], 1)]
+    image_far = [rounded(hop(image_parts, "ilo", f)) for f in range(1, chi)]
+    caption_far = [rounded(hop(caption_parts, "ihi", f)) for f in range(1, clo)]
+    rest = call(
+        functools.partial(image_kernel, width, chi * rows),
+        pieces(near_blocks),
+        [after(tile, image_far[0])] + cap,
+        2 * total * columns * width // chi,
+    )
+    image_parts.update(zip(near_blocks, rest))
+    image_terms, caption_terms = hop(image_parts, "ilo", 0), hop(caption_parts, "ihi", 0)
     image_terms += [swap(image_far[f - 1], "chi", f) for f in range(1, chi)]
     caption_terms += [swap(caption_far[f - 1], "clo", f) for f in range(1, clo)]
     out = shape((rows, width), f32)

time: 65.8 us -> 66.2 us (level)
  starting transfers between devices: 25.1 us -> 29.1 us
  waiting for transfers between devices: 33.5 us -> 29.7 us
    ppermute x22, starting transfers between devices: 25.1 us -> 29.1 us  [swap(): return lax.ppermute(value, axis, [(j, j ^ mask) for j in range(size)])]
    ppermute x22, waiting for transfers between devices: 33.5 us -> 29.7 us  [swap(): return lax.ppermute(value, axis, [(j, j ^ mask) for j in range(size)])]
    pallas_call x9 -> x10, Pallas kernels: 6.19 us -> 6.57 us  [call(): pl.pallas_call(kernel, out_shape=[out_space(out.shape, out.dtype) for out...]
  transfers between devices with their start and end apart: 22 -> 22, of which waited for: 10 -> 11; matrix products, arithmetic and copies ran while one was open for 0% -> 0% of each run, Pallas kernels for 2% -> 2%
where the time goes in v7:
time: 66.2 us; the launch traced here: 66.1 us
  waiting for transfers between devices  29.7 us (45%)
  starting transfers between devices  29.1 us (44%)
  Pallas kernels  6.57 us (10%)
  between operations  0.74 us (1%)
    ppermute x22, waiting for transfers between devices, swap(): return lax.ppermute(value, axis, [(j, j ^ mask) for j in range(size)])  29.7 us
    ppermute x22, starting transfers between devices, swap(): return lax.ppermute(value, axis, [(j, j ^ mask) for j in range(size)])  29.1 us
    pallas_call x10, Pallas kernels, call(): pl.pallas_call(kernel, out_shape=[out_space(out.shape, out.dtype) for out...  6.57 us
  transfers between devices with their start and end apart: 22, of which 11 were waited for; matrix products, arithmetic and copies ran while one was open for 0% of the time, Pallas kernels for 2%

profile of v7, /device:TPU:0, one launch (start us, length us, event | category | flops | bytes accessed | tf_op | source)
XLA Modules:
  0.0 66.1 jit_solution(17102207034342974154)
XLA Ops:
  0.6 1.2 %shard_map.59 = (bf16[80,1792]{1,0:T(8,128)(2,1)S(1)}, bf16[80,1792]{1,0:T(8,128)(2,1)S(1)}) custom-call(bf16[80,1024]{1,0:T(8,128)(2,1)} %image_s.1, bf16[80,768]{1,0:T(8,128)(2,1)} %image_t.1, bf16[80,1024]{1,0:T(8,128)(2,1)} %caption_s.1, bf16[80,768]{1,0:T(8,128)(2,1)} %caption_t.1), custom_call_target="tpu_custom_call" | custom-call | bytes 1146880 | tf_op jit(solution)/shard_map/pallas_call | solution.py:262
  1.8 4.1 %collective-permute-start = (bf16[80,1792]{1,0:T(8,128)(2,1)S(1)}, bf16[80,1792]{1,0:T(8,128)(2,1)S(1)}, u32[]{:S(2)}, u32[]{:S(2)}) collective-permute-start(bf16[80,1792]{1,0:T(8,128)(2,1)S(1)} %get-tuple-element.29.refs_0_), channel_id=1, source_target_pairs={{0,2},{2,0},{1,3},{3,1},{4,6},{6,4},{5,7},{7,5},{8,10},{10,8},{9,1... | collective-permute-start | bytes 860168 | tf_op jit(solution)/shard_map/ppermute | solution.py:24
  5.9 1.6 %collective-permute-start.4 = (bf16[80,1792]{1,0:T(8,128)(2,1)S(1)}, bf16[80,1792]{1,0:T(8,128)(2,1)S(1)}, u32[]{:S(2)}, u32[]{:S(2)}) collective-permute-start(bf16[80,1792]{1,0:T(8,128)(2,1)S(1)} %get-tuple-element.32.refs_1_.refs_0_), channel_id=1, source_target_pairs={{0,1},{1,0},{2,3},{3,2},{4,5},{5,4},{6,7},{7,6},{8,9},{9,8},{10,11... | collective-permute-start | bytes 860168 | tf_op jit(solution)/shard_map/ppermute | solution.py:24
  7.5 1.6 %collective-permute-start.1 = (bf16[80,1792]{1,0:T(8,128)(2,1)S(1)}, bf16[80,1792]{1,0:T(8,128)(2,1)S(1)}, u32[]{:S(2)}, u32[]{:S(2)}) collective-permute-start(bf16[80,1792]{1,0:T(8,128)(2,1)S(1)} %get-tuple-element.31), channel_id=1, source_target_pairs={{0,8},{8,0},{1,9},{9,1},{2,10},{10,2},{3,11},{11,3},{4,12},{12,4},... | collective-permute-start | bytes 860168 | tf_op jit(solution)/shard_map/ppermute | solution.py:24
  9.1 1.5 %collective-permute-start.3 = (bf16[80,1792]{1,0:T(8,128)(2,1)S(1)}, bf16[80,1792]{1,0:T(8,128)(2,1)S(1)}, u32[]{:S(2)}, u32[]{:S(2)}) collective-permute-start(bf16[80,1792]{1,0:T(8,128)(2,1)S(1)} %get-tuple-element.33), channel_id=1, source_target_pairs={{0,16},{16,0},{1,17},{17,1},{2,18},{18,2},{3,19},{19,3},{4,20},{20... | collective-permute-start | bytes 860168 | tf_op jit(solution)/shard_map/ppermute | solution.py:24
  10.6 8.4 %collective-permute-done.refs_1_ = bf16[80,1792]{1,0:T(8,128)(2,1)S(1)} collective-permute-done((bf16[80,1792]{1,0:T(8,128)(2,1)S(1)}, bf16[80,1792]{1,0:T(8,128)(2,1)S(1)}, u32[]{:S(2)}, u32[]{:S(2)}) %collective-permute-start) | collective-permute-done | bytes 286752 | tf_op jit(solution)/shard_map/ppermute | solution.py:24
  19.0 1.5 %collective-permute-start.2 = (bf16[80,1792]{1,0:T(8,128)(2,1)S(1)}, bf16[80,1792]{1,0:T(8,128)(2,1)S(1)}, u32[]{:S(2)}, u32[]{:S(2)}) collective-permute-start(bf16[80,1792]{1,0:T(8,128)(2,1)S(1)} %collective-permute-done.refs_1_), channel_id=1, source_target_pairs={{0,8},{8,0},{1,9},{9,1},{2,10},{10,2},{3,11},{11,3},{4,12},{12,4},... | collective-permute-start | bytes 860168 | tf_op jit(solution)/shard_map/ppermute | solution.py:24
  20.5 1.5 %collective-permute-start.5 = (bf16[80,1792]{1,0:T(8,128)(2,1)S(1)}, bf16[80,1792]{1,0:T(8,128)(2,1)S(1)}, u32[]{:S(2)}, u32[]{:S(2)}) collective-permute-start(bf16[80,1792]{1,0:T(8,128)(2,1)S(1)} %collective-permute-done.4.refs_0_), channel_id=1, source_target_pairs={{0,16},{16,0},{1,17},{17,1},{2,18},{18,2},{3,19},{19,3},{4,20},{20... | collective-permute-start | bytes 860168 | tf_op jit(solution)/shard_map/ppermute | solution.py:24
  22.2 4.8 %collective-permute-done.2.refs_3_ = bf16[80,1792]{1,0:T(8,128)(2,1)S(1)} collective-permute-done((bf16[80,1792]{1,0:T(8,128)(2,1)S(1)}, bf16[80,1792]{1,0:T(8,128)(2,1)S(1)}, u32[]{:S(2)}, u32[]{:S(2)}) %collective-permute-start.2) | collective-permute-done | bytes 286752 | tf_op jit(solution)/shard_map/ppermute | solution.py:24
  26.9 1.0 %collective-permute-done.5.refs_1_ = bf16[80,1792]{1,0:T(8,128)(2,1)S(1)} collective-permute-done((bf16[80,1792]{1,0:T(8,128)(2,1)S(1)}, bf16[80,1792]{1,0:T(8,128)(2,1)S(1)}, u32[]{:S(2)}, u32[]{:S(2)}) %collective-permute-start.5) | collective-permute-done | bytes 286752 | tf_op jit(solution)/shard_map/ppermute | solution.py:24
  28.0 2.0 %collective-permute-done.7.refs_7_.refs_3_ = bf16[160,1792]{1,0:T(8,128)(2,1)S(1)} collective-permute-done((bf16[160,1792]{1,0:T(8,128)(2,1)S(1)}, bf16[160,1792]{1,0:T(8,128)(2,1)S(1)}, u32[]{:S(2)}, u32[]{:S(2)}) %collective-permute-start.7) | collective-permute-done | bytes 573472 | tf_op jit(solution)/shard_map/ppermute | solution.py:24
  30.0 1.6 %shard_map.63 = (f32[320,640]{1,0:T(8,128)S(1)}, f32[320,640]{1,0:T(8,128)S(1)}, f32[4,8,128]{2,1,0:T(8,128)S(1)}, f32[8,8,128]{2,1,0:T(8,128)S(1)}, bf16[320,1024]{1,0:T(8,128)(2,1)S(1)}) custom-call(bf16[80,1792]{1,0:T(8,128)(2,1)S(1)} %get-tuple-element.29.refs_0_, bf16[80,1792]{1,0:T(8,128)(2,1)S(1)} %collective-permute-done.refs_1_, ...), custom_call_target="tpu_custom_call" | custom-call | flops 734003200 | bytes 5783552 | tf_op jit(solution)/shard_map/pallas_call | solution.py:262
  31.8 2.6 %collective-permute-start.12 = (f32[8,8,128]{2,1,0:T(8,128)S(1)}, f32[8,8,128]{2,1,0:T(8,128)S(1)}, u32[]{:S(2)}, u32[]{:S(2)}) collective-permute-start(f32[8,8,128]{2,1,0:T(8,128)S(1)} %get-tuple-element.40.refs_2_), channel_id=1, source_target_pairs={{0,17},{1,16},{16,1},{17,0},{2,19},{3,18},{18,3},{19,2},{4,21},{5,... | collective-permute-start | bytes 98312 | tf_op jit(solution)/shard_map/ppermute | solution.py:24
  35.3 0.8 %collective-permute-start.9 = (f32[4,8,128]{2,1,0:T(8,128)S(1)}, f32[4,8,128]{2,1,0:T(8,128)S(1)}, u32[]{:S(2)}, u32[]{:S(2)}) collective-permute-start(f32[4,8,128]{2,1,0:T(8,128)S(1)} %get-tuple-element.39.refs_0_), channel_id=1, source_target_pairs={{0,8},{8,0},{1,9},{9,1},{2,10},{10,2},{3,11},{11,3},{4,12},{12,4},... | collective-permute-start | bytes 49160 | tf_op jit(solution)/shard_map/ppermute | solution.py:24
  36.1 3.0 %collective-permute-done.9.refs_1_ = f32[4,8,128]{2,1,0:T(8,128)S(1)} collective-permute-done((f32[4,8,128]{2,1,0:T(8,128)S(1)}, f32[4,8,128]{2,1,0:T(8,128)S(1)}, u32[]{:S(2)}, u32[]{:S(2)}) %collective-permute-start.9) | collective-permute-done | bytes 16416 | tf_op jit(solution)/shard_map/ppermute | solution.py:24
  39.2 3.2 %collective-permute-start.13 = (f32[4,8,128]{2,1,0:T(8,128)S(1)}, f32[4,8,128]{2,1,0:T(8,128)S(1)}, u32[]{:S(2)}, u32[]{:S(2)}) collective-permute-start(f32[4,8,128]{2,1,0:T(8,128)S(1)} %get-tuple-element.41.refs_0_), channel_id=1, source_target_pairs={{0,2},{2,0},{1,3},{3,1},{4,6},{6,4},{5,7},{7,5},{8,10},{10,8},{9,1... | collective-permute-start | bytes 49160 | tf_op jit(solution)/shard_map/ppermute | solution.py:24
  42.5 1.7 %collective-permute-done.13.refs_1_ = f32[4,8,128]{2,1,0:T(8,128)S(1)} collective-permute-done((f32[4,8,128]{2,1,0:T(8,128)S(1)}, f32[4,8,128]{2,1,0:T(8,128)S(1)}, u32[]{:S(2)}, u32[]{:S(2)}) %collective-permute-start.13) | collective-permute-done | bytes 16416 | tf_op jit(solution)/shard_map/ppermute | solution.py:24
  44.2 1.3 %shard_map.65 = (bf16[320,640]{1,0:T(8,128)(2,1)S(1)}, bf16[320,320]{1,0:T(8,128)(2,1)S(1)}, f32[80,1024]{1,0:T(8,128)S(1)}, bf16[80,1024]{1,0:T(8,128)(2,1)S(1)}) custom-call(f32[320,640]{1,0:T(8,128)S(1)} %get-tuple-element.35.student_ref, f32[320,640]{1,0:T(8,128)S(1)} %get-tuple-element.36.teacher_ref, f32[4,8,128]{2,1,0:T(8,128)S(1)} %get-tuple-element.41.refs_0_, ...), custom_call_target="tpu_custom_call" | custom-call | flops 209715200 | bytes 5136384 | tf_op jit(solution)/shard_map/pallas_call | solution.py:262
  45.5 0.6 collective-permute-start.19
  46.1 0.9 %collective-permute-done.15.tile_other = bf16[320,320]{1,0:T(8,128)(2,1)S(1)} collective-permute-done((bf16[320,320]{1,0:T(8,128)(2,1)S(1)}, bf16[320,320]{1,0:T(8,128)(2,1)S(1)}, u32[]{:S(2)}, u32[]{:S(2)}) %collective-permute-start.15) | collective-permute-done | bytes 204832 | tf_op jit(solution)/shard_map/ppermute | solution.py:24
  47.0 0.9 %shard_map.66 = (f32[80,1024]{1,0:T(8,128)S(1)}, bf16[80,1024]{1,0:T(8,128)(2,1)S(1)}, f32[80,1024]{1,0:T(8,128)S(1)}, bf16[80,1024]{1,0:T(8,128)(2,1)S(1)}) custom-call(bf16[320,640]{1,0:T(8,128)(2,1)S(1)} %get-tuple-element.51.tile_ref, bf16[320,320]{1,0:T(8,128)(2,1)S(1)} %collective-permute-done.15.tile_other, ...), custom_call_target="tpu_custom_call" | custom-call | flops 419430400 | bytes 2908160 | tf_op jit(solution)/shard_map/pallas_call | solution.py:262
  47.9 1.6 %collective-permute-start.17 = (bf16[80,1024]{1,0:T(8,128)(2,1)S(1)}, bf16[80,1024]{1,0:T(8,128)(2,1)S(1)}, u32[]{:S(2)}, u32[]{:S(2)}) collective-permute-start(bf16[80,1024]{1,0:T(8,128)(2,1)S(1)} %get-tuple-element.48), channel_id=1, source_target_pairs={{0,16},{16,0},{1,17},{17,1},{2,18},{18,2},{3,19},{19,3},{4,20},{20... | collective-permute-start | bytes 491528 | tf_op jit(solution)/shard_map/ppermute | solution.py:24
  49.5 2.7 %collective-permute-done.19 = bf16[80,1024]{1,0:T(8,128)(2,1)S(1)} collective-permute-done((bf16[80,1024]{1,0:T(8,128)(2,1)S(1)}, bf16[80,1024]{1,0:T(8,128)(2,1)S(1)}, u32[]{:S(2)}, u32[]{:S(2)}) %collective-permute-start.19) | collective-permute-done | bytes 163872 | tf_op jit(solution)/shard_map/ppermute | solution.py:24
  52.2 3.0 %collective-permute-start.21 = (bf16[80,1024]{1,0:T(8,128)(2,1)S(1)}, bf16[80,1024]{1,0:T(8,128)(2,1)S(1)}, u32[]{:S(2)}, u32[]{:S(2)}) collective-permute-start(bf16[80,1024]{1,0:T(8,128)(2,1)S(1)} %add_convert_fusion), channel_id=1, source_target_pairs={{0,2},{2,0},{1,3},{3,1},{4,6},{6,4},{5,7},{7,5},{8,10},{10,8},{9,1... | collective-permute-start | bytes 491528 | tf_op jit(solution)/shard_map/ppermute | solution.py:24
  55.2 0.6 shard_map.67
  55.8 0.6 collective-permute-start.20
  56.4 1.5 %collective-permute-start.16 = (bf16[80,1024]{1,0:T(8,128)(2,1)S(1)}, bf16[80,1024]{1,0:T(8,128)(2,1)S(1)}, u32[]{:S(2)}, u32[]{:S(2)}) collective-permute-start(bf16[80,1024]{1,0:T(8,128)(2,1)S(1)} %get-tuple-element.46), channel_id=1, source_target_pairs={{0,16},{16,0},{1,17},{17,1},{2,18},{18,2},{3,19},{19,3},{4,20},{20... | collective-permute-start | bytes 491528 | tf_op jit(solution)/shard_map/ppermute | solution.py:24
  58.0 1.9 %collective-permute-start.18 = (bf16[80,1024]{1,0:T(8,128)(2,1)S(1)}, bf16[80,1024]{1,0:T(8,128)(2,1)S(1)}, u32[]{:S(2)}, u32[]{:S(2)}) collective-permute-start(bf16[80,1024]{1,0:T(8,128)(2,1)S(1)} %add_convert_fusion.1), channel_id=1, source_target_pairs={{0,1},{1,0},{2,3},{3,2},{4,5},{5,4},{6,7},{7,6},{8,9},{9,8},{10,11... | collective-permute-start | bytes 491528 | tf_op jit(solution)/shard_map/ppermute | solution.py:24
  59.9 1.5 %collective-permute-done.20.refs_4_ = bf16[80,1024]{1,0:T(8,128)(2,1)S(1)} collective-permute-done((bf16[80,1024]{1,0:T(8,128)(2,1)S(1)}, bf16[80,1024]{1,0:T(8,128)(2,1)S(1)}, u32[]{:S(2)}, u32[]{:S(2)}) %collective-permute-start.20) | collective-permute-done | bytes 163872 | tf_op jit(solution)/shard_map/ppermute | solution.py:24
  61.4 1.5 %collective-permute-done.21.refs_5_ = bf16[80,1024]{1,0:T(8,128)(2,1)S(1)} collective-permute-done((bf16[80,1024]{1,0:T(8,128)(2,1)S(1)}, bf16[80,1024]{1,0:T(8,128)(2,1)S(1)}, u32[]{:S(2)}, u32[]{:S(2)}) %collective-permute-start.21) | collective-permute-done | bytes 163872 | tf_op jit(solution)/shard_map/ppermute | solution.py:24
  62.9 2.3 %collective-permute-done.18.refs_2_ = bf16[80,1024]{1,0:T(8,128)(2,1)S(1)} collective-permute-done((bf16[80,1024]{1,0:T(8,128)(2,1)S(1)}, bf16[80,1024]{1,0:T(8,128)(2,1)S(1)}, u32[]{:S(2)}, u32[]{:S(2)}) %collective-permute-start.18) | collective-permute-done | bytes 163872 | tf_op jit(solution)/shard_map/ppermute | solution.py:24
  65.2 0.9 %shard_map.68 = (f32[80,1024]{1,0:T(8,128)}, f32[80,1024]{1,0:T(8,128)}) custom-call(f32[80,1024]{1,0:T(8,128)S(1)} %get-tuple-element.45.refs_0_, bf16[80,1024]{1,0:T(8,128)(2,1)S(1)} %collective-permute-done.16.refs_1_, bf16[80,1024]{1,0:T(8,128)(2,1)S(1)} %collective-permute-done.18.refs_2_, f32[80,1024]{1,0:T(8,128)S(1)} %get-tuple-element.52.refs_3_, ...), custom_call_target="tpu_custom_call" | custom-call | bytes 1966080 | tf_op jit(solution)/shard_map/pallas_call | solution.py:262
  (24 shorter events, 1.7 us)
Async XLA Ops:
  1.8 17.2 %collective-permute-start = (bf16[80,1792]{1,0:T(8,128)(2,1)S(1)}, bf16[80,1792]{1,0:T(8,128)(2,1)S(1)}, u32[]{:S(2)}, u32[]{:S(2)}) collective-permute-start(bf16[80,1792]{1,0:T(8,128)(2,1)S(1)} %get-tuple-element.29.refs_0_), channel_id=1, source_target_pairs={{0,2},{2,0},{1,3},{3,1},{4,6},{6,4},{5,7},{7,5},{8,10},{10,8},{9,1... | collective-permute-start | bytes 860168 | tf_op jit(solution)/shard_map/ppermute | solution.py:24
  5.9 14.6 %collective-permute-start.4 = (bf16[80,1792]{1,0:T(8,128)(2,1)S(1)}, bf16[80,1792]{1,0:T(8,128)(2,1)S(1)}, u32[]{:S(2)}, u32[]{:S(2)}) collective-permute-start(bf16[80,1792]{1,0:T(8,128)(2,1)S(1)} %get-tuple-element.32.refs_1_.refs_0_), channel_id=1, source_target_pairs={{0,1},{1,0},{2,3},{3,2},{4,5},{5,4},{6,7},{7,6},{8,9},{9,8},{10,11... | collective-permute-start | bytes 860168 | tf_op jit(solution)/shard_map/ppermute | solution.py:24
  7.5 14.5 %collective-permute-start.1 = (bf16[80,1792]{1,0:T(8,128)(2,1)S(1)}, bf16[80,1792]{1,0:T(8,128)(2,1)S(1)}, u32[]{:S(2)}, u32[]{:S(2)}) collective-permute-start(bf16[80,1792]{1,0:T(8,128)(2,1)S(1)} %get-tuple-element.31), channel_id=1, source_target_pairs={{0,8},{8,0},{1,9},{9,1},{2,10},{10,2},{3,11},{11,3},{4,12},{12,4},... | collective-permute-start | bytes 860168 | tf_op jit(solution)/shard_map/ppermute | solution.py:24
  9.1 13.0 %collective-permute-start.3 = (bf16[80,1792]{1,0:T(8,128)(2,1)S(1)}, bf16[80,1792]{1,0:T(8,128)(2,1)S(1)}, u32[]{:S(2)}, u32[]{:S(2)}) collective-permute-start(bf16[80,1792]{1,0:T(8,128)(2,1)S(1)} %get-tuple-element.33), channel_id=1, source_target_pairs={{0,16},{16,0},{1,17},{17,1},{2,18},{18,2},{3,19},{19,3},{4,20},{20... | collective-permute-start | bytes 860168 | tf_op jit(solution)/shard_map/ppermute | solution.py:24
  19.0 8.0 %collective-permute-start.2 = (bf16[80,1792]{1,0:T(8,128)(2,1)S(1)}, bf16[80,1792]{1,0:T(8,128)(2,1)S(1)}, u32[]{:S(2)}, u32[]{:S(2)}) collective-permute-start(bf16[80,1792]{1,0:T(8,128)(2,1)S(1)} %collective-permute-done.refs_1_), channel_id=1, source_target_pairs={{0,8},{8,0},{1,9},{9,1},{2,10},{10,2},{3,11},{11,3},{4,12},{12,4},... | collective-permute-start | bytes 860168 | tf_op jit(solution)/shard_map/ppermute | solution.py:24
  20.5 7.4 %collective-permute-start.5 = (bf16[80,1792]{1,0:T(8,128)(2,1)S(1)}, bf16[80,1792]{1,0:T(8,128)(2,1)S(1)}, u32[]{:S(2)}, u32[]{:S(2)}) collective-permute-start(bf16[80,1792]{1,0:T(8,128)(2,1)S(1)} %collective-permute-done.4.refs_0_), channel_id=1, source_target_pairs={{0,16},{16,0},{1,17},{17,1},{2,18},{18,2},{3,19},{19,3},{4,20},{20... | collective-permute-start | bytes 860168 | tf_op jit(solution)/shard_map/ppermute | solution.py:24
  22.1 5.9 %collective-permute-start.6 = (bf16[160,1792]{1,0:T(8,128)(2,1)S(1)}, bf16[160,1792]{1,0:T(8,128)(2,1)S(1)}, u32[]{:S(2)}, u32[]{:S(2)}) collective-permute-start(bf16[160,1792]{1,0:T(8,128)(2,1)S(1)} %shard_map.61.refs_4_.refs_0_), channel_id=1, source_target_pairs={{0,4},{4,0},{1,5},{5,1},{2,6},{6,2},{3,7},{7,3},{8,12},{12,8},{9,1... | collective-permute-start | bytes 1720328 | tf_op jit(solution)/shard_map/ppermute | solution.py:24
  27.9 2.0 %collective-permute-start.7 = (bf16[160,1792]{1,0:T(8,128)(2,1)S(1)}, bf16[160,1792]{1,0:T(8,128)(2,1)S(1)}, u32[]{:S(2)}, u32[]{:S(2)}) collective-permute-start(bf16[160,1792]{1,0:T(8,128)(2,1)S(1)} %shard_map.62.refs_5_.refs_1_), channel_id=1, source_target_pairs={{0,4},{4,0},{1,5},{5,1},{2,6},{6,2},{3,7},{7,3},{8,12},{12,8},{9,1... | collective-permute-start | bytes 1720328 | tf_op jit(solution)/shard_map/ppermute | solution.py:24
  31.6 4.5 %collective-permute-start.8 = (bf16[320,1024]{1,0:T(8,128)(2,1)S(1)}, bf16[320,1024]{1,0:T(8,128)(2,1)S(1)}, u32[]{:S(2)}, u32[]{:S(2)}) collective-permute-start(bf16[320,1024]{1,0:T(8,128)(2,1)S(1)} %get-tuple-element.38.images), channel_id=1, source_target_pairs={{0,4},{4,0},{1,5},{5,1},{2,6},{6,2},{3,7},{7,3},{8,12},{12,8},{9,1... | collective-permute-start | bytes 1966088 | tf_op jit(solution)/shard_map/ppermute | solution.py:24
  31.8 7.2 %collective-permute-start.12 = (f32[8,8,128]{2,1,0:T(8,128)S(1)}, f32[8,8,128]{2,1,0:T(8,128)S(1)}, u32[]{:S(2)}, u32[]{:S(2)}) collective-permute-start(f32[8,8,128]{2,1,0:T(8,128)S(1)} %get-tuple-element.40.refs_2_), channel_id=1, source_target_pairs={{0,17},{1,16},{16,1},{17,0},{2,19},{3,18},{18,3},{19,2},{4,21},{5,... | collective-permute-start | bytes 98312 | tf_op jit(solution)/shard_map/ppermute | solution.py:24
  34.4 4.6 %collective-permute-start.11 = (f32[8,8,128]{2,1,0:T(8,128)S(1)}, f32[8,8,128]{2,1,0:T(8,128)S(1)}, u32[]{:S(2)}, u32[]{:S(2)}) collective-permute-start(f32[8,8,128]{2,1,0:T(8,128)S(1)} %get-tuple-element.40.refs_2_), channel_id=1, source_target_pairs={{0,16},{1,17},{16,0},{17,1},{2,18},{3,19},{18,2},{19,3},{4,20},{5,... | collective-permute-start | bytes 98312 | tf_op jit(solution)/shard_map/ppermute | solution.py:24
  34.9 4.1 %collective-permute-start.10 = (f32[8,8,128]{2,1,0:T(8,128)S(1)}, f32[8,8,128]{2,1,0:T(8,128)S(1)}, u32[]{:S(2)}, u32[]{:S(2)}) collective-permute-start(f32[8,8,128]{2,1,0:T(8,128)S(1)} %get-tuple-element.40.refs_2_), channel_id=1, source_target_pairs={{0,1},{1,0},{16,17},{17,16},{2,3},{3,2},{18,19},{19,18},{4,5},{5,4... | collective-permute-start | bytes 98312 | tf_op jit(solution)/shard_map/ppermute | solution.py:24
  35.3 3.7 %collective-permute-start.9 = (f32[4,8,128]{2,1,0:T(8,128)S(1)}, f32[4,8,128]{2,1,0:T(8,128)S(1)}, u32[]{:S(2)}, u32[]{:S(2)}) collective-permute-start(f32[4,8,128]{2,1,0:T(8,128)S(1)} %get-tuple-element.39.refs_0_), channel_id=1, source_target_pairs={{0,8},{8,0},{1,9},{9,1},{2,10},{10,2},{3,11},{11,3},{4,12},{12,4},... | collective-permute-start | bytes 49160 | tf_op jit(solution)/shard_map/ppermute | solution.py:24
  39.1 5.0 %collective-permute-start.14 = (f32[8,8,128]{2,1,0:T(8,128)S(1)}, f32[8,8,128]{2,1,0:T(8,128)S(1)}, u32[]{:S(2)}, u32[]{:S(2)}) collective-permute-start(f32[8,8,128]{2,1,0:T(8,128)S(1)} %get-tuple-element.42.refs_2_), channel_id=1, source_target_pairs={{0,4},{4,0},{1,5},{5,1},{2,6},{6,2},{3,7},{7,3},{8,12},{12,8},{9,1... | collective-permute-start | bytes 98312 | tf_op jit(solution)/shard_map/ppermute | solution.py:24
  39.2 4.9 %collective-permute-start.13 = (f32[4,8,128]{2,1,0:T(8,128)S(1)}, f32[4,8,128]{2,1,0:T(8,128)S(1)}, u32[]{:S(2)}, u32[]{:S(2)}) collective-permute-start(f32[4,8,128]{2,1,0:T(8,128)S(1)} %get-tuple-element.41.refs_0_), channel_id=1, source_target_pairs={{0,2},{2,0},{1,3},{3,1},{4,6},{6,4},{5,7},{7,5},{8,10},{10,8},{9,1... | collective-permute-start | bytes 49160 | tf_op jit(solution)/shard_map/ppermute | solution.py:24
  45.5 1.6 %collective-permute-start.15 = (bf16[320,320]{1,0:T(8,128)(2,1)S(1)}, bf16[320,320]{1,0:T(8,128)(2,1)S(1)}, u32[]{:S(2)}, u32[]{:S(2)}) collective-permute-start(bf16[320,320]{1,0:T(8,128)(2,1)S(1)} %get-tuple-element.44), channel_id=1, source_target_pairs={{0,4},{4,0},{1,5},{5,1},{2,6},{6,2},{3,7},{7,3},{8,12},{12,8},{9,1... | collective-permute-start | bytes 614408 | tf_op jit(solution)/shard_map/ppermute | solution.py:24
  45.5 6.6 %collective-permute-start.19 = (bf16[80,1024]{1,0:T(8,128)(2,1)S(1)}, bf16[80,1024]{1,0:T(8,128)(2,1)S(1)}, u32[]{:S(2)}, u32[]{:S(2)}) collective-permute-start(bf16[80,1024]{1,0:T(8,128)(2,1)S(1)} %get-tuple-element.50), channel_id=1, source_target_pairs={{0,8},{8,0},{1,9},{9,1},{2,10},{10,2},{3,11},{11,3},{4,12},{12,4},... | collective-permute-start | bytes 491528 | tf_op jit(solution)/shard_map/ppermute | solution.py:24
  47.9 10.0 %collective-permute-start.17 = (bf16[80,1024]{1,0:T(8,128)(2,1)S(1)}, bf16[80,1024]{1,0:T(8,128)(2,1)S(1)}, u32[]{:S(2)}, u32[]{:S(2)}) collective-permute-start(bf16[80,1024]{1,0:T(8,128)(2,1)S(1)} %get-tuple-element.48), channel_id=1, source_target_pairs={{0,16},{16,0},{1,17},{17,1},{2,18},{18,2},{3,19},{19,3},{4,20},{20... | collective-permute-start | bytes 491528 | tf_op jit(solution)/shard_map/ppermute | solution.py:24
  52.2 10.7 %collective-permute-start.21 = (bf16[80,1024]{1,0:T(8,128)(2,1)S(1)}, bf16[80,1024]{1,0:T(8,128)(2,1)S(1)}, u32[]{:S(2)}, u32[]{:S(2)}) collective-permute-start(bf16[80,1024]{1,0:T(8,128)(2,1)S(1)} %add_convert_fusion), channel_id=1, source_target_pairs={{0,2},{2,0},{1,3},{3,1},{4,6},{6,4},{5,7},{7,5},{8,10},{10,8},{9,1... | collective-permute-start | bytes 491528 | tf_op jit(solution)/shard_map/ppermute | solution.py:24
  55.8 5.5 %collective-permute-start.20 = (bf16[80,1024]{1,0:T(8,128)(2,1)S(1)}, bf16[80,1024]{1,0:T(8,128)(2,1)S(1)}, u32[]{:S(2)}, u32[]{:S(2)}) collective-permute-start(bf16[80,1024]{1,0:T(8,128)(2,1)S(1)} %get-tuple-element.53), channel_id=1, source_target_pairs={{0,8},{8,0},{1,9},{9,1},{2,10},{10,2},{3,11},{11,3},{4,12},{12,4},... | collective-permute-start | bytes 491528 | tf_op jit(solution)/shard_map/ppermute | solution.py:24
  56.4 6.4 %collective-permute-start.16 = (bf16[80,1024]{1,0:T(8,128)(2,1)S(1)}, bf16[80,1024]{1,0:T(8,128)(2,1)S(1)}, u32[]{:S(2)}, u32[]{:S(2)}) collective-permute-start(bf16[80,1024]{1,0:T(8,128)(2,1)S(1)} %get-tuple-element.46), channel_id=1, source_target_pairs={{0,16},{16,0},{1,17},{17,1},{2,18},{18,2},{3,19},{19,3},{4,20},{20... | collective-permute-start | bytes 491528 | tf_op jit(solution)/shard_map/ppermute | solution.py:24
  58.0 7.2 %collective-permute-start.18 = (bf16[80,1024]{1,0:T(8,128)(2,1)S(1)}, bf16[80,1024]{1,0:T(8,128)(2,1)S(1)}, u32[]{:S(2)}, u32[]{:S(2)}) collective-permute-start(bf16[80,1024]{1,0:T(8,128)(2,1)S(1)} %add_convert_fusion.1), channel_id=1, source_target_pairs={{0,1},{1,0},{2,3},{3,2},{4,5},{5,4},{6,7},{7,6},{8,9},{9,8},{10,11... | collective-permute-start | bytes 491528 | tf_op jit(solution)/shard_map/ppermute | solution.py:24

commit v8 on v7

--- a/solution.py
+++ b/solution.py
@@ -113,6 +113,16 @@
     refs[-1][...] = joined(refs[:-1])
 
 
+def window(refs, start, stop, columns):
+    values, first = [], 0
+    for ref in refs:
+        low, high = max(start - first, 0), min(stop - first, ref.shape[0])
+        if low < high:
+            values.append(ref[low:high, columns])
+        first += ref.shape[0]
+    return values[0] if len(values) == 1 else jnp.concatenate(values, axis=0)
+
+
 def logits(left, right, out):
     gain = logit_gain / math.sqrt(left.shape[1])
     out[...] = gain * lax.dot_general(left, right, (((1,), (1,)), ((), ())), preferred_element_type=jnp.float32)
@@ -123,22 +133,53 @@
     return columns, [peak, jnp.sum(jnp.exp(matrix - peak), axis=0, keepdims=True)]
 
 
-def logits_kernel(n_img, rows, width, *refs):
+def stacked(lines):
+    count = lines[0].shape[1]
+    row = lax.broadcasted_iota(jnp.int32, (8, count), 0)
+    result = jnp.zeros((8, count), jnp.float32)
+    for k, line in enumerate(lines):
+        result = jnp.where(row == k, line, result)
+    return result
+
+
+def head_kernel(n_img, width, *refs):
+    img_parts, cap_parts = refs[:n_img], refs[n_img:-4]
+    student_ref, teacher_ref, wide_ref, lines_ref = refs[-4:]
+    count = student_ref.shape[1]
+    columns, lines = [], []
+    for part, out in ((slice(0, width), student_ref), (slice(width, None), teacher_ref)):
+        left = joined(img_parts, part)
+        more = logits(left, window(cap_parts, 0, count, part), out)
+        columns, lines = columns + more[0], lines + more[1]
+    lane = lax.broadcasted_iota(jnp.int32, wide_ref.shape, 1)
+    wide = jnp.zeros(wide_ref.shape, jnp.float32)
+    for k, column in enumerate(columns):
+        wide = jnp.where(lane == k, column, wide)
+    wide_ref[...] = wide
+    lines_ref[...] = stacked(lines)
+
+
+def tail_kernel(n_img, start, rows, width, wide_ref, lines_ref, *refs):
     img_parts, cap_parts = refs[:n_img], refs[n_img:-5]
     student_ref, teacher_ref, row_ref, col_ref, images = refs[-5:]
+    stop = start + student_ref.shape[1]
     columns, lines = [], []
     for part, out in ((slice(0, width), student_ref), (slice(width, None), teacher_ref)):
         left = joined(img_parts, part)
         if out is student_ref:
             images[...] = left
-        more = logits(left, joined(cap_parts, part), out)
-        columns, lines = columns + more[0], lines + more[1]
-    lines.append(jnp.zeros((4, lines[0].shape[1]), jnp.float32))
+        (peak, total), more = logits(left, window(cap_parts, start, stop, part), out)
+        k = len(columns)
+        before_peak, before = wide_ref[:, k : k + 1], wide_ref[:, k + 1 : k + 2]
+        both = jnp.maximum(peak, before_peak)
+        columns += [both, before * jnp.exp(before_peak - both) + total * jnp.exp(peak - both)]
+        lines += more
+    lines = jnp.concatenate([lines_ref[...], stacked(lines)], axis=1)
     row = lax.broadcasted_iota(jnp.int32, (8, LANES), 0)
     lane = lax.broadcasted_iota(jnp.int32, (8, LANES), 1)
     for ref, values, axes, order in (
         (row_ref, lines_of(columns), ROW_AXES, ROW_ORDER),
-        (col_ref, jnp.concatenate(lines, axis=0), COL_AXES, COL_ORDER),
+        (col_ref, lines, COL_AXES, COL_ORDER),
     ):
         for s, owner in enumerate(owners(axes, order)):
             ref[s] = jnp.zeros((8, LANES), jnp.float32)
@@ -182,12 +223,13 @@
             out[s] = block
 
 
-def tile_kernel(plan, n_cap, rows, width, student_ref, teacher_ref, *refs):
+def tile_kernel(plan, n_cap, rows, width, *refs):
     refs = list(refs)
+    student_refs, teacher_refs = (refs.pop(0), refs.pop(0)), (refs.pop(0), refs.pop(0))
     blocks = take(refs, plan)
     captions = [refs.pop(0) for _ in range(n_cap)]
     tile_ref, send_ref, *outs = refs
-    total, count = teacher_ref.shape
+    total, count = tile_ref.shape
 
     def finish(blocks):
         lines = load_slots(blocks, rows)
@@ -200,7 +242,7 @@
     step = 64 if total % 64 == 0 else total
     for r in range(0, total, step):
         at = slice(r, r + step)
-        s, t = student_ref[at], teacher_ref[at]
+        s, t = (jnp.concatenate([ref[at] for ref in pair], axis=1) for pair in (student_refs, teacher_refs))
         grad = 0.5 * (jnp.exp(s - down[at, 0:1]) + jnp.exp(s - across[0:1]))
         grad = grad - 0.25 * (jnp.exp(t - down[at, 1:2]) + jnp.exp(t - across[1:2]))
         grad = grad - jnp.where(down[at, INDEX : INDEX + 1] == across[INDEX : INDEX + 1], 0.5, 0.0)
@@ -327,11 +369,22 @@
         img, cap = [assemble(img)], [assemble(cap)]
 
     row_shape, col_shape = shape((n_img, 8, LANES), f32), shape((n_cap, 8, LANES), f32)
-    student, teacher, row_stats, col_stats, images = call(
-        functools.partial(logits_kernel, len(img), rows, width),
-        [shape((total, columns), f32)] * 2 + [row_shape, col_shape, shape((total, width), bf16)],
-        img + cap,
-        2 * total * columns * (width + depth),
+    head = (columns - (cap[-1].shape[0] if aligned else rows)) // LANES * LANES
+    ready = cap[:-1] if aligned else cap
+    skipped = [part for k, part in enumerate(cap) if sum(p.shape[0] for p in cap[: k + 1]) <= head]
+    needed = cap[len(skipped) :]
+    start = head - sum(part.shape[0] for part in skipped)
+    student, teacher, wide, lines = call(
+        functools.partial(head_kernel, len(img), width),
+        [shape((total, head), f32)] * 2 + [shape((total, LANES), f32), shape((8, head), f32)],
+        img + ready,
+        2 * total * head * (width + depth),
+    )
+    student_tail, teacher_tail, row_stats, col_stats, images = call(
+        functools.partial(tail_kernel, len(img), start, rows, width),
+        [shape((total, columns - head), f32)] * 2 + [row_shape, col_shape, shape((total, width), bf16)],
+        [wide, lines] + img + needed,
+        2 * total * (columns - head) * (width + depth),
     )
 
     images_other = swap(images, "core", 1)
@@ -355,7 +408,7 @@
     tile, tile_send, *image_parts = call(
         functools.partial(tile_kernel, plan, len(cap), rows, width),
         [shape((total, columns), bf16), shape((total, columns // 2), bf16)] + pieces(far_blocks),
-        [student, teacher] + blocks + cap,
+        [student, student_tail, teacher, teacher_tail] + blocks + cap,
         2 * total * columns * width // 2,
     )
     image_parts = dict(zip(far_blocks, image_parts))

time: 66.2 us -> 66.9 us (1.011)
  Pallas kernels: 6.57 us -> 8.28 us
  waiting for transfers between devices: 29.7 us -> 28.6 us
    pallas_call x10 -> x11, Pallas kernels: 6.57 us -> 8.28 us  [call(): pl.pallas_call(kernel, out_shape=[out_space(out.shape, out.dtype) for out...]
    ppermute x22, waiting for transfers between devices: 29.7 us -> 28.6 us  [swap(): return lax.ppermute(value, axis, [(j, j ^ mask) for j in range(size)])]
  transfers between devices with their start and end apart: 22 -> 22, of which waited for: 11 -> 11; matrix products, arithmetic and copies ran while one was open for 0% -> 0% of each run, Pallas kernels for 2% -> 4%
where the time goes in v8:
time: 66.9 us; the launch traced here: 66.8 us
  starting transfers between devices  29 us (43%)
  waiting for transfers between devices  28.6 us (43%)
  Pallas kernels  8.28 us (12%)
  between operations  0.75 us (1%)
    ppermute x22, starting transfers between devices, swap(): return lax.ppermute(value, axis, [(j, j ^ mask) for j in range(size)])  29 us
    ppermute x22, waiting for transfers between devices, swap(): return lax.ppermute(value, axis, [(j, j ^ mask) for j in range(size)])  28.6 us
    pallas_call x11, Pallas kernels, call(): pl.pallas_call(kernel, out_shape=[out_space(out.shape, out.dtype) for out...  8.28 us
  transfers between devices with their start and end apart: 22, of which 11 were waited for; matrix products, arithmetic and copies ran while one was open for 0% of the time, Pallas kernels for 4%

profile of v8, /device:TPU:0, one launch (start us, length us, event | category | flops | bytes accessed | tf_op | source)
XLA Modules:
  0.0 66.8 jit_solution(7548848885274564412)
XLA Ops:
  0.6 1.2 %shard_map.59 = (bf16[80,1792]{1,0:T(8,128)(2,1)S(1)}, bf16[80,1792]{1,0:T(8,128)(2,1)S(1)}) custom-call(bf16[80,1024]{1,0:T(8,128)(2,1)} %image_s.1, bf16[80,768]{1,0:T(8,128)(2,1)} %image_t.1, bf16[80,1024]{1,0:T(8,128)(2,1)} %caption_s.1, bf16[80,768]{1,0:T(8,128)(2,1)} %caption_t.1), custom_call_target="tpu_custom_call" | custom-call | bytes 1146880 | tf_op jit(solution)/shard_map/pallas_call | solution.py:304
  1.8 4.1 %collective-permute-start = (bf16[80,1792]{1,0:T(8,128)(2,1)S(1)}, bf16[80,1792]{1,0:T(8,128)(2,1)S(1)}, u32[]{:S(2)}, u32[]{:S(2)}) collective-permute-start(bf16[80,1792]{1,0:T(8,128)(2,1)S(1)} %get-tuple-element.33.refs_0_), channel_id=1, source_target_pairs={{0,2},{2,0},{1,3},{3,1},{4,6},{6,4},{5,7},{7,5},{8,10},{10,8},{9,1... | collective-permute-start | bytes 860168 | tf_op jit(solution)/shard_map/ppermute | solution.py:24
  5.9 1.6 %collective-permute-start.4 = (bf16[80,1792]{1,0:T(8,128)(2,1)S(1)}, bf16[80,1792]{1,0:T(8,128)(2,1)S(1)}, u32[]{:S(2)}, u32[]{:S(2)}) collective-permute-start(bf16[80,1792]{1,0:T(8,128)(2,1)S(1)} %get-tuple-element.36.refs_1_.refs_0_), channel_id=1, source_target_pairs={{0,1},{1,0},{2,3},{3,2},{4,5},{5,4},{6,7},{7,6},{8,9},{9,8},{10,11... | collective-permute-start | bytes 860168 | tf_op jit(solution)/shard_map/ppermute | solution.py:24
  7.5 1.6 %collective-permute-start.1 = (bf16[80,1792]{1,0:T(8,128)(2,1)S(1)}, bf16[80,1792]{1,0:T(8,128)(2,1)S(1)}, u32[]{:S(2)}, u32[]{:S(2)}) collective-permute-start(bf16[80,1792]{1,0:T(8,128)(2,1)S(1)} %get-tuple-element.35), channel_id=1, source_target_pairs={{0,8},{8,0},{1,9},{9,1},{2,10},{10,2},{3,11},{11,3},{4,12},{12,4},... | collective-permute-start | bytes 860168 | tf_op jit(solution)/shard_map/ppermute | solution.py:24
  9.1 1.5 %collective-permute-start.3 = (bf16[80,1792]{1,0:T(8,128)(2,1)S(1)}, bf16[80,1792]{1,0:T(8,128)(2,1)S(1)}, u32[]{:S(2)}, u32[]{:S(2)}) collective-permute-start(bf16[80,1792]{1,0:T(8,128)(2,1)S(1)} %get-tuple-element.37), channel_id=1, source_target_pairs={{0,16},{16,0},{1,17},{17,1},{2,18},{18,2},{3,19},{19,3},{4,20},{20... | collective-permute-start | bytes 860168 | tf_op jit(solution)/shard_map/ppermute | solution.py:24
  10.6 8.4 %collective-permute-done.refs_1_ = bf16[80,1792]{1,0:T(8,128)(2,1)S(1)} collective-permute-done((bf16[80,1792]{1,0:T(8,128)(2,1)S(1)}, bf16[80,1792]{1,0:T(8,128)(2,1)S(1)}, u32[]{:S(2)}, u32[]{:S(2)}) %collective-permute-start) | collective-permute-done | bytes 286752 | tf_op jit(solution)/shard_map/ppermute | solution.py:24
  19.0 1.5 %collective-permute-start.2 = (bf16[80,1792]{1,0:T(8,128)(2,1)S(1)}, bf16[80,1792]{1,0:T(8,128)(2,1)S(1)}, u32[]{:S(2)}, u32[]{:S(2)}) collective-permute-start(bf16[80,1792]{1,0:T(8,128)(2,1)S(1)} %collective-permute-done.refs_1_), channel_id=1, source_target_pairs={{0,8},{8,0},{1,9},{9,1},{2,10},{10,2},{3,11},{11,3},{4,12},{12,4},... | collective-permute-start | bytes 860168 | tf_op jit(solution)/shard_map/ppermute | solution.py:24
  20.5 1.5 %collective-permute-start.5 = (bf16[80,1792]{1,0:T(8,128)(2,1)S(1)}, bf16[80,1792]{1,0:T(8,128)(2,1)S(1)}, u32[]{:S(2)}, u32[]{:S(2)}) collective-permute-start(bf16[80,1792]{1,0:T(8,128)(2,1)S(1)} %collective-permute-done.4.refs_0_), channel_id=1, source_target_pairs={{0,16},{16,0},{1,17},{17,1},{2,18},{18,2},{3,19},{19,3},{4,20},{20... | collective-permute-start | bytes 860168 | tf_op jit(solution)/shard_map/ppermute | solution.py:24
  22.2 4.8 %collective-permute-done.2.refs_3_ = bf16[80,1792]{1,0:T(8,128)(2,1)S(1)} collective-permute-done((bf16[80,1792]{1,0:T(8,128)(2,1)S(1)}, bf16[80,1792]{1,0:T(8,128)(2,1)S(1)}, u32[]{:S(2)}, u32[]{:S(2)}) %collective-permute-start.2) | collective-permute-done | bytes 286752 | tf_op jit(solution)/shard_map/ppermute | solution.py:24
  26.9 1.0 %collective-permute-done.5.refs_1_ = bf16[80,1792]{1,0:T(8,128)(2,1)S(1)} collective-permute-done((bf16[80,1792]{1,0:T(8,128)(2,1)S(1)}, bf16[80,1792]{1,0:T(8,128)(2,1)S(1)}, u32[]{:S(2)}, u32[]{:S(2)}) %collective-permute-start.5) | collective-permute-done | bytes 286752 | tf_op jit(solution)/shard_map/ppermute | solution.py:24
  28.0 1.0 %shard_map.63 = (f32[320,384]{1,0:T(8,128)S(1)}, f32[320,384]{1,0:T(8,128)S(1)}, f32[320,128]{1,0:T(8,128)S(1)}, f32[8,384]{1,0:T(8,128)S(1)}) custom-call(bf16[80,1792]{1,0:T(8,128)(2,1)S(1)} %get-tuple-element.33.refs_0_, bf16[80,1792]{1,0:T(8,128)(2,1)S(1)} %collective-permute-done.refs_1_, bf16[80,1792]{1,0:T(8,128)(2,1)S(1)} %collective-permute-done.1.refs_2_, ...), custom_call_target="tpu_custom_call" | custom-call | flops 440401920 | bytes 4026368 | tf_op jit(solution)/shard_map/pallas_call | solution.py:304
  29.1 0.9 %collective-permute-done.7.refs_5_.refs_11_.refs_3_ = bf16[160,1792]{1,0:T(8,128)(2,1)S(1)} collective-permute-done((bf16[160,1792]{1,0:T(8,128)(2,1)S(1)}, bf16[160,1792]{1,0:T(8,128)(2,1)S(1)}, u32[]{:S(2)}, u32[]{:S(2)}) %collective-permute-start.7) | collective-permute-done | bytes 573472 | tf_op jit(solution)/shard_map/ppermute | solution.py:24
  30.0 2.3 %shard_map.64 = (f32[320,256]{1,0:T(8,128)S(1)}, f32[320,256]{1,0:T(8,128)S(1)}, f32[4,8,128]{2,1,0:T(8,128)S(1)}, f32[8,8,128]{2,1,0:T(8,128)S(1)}, bf16[320,1024]{1,0:T(8,128)(2,1)S(1)}) custom-call(f32[320,128]{1,0:T(8,128)S(1)} %get-tuple-element.40.wide_ref, f32[8,384]{1,0:T(8,128)S(1)} %get-tuple-element.41.lines_ref, ...), custom_call_target="tpu_custom_call" | custom-call | flops 293601280 | bytes 3829760 | tf_op jit(solution)/shard_map/pallas_call | solution.py:304
  32.5 2.6 %collective-permute-start.12 = (f32[8,8,128]{2,1,0:T(8,128)S(1)}, f32[8,8,128]{2,1,0:T(8,128)S(1)}, u32[]{:S(2)}, u32[]{:S(2)}) collective-permute-start(f32[8,8,128]{2,1,0:T(8,128)S(1)} %get-tuple-element.48.refs_2_), channel_id=1, source_target_pairs={{0,17},{1,16},{16,1},{17,0},{2,19},{3,18},{18,3},{19,2},{4,21},{5,... | collective-permute-start | bytes 98312 | tf_op jit(solution)/shard_map/ppermute | solution.py:24
  36.0 0.8 %collective-permute-start.9 = (f32[4,8,128]{2,1,0:T(8,128)S(1)}, f32[4,8,128]{2,1,0:T(8,128)S(1)}, u32[]{:S(2)}, u32[]{:S(2)}) collective-permute-start(f32[4,8,128]{2,1,0:T(8,128)S(1)} %get-tuple-element.47.refs_0_), channel_id=1, source_target_pairs={{0,8},{8,0},{1,9},{9,1},{2,10},{10,2},{3,11},{11,3},{4,12},{12,4},... | collective-permute-start | bytes 49160 | tf_op jit(solution)/shard_map/ppermute | solution.py:24
  36.8 3.0 %collective-permute-done.9.refs_1_ = f32[4,8,128]{2,1,0:T(8,128)S(1)} collective-permute-done((f32[4,8,128]{2,1,0:T(8,128)S(1)}, f32[4,8,128]{2,1,0:T(8,128)S(1)}, u32[]{:S(2)}, u32[]{:S(2)}) %collective-permute-start.9) | collective-permute-done | bytes 16416 | tf_op jit(solution)/shard_map/ppermute | solution.py:24
  39.9 3.2 %collective-permute-start.13 = (f32[4,8,128]{2,1,0:T(8,128)S(1)}, f32[4,8,128]{2,1,0:T(8,128)S(1)}, u32[]{:S(2)}, u32[]{:S(2)}) collective-permute-start(f32[4,8,128]{2,1,0:T(8,128)S(1)} %get-tuple-element.49.refs_4_), channel_id=1, source_target_pairs={{0,2},{2,0},{1,3},{3,1},{4,6},{6,4},{5,7},{7,5},{8,10},{10,8},{9,1... | collective-permute-start | bytes 49160 | tf_op jit(solution)/shard_map/ppermute | solution.py:24
  43.1 1.7 %collective-permute-done.13.refs_5_ = f32[4,8,128]{2,1,0:T(8,128)S(1)} collective-permute-done((f32[4,8,128]{2,1,0:T(8,128)S(1)}, f32[4,8,128]{2,1,0:T(8,128)S(1)}, u32[]{:S(2)}, u32[]{:S(2)}) %collective-permute-start.13) | collective-permute-done | bytes 16416 | tf_op jit(solution)/shard_map/ppermute | solution.py:24
  44.8 1.3 %shard_map.66 = (bf16[320,640]{1,0:T(8,128)(2,1)S(1)}, bf16[320,320]{1,0:T(8,128)(2,1)S(1)}, f32[80,1024]{1,0:T(8,128)S(1)}, bf16[80,1024]{1,0:T(8,128)(2,1)S(1)}) custom-call(f32[320,384]{1,0:T(8,128)S(1)} %get-tuple-element.39.refs_0_, f32[320,256]{1,0:T(8,128)S(1)} %get-tuple-element.42.refs_1_, f32[320,384]{1,0:T(8,128)S(1)} %get-tuple-element.43.refs_2_, ...), custom_call_target="tpu_custom_call" | custom-call | flops 209715200 | bytes 5136384 | tf_op jit(solution)/shard_map/pallas_call | solution.py:304
  46.2 0.6 collective-permute-start.19
  46.8 0.9 %collective-permute-done.15.tile_other = bf16[320,320]{1,0:T(8,128)(2,1)S(1)} collective-permute-done((bf16[320,320]{1,0:T(8,128)(2,1)S(1)}, bf16[320,320]{1,0:T(8,128)(2,1)S(1)}, u32[]{:S(2)}, u32[]{:S(2)}) %collective-permute-start.15) | collective-permute-done | bytes 204832 | tf_op jit(solution)/shard_map/ppermute | solution.py:24
  47.7 0.9 %shard_map.67 = (f32[80,1024]{1,0:T(8,128)S(1)}, bf16[80,1024]{1,0:T(8,128)(2,1)S(1)}, f32[80,1024]{1,0:T(8,128)S(1)}, bf16[80,1024]{1,0:T(8,128)(2,1)S(1)}) custom-call(bf16[320,640]{1,0:T(8,128)(2,1)S(1)} %get-tuple-element.59.tile_ref, bf16[320,320]{1,0:T(8,128)(2,1)S(1)} %collective-permute-done.15.tile_other, ...), custom_call_target="tpu_custom_call" | custom-call | flops 419430400 | bytes 2908160 | tf_op jit(solution)/shard_map/pallas_call | solution.py:304
  48.6 1.6 %collective-permute-start.17 = (bf16[80,1024]{1,0:T(8,128)(2,1)S(1)}, bf16[80,1024]{1,0:T(8,128)(2,1)S(1)}, u32[]{:S(2)}, u32[]{:S(2)}) collective-permute-start(bf16[80,1024]{1,0:T(8,128)(2,1)S(1)} %get-tuple-element.56), channel_id=1, source_target_pairs={{0,16},{16,0},{1,17},{17,1},{2,18},{18,2},{3,19},{19,3},{4,20},{20... | collective-permute-start | bytes 491528 | tf_op jit(solution)/shard_map/ppermute | solution.py:24
  50.2 2.7 %collective-permute-done.19 = bf16[80,1024]{1,0:T(8,128)(2,1)S(1)} collective-permute-done((bf16[80,1024]{1,0:T(8,128)(2,1)S(1)}, bf16[80,1024]{1,0:T(8,128)(2,1)S(1)}, u32[]{:S(2)}, u32[]{:S(2)}) %collective-permute-start.19) | collective-permute-done | bytes 163872 | tf_op jit(solution)/shard_map/ppermute | solution.py:24
  52.9 3.0 %collective-permute-start.21 = (bf16[80,1024]{1,0:T(8,128)(2,1)S(1)}, bf16[80,1024]{1,0:T(8,128)(2,1)S(1)}, u32[]{:S(2)}, u32[]{:S(2)}) collective-permute-start(bf16[80,1024]{1,0:T(8,128)(2,1)S(1)} %add_convert_fusion), channel_id=1, source_target_pairs={{0,2},{2,0},{1,3},{3,1},{4,6},{6,4},{5,7},{7,5},{8,10},{10,8},{9,1... | collective-permute-start | bytes 491528 | tf_op jit(solution)/shard_map/ppermute | solution.py:24
  56.5 0.6 collective-permute-start.20
  57.1 1.5 %collective-permute-start.16 = (bf16[80,1024]{1,0:T(8,128)(2,1)S(1)}, bf16[80,1024]{1,0:T(8,128)(2,1)S(1)}, u32[]{:S(2)}, u32[]{:S(2)}) collective-permute-start(bf16[80,1024]{1,0:T(8,128)(2,1)S(1)} %get-tuple-element.54), channel_id=1, source_target_pairs={{0,16},{16,0},{1,17},{17,1},{2,18},{18,2},{3,19},{19,3},{4,20},{20... | collective-permute-start | bytes 491528 | tf_op jit(solution)/shard_map/ppermute | solution.py:24
  58.7 1.9 %collective-permute-start.18 = (bf16[80,1024]{1,0:T(8,128)(2,1)S(1)}, bf16[80,1024]{1,0:T(8,128)(2,1)S(1)}, u32[]{:S(2)}, u32[]{:S(2)}) collective-permute-start(bf16[80,1024]{1,0:T(8,128)(2,1)S(1)} %add_convert_fusion.1), channel_id=1, source_target_pairs={{0,1},{1,0},{2,3},{3,2},{4,5},{5,4},{6,7},{7,6},{8,9},{9,8},{10,11... | collective-permute-start | bytes 491528 | tf_op jit(solution)/shard_map/ppermute | solution.py:24
  60.5 1.5 %collective-permute-done.20.refs_4_ = bf16[80,1024]{1,0:T(8,128)(2,1)S(1)} collective-permute-done((bf16[80,1024]{1,0:T(8,128)(2,1)S(1)}, bf16[80,1024]{1,0:T(8,128)(2,1)S(1)}, u32[]{:S(2)}, u32[]{:S(2)}) %collective-permute-start.20) | collective-permute-done | bytes 163872 | tf_op jit(solution)/shard_map/ppermute | solution.py:24
  62.0 1.5 %collective-permute-done.21.refs_5_ = bf16[80,1024]{1,0:T(8,128)(2,1)S(1)} collective-permute-done((bf16[80,1024]{1,0:T(8,128)(2,1)S(1)}, bf16[80,1024]{1,0:T(8,128)(2,1)S(1)}, u32[]{:S(2)}, u32[]{:S(2)}) %collective-permute-start.21) | collective-permute-done | bytes 163872 | tf_op jit(solution)/shard_map/ppermute | solution.py:24
  63.5 2.3 %collective-permute-done.18.refs_2_ = bf16[80,1024]{1,0:T(8,128)(2,1)S(1)} collective-permute-done((bf16[80,1024]{1,0:T(8,128)(2,1)S(1)}, bf16[80,1024]{1,0:T(8,128)(2,1)S(1)}, u32[]{:S(2)}, u32[]{:S(2)}) %collective-permute-start.18) | collective-permute-done | bytes 163872 | tf_op jit(solution)/shard_map/ppermute | solution.py:24
  65.9 0.9 %shard_map.69 = (f32[80,1024]{1,0:T(8,128)}, f32[80,1024]{1,0:T(8,128)}) custom-call(f32[80,1024]{1,0:T(8,128)S(1)} %get-tuple-element.53.refs_0_, bf16[80,1024]{1,0:T(8,128)(2,1)S(1)} %collective-permute-done.16.refs_1_, bf16[80,1024]{1,0:T(8,128)(2,1)S(1)} %collective-permute-done.18.refs_2_, f32[80,1024]{1,0:T(8,128)S(1)} %get-tuple-element.60.refs_3_, ...), custom_call_target="tpu_custom_call" | custom-call | bytes 1966080 | tf_op jit(solution)/shard_map/pallas_call | solution.py:304
  (25 shorter events, 2.2 us)
Async XLA Ops:
  1.8 17.2 %collective-permute-start = (bf16[80,1792]{1,0:T(8,128)(2,1)S(1)}, bf16[80,1792]{1,0:T(8,128)(2,1)S(1)}, u32[]{:S(2)}, u32[]{:S(2)}) collective-permute-start(bf16[80,1792]{1,0:T(8,128)(2,1)S(1)} %get-tuple-element.33.refs_0_), channel_id=1, source_target_pairs={{0,2},{2,0},{1,3},{3,1},{4,6},{6,4},{5,7},{7,5},{8,10},{10,8},{9,1... | collective-permute-start | bytes 860168 | tf_op jit(solution)/shard_map/ppermute | solution.py:24
  5.9 14.6 %collective-permute-start.4 = (bf16[80,1792]{1,0:T(8,128)(2,1)S(1)}, bf16[80,1792]{1,0:T(8,128)(2,1)S(1)}, u32[]{:S(2)}, u32[]{:S(2)}) collective-permute-start(bf16[80,1792]{1,0:T(8,128)(2,1)S(1)} %get-tuple-element.36.refs_1_.refs_0_), channel_id=1, source_target_pairs={{0,1},{1,0},{2,3},{3,2},{4,5},{5,4},{6,7},{7,6},{8,9},{9,8},{10,11... | collective-permute-start | bytes 860168 | tf_op jit(solution)/shard_map/ppermute | solution.py:24
  7.5 14.5 %collective-permute-start.1 = (bf16[80,1792]{1,0:T(8,128)(2,1)S(1)}, bf16[80,1792]{1,0:T(8,128)(2,1)S(1)}, u32[]{:S(2)}, u32[]{:S(2)}) collective-permute-start(bf16[80,1792]{1,0:T(8,128)(2,1)S(1)} %get-tuple-element.35), channel_id=1, source_target_pairs={{0,8},{8,0},{1,9},{9,1},{2,10},{10,2},{3,11},{11,3},{4,12},{12,4},... | collective-permute-start | bytes 860168 | tf_op jit(solution)/shard_map/ppermute | solution.py:24
  9.1 13.0 %collective-permute-start.3 = (bf16[80,1792]{1,0:T(8,128)(2,1)S(1)}, bf16[80,1792]{1,0:T(8,128)(2,1)S(1)}, u32[]{:S(2)}, u32[]{:S(2)}) collective-permute-start(bf16[80,1792]{1,0:T(8,128)(2,1)S(1)} %get-tuple-element.37), channel_id=1, source_target_pairs={{0,16},{16,0},{1,17},{17,1},{2,18},{18,2},{3,19},{19,3},{4,20},{20... | collective-permute-start | bytes 860168 | tf_op jit(solution)/shard_map/ppermute | solution.py:24
  19.0 8.0 %collective-permute-start.2 = (bf16[80,1792]{1,0:T(8,128)(2,1)S(1)}, bf16[80,1792]{1,0:T(8,128)(2,1)S(1)}, u32[]{:S(2)}, u32[]{:S(2)}) collective-permute-start(bf16[80,1792]{1,0:T(8,128)(2,1)S(1)} %collective-permute-done.refs_1_), channel_id=1, source_target_pairs={{0,8},{8,0},{1,9},{9,1},{2,10},{10,2},{3,11},{11,3},{4,12},{12,4},... | collective-permute-start | bytes 860168 | tf_op jit(solution)/shard_map/ppermute | solution.py:24
  20.5 7.4 %collective-permute-start.5 = (bf16[80,1792]{1,0:T(8,128)(2,1)S(1)}, bf16[80,1792]{1,0:T(8,128)(2,1)S(1)}, u32[]{:S(2)}, u32[]{:S(2)}) collective-permute-start(bf16[80,1792]{1,0:T(8,128)(2,1)S(1)} %collective-permute-done.4.refs_0_), channel_id=1, source_target_pairs={{0,16},{16,0},{1,17},{17,1},{2,18},{18,2},{3,19},{19,3},{4,20},{20... | collective-permute-start | bytes 860168 | tf_op jit(solution)/shard_map/ppermute | solution.py:24
  22.1 5.9 %collective-permute-start.6 = (bf16[160,1792]{1,0:T(8,128)(2,1)S(1)}, bf16[160,1792]{1,0:T(8,128)(2,1)S(1)}, u32[]{:S(2)}, u32[]{:S(2)}) collective-permute-start(bf16[160,1792]{1,0:T(8,128)(2,1)S(1)} %shard_map.61.refs_4_.refs_8_.refs_0_), channel_id=1, source_target_pairs={{0,4},{4,0},{1,5},{5,1},{2,6},{6,2},{3,7},{7,3},{8,12},{12,8},{9,1... | collective-permute-start | bytes 1720328 | tf_op jit(solution)/shard_map/ppermute | solution.py:24
  27.9 2.0 %collective-permute-start.7 = (bf16[160,1792]{1,0:T(8,128)(2,1)S(1)}, bf16[160,1792]{1,0:T(8,128)(2,1)S(1)}, u32[]{:S(2)}, u32[]{:S(2)}) collective-permute-start(bf16[160,1792]{1,0:T(8,128)(2,1)S(1)} %shard_map.62.refs_5_.refs_9_.refs_1_), channel_id=1, source_target_pairs={{0,4},{4,0},{1,5},{5,1},{2,6},{6,2},{3,7},{7,3},{8,12},{12,8},{9,1... | collective-permute-start | bytes 1720328 | tf_op jit(solution)/shard_map/ppermute | solution.py:24
  32.3 4.5 %collective-permute-start.8 = (bf16[320,1024]{1,0:T(8,128)(2,1)S(1)}, bf16[320,1024]{1,0:T(8,128)(2,1)S(1)}, u32[]{:S(2)}, u32[]{:S(2)}) collective-permute-start(bf16[320,1024]{1,0:T(8,128)(2,1)S(1)} %get-tuple-element.46.images), channel_id=1, source_target_pairs={{0,4},{4,0},{1,5},{5,1},{2,6},{6,2},{3,7},{7,3},{8,12},{12,8},{9,1... | collective-permute-start | bytes 1966088 | tf_op jit(solution)/shard_map/ppermute | solution.py:24
  32.5 7.2 %collective-permute-start.12 = (f32[8,8,128]{2,1,0:T(8,128)S(1)}, f32[8,8,128]{2,1,0:T(8,128)S(1)}, u32[]{:S(2)}, u32[]{:S(2)}) collective-permute-start(f32[8,8,128]{2,1,0:T(8,128)S(1)} %get-tuple-element.48.refs_2_), channel_id=1, source_target_pairs={{0,17},{1,16},{16,1},{17,0},{2,19},{3,18},{18,3},{19,2},{4,21},{5,... | collective-permute-start | bytes 98312 | tf_op jit(solution)/shard_map/ppermute | solution.py:24
  35.1 4.6 %collective-permute-start.11 = (f32[8,8,128]{2,1,0:T(8,128)S(1)}, f32[8,8,128]{2,1,0:T(8,128)S(1)}, u32[]{:S(2)}, u32[]{:S(2)}) collective-permute-start(f32[8,8,128]{2,1,0:T(8,128)S(1)} %get-tuple-element.48.refs_2_), channel_id=1, source_target_pairs={{0,16},{1,17},{16,0},{17,1},{2,18},{3,19},{18,2},{19,3},{4,20},{5,... | collective-permute-start | bytes 98312 | tf_op jit(solution)/shard_map/ppermute | solution.py:24
  35.6 4.1 %collective-permute-start.10 = (f32[8,8,128]{2,1,0:T(8,128)S(1)}, f32[8,8,128]{2,1,0:T(8,128)S(1)}, u32[]{:S(2)}, u32[]{:S(2)}) collective-permute-start(f32[8,8,128]{2,1,0:T(8,128)S(1)} %get-tuple-element.48.refs_2_), channel_id=1, source_target_pairs={{0,1},{1,0},{16,17},{17,16},{2,3},{3,2},{18,19},{19,18},{4,5},{5,4... | collective-permute-start | bytes 98312 | tf_op jit(solution)/shard_map/ppermute | solution.py:24
  36.0 3.7 %collective-permute-start.9 = (f32[4,8,128]{2,1,0:T(8,128)S(1)}, f32[4,8,128]{2,1,0:T(8,128)S(1)}, u32[]{:S(2)}, u32[]{:S(2)}) collective-permute-start(f32[4,8,128]{2,1,0:T(8,128)S(1)} %get-tuple-element.47.refs_0_), channel_id=1, source_target_pairs={{0,8},{8,0},{1,9},{9,1},{2,10},{10,2},{3,11},{11,3},{4,12},{12,4},... | collective-permute-start | bytes 49160 | tf_op jit(solution)/shard_map/ppermute | solution.py:24
  39.8 5.0 %collective-permute-start.14 = (f32[8,8,128]{2,1,0:T(8,128)S(1)}, f32[8,8,128]{2,1,0:T(8,128)S(1)}, u32[]{:S(2)}, u32[]{:S(2)}) collective-permute-start(f32[8,8,128]{2,1,0:T(8,128)S(1)} %get-tuple-element.50.refs_6_), channel_id=1, source_target_pairs={{0,4},{4,0},{1,5},{5,1},{2,6},{6,2},{3,7},{7,3},{8,12},{12,8},{9,1... | collective-permute-start | bytes 98312 | tf_op jit(solution)/shard_map/ppermute | solution.py:24
  39.9 5.0 %collective-permute-start.13 = (f32[4,8,128]{2,1,0:T(8,128)S(1)}, f32[4,8,128]{2,1,0:T(8,128)S(1)}, u32[]{:S(2)}, u32[]{:S(2)}) collective-permute-start(f32[4,8,128]{2,1,0:T(8,128)S(1)} %get-tuple-element.49.refs_4_), channel_id=1, source_target_pairs={{0,2},{2,0},{1,3},{3,1},{4,6},{6,4},{5,7},{7,5},{8,10},{10,8},{9,1... | collective-permute-start | bytes 49160 | tf_op jit(solution)/shard_map/ppermute | solution.py:24
  46.1 1.6 %collective-permute-start.15 = (bf16[320,320]{1,0:T(8,128)(2,1)S(1)}, bf16[320,320]{1,0:T(8,128)(2,1)S(1)}, u32[]{:S(2)}, u32[]{:S(2)}) collective-permute-start(bf16[320,320]{1,0:T(8,128)(2,1)S(1)} %get-tuple-element.52), channel_id=1, source_target_pairs={{0,4},{4,0},{1,5},{5,1},{2,6},{6,2},{3,7},{7,3},{8,12},{12,8},{9,1... | collective-permute-start | bytes 614408 | tf_op jit(solution)/shard_map/ppermute | solution.py:24
  46.2 6.6 %collective-permute-start.19 = (bf16[80,1024]{1,0:T(8,128)(2,1)S(1)}, bf16[80,1024]{1,0:T(8,128)(2,1)S(1)}, u32[]{:S(2)}, u32[]{:S(2)}) collective-permute-start(bf16[80,1024]{1,0:T(8,128)(2,1)S(1)} %get-tuple-element.58), channel_id=1, source_target_pairs={{0,8},{8,0},{1,9},{9,1},{2,10},{10,2},{3,11},{11,3},{4,12},{12,4},... | collective-permute-start | bytes 491528 | tf_op jit(solution)/shard_map/ppermute | solution.py:24
  48.6 10.0 %collective-permute-start.17 = (bf16[80,1024]{1,0:T(8,128)(2,1)S(1)}, bf16[80,1024]{1,0:T(8,128)(2,1)S(1)}, u32[]{:S(2)}, u32[]{:S(2)}) collective-permute-start(bf16[80,1024]{1,0:T(8,128)(2,1)S(1)} %get-tuple-element.56), channel_id=1, source_target_pairs={{0,16},{16,0},{1,17},{17,1},{2,18},{18,2},{3,19},{19,3},{4,20},{20... | collective-permute-start | bytes 491528 | tf_op jit(solution)/shard_map/ppermute | solution.py:24
  52.9 10.7 %collective-permute-start.21 = (bf16[80,1024]{1,0:T(8,128)(2,1)S(1)}, bf16[80,1024]{1,0:T(8,128)(2,1)S(1)}, u32[]{:S(2)}, u32[]{:S(2)}) collective-permute-start(bf16[80,1024]{1,0:T(8,128)(2,1)S(1)} %add_convert_fusion), channel_id=1, source_target_pairs={{0,2},{2,0},{1,3},{3,1},{4,6},{6,4},{5,7},{7,5},{8,10},{10,8},{9,1... | collective-permute-start | bytes 491528 | tf_op jit(solution)/shard_map/ppermute | solution.py:24
  56.5 5.6 %collective-permute-start.20 = (bf16[80,1024]{1,0:T(8,128)(2,1)S(1)}, bf16[80,1024]{1,0:T(8,128)(2,1)S(1)}, u32[]{:S(2)}, u32[]{:S(2)}) collective-permute-start(bf16[80,1024]{1,0:T(8,128)(2,1)S(1)} %get-tuple-element.61), channel_id=1, source_target_pairs={{0,8},{8,0},{1,9},{9,1},{2,10},{10,2},{3,11},{11,3},{4,12},{12,4},... | collective-permute-start | bytes 491528 | tf_op jit(solution)/shard_map/ppermute | solution.py:24
  57.1 6.4 %collective-permute-start.16 = (bf16[80,1024]{1,0:T(8,128)(2,1)S(1)}, bf16[80,1024]{1,0:T(8,128)(2,1)S(1)}, u32[]{:S(2)}, u32[]{:S(2)}) collective-permute-start(bf16[80,1024]{1,0:T(8,128)(2,1)S(1)} %get-tuple-element.54), channel_id=1, source_target_pairs={{0,16},{16,0},{1,17},{17,1},{2,18},{18,2},{3,19},{19,3},{4,20},{20... | collective-permute-start | bytes 491528 | tf_op jit(solution)/shard_map/ppermute | solution.py:24
  58.7 7.2 %collective-permute-start.18 = (bf16[80,1024]{1,0:T(8,128)(2,1)S(1)}, bf16[80,1024]{1,0:T(8,128)(2,1)S(1)}, u32[]{:S(2)}, u32[]{:S(2)}) collective-permute-start(bf16[80,1024]{1,0:T(8,128)(2,1)S(1)} %add_convert_fusion.1), channel_id=1, source_target_pairs={{0,1},{1,0},{2,3},{3,2},{4,5},{5,4},{6,7},{7,6},{8,9},{9,8},{10,11... | collective-permute-start | bytes 491528 | tf_op jit(solution)/shard_map/ppermute | solution.py:24

commit v9 on v8

--- a/solution.py
+++ b/solution.py
@@ -56,6 +56,12 @@
         lines = jnp.concatenate([lines, jnp.zeros((8, spare), jnp.float32)], axis=1)
     tall = jnp.concatenate([lines, jnp.zeros((LANES - 8, count + spare), jnp.float32)], axis=0)
     return tall.T[:count]
+
+
+def store_slots(ref, lines, rows):
+    ref[...] = jnp.zeros_like(ref)
+    for s in range(ref.shape[0]):
+        ref[s, :, :rows] = lines[:, s * rows : (s + 1) * rows]
 
 
 def load_slots(blocks, rows):
@@ -142,24 +148,19 @@
     return result
 
 
-def head_kernel(n_img, width, *refs):
+def head_kernel(n_img, rows, width, *refs):
     img_parts, cap_parts = refs[:n_img], refs[n_img:-4]
-    student_ref, teacher_ref, wide_ref, lines_ref = refs[-4:]
+    student_ref, teacher_ref, row_ref, lines_ref = refs[-4:]
     count = student_ref.shape[1]
     columns, lines = [], []
     for part, out in ((slice(0, width), student_ref), (slice(width, None), teacher_ref)):
-        left = joined(img_parts, part)
-        more = logits(left, window(cap_parts, 0, count, part), out)
+        more = logits(joined(img_parts, part), window(cap_parts, 0, count, part), out)
         columns, lines = columns + more[0], lines + more[1]
-    lane = lax.broadcasted_iota(jnp.int32, wide_ref.shape, 1)
-    wide = jnp.zeros(wide_ref.shape, jnp.float32)
-    for k, column in enumerate(columns):
-        wide = jnp.where(lane == k, column, wide)
-    wide_ref[...] = wide
+    store_slots(row_ref, lines_of(columns), rows)
     lines_ref[...] = stacked(lines)
 
 
-def tail_kernel(n_img, start, rows, width, wide_ref, lines_ref, *refs):
+def tail_kernel(n_img, start, rows, width, head_ref, lines_ref, *refs):
     img_parts, cap_parts = refs[:n_img], refs[n_img:-5]
     student_ref, teacher_ref, row_ref, col_ref, images = refs[-5:]
     stop = start + student_ref.shape[1]
@@ -168,24 +169,16 @@
         left = joined(img_parts, part)
         if out is student_ref:
             images[...] = left
-        (peak, total), more = logits(left, window(cap_parts, start, stop, part), out)
-        k = len(columns)
-        before_peak, before = wide_ref[:, k : k + 1], wide_ref[:, k + 1 : k + 2]
-        both = jnp.maximum(peak, before_peak)
-        columns += [both, before * jnp.exp(before_peak - both) + total * jnp.exp(peak - both)]
-        lines += more
-    lines = jnp.concatenate([lines_ref[...], stacked(lines)], axis=1)
+        more = logits(left, window(cap_parts, start, stop, part), out)
+        columns, lines = columns + more[0], lines + more[1]
+    store_slots(row_ref, lines_of(columns), rows)
+    store_slots(col_ref, jnp.concatenate([lines_ref[...], stacked(lines)], axis=1), rows)
     row = lax.broadcasted_iota(jnp.int32, (8, LANES), 0)
     lane = lax.broadcasted_iota(jnp.int32, (8, LANES), 1)
-    for ref, values, axes, order in (
-        (row_ref, lines_of(columns), ROW_AXES, ROW_ORDER),
-        (col_ref, lines, COL_AXES, COL_ORDER),
-    ):
+    for ref, axes, order in ((row_ref, ROW_AXES, ROW_ORDER), (col_ref, COL_AXES, COL_ORDER)):
         for s, owner in enumerate(owners(axes, order)):
-            ref[s] = jnp.zeros((8, LANES), jnp.float32)
-            ref[s, :, :rows] = values[:, s * rows : (s + 1) * rows]
-            index = (owner * rows + lane).astype(jnp.float32)
-            ref[s] = jnp.where(row == INDEX, index, ref[s])
+            block = merged(head_ref[s], ref[s]) if ref is row_ref else ref[s]
+            ref[s] = jnp.where(row == INDEX, (owner * rows + lane).astype(jnp.float32), block)
 
 
 def merged(x, y):
@@ -228,7 +221,7 @@
     student_refs, teacher_refs = (refs.pop(0), refs.pop(0)), (refs.pop(0), refs.pop(0))
     blocks = take(refs, plan)
     captions = [refs.pop(0) for _ in range(n_cap)]
-    tile_ref, send_ref, *outs = refs
+    tile_ref, send_ref, first_ref = refs
     total, count = tile_ref.shape
 
     def finish(blocks):
@@ -249,11 +242,8 @@
         tile_ref[at] = grad.astype(jnp.bfloat16)
     send_ref[...] = tile_ref[:, count // 2 :]
     right = joined(captions, slice(0, width))
-    each = len(outs) * rows // lax.axis_size("ilo")
-    step = each + rows
-    for k in range(lax.axis_size("ilo")):
-        part = jnp.dot(tile_ref[k * step + rows : (k + 1) * step], right, preferred_element_type=jnp.float32)
-        spread(part, outs[k * each // rows : (k + 1) * each // rows])
+    part = jnp.dot(tile_ref[total - first_ref.shape[0] :], right, preferred_element_type=jnp.float32)
+    first_ref[...] = part.astype(jnp.bfloat16)
 
 
 def spread(part, outs):
@@ -263,12 +253,12 @@
         start += out.shape[0]
 
 
-def image_kernel(width, step, tile_ref, *refs):
+def image_kernel(width, tile_ref, *refs):
     parts = [ref for ref in refs if ref.dtype == jnp.bfloat16 and ref.shape[1] > width]
     right = joined(parts, slice(0, width))
-    for k, out in enumerate(refs[len(parts) :]):
-        start = k * step
-        spread(jnp.dot(tile_ref[start : start + out.shape[0]], right, preferred_element_type=jnp.float32), [out])
+    outs = refs[len(parts) :]
+    count = sum(out.shape[0] for out in outs)
+    spread(jnp.dot(tile_ref[:count], right, preferred_element_type=jnp.float32), outs)
 
 
 def caption_kernel(tile_ref, tile_other, images, images_other, *outs):
@@ -374,16 +364,16 @@
     skipped = [part for k, part in enumerate(cap) if sum(p.shape[0] for p in cap[: k + 1]) <= head]
     needed = cap[len(skipped) :]
     start = head - sum(part.shape[0] for part in skipped)
-    student, teacher, wide, lines = call(
-        functools.partial(head_kernel, len(img), width),
-        [shape((total, head), f32)] * 2 + [shape((total, LANES), f32), shape((8, head), f32)],
+    student, teacher, row_head, lines = call(
+        functools.partial(head_kernel, len(img), rows, width),
+        [shape((total, head), f32)] * 2 + [row_shape, shape((8, head), f32)],
         img + ready,
         2 * total * head * (width + depth),
     )
     student_tail, teacher_tail, row_stats, col_stats, images = call(
         functools.partial(tail_kernel, len(img), start, rows, width),
         [shape((total, columns - head), f32)] * 2 + [row_shape, col_shape, shape((total, width), bf16)],
-        [wide, lines] + img + needed,
+        [row_head, lines] + img + needed,
         2 * total * (columns - head) * (width + depth),
     )
 
@@ -399,22 +389,27 @@
             blocks[0] = after(blocks[0], images_other)
             stats = call(functools.partial(merge_kernel, plan), [row_shape, col_shape], blocks)
 
-    far_blocks = [(h, c) for h in range(ilo) for c in range(1, chi)]
-    near_blocks = [(h, 0) for h in range(ilo)]
+    image_blocks = [(h, c) for h in range(ilo) for c in range(chi)]
+    caption_blocks = [(h, c) for c in range(clo) for h in range(ihi)]
 
     def pieces(blocks):
         return [shape((rows, width), bf16 if h else f32) for h, _ in blocks]
 
-    tile, tile_send, *image_parts = call(
+    tile, tile_send, image_first = call(
         functools.partial(tile_kernel, plan, len(cap), rows, width),
-        [shape((total, columns), bf16), shape((total, columns // 2), bf16)] + pieces(far_blocks),
+        [shape((total, columns), bf16), shape((total, columns // 2), bf16), shape((rows, width), bf16)],
         [student, student_tail, teacher, teacher_tail] + blocks + cap,
-        2 * total * columns * width // 2,
-    )
-    image_parts = dict(zip(far_blocks, image_parts))
+        2 * rows * columns * width,
+    )
     tile_other = swap(tile_send, "core", 1)
 
-    caption_blocks = [(h, c) for c in range(clo) for h in range(ihi)]
+    image_parts = call(
+        functools.partial(image_kernel, width),
+        pieces(image_blocks)[:-1],
+        [tile] + cap,
+        2 * total * columns * width,
+    )
+    image_parts = dict(zip(image_blocks, list(image_parts) + [image_first]))
     caption_parts = call(
         caption_kernel,
         pieces(caption_blocks),
@@ -434,13 +429,6 @@
 
     image_far = [rounded(hop(image_parts, "ilo", f)) for f in range(1, chi)]
     caption_far = [rounded(hop(caption_parts, "ihi", f)) for f in range(1, clo)]
-    rest = call(
-        functools.partial(image_kernel, width, chi * rows),
-        pieces(near_blocks),
-        [after(tile, image_far[0])] + cap,
-        2 * total * columns * width // chi,
-    )
-    image_parts.update(zip(near_blocks, rest))
     image_terms, caption_terms = hop(image_parts, "ilo", 0), hop(caption_parts, "ihi", 0)
     image_terms += [swap(image_far[f - 1], "chi", f) for f in range(1, chi)]
     caption_terms += [swap(caption_far[f - 1], "clo", f) for f in range(1, clo)]

time: 66.9 us -> 64.4 us (0.963)
  waiting for transfers between devices: 28.6 us -> 26.7 us
  Pallas kernels: 8.28 us -> 6.67 us
  starting transfers between devices: 29 us -> 30 us
    ppermute x22, waiting for transfers between devices: 28.6 us -> 26.7 us  [swap(): return lax.ppermute(value, axis, [(j, j ^ mask) for j in range(size)])]
    pallas_call x11, Pallas kernels: 8.28 us -> 6.67 us  [call(): pl.pallas_call(kernel, out_shape=[out_space(out.shape, out.dtype) for out...]
    ppermute x22, starting transfers between devices: 29 us -> 30 us  [swap(): return lax.ppermute(value, axis, [(j, j ^ mask) for j in range(size)])]
  transfers between devices with their start and end apart: 22 -> 22, of which waited for: 11 -> 9; matrix products, arithmetic and copies ran while one was open for 0% -> 0% of each run, Pallas kernels for 4% -> 4%
where the time goes in v9:
time: 64.4 us; the launch traced here: 64.2 us
  starting transfers between devices  30 us (47%)
  waiting for transfers between devices  26.7 us (41%)
  Pallas kernels  6.67 us (10%)
  between operations  0.76 us (1%)
    ppermute x22, starting transfers between devices, swap(): return lax.ppermute(value, axis, [(j, j ^ mask) for j in range(size)])  30 us
    ppermute x22, waiting for transfers between devices, swap(): return lax.ppermute(value, axis, [(j, j ^ mask) for j in range(size)])  26.7 us
    pallas_call x11, Pallas kernels, call(): pl.pallas_call(kernel, out_shape=[out_space(out.shape, out.dtype) for out...  6.67 us
  transfers between devices with their start and end apart: 22, of which 9 were waited for; matrix products, arithmetic and copies ran while one was open for 0% of the time, Pallas kernels for 4%

profile of v9, /device:TPU:0, one launch (start us, length us, event | category | flops | bytes accessed | tf_op | source)
XLA Modules:
  0.0 64.2 jit_solution(14308138659854724206)
XLA Ops:
  0.6 1.2 %shard_map.59 = (bf16[80,1792]{1,0:T(8,128)(2,1)S(1)}, bf16[80,1792]{1,0:T(8,128)(2,1)S(1)}) custom-call(bf16[80,1024]{1,0:T(8,128)(2,1)} %image_s.1, bf16[80,768]{1,0:T(8,128)(2,1)} %image_t.1, bf16[80,1024]{1,0:T(8,128)(2,1)} %caption_s.1, bf16[80,768]{1,0:T(8,128)(2,1)} %caption_t.1), custom_call_target="tpu_custom_call" | custom-call | bytes 1146880 | tf_op jit(solution)/shard_map/pallas_call | solution.py:294
  1.8 4.1 %collective-permute-start = (bf16[80,1792]{1,0:T(8,128)(2,1)S(1)}, bf16[80,1792]{1,0:T(8,128)(2,1)S(1)}, u32[]{:S(2)}, u32[]{:S(2)}) collective-permute-start(bf16[80,1792]{1,0:T(8,128)(2,1)S(1)} %get-tuple-element.32.refs_0_), channel_id=1, source_target_pairs={{0,2},{2,0},{1,3},{3,1},{4,6},{6,4},{5,7},{7,5},{8,10},{10,8},{9,1... | collective-permute-start | bytes 860168 | tf_op jit(solution)/shard_map/ppermute | solution.py:24
  5.9 1.6 %collective-permute-start.4 = (bf16[80,1792]{1,0:T(8,128)(2,1)S(1)}, bf16[80,1792]{1,0:T(8,128)(2,1)S(1)}, u32[]{:S(2)}, u32[]{:S(2)}) collective-permute-start(bf16[80,1792]{1,0:T(8,128)(2,1)S(1)} %get-tuple-element.35.refs_1_.refs_0_), channel_id=1, source_target_pairs={{0,1},{1,0},{2,3},{3,2},{4,5},{5,4},{6,7},{7,6},{8,9},{9,8},{10,11... | collective-permute-start | bytes 860168 | tf_op jit(solution)/shard_map/ppermute | solution.py:24
  7.5 1.6 %collective-permute-start.1 = (bf16[80,1792]{1,0:T(8,128)(2,1)S(1)}, bf16[80,1792]{1,0:T(8,128)(2,1)S(1)}, u32[]{:S(2)}, u32[]{:S(2)}) collective-permute-start(bf16[80,1792]{1,0:T(8,128)(2,1)S(1)} %get-tuple-element.34), channel_id=1, source_target_pairs={{0,8},{8,0},{1,9},{9,1},{2,10},{10,2},{3,11},{11,3},{4,12},{12,4},... | collective-permute-start | bytes 860168 | tf_op jit(solution)/shard_map/ppermute | solution.py:24
  9.1 1.5 %collective-permute-start.3 = (bf16[80,1792]{1,0:T(8,128)(2,1)S(1)}, bf16[80,1792]{1,0:T(8,128)(2,1)S(1)}, u32[]{:S(2)}, u32[]{:S(2)}) collective-permute-start(bf16[80,1792]{1,0:T(8,128)(2,1)S(1)} %get-tuple-element.36), channel_id=1, source_target_pairs={{0,16},{16,0},{1,17},{17,1},{2,18},{18,2},{3,19},{19,3},{4,20},{20... | collective-permute-start | bytes 860168 | tf_op jit(solution)/shard_map/ppermute | solution.py:24
  10.6 8.4 %collective-permute-done.refs_1_ = bf16[80,1792]{1,0:T(8,128)(2,1)S(1)} collective-permute-done((bf16[80,1792]{1,0:T(8,128)(2,1)S(1)}, bf16[80,1792]{1,0:T(8,128)(2,1)S(1)}, u32[]{:S(2)}, u32[]{:S(2)}) %collective-permute-start) | collective-permute-done | bytes 286752 | tf_op jit(solution)/shard_map/ppermute | solution.py:24
  19.0 1.5 %collective-permute-start.2 = (bf16[80,1792]{1,0:T(8,128)(2,1)S(1)}, bf16[80,1792]{1,0:T(8,128)(2,1)S(1)}, u32[]{:S(2)}, u32[]{:S(2)}) collective-permute-start(bf16[80,1792]{1,0:T(8,128)(2,1)S(1)} %collective-permute-done.refs_1_), channel_id=1, source_target_pairs={{0,8},{8,0},{1,9},{9,1},{2,10},{10,2},{3,11},{11,3},{4,12},{12,4},... | collective-permute-start | bytes 860168 | tf_op jit(solution)/shard_map/ppermute | solution.py:24
  20.5 1.5 %collective-permute-start.5 = (bf16[80,1792]{1,0:T(8,128)(2,1)S(1)}, bf16[80,1792]{1,0:T(8,128)(2,1)S(1)}, u32[]{:S(2)}, u32[]{:S(2)}) collective-permute-start(bf16[80,1792]{1,0:T(8,128)(2,1)S(1)} %collective-permute-done.4.refs_0_), channel_id=1, source_target_pairs={{0,16},{16,0},{1,17},{17,1},{2,18},{18,2},{3,19},{19,3},{4,20},{20... | collective-permute-start | bytes 860168 | tf_op jit(solution)/shard_map/ppermute | solution.py:24
  22.2 4.8 %collective-permute-done.2.refs_3_ = bf16[80,1792]{1,0:T(8,128)(2,1)S(1)} collective-permute-done((bf16[80,1792]{1,0:T(8,128)(2,1)S(1)}, bf16[80,1792]{1,0:T(8,128)(2,1)S(1)}, u32[]{:S(2)}, u32[]{:S(2)}) %collective-permute-start.2) | collective-permute-done | bytes 286752 | tf_op jit(solution)/shard_map/ppermute | solution.py:24
  26.9 1.0 %collective-permute-done.5.refs_1_ = bf16[80,1792]{1,0:T(8,128)(2,1)S(1)} collective-permute-done((bf16[80,1792]{1,0:T(8,128)(2,1)S(1)}, bf16[80,1792]{1,0:T(8,128)(2,1)S(1)}, u32[]{:S(2)}, u32[]{:S(2)}) %collective-permute-start.5) | collective-permute-done | bytes 286752 | tf_op jit(solution)/shard_map/ppermute | solution.py:24
  28.0 1.1 %shard_map.63 = (f32[320,384]{1,0:T(8,128)S(1)}, f32[320,384]{1,0:T(8,128)S(1)}, f32[4,8,128]{2,1,0:T(8,128)S(1)}, f32[8,384]{1,0:T(8,128)S(1)}) custom-call(bf16[80,1792]{1,0:T(8,128)(2,1)S(1)} %get-tuple-element.32.refs_0_, bf16[80,1792]{1,0:T(8,128)(2,1)S(1)} %collective-permute-done.refs_1_, bf16[80,1792]{1,0:T(8,128)(2,1)S(1)} %collective-permute-done.1.refs_2_, ...), custom_call_target="tpu_custom_call" | custom-call | flops 440401920 | bytes 3878912 | tf_op jit(solution)/shard_map/pallas_call | solution.py:294
  29.2 0.8 %collective-permute-done.7.refs_5_.refs_11_.refs_3_ = bf16[160,1792]{1,0:T(8,128)(2,1)S(1)} collective-permute-done((bf16[160,1792]{1,0:T(8,128)(2,1)S(1)}, bf16[160,1792]{1,0:T(8,128)(2,1)S(1)}, u32[]{:S(2)}, u32[]{:S(2)}) %collective-permute-start.7) | collective-permute-done | bytes 573472 | tf_op jit(solution)/shard_map/ppermute | solution.py:24
  30.0 0.9 %shard_map.64 = (f32[320,256]{1,0:T(8,128)S(1)}, f32[320,256]{1,0:T(8,128)S(1)}, f32[4,8,128]{2,1,0:T(8,128)S(1)}, f32[8,8,128]{2,1,0:T(8,128)S(1)}, bf16[320,1024]{1,0:T(8,128)(2,1)S(1)}) custom-call(f32[4,8,128]{2,1,0:T(8,128)S(1)} %get-tuple-element.39.head_ref, f32[8,384]{1,0:T(8,128)S(1)} %get-tuple-element.40.lines_ref, ...), custom_call_target="tpu_custom_call" | custom-call | flops 293601280 | bytes 3682304 | tf_op jit(solution)/shard_map/pallas_call | solution.py:294
  31.1 2.6 %collective-permute-start.12 = (f32[8,8,128]{2,1,0:T(8,128)S(1)}, f32[8,8,128]{2,1,0:T(8,128)S(1)}, u32[]{:S(2)}, u32[]{:S(2)}) collective-permute-start(f32[8,8,128]{2,1,0:T(8,128)S(1)} %get-tuple-element.47.refs_2_), channel_id=1, source_target_pairs={{0,17},{1,16},{16,1},{17,0},{2,19},{3,18},{18,3},{19,2},{4,21},{5,... | collective-permute-start | bytes 98312 | tf_op jit(solution)/shard_map/ppermute | solution.py:24
  33.8 0.5 collective-permute-start.11
  34.6 0.8 %collective-permute-start.9 = (f32[4,8,128]{2,1,0:T(8,128)S(1)}, f32[4,8,128]{2,1,0:T(8,128)S(1)}, u32[]{:S(2)}, u32[]{:S(2)}) collective-permute-start(f32[4,8,128]{2,1,0:T(8,128)S(1)} %get-tuple-element.46.refs_0_), channel_id=1, source_target_pairs={{0,8},{8,0},{1,9},{9,1},{2,10},{10,2},{3,11},{11,3},{4,12},{12,4},... | collective-permute-start | bytes 49160 | tf_op jit(solution)/shard_map/ppermute | solution.py:24
  35.4 3.0 %collective-permute-done.9.refs_1_ = f32[4,8,128]{2,1,0:T(8,128)S(1)} collective-permute-done((f32[4,8,128]{2,1,0:T(8,128)S(1)}, f32[4,8,128]{2,1,0:T(8,128)S(1)}, u32[]{:S(2)}, u32[]{:S(2)}) %collective-permute-start.9) | collective-permute-done | bytes 16416 | tf_op jit(solution)/shard_map/ppermute | solution.py:24
  38.6 3.2 %collective-permute-start.13 = (f32[4,8,128]{2,1,0:T(8,128)S(1)}, f32[4,8,128]{2,1,0:T(8,128)S(1)}, u32[]{:S(2)}, u32[]{:S(2)}) collective-permute-start(f32[4,8,128]{2,1,0:T(8,128)S(1)} %get-tuple-element.48.refs_4_), channel_id=1, source_target_pairs={{0,2},{2,0},{1,3},{3,1},{4,6},{6,4},{5,7},{7,5},{8,10},{10,8},{9,1... | collective-permute-start | bytes 49160 | tf_op jit(solution)/shard_map/ppermute | solution.py:24
  41.8 1.7 %collective-permute-done.13.refs_5_ = f32[4,8,128]{2,1,0:T(8,128)S(1)} collective-permute-done((f32[4,8,128]{2,1,0:T(8,128)S(1)}, f32[4,8,128]{2,1,0:T(8,128)S(1)}, u32[]{:S(2)}, u32[]{:S(2)}) %collective-permute-start.13) | collective-permute-done | bytes 16416 | tf_op jit(solution)/shard_map/ppermute | solution.py:24
  43.5 1.0 %shard_map.66 = (bf16[320,640]{1,0:T(8,128)(2,1)S(1)}, bf16[320,320]{1,0:T(8,128)(2,1)S(1)}, bf16[80,1024]{1,0:T(8,128)(2,1)S(1)}) custom-call(f32[320,384]{1,0:T(8,128)S(1)} %get-tuple-element.38.refs_0_, f32[320,256]{1,0:T(8,128)S(1)} %get-tuple-element.41.refs_1_, f32[320,384]{1,0:T(8,128)S(1)} %get-tuple-element.42.refs_2_, ...), custom_call_target="tpu_custom_call" | custom-call | flops 104857600 | bytes 4808704 | tf_op jit(solution)/shard_map/pallas_call | solution.py:294
  44.6 0.6 collective-permute-start.20
  45.2 0.5 shard_map.68
  45.7 1.6 %collective-permute-start.19 = (bf16[80,1024]{1,0:T(8,128)(2,1)S(1)}, bf16[80,1024]{1,0:T(8,128)(2,1)S(1)}, u32[]{:S(2)}, u32[]{:S(2)}) collective-permute-start(bf16[80,1024]{1,0:T(8,128)(2,1)S(1)} %get-tuple-element.57), channel_id=1, source_target_pairs={{0,8},{8,0},{1,9},{9,1},{2,10},{10,2},{3,11},{11,3},{4,12},{12,4},... | collective-permute-start | bytes 491528 | tf_op jit(solution)/shard_map/ppermute | solution.py:24
  47.3 0.9 %shard_map.67 = (f32[80,1024]{1,0:T(8,128)S(1)}, bf16[80,1024]{1,0:T(8,128)(2,1)S(1)}, f32[80,1024]{1,0:T(8,128)S(1)}, bf16[80,1024]{1,0:T(8,128)(2,1)S(1)}) custom-call(bf16[320,640]{1,0:T(8,128)(2,1)S(1)} %get-tuple-element.50.tile_ref, bf16[320,320]{1,0:T(8,128)(2,1)S(1)} %collective-permute-done.15.tile_other, ...), custom_call_target="tpu_custom_call" | custom-call | flops 419430400 | bytes 2908160 | tf_op jit(solution)/shard_map/pallas_call | solution.py:294
  48.1 1.6 %collective-permute-start.17 = (bf16[80,1024]{1,0:T(8,128)(2,1)S(1)}, bf16[80,1024]{1,0:T(8,128)(2,1)S(1)}, u32[]{:S(2)}, u32[]{:S(2)}) collective-permute-start(bf16[80,1024]{1,0:T(8,128)(2,1)S(1)} %get-tuple-element.55), channel_id=1, source_target_pairs={{0,16},{16,0},{1,17},{17,1},{2,18},{18,2},{3,19},{19,3},{4,20},{20... | collective-permute-start | bytes 491528 | tf_op jit(solution)/shard_map/ppermute | solution.py:24
  49.7 1.9 %collective-permute-done.20 = bf16[80,1024]{1,0:T(8,128)(2,1)S(1)} collective-permute-done((bf16[80,1024]{1,0:T(8,128)(2,1)S(1)}, bf16[80,1024]{1,0:T(8,128)(2,1)S(1)}, u32[]{:S(2)}, u32[]{:S(2)}) %collective-permute-start.20) | collective-permute-done | bytes 163872 | tf_op jit(solution)/shard_map/ppermute | solution.py:24
  51.7 3.0 %collective-permute-start.21 = (bf16[80,1024]{1,0:T(8,128)(2,1)S(1)}, bf16[80,1024]{1,0:T(8,128)(2,1)S(1)}, u32[]{:S(2)}, u32[]{:S(2)}) collective-permute-start(bf16[80,1024]{1,0:T(8,128)(2,1)S(1)} %add_convert_fusion), channel_id=1, source_target_pairs={{0,2},{2,0},{1,3},{3,1},{4,6},{6,4},{5,7},{7,5},{8,10},{10,8},{9,1... | collective-permute-start | bytes 491528 | tf_op jit(solution)/shard_map/ppermute | solution.py:24
  54.7 1.5 %collective-permute-start.16 = (bf16[80,1024]{1,0:T(8,128)(2,1)S(1)}, bf16[80,1024]{1,0:T(8,128)(2,1)S(1)}, u32[]{:S(2)}, u32[]{:S(2)}) collective-permute-start(bf16[80,1024]{1,0:T(8,128)(2,1)S(1)} %get-tuple-element.53), channel_id=1, source_target_pairs={{0,16},{16,0},{1,17},{17,1},{2,18},{18,2},{3,19},{19,3},{4,20},{20... | collective-permute-start | bytes 491528 | tf_op jit(solution)/shard_map/ppermute | solution.py:24
  56.3 1.9 %collective-permute-start.18 = (bf16[80,1024]{1,0:T(8,128)(2,1)S(1)}, bf16[80,1024]{1,0:T(8,128)(2,1)S(1)}, u32[]{:S(2)}, u32[]{:S(2)}) collective-permute-start(bf16[80,1024]{1,0:T(8,128)(2,1)S(1)} %add_convert_fusion.1), channel_id=1, source_target_pairs={{0,1},{1,0},{2,3},{3,2},{4,5},{5,4},{6,7},{7,6},{8,9},{9,8},{10,11... | collective-permute-start | bytes 491528 | tf_op jit(solution)/shard_map/ppermute | solution.py:24
  58.1 3.8 %collective-permute-done.21.refs_5_ = bf16[80,1024]{1,0:T(8,128)(2,1)S(1)} collective-permute-done((bf16[80,1024]{1,0:T(8,128)(2,1)S(1)}, bf16[80,1024]{1,0:T(8,128)(2,1)S(1)}, u32[]{:S(2)}, u32[]{:S(2)}) %collective-permute-start.21) | collective-permute-done | bytes 163872 | tf_op jit(solution)/shard_map/ppermute | solution.py:24
  61.9 1.4 %collective-permute-done.18.refs_2_ = bf16[80,1024]{1,0:T(8,128)(2,1)S(1)} collective-permute-done((bf16[80,1024]{1,0:T(8,128)(2,1)S(1)}, bf16[80,1024]{1,0:T(8,128)(2,1)S(1)}, u32[]{:S(2)}, u32[]{:S(2)}) %collective-permute-start.18) | collective-permute-done | bytes 163872 | tf_op jit(solution)/shard_map/ppermute | solution.py:24
  63.3 0.9 %shard_map.69 = (f32[80,1024]{1,0:T(8,128)}, f32[80,1024]{1,0:T(8,128)}) custom-call(f32[80,1024]{1,0:T(8,128)S(1)} %get-tuple-element.52.refs_0_, bf16[80,1024]{1,0:T(8,128)(2,1)S(1)} %collective-permute-done.16.refs_1_, bf16[80,1024]{1,0:T(8,128)(2,1)S(1)} %collective-permute-done.18.refs_2_, f32[80,1024]{1,0:T(8,128)S(1)} %get-tuple-element.56.refs_3_, ...), custom_call_target="tpu_custom_call" | custom-call | bytes 1966080 | tf_op jit(solution)/shard_map/pallas_call | solution.py:294
  (25 shorter events, 1.1 us)
Async XLA Ops:
  1.8 17.2 %collective-permute-start = (bf16[80,1792]{1,0:T(8,128)(2,1)S(1)}, bf16[80,1792]{1,0:T(8,128)(2,1)S(1)}, u32[]{:S(2)}, u32[]{:S(2)}) collective-permute-start(bf16[80,1792]{1,0:T(8,128)(2,1)S(1)} %get-tuple-element.32.refs_0_), channel_id=1, source_target_pairs={{0,2},{2,0},{1,3},{3,1},{4,6},{6,4},{5,7},{7,5},{8,10},{10,8},{9,1... | collective-permute-start | bytes 860168 | tf_op jit(solution)/shard_map/ppermute | solution.py:24
  5.9 14.6 %collective-permute-start.4 = (bf16[80,1792]{1,0:T(8,128)(2,1)S(1)}, bf16[80,1792]{1,0:T(8,128)(2,1)S(1)}, u32[]{:S(2)}, u32[]{:S(2)}) collective-permute-start(bf16[80,1792]{1,0:T(8,128)(2,1)S(1)} %get-tuple-element.35.refs_1_.refs_0_), channel_id=1, source_target_pairs={{0,1},{1,0},{2,3},{3,2},{4,5},{5,4},{6,7},{7,6},{8,9},{9,8},{10,11... | collective-permute-start | bytes 860168 | tf_op jit(solution)/shard_map/ppermute | solution.py:24
  7.5 14.5 %collective-permute-start.1 = (bf16[80,1792]{1,0:T(8,128)(2,1)S(1)}, bf16[80,1792]{1,0:T(8,128)(2,1)S(1)}, u32[]{:S(2)}, u32[]{:S(2)}) collective-permute-start(bf16[80,1792]{1,0:T(8,128)(2,1)S(1)} %get-tuple-element.34), channel_id=1, source_target_pairs={{0,8},{8,0},{1,9},{9,1},{2,10},{10,2},{3,11},{11,3},{4,12},{12,4},... | collective-permute-start | bytes 860168 | tf_op jit(solution)/shard_map/ppermute | solution.py:24
  9.1 13.0 %collective-permute-start.3 = (bf16[80,1792]{1,0:T(8,128)(2,1)S(1)}, bf16[80,1792]{1,0:T(8,128)(2,1)S(1)}, u32[]{:S(2)}, u32[]{:S(2)}) collective-permute-start(bf16[80,1792]{1,0:T(8,128)(2,1)S(1)} %get-tuple-element.36), channel_id=1, source_target_pairs={{0,16},{16,0},{1,17},{17,1},{2,18},{18,2},{3,19},{19,3},{4,20},{20... | collective-permute-start | bytes 860168 | tf_op jit(solution)/shard_map/ppermute | solution.py:24
  19.0 8.0 %collective-permute-start.2 = (bf16[80,1792]{1,0:T(8,128)(2,1)S(1)}, bf16[80,1792]{1,0:T(8,128)(2,1)S(1)}, u32[]{:S(2)}, u32[]{:S(2)}) collective-permute-start(bf16[80,1792]{1,0:T(8,128)(2,1)S(1)} %collective-permute-done.refs_1_), channel_id=1, source_target_pairs={{0,8},{8,0},{1,9},{9,1},{2,10},{10,2},{3,11},{11,3},{4,12},{12,4},... | collective-permute-start | bytes 860168 | tf_op jit(solution)/shard_map/ppermute | solution.py:24
  20.5 7.4 %collective-permute-start.5 = (bf16[80,1792]{1,0:T(8,128)(2,1)S(1)}, bf16[80,1792]{1,0:T(8,128)(2,1)S(1)}, u32[]{:S(2)}, u32[]{:S(2)}) collective-permute-start(bf16[80,1792]{1,0:T(8,128)(2,1)S(1)} %collective-permute-done.4.refs_0_), channel_id=1, source_target_pairs={{0,16},{16,0},{1,17},{17,1},{2,18},{18,2},{3,19},{19,3},{4,20},{20... | collective-permute-start | bytes 860168 | tf_op jit(solution)/shard_map/ppermute | solution.py:24
  22.1 5.9 %collective-permute-start.6 = (bf16[160,1792]{1,0:T(8,128)(2,1)S(1)}, bf16[160,1792]{1,0:T(8,128)(2,1)S(1)}, u32[]{:S(2)}, u32[]{:S(2)}) collective-permute-start(bf16[160,1792]{1,0:T(8,128)(2,1)S(1)} %shard_map.61.refs_4_.refs_8_.refs_0_), channel_id=1, source_target_pairs={{0,4},{4,0},{1,5},{5,1},{2,6},{6,2},{3,7},{7,3},{8,12},{12,8},{9,1... | collective-permute-start | bytes 1720328 | tf_op jit(solution)/shard_map/ppermute | solution.py:24
  27.9 2.0 %collective-permute-start.7 = (bf16[160,1792]{1,0:T(8,128)(2,1)S(1)}, bf16[160,1792]{1,0:T(8,128)(2,1)S(1)}, u32[]{:S(2)}, u32[]{:S(2)}) collective-permute-start(bf16[160,1792]{1,0:T(8,128)(2,1)S(1)} %shard_map.62.refs_5_.refs_9_.refs_1_), channel_id=1, source_target_pairs={{0,4},{4,0},{1,5},{5,1},{2,6},{6,2},{3,7},{7,3},{8,12},{12,8},{9,1... | collective-permute-start | bytes 1720328 | tf_op jit(solution)/shard_map/ppermute | solution.py:24
  30.9 4.5 %collective-permute-start.8 = (bf16[320,1024]{1,0:T(8,128)(2,1)S(1)}, bf16[320,1024]{1,0:T(8,128)(2,1)S(1)}, u32[]{:S(2)}, u32[]{:S(2)}) collective-permute-start(bf16[320,1024]{1,0:T(8,128)(2,1)S(1)} %get-tuple-element.45.images), channel_id=1, source_target_pairs={{0,4},{4,0},{1,5},{5,1},{2,6},{6,2},{3,7},{7,3},{8,12},{12,8},{9,1... | collective-permute-start | bytes 1966088 | tf_op jit(solution)/shard_map/ppermute | solution.py:24
  31.1 7.2 %collective-permute-start.12 = (f32[8,8,128]{2,1,0:T(8,128)S(1)}, f32[8,8,128]{2,1,0:T(8,128)S(1)}, u32[]{:S(2)}, u32[]{:S(2)}) collective-permute-start(f32[8,8,128]{2,1,0:T(8,128)S(1)} %get-tuple-element.47.refs_2_), channel_id=1, source_target_pairs={{0,17},{1,16},{16,1},{17,0},{2,19},{3,18},{18,3},{19,2},{4,21},{5,... | collective-permute-start | bytes 98312 | tf_op jit(solution)/shard_map/ppermute | solution.py:24
  33.8 4.6 %collective-permute-start.11 = (f32[8,8,128]{2,1,0:T(8,128)S(1)}, f32[8,8,128]{2,1,0:T(8,128)S(1)}, u32[]{:S(2)}, u32[]{:S(2)}) collective-permute-start(f32[8,8,128]{2,1,0:T(8,128)S(1)} %get-tuple-element.47.refs_2_), channel_id=1, source_target_pairs={{0,16},{1,17},{16,0},{17,1},{2,18},{3,19},{18,2},{19,3},{4,20},{5,... | collective-permute-start | bytes 98312 | tf_op jit(solution)/shard_map/ppermute | solution.py:24
  34.3 4.1 %collective-permute-start.10 = (f32[8,8,128]{2,1,0:T(8,128)S(1)}, f32[8,8,128]{2,1,0:T(8,128)S(1)}, u32[]{:S(2)}, u32[]{:S(2)}) collective-permute-start(f32[8,8,128]{2,1,0:T(8,128)S(1)} %get-tuple-element.47.refs_2_), channel_id=1, source_target_pairs={{0,1},{1,0},{16,17},{17,16},{2,3},{3,2},{18,19},{19,18},{4,5},{5,4... | collective-permute-start | bytes 98312 | tf_op jit(solution)/shard_map/ppermute | solution.py:24
  34.6 3.7 %collective-permute-start.9 = (f32[4,8,128]{2,1,0:T(8,128)S(1)}, f32[4,8,128]{2,1,0:T(8,128)S(1)}, u32[]{:S(2)}, u32[]{:S(2)}) collective-permute-start(f32[4,8,128]{2,1,0:T(8,128)S(1)} %get-tuple-element.46.refs_0_), channel_id=1, source_target_pairs={{0,8},{8,0},{1,9},{9,1},{2,10},{10,2},{3,11},{11,3},{4,12},{12,4},... | collective-permute-start | bytes 49160 | tf_op jit(solution)/shard_map/ppermute | solution.py:24
  38.5 5.0 %collective-permute-start.14 = (f32[8,8,128]{2,1,0:T(8,128)S(1)}, f32[8,8,128]{2,1,0:T(8,128)S(1)}, u32[]{:S(2)}, u32[]{:S(2)}) collective-permute-start(f32[8,8,128]{2,1,0:T(8,128)S(1)} %get-tuple-element.49.refs_6_), channel_id=1, source_target_pairs={{0,4},{4,0},{1,5},{5,1},{2,6},{6,2},{3,7},{7,3},{8,12},{12,8},{9,1... | collective-permute-start | bytes 98312 | tf_op jit(solution)/shard_map/ppermute | solution.py:24
  38.6 5.0 %collective-permute-start.13 = (f32[4,8,128]{2,1,0:T(8,128)S(1)}, f32[4,8,128]{2,1,0:T(8,128)S(1)}, u32[]{:S(2)}, u32[]{:S(2)}) collective-permute-start(f32[4,8,128]{2,1,0:T(8,128)S(1)} %get-tuple-element.48.refs_4_), channel_id=1, source_target_pairs={{0,2},{2,0},{1,3},{3,1},{4,6},{6,4},{5,7},{7,5},{8,10},{10,8},{9,1... | collective-permute-start | bytes 49160 | tf_op jit(solution)/shard_map/ppermute | solution.py:24
  44.5 2.8 %collective-permute-start.15 = (bf16[320,320]{1,0:T(8,128)(2,1)S(1)}, bf16[320,320]{1,0:T(8,128)(2,1)S(1)}, u32[]{:S(2)}, u32[]{:S(2)}) collective-permute-start(bf16[320,320]{1,0:T(8,128)(2,1)S(1)} %get-tuple-element.51), channel_id=1, source_target_pairs={{0,4},{4,0},{1,5},{5,1},{2,6},{6,2},{3,7},{7,3},{8,12},{12,8},{9,1... | collective-permute-start | bytes 614408 | tf_op jit(solution)/shard_map/ppermute | solution.py:24
  44.6 7.1 %collective-permute-start.20 = (bf16[80,1024]{1,0:T(8,128)(2,1)S(1)}, bf16[80,1024]{1,0:T(8,128)(2,1)S(1)}, u32[]{:S(2)}, u32[]{:S(2)}) collective-permute-start(bf16[80,1024]{1,0:T(8,128)(2,1)S(1)} %get-tuple-element.59), channel_id=1, source_target_pairs={{0,8},{8,0},{1,9},{9,1},{2,10},{10,2},{3,11},{11,3},{4,12},{12,4},... | collective-permute-start | bytes 491528 | tf_op jit(solution)/shard_map/ppermute | solution.py:24
  45.7 12.4 %collective-permute-start.19 = (bf16[80,1024]{1,0:T(8,128)(2,1)S(1)}, bf16[80,1024]{1,0:T(8,128)(2,1)S(1)}, u32[]{:S(2)}, u32[]{:S(2)}) collective-permute-start(bf16[80,1024]{1,0:T(8,128)(2,1)S(1)} %get-tuple-element.57), channel_id=1, source_target_pairs={{0,8},{8,0},{1,9},{9,1},{2,10},{10,2},{3,11},{11,3},{4,12},{12,4},... | collective-permute-start | bytes 491528 | tf_op jit(solution)/shard_map/ppermute | solution.py:24
  48.1 8.1 %collective-permute-start.17 = (bf16[80,1024]{1,0:T(8,128)(2,1)S(1)}, bf16[80,1024]{1,0:T(8,128)(2,1)S(1)}, u32[]{:S(2)}, u32[]{:S(2)}) collective-permute-start(bf16[80,1024]{1,0:T(8,128)(2,1)S(1)} %get-tuple-element.55), channel_id=1, source_target_pairs={{0,16},{16,0},{1,17},{17,1},{2,18},{18,2},{3,19},{19,3},{4,20},{20... | collective-permute-start | bytes 491528 | tf_op jit(solution)/shard_map/ppermute | solution.py:24
  51.7 10.2 %collective-permute-start.21 = (bf16[80,1024]{1,0:T(8,128)(2,1)S(1)}, bf16[80,1024]{1,0:T(8,128)(2,1)S(1)}, u32[]{:S(2)}, u32[]{:S(2)}) collective-permute-start(bf16[80,1024]{1,0:T(8,128)(2,1)S(1)} %add_convert_fusion), channel_id=1, source_target_pairs={{0,2},{2,0},{1,3},{3,1},{4,6},{6,4},{5,7},{7,5},{8,10},{10,8},{9,1... | collective-permute-start | bytes 491528 | tf_op jit(solution)/shard_map/ppermute | solution.py:24
  54.7 7.2 %collective-permute-start.16 = (bf16[80,1024]{1,0:T(8,128)(2,1)S(1)}, bf16[80,1024]{1,0:T(8,128)(2,1)S(1)}, u32[]{:S(2)}, u32[]{:S(2)}) collective-permute-start(bf16[80,1024]{1,0:T(8,128)(2,1)S(1)} %get-tuple-element.53), channel_id=1, source_target_pairs={{0,16},{16,0},{1,17},{17,1},{2,18},{18,2},{3,19},{19,3},{4,20},{20... | collective-permute-start | bytes 491528 | tf_op jit(solution)/shard_map/ppermute | solution.py:24
  56.3 7.1 %collective-permute-start.18 = (bf16[80,1024]{1,0:T(8,128)(2,1)S(1)}, bf16[80,1024]{1,0:T(8,128)(2,1)S(1)}, u32[]{:S(2)}, u32[]{:S(2)}) collective-permute-start(bf16[80,1024]{1,0:T(8,128)(2,1)S(1)} %add_convert_fusion.1), channel_id=1, source_target_pairs={{0,1},{1,0},{2,3},{3,2},{4,5},{5,4},{6,7},{7,6},{8,9},{9,8},{10,11... | collective-permute-start | bytes 491528 | tf_op jit(solution)/shard_map/ppermute | solution.py:24

commit v10 on v9

--- a/solution.py
+++ b/solution.py
@@ -11,8 +11,8 @@
 logit_gain = 3.0
 ROW_AXES = ("ilo", "chi")
 COL_AXES = ("core", "clo", "ihi")
-ROW_STAGES = (("ilo",), ("chi",))
-COL_STAGES = (("ihi", "clo"), ("core",))
+ROW_STAGES = (("chi",), ("ilo",), ())
+COL_STAGES = (("ihi",), ("clo",), ("core",))
 ROW_ORDER = ("ihi", "ilo", "core", "chi", "clo")
 COL_ORDER = ("chi", "clo", "ihi", "ilo", "core")
 LANES = 128
@@ -385,8 +385,9 @@
             others = partners(names, axes)
             plan.append([distance for _, distance in others])
             blocks += [block] + [swap(block, names, mask) for mask, _ in others]
-        if row_names != ROW_STAGES[-1]:
+        if col_names == COL_STAGES[0]:
             blocks[0] = after(blocks[0], images_other)
+        if col_names != COL_STAGES[-1]:
             stats = call(functools.partial(merge_kernel, plan), [row_shape, col_shape], blocks)
 
     image_blocks = [(h, c) for h in range(ilo) for c in range(chi)]

time: 64.4 us -> 65.4 us (1.016)
  waiting for transfers between devices: 26.7 us -> 34.3 us
  starting transfers between devices: 30 us -> 23.5 us
    ppermute x22 -> x21, waiting for transfers between devices: 26.7 us -> 34.3 us  [swap(): return lax.ppermute(value, axis, [(j, j ^ mask) for j in range(size)])]
    ppermute x22 -> x21, starting transfers between devices: 30 us -> 23.5 us  [swap(): return lax.ppermute(value, axis, [(j, j ^ mask) for j in range(size)])]
    pallas_call x11 -> x12, Pallas kernels: 6.67 us -> 6.68 us  [call(): pl.pallas_call(kernel, out_shape=[out_space(out.shape, out.dtype) for out...]
  transfers between devices with their start and end apart: 22 -> 21, of which waited for: 9 -> 10; matrix products, arithmetic and copies ran while one was open for 0% -> 0% of each run, Pallas kernels for 4% -> 4%
where the time goes in v10:
time: 65.4 us; the launch traced here: 65.3 us
  waiting for transfers between devices  34.3 us (52%)
  starting transfers between devices  23.5 us (36%)
  Pallas kernels  6.68 us (10%)
  between operations  0.75 us (1%)
    ppermute x21, waiting for transfers between devices, swap(): return lax.ppermute(value, axis, [(j, j ^ mask) for j in range(size)])  34.3 us
    ppermute x21, starting transfers between devices, swap(): return lax.ppermute(value, axis, [(j, j ^ mask) for j in range(size)])  23.5 us
    pallas_call x12, Pallas kernels, call(): pl.pallas_call(kernel, out_shape=[out_space(out.shape, out.dtype) for out...  6.68 us
  transfers between devices with their start and end apart: 21, of which 10 were waited for; matrix products, arithmetic and copies ran while one was open for 0% of the time, Pallas kernels for 4%

profile of v10, /device:TPU:0, one launch (start us, length us, event | category | flops | bytes accessed | tf_op | source)
XLA Modules:
  0.0 65.3 jit_solution(11856915488464021211)
XLA Ops:
  0.6 1.2 %shard_map.59 = (bf16[80,1792]{1,0:T(8,128)(2,1)S(1)}, bf16[80,1792]{1,0:T(8,128)(2,1)S(1)}) custom-call(bf16[80,1024]{1,0:T(8,128)(2,1)} %image_s.1, bf16[80,768]{1,0:T(8,128)(2,1)} %image_t.1, bf16[80,1024]{1,0:T(8,128)(2,1)} %caption_s.1, bf16[80,768]{1,0:T(8,128)(2,1)} %caption_t.1), custom_call_target="tpu_custom_call" | custom-call | bytes 1146880 | tf_op jit(solution)/shard_map/pallas_call | solution.py:294
  1.8 4.1 %collective-permute-start = (bf16[80,1792]{1,0:T(8,128)(2,1)S(1)}, bf16[80,1792]{1,0:T(8,128)(2,1)S(1)}, u32[]{:S(2)}, u32[]{:S(2)}) collective-permute-start(bf16[80,1792]{1,0:T(8,128)(2,1)S(1)} %get-tuple-element.34.refs_0_), channel_id=1, source_target_pairs={{0,2},{2,0},{1,3},{3,1},{4,6},{6,4},{5,7},{7,5},{8,10},{10,8},{9,1... | collective-permute-start | bytes 860168 | tf_op jit(solution)/shard_map/ppermute | solution.py:24
  5.9 1.6 %collective-permute-start.4 = (bf16[80,1792]{1,0:T(8,128)(2,1)S(1)}, bf16[80,1792]{1,0:T(8,128)(2,1)S(1)}, u32[]{:S(2)}, u32[]{:S(2)}) collective-permute-start(bf16[80,1792]{1,0:T(8,128)(2,1)S(1)} %get-tuple-element.37.refs_1_.refs_0_), channel_id=1, source_target_pairs={{0,1},{1,0},{2,3},{3,2},{4,5},{5,4},{6,7},{7,6},{8,9},{9,8},{10,11... | collective-permute-start | bytes 860168 | tf_op jit(solution)/shard_map/ppermute | solution.py:24
  7.5 1.6 %collective-permute-start.1 = (bf16[80,1792]{1,0:T(8,128)(2,1)S(1)}, bf16[80,1792]{1,0:T(8,128)(2,1)S(1)}, u32[]{:S(2)}, u32[]{:S(2)}) collective-permute-start(bf16[80,1792]{1,0:T(8,128)(2,1)S(1)} %get-tuple-element.36), channel_id=1, source_target_pairs={{0,8},{8,0},{1,9},{9,1},{2,10},{10,2},{3,11},{11,3},{4,12},{12,4},... | collective-permute-start | bytes 860168 | tf_op jit(solution)/shard_map/ppermute | solution.py:24
  9.1 1.5 %collective-permute-start.3 = (bf16[80,1792]{1,0:T(8,128)(2,1)S(1)}, bf16[80,1792]{1,0:T(8,128)(2,1)S(1)}, u32[]{:S(2)}, u32[]{:S(2)}) collective-permute-start(bf16[80,1792]{1,0:T(8,128)(2,1)S(1)} %get-tuple-element.38), channel_id=1, source_target_pairs={{0,16},{16,0},{1,17},{17,1},{2,18},{18,2},{3,19},{19,3},{4,20},{20... | collective-permute-start | bytes 860168 | tf_op jit(solution)/shard_map/ppermute | solution.py:24
  10.6 8.4 %collective-permute-done.refs_1_ = bf16[80,1792]{1,0:T(8,128)(2,1)S(1)} collective-permute-done((bf16[80,1792]{1,0:T(8,128)(2,1)S(1)}, bf16[80,1792]{1,0:T(8,128)(2,1)S(1)}, u32[]{:S(2)}, u32[]{:S(2)}) %collective-permute-start) | collective-permute-done | bytes 286752 | tf_op jit(solution)/shard_map/ppermute | solution.py:24
  19.0 1.5 %collective-permute-start.2 = (bf16[80,1792]{1,0:T(8,128)(2,1)S(1)}, bf16[80,1792]{1,0:T(8,128)(2,1)S(1)}, u32[]{:S(2)}, u32[]{:S(2)}) collective-permute-start(bf16[80,1792]{1,0:T(8,128)(2,1)S(1)} %collective-permute-done.refs_1_), channel_id=1, source_target_pairs={{0,8},{8,0},{1,9},{9,1},{2,10},{10,2},{3,11},{11,3},{4,12},{12,4},... | collective-permute-start | bytes 860168 | tf_op jit(solution)/shard_map/ppermute | solution.py:24
  20.5 1.5 %collective-permute-start.5 = (bf16[80,1792]{1,0:T(8,128)(2,1)S(1)}, bf16[80,1792]{1,0:T(8,128)(2,1)S(1)}, u32[]{:S(2)}, u32[]{:S(2)}) collective-permute-start(bf16[80,1792]{1,0:T(8,128)(2,1)S(1)} %collective-permute-done.4.refs_0_), channel_id=1, source_target_pairs={{0,16},{16,0},{1,17},{17,1},{2,18},{18,2},{3,19},{19,3},{4,20},{20... | collective-permute-start | bytes 860168 | tf_op jit(solution)/shard_map/ppermute | solution.py:24
  22.2 4.8 %collective-permute-done.2.refs_3_ = bf16[80,1792]{1,0:T(8,128)(2,1)S(1)} collective-permute-done((bf16[80,1792]{1,0:T(8,128)(2,1)S(1)}, bf16[80,1792]{1,0:T(8,128)(2,1)S(1)}, u32[]{:S(2)}, u32[]{:S(2)}) %collective-permute-start.2) | collective-permute-done | bytes 286752 | tf_op jit(solution)/shard_map/ppermute | solution.py:24
  26.9 1.0 %collective-permute-done.5.refs_1_ = bf16[80,1792]{1,0:T(8,128)(2,1)S(1)} collective-permute-done((bf16[80,1792]{1,0:T(8,128)(2,1)S(1)}, bf16[80,1792]{1,0:T(8,128)(2,1)S(1)}, u32[]{:S(2)}, u32[]{:S(2)}) %collective-permute-start.5) | collective-permute-done | bytes 286752 | tf_op jit(solution)/shard_map/ppermute | solution.py:24
  28.0 1.1 %shard_map.63 = (f32[320,384]{1,0:T(8,128)S(1)}, f32[320,384]{1,0:T(8,128)S(1)}, f32[4,8,128]{2,1,0:T(8,128)S(1)}, f32[8,384]{1,0:T(8,128)S(1)}) custom-call(bf16[80,1792]{1,0:T(8,128)(2,1)S(1)} %get-tuple-element.34.refs_0_, bf16[80,1792]{1,0:T(8,128)(2,1)S(1)} %collective-permute-done.refs_1_, bf16[80,1792]{1,0:T(8,128)(2,1)S(1)} %collective-permute-done.1.refs_2_, ...), custom_call_target="tpu_custom_call" | custom-call | flops 440401920 | bytes 3878912 | tf_op jit(solution)/shard_map/pallas_call | solution.py:294
  29.2 0.8 %collective-permute-done.7.refs_5_.refs_10_.refs_3_ = bf16[160,1792]{1,0:T(8,128)(2,1)S(1)} collective-permute-done((bf16[160,1792]{1,0:T(8,128)(2,1)S(1)}, bf16[160,1792]{1,0:T(8,128)(2,1)S(1)}, u32[]{:S(2)}, u32[]{:S(2)}) %collective-permute-start.7) | collective-permute-done | bytes 573472 | tf_op jit(solution)/shard_map/ppermute | solution.py:24
  30.0 0.9 %shard_map.64 = (f32[320,256]{1,0:T(8,128)S(1)}, f32[320,256]{1,0:T(8,128)S(1)}, f32[4,8,128]{2,1,0:T(8,128)S(1)}, f32[8,8,128]{2,1,0:T(8,128)S(1)}, bf16[320,1024]{1,0:T(8,128)(2,1)S(1)}) custom-call(f32[4,8,128]{2,1,0:T(8,128)S(1)} %get-tuple-element.41.head_ref, f32[8,384]{1,0:T(8,128)S(1)} %get-tuple-element.42.lines_ref, ...), custom_call_target="tpu_custom_call" | custom-call | flops 293601280 | bytes 3682304 | tf_op jit(solution)/shard_map/pallas_call | solution.py:294
  31.1 1.5 %collective-permute-start.10 = (f32[8,8,128]{2,1,0:T(8,128)S(1)}, f32[8,8,128]{2,1,0:T(8,128)S(1)}, u32[]{:S(2)}, u32[]{:S(2)}) collective-permute-start(f32[8,8,128]{2,1,0:T(8,128)S(1)} %get-tuple-element.49.refs_2_), channel_id=1, source_target_pairs={{0,16},{16,0},{1,17},{17,1},{2,18},{18,2},{3,19},{19,3},{4,20},{20... | collective-permute-start | bytes 98312 | tf_op jit(solution)/shard_map/ppermute | solution.py:24
  32.7 0.4 collective-permute-start.9
  33.1 4.2 %collective-permute-done.9.refs_1_ = f32[4,8,128]{2,1,0:T(8,128)S(1)} collective-permute-done((f32[4,8,128]{2,1,0:T(8,128)S(1)}, f32[4,8,128]{2,1,0:T(8,128)S(1)}, u32[]{:S(2)}, u32[]{:S(2)}) %collective-permute-start.9) | collective-permute-done | bytes 16416 | tf_op jit(solution)/shard_map/ppermute | solution.py:24
  37.3 2.2 %collective-permute-start.12 = (f32[8,8,128]{2,1,0:T(8,128)S(1)}, f32[8,8,128]{2,1,0:T(8,128)S(1)}, u32[]{:S(2)}, u32[]{:S(2)}) collective-permute-start(f32[8,8,128]{2,1,0:T(8,128)S(1)} %get-tuple-element.51.refs_2_), channel_id=1, source_target_pairs={{0,1},{1,0},{2,3},{3,2},{4,5},{5,4},{6,7},{7,6},{8,9},{9,8},{10,11... | collective-permute-start | bytes 98312 | tf_op jit(solution)/shard_map/ppermute | solution.py:24
  39.5 0.5 collective-permute-start.11
  40.1 3.2 %collective-permute-done.11.refs_1_ = f32[4,8,128]{2,1,0:T(8,128)S(1)} collective-permute-done((f32[4,8,128]{2,1,0:T(8,128)S(1)}, f32[4,8,128]{2,1,0:T(8,128)S(1)}, u32[]{:S(2)}, u32[]{:S(2)}) %collective-permute-start.11) | collective-permute-done | bytes 16416 | tf_op jit(solution)/shard_map/ppermute | solution.py:24
  43.4 1.2 %collective-permute-done.13.refs_6_ = f32[8,8,128]{2,1,0:T(8,128)S(1)} collective-permute-done((f32[8,8,128]{2,1,0:T(8,128)S(1)}, f32[8,8,128]{2,1,0:T(8,128)S(1)}, u32[]{:S(2)}, u32[]{:S(2)}) %collective-permute-start.13) | collective-permute-done | bytes 32800 | tf_op jit(solution)/shard_map/ppermute | solution.py:24
  44.6 1.0 %shard_map.67 = (bf16[320,640]{1,0:T(8,128)(2,1)S(1)}, bf16[320,320]{1,0:T(8,128)(2,1)S(1)}, bf16[80,1024]{1,0:T(8,128)(2,1)S(1)}) custom-call(f32[320,384]{1,0:T(8,128)S(1)} %get-tuple-element.40.refs_0_, f32[320,256]{1,0:T(8,128)S(1)} %get-tuple-element.43.refs_1_, f32[320,384]{1,0:T(8,128)S(1)} %get-tuple-element.44.refs_2_, ...), custom_call_target="tpu_custom_call" | custom-call | flops 104857600 | bytes 4792320 | tf_op jit(solution)/shard_map/pallas_call | solution.py:294
  45.8 0.5 collective-permute-start.19
  46.3 0.5 shard_map.69
  46.9 1.6 %collective-permute-start.18 = (bf16[80,1024]{1,0:T(8,128)(2,1)S(1)}, bf16[80,1024]{1,0:T(8,128)(2,1)S(1)}, u32[]{:S(2)}, u32[]{:S(2)}) collective-permute-start(bf16[80,1024]{1,0:T(8,128)(2,1)S(1)} %get-tuple-element.61), channel_id=1, source_target_pairs={{0,8},{8,0},{1,9},{9,1},{2,10},{10,2},{3,11},{11,3},{4,12},{12,4},... | collective-permute-start | bytes 491528 | tf_op jit(solution)/shard_map/ppermute | solution.py:24
  48.4 0.9 %shard_map.68 = (f32[80,1024]{1,0:T(8,128)S(1)}, bf16[80,1024]{1,0:T(8,128)(2,1)S(1)}, f32[80,1024]{1,0:T(8,128)S(1)}, bf16[80,1024]{1,0:T(8,128)(2,1)S(1)}) custom-call(bf16[320,640]{1,0:T(8,128)(2,1)S(1)} %get-tuple-element.54.tile_ref, bf16[320,320]{1,0:T(8,128)(2,1)S(1)} %collective-permute-done.14.tile_other, ...), custom_call_target="tpu_custom_call" | custom-call | flops 419430400 | bytes 2908160 | tf_op jit(solution)/shard_map/pallas_call | solution.py:294
  49.3 0.6 collective-permute-start.16
  49.9 2.9 %collective-permute-done.19 = bf16[80,1024]{1,0:T(8,128)(2,1)S(1)} collective-permute-done((bf16[80,1024]{1,0:T(8,128)(2,1)S(1)}, bf16[80,1024]{1,0:T(8,128)(2,1)S(1)}, u32[]{:S(2)}, u32[]{:S(2)}) %collective-permute-start.19) | collective-permute-done | bytes 163872 | tf_op jit(solution)/shard_map/ppermute | solution.py:24
  52.8 3.0 %collective-permute-start.20 = (bf16[80,1024]{1,0:T(8,128)(2,1)S(1)}, bf16[80,1024]{1,0:T(8,128)(2,1)S(1)}, u32[]{:S(2)}, u32[]{:S(2)}) collective-permute-start(bf16[80,1024]{1,0:T(8,128)(2,1)S(1)} %add_convert_fusion), channel_id=1, source_target_pairs={{0,2},{2,0},{1,3},{3,1},{4,6},{6,4},{5,7},{7,5},{8,10},{10,8},{9,1... | collective-permute-start | bytes 491528 | tf_op jit(solution)/shard_map/ppermute | solution.py:24
  55.8 0.5 collective-permute-start.15
  56.6 5.8 %collective-permute-done.20.refs_5_ = bf16[80,1024]{1,0:T(8,128)(2,1)S(1)} collective-permute-done((bf16[80,1024]{1,0:T(8,128)(2,1)S(1)}, bf16[80,1024]{1,0:T(8,128)(2,1)S(1)}, u32[]{:S(2)}, u32[]{:S(2)}) %collective-permute-start.20) | collective-permute-done | bytes 163872 | tf_op jit(solution)/shard_map/ppermute | solution.py:24
  62.4 2.0 %collective-permute-done.17.refs_2_ = bf16[80,1024]{1,0:T(8,128)(2,1)S(1)} collective-permute-done((bf16[80,1024]{1,0:T(8,128)(2,1)S(1)}, bf16[80,1024]{1,0:T(8,128)(2,1)S(1)}, u32[]{:S(2)}, u32[]{:S(2)}) %collective-permute-start.17) | collective-permute-done | bytes 163872 | tf_op jit(solution)/shard_map/ppermute | solution.py:24
  64.4 0.9 %shard_map.70 = (f32[80,1024]{1,0:T(8,128)}, f32[80,1024]{1,0:T(8,128)}) custom-call(f32[80,1024]{1,0:T(8,128)S(1)} %get-tuple-element.56.refs_0_, bf16[80,1024]{1,0:T(8,128)(2,1)S(1)} %collective-permute-done.15.refs_1_, bf16[80,1024]{1,0:T(8,128)(2,1)S(1)} %collective-permute-done.17.refs_2_, f32[80,1024]{1,0:T(8,128)S(1)} %get-tuple-element.60.refs_3_, ...), custom_call_target="tpu_custom_call" | custom-call | bytes 1966080 | tf_op jit(solution)/shard_map/pallas_call | solution.py:294
  (24 shorter events, 1.2 us)
Async XLA Ops:
  1.8 17.2 %collective-permute-start = (bf16[80,1792]{1,0:T(8,128)(2,1)S(1)}, bf16[80,1792]{1,0:T(8,128)(2,1)S(1)}, u32[]{:S(2)}, u32[]{:S(2)}) collective-permute-start(bf16[80,1792]{1,0:T(8,128)(2,1)S(1)} %get-tuple-element.34.refs_0_), channel_id=1, source_target_pairs={{0,2},{2,0},{1,3},{3,1},{4,6},{6,4},{5,7},{7,5},{8,10},{10,8},{9,1... | collective-permute-start | bytes 860168 | tf_op jit(solution)/shard_map/ppermute | solution.py:24
  5.9 14.6 %collective-permute-start.4 = (bf16[80,1792]{1,0:T(8,128)(2,1)S(1)}, bf16[80,1792]{1,0:T(8,128)(2,1)S(1)}, u32[]{:S(2)}, u32[]{:S(2)}) collective-permute-start(bf16[80,1792]{1,0:T(8,128)(2,1)S(1)} %get-tuple-element.37.refs_1_.refs_0_), channel_id=1, source_target_pairs={{0,1},{1,0},{2,3},{3,2},{4,5},{5,4},{6,7},{7,6},{8,9},{9,8},{10,11... | collective-permute-start | bytes 860168 | tf_op jit(solution)/shard_map/ppermute | solution.py:24
  7.5 14.5 %collective-permute-start.1 = (bf16[80,1792]{1,0:T(8,128)(2,1)S(1)}, bf16[80,1792]{1,0:T(8,128)(2,1)S(1)}, u32[]{:S(2)}, u32[]{:S(2)}) collective-permute-start(bf16[80,1792]{1,0:T(8,128)(2,1)S(1)} %get-tuple-element.36), channel_id=1, source_target_pairs={{0,8},{8,0},{1,9},{9,1},{2,10},{10,2},{3,11},{11,3},{4,12},{12,4},... | collective-permute-start | bytes 860168 | tf_op jit(solution)/shard_map/ppermute | solution.py:24
  9.1 13.0 %collective-permute-start.3 = (bf16[80,1792]{1,0:T(8,128)(2,1)S(1)}, bf16[80,1792]{1,0:T(8,128)(2,1)S(1)}, u32[]{:S(2)}, u32[]{:S(2)}) collective-permute-start(bf16[80,1792]{1,0:T(8,128)(2,1)S(1)} %get-tuple-element.38), channel_id=1, source_target_pairs={{0,16},{16,0},{1,17},{17,1},{2,18},{18,2},{3,19},{19,3},{4,20},{20... | collective-permute-start | bytes 860168 | tf_op jit(solution)/shard_map/ppermute | solution.py:24
  19.0 8.0 %collective-permute-start.2 = (bf16[80,1792]{1,0:T(8,128)(2,1)S(1)}, bf16[80,1792]{1,0:T(8,128)(2,1)S(1)}, u32[]{:S(2)}, u32[]{:S(2)}) collective-permute-start(bf16[80,1792]{1,0:T(8,128)(2,1)S(1)} %collective-permute-done.refs_1_), channel_id=1, source_target_pairs={{0,8},{8,0},{1,9},{9,1},{2,10},{10,2},{3,11},{11,3},{4,12},{12,4},... | collective-permute-start | bytes 860168 | tf_op jit(solution)/shard_map/ppermute | solution.py:24
  20.5 7.4 %collective-permute-start.5 = (bf16[80,1792]{1,0:T(8,128)(2,1)S(1)}, bf16[80,1792]{1,0:T(8,128)(2,1)S(1)}, u32[]{:S(2)}, u32[]{:S(2)}) collective-permute-start(bf16[80,1792]{1,0:T(8,128)(2,1)S(1)} %collective-permute-done.4.refs_0_), channel_id=1, source_target_pairs={{0,16},{16,0},{1,17},{17,1},{2,18},{18,2},{3,19},{19,3},{4,20},{20... | collective-permute-start | bytes 860168 | tf_op jit(solution)/shard_map/ppermute | solution.py:24
  22.1 5.9 %collective-permute-start.6 = (bf16[160,1792]{1,0:T(8,128)(2,1)S(1)}, bf16[160,1792]{1,0:T(8,128)(2,1)S(1)}, u32[]{:S(2)}, u32[]{:S(2)}) collective-permute-start(bf16[160,1792]{1,0:T(8,128)(2,1)S(1)} %shard_map.61.refs_4_.refs_7_.refs_0_), channel_id=1, source_target_pairs={{0,4},{4,0},{1,5},{5,1},{2,6},{6,2},{3,7},{7,3},{8,12},{12,8},{9,1... | collective-permute-start | bytes 1720328 | tf_op jit(solution)/shard_map/ppermute | solution.py:24
  27.9 2.0 %collective-permute-start.7 = (bf16[160,1792]{1,0:T(8,128)(2,1)S(1)}, bf16[160,1792]{1,0:T(8,128)(2,1)S(1)}, u32[]{:S(2)}, u32[]{:S(2)}) collective-permute-start(bf16[160,1792]{1,0:T(8,128)(2,1)S(1)} %shard_map.62.refs_5_.refs_8_.refs_1_), channel_id=1, source_target_pairs={{0,4},{4,0},{1,5},{5,1},{2,6},{6,2},{3,7},{7,3},{8,12},{12,8},{9,1... | collective-permute-start | bytes 1720328 | tf_op jit(solution)/shard_map/ppermute | solution.py:24
  30.9 2.2 %collective-permute-start.8 = (bf16[320,1024]{1,0:T(8,128)(2,1)S(1)}, bf16[320,1024]{1,0:T(8,128)(2,1)S(1)}, u32[]{:S(2)}, u32[]{:S(2)}) collective-permute-start(bf16[320,1024]{1,0:T(8,128)(2,1)S(1)} %get-tuple-element.47.images), channel_id=1, source_target_pairs={{0,4},{4,0},{1,5},{5,1},{2,6},{6,2},{3,7},{7,3},{8,12},{12,8},{9,1... | collective-permute-start | bytes 1966088 | tf_op jit(solution)/shard_map/ppermute | solution.py:24
  31.1 6.2 %collective-permute-start.10 = (f32[8,8,128]{2,1,0:T(8,128)S(1)}, f32[8,8,128]{2,1,0:T(8,128)S(1)}, u32[]{:S(2)}, u32[]{:S(2)}) collective-permute-start(f32[8,8,128]{2,1,0:T(8,128)S(1)} %get-tuple-element.49.refs_2_), channel_id=1, source_target_pairs={{0,16},{16,0},{1,17},{17,1},{2,18},{18,2},{3,19},{19,3},{4,20},{20... | collective-permute-start | bytes 98312 | tf_op jit(solution)/shard_map/ppermute | solution.py:24
  32.7 4.6 %collective-permute-start.9 = (f32[4,8,128]{2,1,0:T(8,128)S(1)}, f32[4,8,128]{2,1,0:T(8,128)S(1)}, u32[]{:S(2)}, u32[]{:S(2)}) collective-permute-start(f32[4,8,128]{2,1,0:T(8,128)S(1)} %get-tuple-element.48.refs_0_), channel_id=1, source_target_pairs={{0,2},{2,0},{1,3},{3,1},{4,6},{6,4},{5,7},{7,5},{8,10},{10,8},{9,1... | collective-permute-start | bytes 49160 | tf_op jit(solution)/shard_map/ppermute | solution.py:24
  37.3 5.9 %collective-permute-start.12 = (f32[8,8,128]{2,1,0:T(8,128)S(1)}, f32[8,8,128]{2,1,0:T(8,128)S(1)}, u32[]{:S(2)}, u32[]{:S(2)}) collective-permute-start(f32[8,8,128]{2,1,0:T(8,128)S(1)} %get-tuple-element.51.refs_2_), channel_id=1, source_target_pairs={{0,1},{1,0},{2,3},{3,2},{4,5},{5,4},{6,7},{7,6},{8,9},{9,8},{10,11... | collective-permute-start | bytes 98312 | tf_op jit(solution)/shard_map/ppermute | solution.py:24
  39.5 3.7 %collective-permute-start.11 = (f32[4,8,128]{2,1,0:T(8,128)S(1)}, f32[4,8,128]{2,1,0:T(8,128)S(1)}, u32[]{:S(2)}, u32[]{:S(2)}) collective-permute-start(f32[4,8,128]{2,1,0:T(8,128)S(1)} %get-tuple-element.50.refs_0_), channel_id=1, source_target_pairs={{0,8},{8,0},{1,9},{9,1},{2,10},{10,2},{3,11},{11,3},{4,12},{12,4},... | collective-permute-start | bytes 49160 | tf_op jit(solution)/shard_map/ppermute | solution.py:24
  43.3 1.3 %collective-permute-start.13 = (f32[8,8,128]{2,1,0:T(8,128)S(1)}, f32[8,8,128]{2,1,0:T(8,128)S(1)}, u32[]{:S(2)}, u32[]{:S(2)}) collective-permute-start(f32[8,8,128]{2,1,0:T(8,128)S(1)} %get-tuple-element.53.refs_5_), channel_id=1, source_target_pairs={{0,4},{4,0},{1,5},{5,1},{2,6},{6,2},{3,7},{7,3},{8,12},{12,8},{9,1... | collective-permute-start | bytes 98312 | tf_op jit(solution)/shard_map/ppermute | solution.py:24
  45.6 2.9 %collective-permute-start.14 = (bf16[320,320]{1,0:T(8,128)(2,1)S(1)}, bf16[320,320]{1,0:T(8,128)(2,1)S(1)}, u32[]{:S(2)}, u32[]{:S(2)}) collective-permute-start(bf16[320,320]{1,0:T(8,128)(2,1)S(1)} %get-tuple-element.55), channel_id=1, source_target_pairs={{0,4},{4,0},{1,5},{5,1},{2,6},{6,2},{3,7},{7,3},{8,12},{12,8},{9,1... | collective-permute-start | bytes 614408 | tf_op jit(solution)/shard_map/ppermute | solution.py:24
  45.8 7.0 %collective-permute-start.19 = (bf16[80,1024]{1,0:T(8,128)(2,1)S(1)}, bf16[80,1024]{1,0:T(8,128)(2,1)S(1)}, u32[]{:S(2)}, u32[]{:S(2)}) collective-permute-start(bf16[80,1024]{1,0:T(8,128)(2,1)S(1)} %get-tuple-element.63), channel_id=1, source_target_pairs={{0,8},{8,0},{1,9},{9,1},{2,10},{10,2},{3,11},{11,3},{4,12},{12,4},... | collective-permute-start | bytes 491528 | tf_op jit(solution)/shard_map/ppermute | solution.py:24
  46.9 9.7 %collective-permute-start.18 = (bf16[80,1024]{1,0:T(8,128)(2,1)S(1)}, bf16[80,1024]{1,0:T(8,128)(2,1)S(1)}, u32[]{:S(2)}, u32[]{:S(2)}) collective-permute-start(bf16[80,1024]{1,0:T(8,128)(2,1)S(1)} %get-tuple-element.61), channel_id=1, source_target_pairs={{0,8},{8,0},{1,9},{9,1},{2,10},{10,2},{3,11},{11,3},{4,12},{12,4},... | collective-permute-start | bytes 491528 | tf_op jit(solution)/shard_map/ppermute | solution.py:24
  49.3 7.0 %collective-permute-start.16 = (bf16[80,1024]{1,0:T(8,128)(2,1)S(1)}, bf16[80,1024]{1,0:T(8,128)(2,1)S(1)}, u32[]{:S(2)}, u32[]{:S(2)}) collective-permute-start(bf16[80,1024]{1,0:T(8,128)(2,1)S(1)} %get-tuple-element.59), channel_id=1, source_target_pairs={{0,16},{16,0},{1,17},{17,1},{2,18},{18,2},{3,19},{19,3},{4,20},{20... | collective-permute-start | bytes 491528 | tf_op jit(solution)/shard_map/ppermute | solution.py:24
  52.8 9.6 %collective-permute-start.20 = (bf16[80,1024]{1,0:T(8,128)(2,1)S(1)}, bf16[80,1024]{1,0:T(8,128)(2,1)S(1)}, u32[]{:S(2)}, u32[]{:S(2)}) collective-permute-start(bf16[80,1024]{1,0:T(8,128)(2,1)S(1)} %add_convert_fusion), channel_id=1, source_target_pairs={{0,2},{2,0},{1,3},{3,1},{4,6},{6,4},{5,7},{7,5},{8,10},{10,8},{9,1... | collective-permute-start | bytes 491528 | tf_op jit(solution)/shard_map/ppermute | solution.py:24
  55.8 6.6 %collective-permute-start.15 = (bf16[80,1024]{1,0:T(8,128)(2,1)S(1)}, bf16[80,1024]{1,0:T(8,128)(2,1)S(1)}, u32[]{:S(2)}, u32[]{:S(2)}) collective-permute-start(bf16[80,1024]{1,0:T(8,128)(2,1)S(1)} %get-tuple-element.57), channel_id=1, source_target_pairs={{0,16},{16,0},{1,17},{17,1},{2,18},{18,2},{3,19},{19,3},{4,20},{20... | collective-permute-start | bytes 491528 | tf_op jit(solution)/shard_map/ppermute | solution.py:24
  56.4 8.0 %collective-permute-start.17 = (bf16[80,1024]{1,0:T(8,128)(2,1)S(1)}, bf16[80,1024]{1,0:T(8,128)(2,1)S(1)}, u32[]{:S(2)}, u32[]{:S(2)}) collective-permute-start(bf16[80,1024]{1,0:T(8,128)(2,1)S(1)} %add_convert_fusion.1), channel_id=1, source_target_pairs={{0,1},{1,0},{2,3},{3,2},{4,5},{5,4},{6,7},{7,6},{8,9},{9,8},{10,11... | collective-permute-start | bytes 491528 | tf_op jit(solution)/shard_map/ppermute | solution.py:24

commit v11 on v9

--- a/solution.py
+++ b/solution.py
@@ -11,7 +11,7 @@
 logit_gain = 3.0
 ROW_AXES = ("ilo", "chi")
 COL_AXES = ("core", "clo", "ihi")
-ROW_STAGES = (("ilo",), ("chi",))
+ROW_STAGES = (("chi",), ("ilo",))
 COL_STAGES = (("ihi", "clo"), ("core",))
 ROW_ORDER = ("ihi", "ilo", "core", "chi", "clo")
 COL_ORDER = ("chi", "clo", "ihi", "ilo", "core")
@@ -269,20 +269,15 @@
     spread(part, outs)
 
 
-def sum_kernel(counts, *refs):
-    refs = list(refs)
-    terms = [[refs.pop(0) for _ in range(count)] for count in counts]
-    outs, held, sems = refs[: len(counts)], refs[len(counts) : -1], refs[-1]
-    copies = []
-    for k, (group, out, here) in enumerate(zip(terms, outs, held)):
-        total = group[0][...]
-        for term in group[1:]:
-            total = total + term[...].astype(jnp.float32)
-        here[...] = total
-        copies.append(pltpu.make_async_copy(here, out, sems.at[k]))
-        copies[-1].start()
-    for copy in copies:
-        copy.wait()
+def sum_kernel(*refs):
+    *terms, out, held, sem = refs
+    total = terms[0][...]
+    for term in terms[1:]:
+        total = total + term[...].astype(jnp.float32)
+    held[...] = total
+    copy = pltpu.make_async_copy(held, out, sem)
+    copy.start()
+    copy.wait()
 
 
 VMEM, HBM = pltpu.VMEM, pltpu.HBM
@@ -432,15 +427,17 @@
     image_terms, caption_terms = hop(image_parts, "ilo", 0), hop(caption_parts, "ihi", 0)
     image_terms += [swap(image_far[f - 1], "chi", f) for f in range(1, chi)]
     caption_terms += [swap(caption_far[f - 1], "clo", f) for f in range(1, clo)]
-    out = shape((rows, width), f32)
-    caption_grad, image_grad = call(
-        functools.partial(sum_kernel, (len(caption_terms), len(image_terms))),
-        [out, out],
-        caption_terms + image_terms,
-        scratch=[pltpu.VMEM((rows, width), f32)] * 2 + [dma((2,))],
-        out_space=HBM,
-    )
-    return (image_grad, caption_grad)
+
+    def total_of(terms):
+        return call(
+            sum_kernel,
+            [shape((rows, width), f32)],
+            terms,
+            scratch=[pltpu.VMEM((rows, width), f32), dma],
+            out_space=HBM,
+        )[0]
+
+    return (total_of(image_terms), total_of(caption_terms))
 
 
 def split(count):

time: 64.4 us -> 64 us (level)
  waiting for transfers between devices: 26.7 us -> 25.9 us
  Pallas kernels: 6.67 us -> 7.33 us
    ppermute x22, waiting for transfers between devices: 26.7 us -> 25.9 us  [swap(): return lax.ppermute(value, axis, [(j, j ^ mask) for j in range(size)])]
    pallas_call x11 -> x12, Pallas kernels: 6.67 us -> 7.33 us  [call(): pl.pallas_call(kernel, out_shape=[out_space(out.shape, out.dtype) for out...]
  transfers between devices with their start and end apart: 22 -> 22, of which waited for: 9 -> 9; matrix products, arithmetic and copies ran while one was open for 0% -> 0% of each run, Pallas kernels for 4% -> 5%
where the time goes in v11:
time: 64 us; the launch traced here: 63.9 us
  starting transfers between devices  29.8 us (47%)
  waiting for transfers between devices  25.9 us (40%)
  Pallas kernels  7.33 us (11%)
  between operations  0.77 us (1%)
    ppermute x22, starting transfers between devices, swap(): return lax.ppermute(value, axis, [(j, j ^ mask) for j in range(size)])  29.8 us
    ppermute x22, waiting for transfers between devices, swap(): return lax.ppermute(value, axis, [(j, j ^ mask) for j in range(size)])  25.9 us
    pallas_call x12, Pallas kernels, call(): pl.pallas_call(kernel, out_shape=[out_space(out.shape, out.dtype) for out...  7.33 us
  transfers between devices with their start and end apart: 22, of which 9 were waited for; matrix products, arithmetic and copies ran while one was open for 0% of the time, Pallas kernels for 5%

profile of v11, /device:TPU:0, one launch (start us, length us, event | category | flops | bytes accessed | tf_op | source)
XLA Modules:
  0.0 63.9 jit_solution(10674856432569361082)
XLA Ops:
  0.6 1.2 %shard_map.59 = (bf16[80,1792]{1,0:T(8,128)(2,1)S(1)}, bf16[80,1792]{1,0:T(8,128)(2,1)S(1)}) custom-call(bf16[80,1024]{1,0:T(8,128)(2,1)} %image_s.1, bf16[80,768]{1,0:T(8,128)(2,1)} %image_t.1, bf16[80,1024]{1,0:T(8,128)(2,1)} %caption_s.1, bf16[80,768]{1,0:T(8,128)(2,1)} %caption_t.1), custom_call_target="tpu_custom_call" | custom-call | bytes 1146880 | tf_op jit(solution)/shard_map/pallas_call | solution.py:289
  1.8 4.1 %collective-permute-start = (bf16[80,1792]{1,0:T(8,128)(2,1)S(1)}, bf16[80,1792]{1,0:T(8,128)(2,1)S(1)}, u32[]{:S(2)}, u32[]{:S(2)}) collective-permute-start(bf16[80,1792]{1,0:T(8,128)(2,1)S(1)} %get-tuple-element.30.refs_0_), channel_id=1, source_target_pairs={{0,2},{2,0},{1,3},{3,1},{4,6},{6,4},{5,7},{7,5},{8,10},{10,8},{9,1... | collective-permute-start | bytes 860168 | tf_op jit(solution)/shard_map/ppermute | solution.py:24
  5.9 1.6 %collective-permute-start.4 = (bf16[80,1792]{1,0:T(8,128)(2,1)S(1)}, bf16[80,1792]{1,0:T(8,128)(2,1)S(1)}, u32[]{:S(2)}, u32[]{:S(2)}) collective-permute-start(bf16[80,1792]{1,0:T(8,128)(2,1)S(1)} %get-tuple-element.33.refs_1_.refs_0_), channel_id=1, source_target_pairs={{0,1},{1,0},{2,3},{3,2},{4,5},{5,4},{6,7},{7,6},{8,9},{9,8},{10,11... | collective-permute-start | bytes 860168 | tf_op jit(solution)/shard_map/ppermute | solution.py:24
  7.5 1.6 %collective-permute-start.1 = (bf16[80,1792]{1,0:T(8,128)(2,1)S(1)}, bf16[80,1792]{1,0:T(8,128)(2,1)S(1)}, u32[]{:S(2)}, u32[]{:S(2)}) collective-permute-start(bf16[80,1792]{1,0:T(8,128)(2,1)S(1)} %get-tuple-element.32), channel_id=1, source_target_pairs={{0,8},{8,0},{1,9},{9,1},{2,10},{10,2},{3,11},{11,3},{4,12},{12,4},... | collective-permute-start | bytes 860168 | tf_op jit(solution)/shard_map/ppermute | solution.py:24
  9.1 1.5 %collective-permute-start.3 = (bf16[80,1792]{1,0:T(8,128)(2,1)S(1)}, bf16[80,1792]{1,0:T(8,128)(2,1)S(1)}, u32[]{:S(2)}, u32[]{:S(2)}) collective-permute-start(bf16[80,1792]{1,0:T(8,128)(2,1)S(1)} %get-tuple-element.34), channel_id=1, source_target_pairs={{0,16},{16,0},{1,17},{17,1},{2,18},{18,2},{3,19},{19,3},{4,20},{20... | collective-permute-start | bytes 860168 | tf_op jit(solution)/shard_map/ppermute | solution.py:24
  10.6 8.4 %collective-permute-done.refs_1_ = bf16[80,1792]{1,0:T(8,128)(2,1)S(1)} collective-permute-done((bf16[80,1792]{1,0:T(8,128)(2,1)S(1)}, bf16[80,1792]{1,0:T(8,128)(2,1)S(1)}, u32[]{:S(2)}, u32[]{:S(2)}) %collective-permute-start) | collective-permute-done | bytes 286752 | tf_op jit(solution)/shard_map/ppermute | solution.py:24
  19.0 1.5 %collective-permute-start.2 = (bf16[80,1792]{1,0:T(8,128)(2,1)S(1)}, bf16[80,1792]{1,0:T(8,128)(2,1)S(1)}, u32[]{:S(2)}, u32[]{:S(2)}) collective-permute-start(bf16[80,1792]{1,0:T(8,128)(2,1)S(1)} %collective-permute-done.refs_1_), channel_id=1, source_target_pairs={{0,8},{8,0},{1,9},{9,1},{2,10},{10,2},{3,11},{11,3},{4,12},{12,4},... | collective-permute-start | bytes 860168 | tf_op jit(solution)/shard_map/ppermute | solution.py:24
  20.5 1.5 %collective-permute-start.5 = (bf16[80,1792]{1,0:T(8,128)(2,1)S(1)}, bf16[80,1792]{1,0:T(8,128)(2,1)S(1)}, u32[]{:S(2)}, u32[]{:S(2)}) collective-permute-start(bf16[80,1792]{1,0:T(8,128)(2,1)S(1)} %collective-permute-done.4.refs_0_), channel_id=1, source_target_pairs={{0,16},{16,0},{1,17},{17,1},{2,18},{18,2},{3,19},{19,3},{4,20},{20... | collective-permute-start | bytes 860168 | tf_op jit(solution)/shard_map/ppermute | solution.py:24
  22.2 4.8 %collective-permute-done.2.refs_3_ = bf16[80,1792]{1,0:T(8,128)(2,1)S(1)} collective-permute-done((bf16[80,1792]{1,0:T(8,128)(2,1)S(1)}, bf16[80,1792]{1,0:T(8,128)(2,1)S(1)}, u32[]{:S(2)}, u32[]{:S(2)}) %collective-permute-start.2) | collective-permute-done | bytes 286752 | tf_op jit(solution)/shard_map/ppermute | solution.py:24
  26.9 1.0 %collective-permute-done.5.refs_1_ = bf16[80,1792]{1,0:T(8,128)(2,1)S(1)} collective-permute-done((bf16[80,1792]{1,0:T(8,128)(2,1)S(1)}, bf16[80,1792]{1,0:T(8,128)(2,1)S(1)}, u32[]{:S(2)}, u32[]{:S(2)}) %collective-permute-start.5) | collective-permute-done | bytes 286752 | tf_op jit(solution)/shard_map/ppermute | solution.py:24
  28.0 1.1 %shard_map.63 = (f32[320,384]{1,0:T(8,128)S(1)}, f32[320,384]{1,0:T(8,128)S(1)}, f32[4,8,128]{2,1,0:T(8,128)S(1)}, f32[8,384]{1,0:T(8,128)S(1)}) custom-call(bf16[80,1792]{1,0:T(8,128)(2,1)S(1)} %get-tuple-element.30.refs_0_, bf16[80,1792]{1,0:T(8,128)(2,1)S(1)} %collective-permute-done.refs_1_, bf16[80,1792]{1,0:T(8,128)(2,1)S(1)} %collective-permute-done.1.refs_2_, ...), custom_call_target="tpu_custom_call" | custom-call | flops 440401920 | bytes 3878912 | tf_op jit(solution)/shard_map/pallas_call | solution.py:289
  29.2 0.8 %collective-permute-done.7.refs_5_.refs_11_.refs_3_ = bf16[160,1792]{1,0:T(8,128)(2,1)S(1)} collective-permute-done((bf16[160,1792]{1,0:T(8,128)(2,1)S(1)}, bf16[160,1792]{1,0:T(8,128)(2,1)S(1)}, u32[]{:S(2)}, u32[]{:S(2)}) %collective-permute-start.7) | collective-permute-done | bytes 573472 | tf_op jit(solution)/shard_map/ppermute | solution.py:24
  30.0 0.9 %shard_map.64 = (f32[320,256]{1,0:T(8,128)S(1)}, f32[320,256]{1,0:T(8,128)S(1)}, f32[4,8,128]{2,1,0:T(8,128)S(1)}, f32[8,8,128]{2,1,0:T(8,128)S(1)}, bf16[320,1024]{1,0:T(8,128)(2,1)S(1)}) custom-call(f32[4,8,128]{2,1,0:T(8,128)S(1)} %get-tuple-element.37.head_ref, f32[8,384]{1,0:T(8,128)S(1)} %get-tuple-element.38.lines_ref, ...), custom_call_target="tpu_custom_call" | custom-call | flops 293601280 | bytes 3682304 | tf_op jit(solution)/shard_map/pallas_call | solution.py:289
  31.1 2.6 %collective-permute-start.12 = (f32[8,8,128]{2,1,0:T(8,128)S(1)}, f32[8,8,128]{2,1,0:T(8,128)S(1)}, u32[]{:S(2)}, u32[]{:S(2)}) collective-permute-start(f32[8,8,128]{2,1,0:T(8,128)S(1)} %get-tuple-element.45.refs_2_), channel_id=1, source_target_pairs={{0,17},{1,16},{16,1},{17,0},{2,19},{3,18},{18,3},{19,2},{4,21},{5,... | collective-permute-start | bytes 98312 | tf_op jit(solution)/shard_map/ppermute | solution.py:24
  34.6 3.1 %collective-permute-start.9 = (f32[4,8,128]{2,1,0:T(8,128)S(1)}, f32[4,8,128]{2,1,0:T(8,128)S(1)}, u32[]{:S(2)}, u32[]{:S(2)}) collective-permute-start(f32[4,8,128]{2,1,0:T(8,128)S(1)} %get-tuple-element.44.refs_0_), channel_id=1, source_target_pairs={{0,2},{2,0},{1,3},{3,1},{4,6},{6,4},{5,7},{7,5},{8,10},{10,8},{9,1... | collective-permute-start | bytes 49160 | tf_op jit(solution)/shard_map/ppermute | solution.py:24
  37.7 1.7 %collective-permute-done.9.refs_1_ = f32[4,8,128]{2,1,0:T(8,128)S(1)} collective-permute-done((f32[4,8,128]{2,1,0:T(8,128)S(1)}, f32[4,8,128]{2,1,0:T(8,128)S(1)}, u32[]{:S(2)}, u32[]{:S(2)}) %collective-permute-start.9) | collective-permute-done | bytes 16416 | tf_op jit(solution)/shard_map/ppermute | solution.py:24
  39.6 0.7 %collective-permute-start.13 = (f32[4,8,128]{2,1,0:T(8,128)S(1)}, f32[4,8,128]{2,1,0:T(8,128)S(1)}, u32[]{:S(2)}, u32[]{:S(2)}) collective-permute-start(f32[4,8,128]{2,1,0:T(8,128)S(1)} %get-tuple-element.46.refs_4_), channel_id=1, source_target_pairs={{0,8},{8,0},{1,9},{9,1},{2,10},{10,2},{3,11},{11,3},{4,12},{12,4},... | collective-permute-start | bytes 49160 | tf_op jit(solution)/shard_map/ppermute | solution.py:24
  40.3 3.1 %collective-permute-done.13.refs_5_ = f32[4,8,128]{2,1,0:T(8,128)S(1)} collective-permute-done((f32[4,8,128]{2,1,0:T(8,128)S(1)}, f32[4,8,128]{2,1,0:T(8,128)S(1)}, u32[]{:S(2)}, u32[]{:S(2)}) %collective-permute-start.13) | collective-permute-done | bytes 16416 | tf_op jit(solution)/shard_map/ppermute | solution.py:24
  43.4 1.0 %shard_map.66 = (bf16[320,640]{1,0:T(8,128)(2,1)S(1)}, bf16[320,320]{1,0:T(8,128)(2,1)S(1)}, bf16[80,1024]{1,0:T(8,128)(2,1)S(1)}) custom-call(f32[320,384]{1,0:T(8,128)S(1)} %get-tuple-element.36.refs_0_, f32[320,256]{1,0:T(8,128)S(1)} %get-tuple-element.39.refs_1_, f32[320,384]{1,0:T(8,128)S(1)} %get-tuple-element.40.refs_2_, ...), custom_call_target="tpu_custom_call" | custom-call | flops 104857600 | bytes 4808704 | tf_op jit(solution)/shard_map/pallas_call | solution.py:289
  44.5 0.7 %collective-permute-start.16 = (bf16[80,1024]{1,0:T(8,128)(2,1)S(1)}, bf16[80,1024]{1,0:T(8,128)(2,1)S(1)}, u32[]{:S(2)}, u32[]{:S(2)}) collective-permute-start(bf16[80,1024]{1,0:T(8,128)(2,1)S(1)} %get-tuple-element.52), channel_id=1, source_target_pairs={{0,8},{8,0},{1,9},{9,1},{2,10},{10,2},{3,11},{11,3},{4,12},{12,4},... | collective-permute-start | bytes 491528 | tf_op jit(solution)/shard_map/ppermute | solution.py:24
  45.1 0.5 shard_map.67
  45.7 1.5 %collective-permute-start.15 = (bf16[80,1024]{1,0:T(8,128)(2,1)S(1)}, bf16[80,1024]{1,0:T(8,128)(2,1)S(1)}, u32[]{:S(2)}, u32[]{:S(2)}) collective-permute-start(bf16[80,1024]{1,0:T(8,128)(2,1)S(1)} %get-tuple-element.50), channel_id=1, source_target_pairs={{0,8},{8,0},{1,9},{9,1},{2,10},{10,2},{3,11},{11,3},{4,12},{12,4},... | collective-permute-start | bytes 491528 | tf_op jit(solution)/shard_map/ppermute | solution.py:24
  47.2 0.9 %shard_map.69 = (f32[80,1024]{1,0:T(8,128)S(1)}, bf16[80,1024]{1,0:T(8,128)(2,1)S(1)}, f32[80,1024]{1,0:T(8,128)S(1)}, bf16[80,1024]{1,0:T(8,128)(2,1)S(1)}) custom-call(bf16[320,640]{1,0:T(8,128)(2,1)S(1)} %get-tuple-element.48.tile_ref, bf16[320,320]{1,0:T(8,128)(2,1)S(1)} %collective-permute-done.18.tile_other, ...), custom_call_target="tpu_custom_call" | custom-call | flops 419430400 | bytes 2908160 | tf_op jit(solution)/shard_map/pallas_call | solution.py:289
  48.0 1.5 %collective-permute-start.20 = (bf16[80,1024]{1,0:T(8,128)(2,1)S(1)}, bf16[80,1024]{1,0:T(8,128)(2,1)S(1)}, u32[]{:S(2)}, u32[]{:S(2)}) collective-permute-start(bf16[80,1024]{1,0:T(8,128)(2,1)S(1)} %get-tuple-element.57), channel_id=1, source_target_pairs={{0,16},{16,0},{1,17},{17,1},{2,18},{18,2},{3,19},{19,3},{4,20},{20... | collective-permute-start | bytes 491528 | tf_op jit(solution)/shard_map/ppermute | solution.py:24
  49.6 2.0 %collective-permute-done.16 = bf16[80,1024]{1,0:T(8,128)(2,1)S(1)} collective-permute-done((bf16[80,1024]{1,0:T(8,128)(2,1)S(1)}, bf16[80,1024]{1,0:T(8,128)(2,1)S(1)}, u32[]{:S(2)}, u32[]{:S(2)}) %collective-permute-start.16) | collective-permute-done | bytes 163872 | tf_op jit(solution)/shard_map/ppermute | solution.py:24
  51.6 3.0 %collective-permute-start.17 = (bf16[80,1024]{1,0:T(8,128)(2,1)S(1)}, bf16[80,1024]{1,0:T(8,128)(2,1)S(1)}, u32[]{:S(2)}, u32[]{:S(2)}) collective-permute-start(bf16[80,1024]{1,0:T(8,128)(2,1)S(1)} %add_convert_fusion.1), channel_id=1, source_target_pairs={{0,2},{2,0},{1,3},{3,1},{4,6},{6,4},{5,7},{7,5},{8,10},{10,8},{9,1... | collective-permute-start | bytes 491528 | tf_op jit(solution)/shard_map/ppermute | solution.py:24
  54.5 1.5 %collective-permute-start.19 = (bf16[80,1024]{1,0:T(8,128)(2,1)S(1)}, bf16[80,1024]{1,0:T(8,128)(2,1)S(1)}, u32[]{:S(2)}, u32[]{:S(2)}) collective-permute-start(bf16[80,1024]{1,0:T(8,128)(2,1)S(1)} %get-tuple-element.55), channel_id=1, source_target_pairs={{0,16},{16,0},{1,17},{17,1},{2,18},{18,2},{3,19},{19,3},{4,20},{20... | collective-permute-start | bytes 491528 | tf_op jit(solution)/shard_map/ppermute | solution.py:24
  56.0 2.1 %collective-permute-start.21 = (bf16[80,1024]{1,0:T(8,128)(2,1)S(1)}, bf16[80,1024]{1,0:T(8,128)(2,1)S(1)}, u32[]{:S(2)}, u32[]{:S(2)}) collective-permute-start(bf16[80,1024]{1,0:T(8,128)(2,1)S(1)} %add_convert_fusion), channel_id=1, source_target_pairs={{0,1},{1,0},{2,3},{3,2},{4,5},{5,4},{6,7},{7,6},{8,9},{9,8},{10,11... | collective-permute-start | bytes 491528 | tf_op jit(solution)/shard_map/ppermute | solution.py:24
  58.1 3.5 %collective-permute-done.17.refs_2_ = bf16[80,1024]{1,0:T(8,128)(2,1)S(1)} collective-permute-done((bf16[80,1024]{1,0:T(8,128)(2,1)S(1)}, bf16[80,1024]{1,0:T(8,128)(2,1)S(1)}, u32[]{:S(2)}, u32[]{:S(2)}) %collective-permute-start.17) | collective-permute-done | bytes 163872 | tf_op jit(solution)/shard_map/ppermute | solution.py:24
  61.7 0.8 %shard_map.68 = f32[80,1024]{1,0:T(8,128)} custom-call(f32[80,1024]{1,0:T(8,128)S(1)} %get-tuple-element.49.refs_0_, bf16[80,1024]{1,0:T(8,128)(2,1)S(1)} %collective-permute-done.15.refs_1_, bf16[80,1024]{1,0:T(8,128)(2,1)S(1)} %collective-permute-done.17.refs_2_), custom_call_target="tpu_custom_call" | custom-call | bytes 983040 | tf_op jit(solution)/shard_map/pallas_call | solution.py:289
  62.5 0.6 collective-permute-done.21.refs_2_
  63.1 0.8 %shard_map.70 = f32[80,1024]{1,0:T(8,128)} custom-call(f32[80,1024]{1,0:T(8,128)S(1)} %get-tuple-element.54.refs_0_, bf16[80,1024]{1,0:T(8,128)(2,1)S(1)} %collective-permute-done.19.refs_1_, bf16[80,1024]{1,0:T(8,128)(2,1)S(1)} %collective-permute-done.21.refs_2_), custom_call_target="tpu_custom_call" | custom-call | bytes 983040 | tf_op jit(solution)/shard_map/pallas_call | solution.py:289
  (26 shorter events, 1.7 us)
Async XLA Ops:
  1.8 17.2 %collective-permute-start = (bf16[80,1792]{1,0:T(8,128)(2,1)S(1)}, bf16[80,1792]{1,0:T(8,128)(2,1)S(1)}, u32[]{:S(2)}, u32[]{:S(2)}) collective-permute-start(bf16[80,1792]{1,0:T(8,128)(2,1)S(1)} %get-tuple-element.30.refs_0_), channel_id=1, source_target_pairs={{0,2},{2,0},{1,3},{3,1},{4,6},{6,4},{5,7},{7,5},{8,10},{10,8},{9,1... | collective-permute-start | bytes 860168 | tf_op jit(solution)/shard_map/ppermute | solution.py:24
  5.9 14.6 %collective-permute-start.4 = (bf16[80,1792]{1,0:T(8,128)(2,1)S(1)}, bf16[80,1792]{1,0:T(8,128)(2,1)S(1)}, u32[]{:S(2)}, u32[]{:S(2)}) collective-permute-start(bf16[80,1792]{1,0:T(8,128)(2,1)S(1)} %get-tuple-element.33.refs_1_.refs_0_), channel_id=1, source_target_pairs={{0,1},{1,0},{2,3},{3,2},{4,5},{5,4},{6,7},{7,6},{8,9},{9,8},{10,11... | collective-permute-start | bytes 860168 | tf_op jit(solution)/shard_map/ppermute | solution.py:24
  7.5 14.5 %collective-permute-start.1 = (bf16[80,1792]{1,0:T(8,128)(2,1)S(1)}, bf16[80,1792]{1,0:T(8,128)(2,1)S(1)}, u32[]{:S(2)}, u32[]{:S(2)}) collective-permute-start(bf16[80,1792]{1,0:T(8,128)(2,1)S(1)} %get-tuple-element.32), channel_id=1, source_target_pairs={{0,8},{8,0},{1,9},{9,1},{2,10},{10,2},{3,11},{11,3},{4,12},{12,4},... | collective-permute-start | bytes 860168 | tf_op jit(solution)/shard_map/ppermute | solution.py:24
  9.1 13.0 %collective-permute-start.3 = (bf16[80,1792]{1,0:T(8,128)(2,1)S(1)}, bf16[80,1792]{1,0:T(8,128)(2,1)S(1)}, u32[]{:S(2)}, u32[]{:S(2)}) collective-permute-start(bf16[80,1792]{1,0:T(8,128)(2,1)S(1)} %get-tuple-element.34), channel_id=1, source_target_pairs={{0,16},{16,0},{1,17},{17,1},{2,18},{18,2},{3,19},{19,3},{4,20},{20... | collective-permute-start | bytes 860168 | tf_op jit(solution)/shard_map/ppermute | solution.py:24
  19.0 8.0 %collective-permute-start.2 = (bf16[80,1792]{1,0:T(8,128)(2,1)S(1)}, bf16[80,1792]{1,0:T(8,128)(2,1)S(1)}, u32[]{:S(2)}, u32[]{:S(2)}) collective-permute-start(bf16[80,1792]{1,0:T(8,128)(2,1)S(1)} %collective-permute-done.refs_1_), channel_id=1, source_target_pairs={{0,8},{8,0},{1,9},{9,1},{2,10},{10,2},{3,11},{11,3},{4,12},{12,4},... | collective-permute-start | bytes 860168 | tf_op jit(solution)/shard_map/ppermute | solution.py:24
  20.5 7.4 %collective-permute-start.5 = (bf16[80,1792]{1,0:T(8,128)(2,1)S(1)}, bf16[80,1792]{1,0:T(8,128)(2,1)S(1)}, u32[]{:S(2)}, u32[]{:S(2)}) collective-permute-start(bf16[80,1792]{1,0:T(8,128)(2,1)S(1)} %collective-permute-done.4.refs_0_), channel_id=1, source_target_pairs={{0,16},{16,0},{1,17},{17,1},{2,18},{18,2},{3,19},{19,3},{4,20},{20... | collective-permute-start | bytes 860168 | tf_op jit(solution)/shard_map/ppermute | solution.py:24
  22.1 5.9 %collective-permute-start.6 = (bf16[160,1792]{1,0:T(8,128)(2,1)S(1)}, bf16[160,1792]{1,0:T(8,128)(2,1)S(1)}, u32[]{:S(2)}, u32[]{:S(2)}) collective-permute-start(bf16[160,1792]{1,0:T(8,128)(2,1)S(1)} %shard_map.61.refs_4_.refs_8_.refs_0_), channel_id=1, source_target_pairs={{0,4},{4,0},{1,5},{5,1},{2,6},{6,2},{3,7},{7,3},{8,12},{12,8},{9,1... | collective-permute-start | bytes 1720328 | tf_op jit(solution)/shard_map/ppermute | solution.py:24
  27.9 2.0 %collective-permute-start.7 = (bf16[160,1792]{1,0:T(8,128)(2,1)S(1)}, bf16[160,1792]{1,0:T(8,128)(2,1)S(1)}, u32[]{:S(2)}, u32[]{:S(2)}) collective-permute-start(bf16[160,1792]{1,0:T(8,128)(2,1)S(1)} %shard_map.62.refs_5_.refs_9_.refs_1_), channel_id=1, source_target_pairs={{0,4},{4,0},{1,5},{5,1},{2,6},{6,2},{3,7},{7,3},{8,12},{12,8},{9,1... | collective-permute-start | bytes 1720328 | tf_op jit(solution)/shard_map/ppermute | solution.py:24
  30.9 6.8 %collective-permute-start.8 = (bf16[320,1024]{1,0:T(8,128)(2,1)S(1)}, bf16[320,1024]{1,0:T(8,128)(2,1)S(1)}, u32[]{:S(2)}, u32[]{:S(2)}) collective-permute-start(bf16[320,1024]{1,0:T(8,128)(2,1)S(1)} %get-tuple-element.43.images), channel_id=1, source_target_pairs={{0,4},{4,0},{1,5},{5,1},{2,6},{6,2},{3,7},{7,3},{8,12},{12,8},{9,1... | collective-permute-start | bytes 1966088 | tf_op jit(solution)/shard_map/ppermute | solution.py:24
  31.1 8.3 %collective-permute-start.12 = (f32[8,8,128]{2,1,0:T(8,128)S(1)}, f32[8,8,128]{2,1,0:T(8,128)S(1)}, u32[]{:S(2)}, u32[]{:S(2)}) collective-permute-start(f32[8,8,128]{2,1,0:T(8,128)S(1)} %get-tuple-element.45.refs_2_), channel_id=1, source_target_pairs={{0,17},{1,16},{16,1},{17,0},{2,19},{3,18},{18,3},{19,2},{4,21},{5,... | collective-permute-start | bytes 98312 | tf_op jit(solution)/shard_map/ppermute | solution.py:24
  33.8 5.7 %collective-permute-start.11 = (f32[8,8,128]{2,1,0:T(8,128)S(1)}, f32[8,8,128]{2,1,0:T(8,128)S(1)}, u32[]{:S(2)}, u32[]{:S(2)}) collective-permute-start(f32[8,8,128]{2,1,0:T(8,128)S(1)} %get-tuple-element.45.refs_2_), channel_id=1, source_target_pairs={{0,16},{1,17},{16,0},{17,1},{2,18},{3,19},{18,2},{19,3},{4,20},{5,... | collective-permute-start | bytes 98312 | tf_op jit(solution)/shard_map/ppermute | solution.py:24
  34.3 5.2 %collective-permute-start.10 = (f32[8,8,128]{2,1,0:T(8,128)S(1)}, f32[8,8,128]{2,1,0:T(8,128)S(1)}, u32[]{:S(2)}, u32[]{:S(2)}) collective-permute-start(f32[8,8,128]{2,1,0:T(8,128)S(1)} %get-tuple-element.45.refs_2_), channel_id=1, source_target_pairs={{0,1},{1,0},{16,17},{17,16},{2,3},{3,2},{18,19},{19,18},{4,5},{5,4... | collective-permute-start | bytes 98312 | tf_op jit(solution)/shard_map/ppermute | solution.py:24
  34.6 4.8 %collective-permute-start.9 = (f32[4,8,128]{2,1,0:T(8,128)S(1)}, f32[4,8,128]{2,1,0:T(8,128)S(1)}, u32[]{:S(2)}, u32[]{:S(2)}) collective-permute-start(f32[4,8,128]{2,1,0:T(8,128)S(1)} %get-tuple-element.44.refs_0_), channel_id=1, source_target_pairs={{0,2},{2,0},{1,3},{3,1},{4,6},{6,4},{5,7},{7,5},{8,10},{10,8},{9,1... | collective-permute-start | bytes 49160 | tf_op jit(solution)/shard_map/ppermute | solution.py:24
  39.5 3.9 %collective-permute-start.14 = (f32[8,8,128]{2,1,0:T(8,128)S(1)}, f32[8,8,128]{2,1,0:T(8,128)S(1)}, u32[]{:S(2)}, u32[]{:S(2)}) collective-permute-start(f32[8,8,128]{2,1,0:T(8,128)S(1)} %get-tuple-element.47.refs_6_), channel_id=1, source_target_pairs={{0,4},{4,0},{1,5},{5,1},{2,6},{6,2},{3,7},{7,3},{8,12},{12,8},{9,1... | collective-permute-start | bytes 98312 | tf_op jit(solution)/shard_map/ppermute | solution.py:24
  39.6 3.8 %collective-permute-start.13 = (f32[4,8,128]{2,1,0:T(8,128)S(1)}, f32[4,8,128]{2,1,0:T(8,128)S(1)}, u32[]{:S(2)}, u32[]{:S(2)}) collective-permute-start(f32[4,8,128]{2,1,0:T(8,128)S(1)} %get-tuple-element.46.refs_4_), channel_id=1, source_target_pairs={{0,8},{8,0},{1,9},{9,1},{2,10},{10,2},{3,11},{11,3},{4,12},{12,4},... | collective-permute-start | bytes 49160 | tf_op jit(solution)/shard_map/ppermute | solution.py:24
  44.4 2.8 %collective-permute-start.18 = (bf16[320,320]{1,0:T(8,128)(2,1)S(1)}, bf16[320,320]{1,0:T(8,128)(2,1)S(1)}, u32[]{:S(2)}, u32[]{:S(2)}) collective-permute-start(bf16[320,320]{1,0:T(8,128)(2,1)S(1)} %get-tuple-element.53), channel_id=1, source_target_pairs={{0,4},{4,0},{1,5},{5,1},{2,6},{6,2},{3,7},{7,3},{8,12},{12,8},{9,1... | collective-permute-start | bytes 614408 | tf_op jit(solution)/shard_map/ppermute | solution.py:24
  44.5 7.1 %collective-permute-start.16 = (bf16[80,1024]{1,0:T(8,128)(2,1)S(1)}, bf16[80,1024]{1,0:T(8,128)(2,1)S(1)}, u32[]{:S(2)}, u32[]{:S(2)}) collective-permute-start(bf16[80,1024]{1,0:T(8,128)(2,1)S(1)} %get-tuple-element.52), channel_id=1, source_target_pairs={{0,8},{8,0},{1,9},{9,1},{2,10},{10,2},{3,11},{11,3},{4,12},{12,4},... | collective-permute-start | bytes 491528 | tf_op jit(solution)/shard_map/ppermute | solution.py:24
  45.7 12.4 %collective-permute-start.15 = (bf16[80,1024]{1,0:T(8,128)(2,1)S(1)}, bf16[80,1024]{1,0:T(8,128)(2,1)S(1)}, u32[]{:S(2)}, u32[]{:S(2)}) collective-permute-start(bf16[80,1024]{1,0:T(8,128)(2,1)S(1)} %get-tuple-element.50), channel_id=1, source_target_pairs={{0,8},{8,0},{1,9},{9,1},{2,10},{10,2},{3,11},{11,3},{4,12},{12,4},... | collective-permute-start | bytes 491528 | tf_op jit(solution)/shard_map/ppermute | solution.py:24
  48.0 8.0 %collective-permute-start.20 = (bf16[80,1024]{1,0:T(8,128)(2,1)S(1)}, bf16[80,1024]{1,0:T(8,128)(2,1)S(1)}, u32[]{:S(2)}, u32[]{:S(2)}) collective-permute-start(bf16[80,1024]{1,0:T(8,128)(2,1)S(1)} %get-tuple-element.57), channel_id=1, source_target_pairs={{0,16},{16,0},{1,17},{17,1},{2,18},{18,2},{3,19},{19,3},{4,20},{20... | collective-permute-start | bytes 491528 | tf_op jit(solution)/shard_map/ppermute | solution.py:24
  51.6 10.1 %collective-permute-start.17 = (bf16[80,1024]{1,0:T(8,128)(2,1)S(1)}, bf16[80,1024]{1,0:T(8,128)(2,1)S(1)}, u32[]{:S(2)}, u32[]{:S(2)}) collective-permute-start(bf16[80,1024]{1,0:T(8,128)(2,1)S(1)} %add_convert_fusion.1), channel_id=1, source_target_pairs={{0,2},{2,0},{1,3},{3,1},{4,6},{6,4},{5,7},{7,5},{8,10},{10,8},{9,1... | collective-permute-start | bytes 491528 | tf_op jit(solution)/shard_map/ppermute | solution.py:24
  54.5 7.9 %collective-permute-start.19 = (bf16[80,1024]{1,0:T(8,128)(2,1)S(1)}, bf16[80,1024]{1,0:T(8,128)(2,1)S(1)}, u32[]{:S(2)}, u32[]{:S(2)}) collective-permute-start(bf16[80,1024]{1,0:T(8,128)(2,1)S(1)} %get-tuple-element.55), channel_id=1, source_target_pairs={{0,16},{16,0},{1,17},{17,1},{2,18},{18,2},{3,19},{19,3},{4,20},{20... | collective-permute-start | bytes 491528 | tf_op jit(solution)/shard_map/ppermute | solution.py:24
  56.0 7.0 %collective-permute-start.21 = (bf16[80,1024]{1,0:T(8,128)(2,1)S(1)}, bf16[80,1024]{1,0:T(8,128)(2,1)S(1)}, u32[]{:S(2)}, u32[]{:S(2)}) collective-permute-start(bf16[80,1024]{1,0:T(8,128)(2,1)S(1)} %add_convert_fusion), channel_id=1, source_target_pairs={{0,1},{1,0},{2,3},{3,2},{4,5},{5,4},{6,7},{7,6},{8,9},{9,8},{10,11... | collective-permute-start | bytes 491528 | tf_op jit(solution)/shard_map/ppermute | solution.py:24

commit v12 on v9

--- a/solution.py
+++ b/solution.py
@@ -429,7 +429,9 @@
 
     image_far = [rounded(hop(image_parts, "ilo", f)) for f in range(1, chi)]
     caption_far = [rounded(hop(caption_parts, "ihi", f)) for f in range(1, clo)]
-    image_terms, caption_terms = hop(image_parts, "ilo", 0), hop(caption_parts, "ihi", 0)
+    image_terms = [image_parts[0, 0]]
+    image_terms += [swap(after(image_parts[h, 0], image_far[0]), "ilo", h) for h in range(1, ilo)]
+    caption_terms = hop(caption_parts, "ihi", 0)
     image_terms += [swap(image_far[f - 1], "chi", f) for f in range(1, chi)]
     caption_terms += [swap(caption_far[f - 1], "clo", f) for f in range(1, clo)]
     out = shape((rows, width), f32)

time: 64.4 us -> 64.6 us (level)
  waiting for transfers between devices: 26.7 us -> 28 us
  starting transfers between devices: 30 us -> 29 us
    ppermute x22, waiting for transfers between devices: 26.7 us -> 28 us  [swap(): return lax.ppermute(value, axis, [(j, j ^ mask) for j in range(size)])]
    ppermute x22, starting transfers between devices: 30 us -> 29 us  [swap(): return lax.ppermute(value, axis, [(j, j ^ mask) for j in range(size)])]
  transfers between devices with their start and end apart: 22 -> 22, of which waited for: 9 -> 11; matrix products, arithmetic and copies ran while one was open for 0% -> 0% of each run, Pallas kernels for 4% -> 4%
where the time goes in v12:
time: 64.6 us; the launch traced here: 64.5 us
  starting transfers between devices  29 us (45%)
  waiting for transfers between devices  28 us (43%)
  Pallas kernels  6.67 us (10%)
  between operations  0.76 us (1%)
    ppermute x22, starting transfers between devices, swap(): return lax.ppermute(value, axis, [(j, j ^ mask) for j in range(size)])  29 us
    ppermute x22, waiting for transfers between devices, swap(): return lax.ppermute(value, axis, [(j, j ^ mask) for j in range(size)])  28 us
    pallas_call x11, Pallas kernels, call(): pl.pallas_call(kernel, out_shape=[out_space(out.shape, out.dtype) for out...  6.67 us
  transfers between devices with their start and end apart: 22, of which 11 were waited for; matrix products, arithmetic and copies ran while one was open for 0% of the time, Pallas kernels for 4%

profile of v12, /device:TPU:0, one launch (start us, length us, event | category | flops | bytes accessed | tf_op | source)
XLA Modules:
  0.0 64.5 jit_solution(9296986092500347314)
XLA Ops:
  0.6 1.2 %shard_map.59 = (bf16[80,1792]{1,0:T(8,128)(2,1)S(1)}, bf16[80,1792]{1,0:T(8,128)(2,1)S(1)}) custom-call(bf16[80,1024]{1,0:T(8,128)(2,1)} %image_s.1, bf16[80,768]{1,0:T(8,128)(2,1)} %image_t.1, bf16[80,1024]{1,0:T(8,128)(2,1)} %caption_s.1, bf16[80,768]{1,0:T(8,128)(2,1)} %caption_t.1), custom_call_target="tpu_custom_call" | custom-call | bytes 1146880 | tf_op jit(solution)/shard_map/pallas_call | solution.py:294
  1.8 4.1 %collective-permute-start = (bf16[80,1792]{1,0:T(8,128)(2,1)S(1)}, bf16[80,1792]{1,0:T(8,128)(2,1)S(1)}, u32[]{:S(2)}, u32[]{:S(2)}) collective-permute-start(bf16[80,1792]{1,0:T(8,128)(2,1)S(1)} %get-tuple-element.33.refs_0_), channel_id=1, source_target_pairs={{0,2},{2,0},{1,3},{3,1},{4,6},{6,4},{5,7},{7,5},{8,10},{10,8},{9,1... | collective-permute-start | bytes 860168 | tf_op jit(solution)/shard_map/ppermute | solution.py:24
  5.9 1.6 %collective-permute-start.4 = (bf16[80,1792]{1,0:T(8,128)(2,1)S(1)}, bf16[80,1792]{1,0:T(8,128)(2,1)S(1)}, u32[]{:S(2)}, u32[]{:S(2)}) collective-permute-start(bf16[80,1792]{1,0:T(8,128)(2,1)S(1)} %get-tuple-element.36.refs_1_.refs_0_), channel_id=1, source_target_pairs={{0,1},{1,0},{2,3},{3,2},{4,5},{5,4},{6,7},{7,6},{8,9},{9,8},{10,11... | collective-permute-start | bytes 860168 | tf_op jit(solution)/shard_map/ppermute | solution.py:24
  7.5 1.6 %collective-permute-start.1 = (bf16[80,1792]{1,0:T(8,128)(2,1)S(1)}, bf16[80,1792]{1,0:T(8,128)(2,1)S(1)}, u32[]{:S(2)}, u32[]{:S(2)}) collective-permute-start(bf16[80,1792]{1,0:T(8,128)(2,1)S(1)} %get-tuple-element.35), channel_id=1, source_target_pairs={{0,8},{8,0},{1,9},{9,1},{2,10},{10,2},{3,11},{11,3},{4,12},{12,4},... | collective-permute-start | bytes 860168 | tf_op jit(solution)/shard_map/ppermute | solution.py:24
  9.1 1.5 %collective-permute-start.3 = (bf16[80,1792]{1,0:T(8,128)(2,1)S(1)}, bf16[80,1792]{1,0:T(8,128)(2,1)S(1)}, u32[]{:S(2)}, u32[]{:S(2)}) collective-permute-start(bf16[80,1792]{1,0:T(8,128)(2,1)S(1)} %get-tuple-element.37), channel_id=1, source_target_pairs={{0,16},{16,0},{1,17},{17,1},{2,18},{18,2},{3,19},{19,3},{4,20},{20... | collective-permute-start | bytes 860168 | tf_op jit(solution)/shard_map/ppermute | solution.py:24
  10.6 8.4 %collective-permute-done.refs_1_ = bf16[80,1792]{1,0:T(8,128)(2,1)S(1)} collective-permute-done((bf16[80,1792]{1,0:T(8,128)(2,1)S(1)}, bf16[80,1792]{1,0:T(8,128)(2,1)S(1)}, u32[]{:S(2)}, u32[]{:S(2)}) %collective-permute-start) | collective-permute-done | bytes 286752 | tf_op jit(solution)/shard_map/ppermute | solution.py:24
  19.0 1.5 %collective-permute-start.2 = (bf16[80,1792]{1,0:T(8,128)(2,1)S(1)}, bf16[80,1792]{1,0:T(8,128)(2,1)S(1)}, u32[]{:S(2)}, u32[]{:S(2)}) collective-permute-start(bf16[80,1792]{1,0:T(8,128)(2,1)S(1)} %collective-permute-done.refs_1_), channel_id=1, source_target_pairs={{0,8},{8,0},{1,9},{9,1},{2,10},{10,2},{3,11},{11,3},{4,12},{12,4},... | collective-permute-start | bytes 860168 | tf_op jit(solution)/shard_map/ppermute | solution.py:24
  20.5 1.5 %collective-permute-start.5 = (bf16[80,1792]{1,0:T(8,128)(2,1)S(1)}, bf16[80,1792]{1,0:T(8,128)(2,1)S(1)}, u32[]{:S(2)}, u32[]{:S(2)}) collective-permute-start(bf16[80,1792]{1,0:T(8,128)(2,1)S(1)} %collective-permute-done.4.refs_0_), channel_id=1, source_target_pairs={{0,16},{16,0},{1,17},{17,1},{2,18},{18,2},{3,19},{19,3},{4,20},{20... | collective-permute-start | bytes 860168 | tf_op jit(solution)/shard_map/ppermute | solution.py:24
  22.2 4.8 %collective-permute-done.2.refs_3_ = bf16[80,1792]{1,0:T(8,128)(2,1)S(1)} collective-permute-done((bf16[80,1792]{1,0:T(8,128)(2,1)S(1)}, bf16[80,1792]{1,0:T(8,128)(2,1)S(1)}, u32[]{:S(2)}, u32[]{:S(2)}) %collective-permute-start.2) | collective-permute-done | bytes 286752 | tf_op jit(solution)/shard_map/ppermute | solution.py:24
  26.9 1.0 %collective-permute-done.5.refs_1_ = bf16[80,1792]{1,0:T(8,128)(2,1)S(1)} collective-permute-done((bf16[80,1792]{1,0:T(8,128)(2,1)S(1)}, bf16[80,1792]{1,0:T(8,128)(2,1)S(1)}, u32[]{:S(2)}, u32[]{:S(2)}) %collective-permute-start.5) | collective-permute-done | bytes 286752 | tf_op jit(solution)/shard_map/ppermute | solution.py:24
  28.0 1.1 %shard_map.63 = (f32[320,384]{1,0:T(8,128)S(1)}, f32[320,384]{1,0:T(8,128)S(1)}, f32[4,8,128]{2,1,0:T(8,128)S(1)}, f32[8,384]{1,0:T(8,128)S(1)}) custom-call(bf16[80,1792]{1,0:T(8,128)(2,1)S(1)} %get-tuple-element.33.refs_0_, bf16[80,1792]{1,0:T(8,128)(2,1)S(1)} %collective-permute-done.refs_1_, bf16[80,1792]{1,0:T(8,128)(2,1)S(1)} %collective-permute-done.1.refs_2_, ...), custom_call_target="tpu_custom_call" | custom-call | flops 440401920 | bytes 3878912 | tf_op jit(solution)/shard_map/pallas_call | solution.py:294
  29.2 0.8 %collective-permute-done.7.refs_5_.refs_11_.refs_3_ = bf16[160,1792]{1,0:T(8,128)(2,1)S(1)} collective-permute-done((bf16[160,1792]{1,0:T(8,128)(2,1)S(1)}, bf16[160,1792]{1,0:T(8,128)(2,1)S(1)}, u32[]{:S(2)}, u32[]{:S(2)}) %collective-permute-start.7) | collective-permute-done | bytes 573472 | tf_op jit(solution)/shard_map/ppermute | solution.py:24
  30.0 0.9 %shard_map.64 = (f32[320,256]{1,0:T(8,128)S(1)}, f32[320,256]{1,0:T(8,128)S(1)}, f32[4,8,128]{2,1,0:T(8,128)S(1)}, f32[8,8,128]{2,1,0:T(8,128)S(1)}, bf16[320,1024]{1,0:T(8,128)(2,1)S(1)}) custom-call(f32[4,8,128]{2,1,0:T(8,128)S(1)} %get-tuple-element.40.head_ref, f32[8,384]{1,0:T(8,128)S(1)} %get-tuple-element.41.lines_ref, ...), custom_call_target="tpu_custom_call" | custom-call | flops 293601280 | bytes 3682304 | tf_op jit(solution)/shard_map/pallas_call | solution.py:294
  31.1 2.6 %collective-permute-start.12 = (f32[8,8,128]{2,1,0:T(8,128)S(1)}, f32[8,8,128]{2,1,0:T(8,128)S(1)}, u32[]{:S(2)}, u32[]{:S(2)}) collective-permute-start(f32[8,8,128]{2,1,0:T(8,128)S(1)} %get-tuple-element.48.refs_2_), channel_id=1, source_target_pairs={{0,17},{1,16},{16,1},{17,0},{2,19},{3,18},{18,3},{19,2},{4,21},{5,... | collective-permute-start | bytes 98312 | tf_op jit(solution)/shard_map/ppermute | solution.py:24
  34.6 0.8 %collective-permute-start.9 = (f32[4,8,128]{2,1,0:T(8,128)S(1)}, f32[4,8,128]{2,1,0:T(8,128)S(1)}, u32[]{:S(2)}, u32[]{:S(2)}) collective-permute-start(f32[4,8,128]{2,1,0:T(8,128)S(1)} %get-tuple-element.47.refs_0_), channel_id=1, source_target_pairs={{0,8},{8,0},{1,9},{9,1},{2,10},{10,2},{3,11},{11,3},{4,12},{12,4},... | collective-permute-start | bytes 49160 | tf_op jit(solution)/shard_map/ppermute | solution.py:24
  35.4 3.0 %collective-permute-done.9.refs_1_ = f32[4,8,128]{2,1,0:T(8,128)S(1)} collective-permute-done((f32[4,8,128]{2,1,0:T(8,128)S(1)}, f32[4,8,128]{2,1,0:T(8,128)S(1)}, u32[]{:S(2)}, u32[]{:S(2)}) %collective-permute-start.9) | collective-permute-done | bytes 16416 | tf_op jit(solution)/shard_map/ppermute | solution.py:24
  38.6 3.2 %collective-permute-start.13 = (f32[4,8,128]{2,1,0:T(8,128)S(1)}, f32[4,8,128]{2,1,0:T(8,128)S(1)}, u32[]{:S(2)}, u32[]{:S(2)}) collective-permute-start(f32[4,8,128]{2,1,0:T(8,128)S(1)} %get-tuple-element.49.refs_4_), channel_id=1, source_target_pairs={{0,2},{2,0},{1,3},{3,1},{4,6},{6,4},{5,7},{7,5},{8,10},{10,8},{9,1... | collective-permute-start | bytes 49160 | tf_op jit(solution)/shard_map/ppermute | solution.py:24
  41.8 1.7 %collective-permute-done.13.refs_5_ = f32[4,8,128]{2,1,0:T(8,128)S(1)} collective-permute-done((f32[4,8,128]{2,1,0:T(8,128)S(1)}, f32[4,8,128]{2,1,0:T(8,128)S(1)}, u32[]{:S(2)}, u32[]{:S(2)}) %collective-permute-start.13) | collective-permute-done | bytes 16416 | tf_op jit(solution)/shard_map/ppermute | solution.py:24
  43.5 1.0 %shard_map.66 = (bf16[320,640]{1,0:T(8,128)(2,1)S(1)}, bf16[320,320]{1,0:T(8,128)(2,1)S(1)}, bf16[80,1024]{1,0:T(8,128)(2,1)S(1)}) custom-call(f32[320,384]{1,0:T(8,128)S(1)} %get-tuple-element.39.refs_0_, f32[320,256]{1,0:T(8,128)S(1)} %get-tuple-element.42.refs_1_, f32[320,384]{1,0:T(8,128)S(1)} %get-tuple-element.43.refs_2_, ...), custom_call_target="tpu_custom_call" | custom-call | flops 104857600 | bytes 4808704 | tf_op jit(solution)/shard_map/pallas_call | solution.py:294
  44.6 0.6 collective-permute-start.19
  45.2 0.5 shard_map.68
  46.1 0.9 %shard_map.67 = (f32[80,1024]{1,0:T(8,128)S(1)}, bf16[80,1024]{1,0:T(8,128)(2,1)S(1)}, f32[80,1024]{1,0:T(8,128)S(1)}, bf16[80,1024]{1,0:T(8,128)(2,1)S(1)}) custom-call(bf16[320,640]{1,0:T(8,128)(2,1)S(1)} %get-tuple-element.51.tile_ref, bf16[320,320]{1,0:T(8,128)(2,1)S(1)} %collective-permute-done.15.tile_other, ...), custom_call_target="tpu_custom_call" | custom-call | flops 419430400 | bytes 2908160 | tf_op jit(solution)/shard_map/pallas_call | solution.py:294
  46.9 1.6 %collective-permute-start.17 = (bf16[80,1024]{1,0:T(8,128)(2,1)S(1)}, bf16[80,1024]{1,0:T(8,128)(2,1)S(1)}, u32[]{:S(2)}, u32[]{:S(2)}) collective-permute-start(bf16[80,1024]{1,0:T(8,128)(2,1)S(1)} %get-tuple-element.56), channel_id=1, source_target_pairs={{0,16},{16,0},{1,17},{17,1},{2,18},{18,2},{3,19},{19,3},{4,20},{20... | collective-permute-start | bytes 491528 | tf_op jit(solution)/shard_map/ppermute | solution.py:24
  48.5 2.7 %collective-permute-done.19 = bf16[80,1024]{1,0:T(8,128)(2,1)S(1)} collective-permute-done((bf16[80,1024]{1,0:T(8,128)(2,1)S(1)}, bf16[80,1024]{1,0:T(8,128)(2,1)S(1)}, u32[]{:S(2)}, u32[]{:S(2)}) %collective-permute-start.19) | collective-permute-done | bytes 163872 | tf_op jit(solution)/shard_map/ppermute | solution.py:24
  51.2 3.0 %collective-permute-start.21 = (bf16[80,1024]{1,0:T(8,128)(2,1)S(1)}, bf16[80,1024]{1,0:T(8,128)(2,1)S(1)}, u32[]{:S(2)}, u32[]{:S(2)}) collective-permute-start(bf16[80,1024]{1,0:T(8,128)(2,1)S(1)} %add_convert_fusion), channel_id=1, source_target_pairs={{0,2},{2,0},{1,3},{3,1},{4,6},{6,4},{5,7},{7,5},{8,10},{10,8},{9,1... | collective-permute-start | bytes 491528 | tf_op jit(solution)/shard_map/ppermute | solution.py:24
  54.3 0.5 collective-permute-start.20
  54.8 1.5 %collective-permute-start.16 = (bf16[80,1024]{1,0:T(8,128)(2,1)S(1)}, bf16[80,1024]{1,0:T(8,128)(2,1)S(1)}, u32[]{:S(2)}, u32[]{:S(2)}) collective-permute-start(bf16[80,1024]{1,0:T(8,128)(2,1)S(1)} %get-tuple-element.54), channel_id=1, source_target_pairs={{0,16},{16,0},{1,17},{17,1},{2,18},{18,2},{3,19},{19,3},{4,20},{20... | collective-permute-start | bytes 491528 | tf_op jit(solution)/shard_map/ppermute | solution.py:24
  56.3 1.9 %collective-permute-start.18 = (bf16[80,1024]{1,0:T(8,128)(2,1)S(1)}, bf16[80,1024]{1,0:T(8,128)(2,1)S(1)}, u32[]{:S(2)}, u32[]{:S(2)}) collective-permute-start(bf16[80,1024]{1,0:T(8,128)(2,1)S(1)} %add_convert_fusion.1), channel_id=1, source_target_pairs={{0,1},{1,0},{2,3},{3,2},{4,5},{5,4},{6,7},{7,6},{8,9},{9,8},{10,11... | collective-permute-start | bytes 491528 | tf_op jit(solution)/shard_map/ppermute | solution.py:24
  58.2 1.5 %collective-permute-done.20.refs_4_ = bf16[80,1024]{1,0:T(8,128)(2,1)S(1)} collective-permute-done((bf16[80,1024]{1,0:T(8,128)(2,1)S(1)}, bf16[80,1024]{1,0:T(8,128)(2,1)S(1)}, u32[]{:S(2)}, u32[]{:S(2)}) %collective-permute-start.20) | collective-permute-done | bytes 163872 | tf_op jit(solution)/shard_map/ppermute | solution.py:24
  59.7 2.2 %collective-permute-done.21.refs_5_ = bf16[80,1024]{1,0:T(8,128)(2,1)S(1)} collective-permute-done((bf16[80,1024]{1,0:T(8,128)(2,1)S(1)}, bf16[80,1024]{1,0:T(8,128)(2,1)S(1)}, u32[]{:S(2)}, u32[]{:S(2)}) %collective-permute-start.21) | collective-permute-done | bytes 163872 | tf_op jit(solution)/shard_map/ppermute | solution.py:24
  61.9 1.7 %collective-permute-done.18.refs_2_ = bf16[80,1024]{1,0:T(8,128)(2,1)S(1)} collective-permute-done((bf16[80,1024]{1,0:T(8,128)(2,1)S(1)}, bf16[80,1024]{1,0:T(8,128)(2,1)S(1)}, u32[]{:S(2)}, u32[]{:S(2)}) %collective-permute-start.18) | collective-permute-done | bytes 163872 | tf_op jit(solution)/shard_map/ppermute | solution.py:24
  63.6 0.9 %shard_map.69 = (f32[80,1024]{1,0:T(8,128)}, f32[80,1024]{1,0:T(8,128)}) custom-call(f32[80,1024]{1,0:T(8,128)S(1)} %get-tuple-element.53.refs_0_, bf16[80,1024]{1,0:T(8,128)(2,1)S(1)} %collective-permute-done.16.refs_1_, bf16[80,1024]{1,0:T(8,128)(2,1)S(1)} %collective-permute-done.18.refs_2_, f32[80,1024]{1,0:T(8,128)S(1)} %get-tuple-element.57.refs_3_, ...), custom_call_target="tpu_custom_call" | custom-call | bytes 1966080 | tf_op jit(solution)/shard_map/pallas_call | solution.py:294
  (25 shorter events, 2.0 us)
Async XLA Ops:
  1.8 17.2 %collective-permute-start = (bf16[80,1792]{1,0:T(8,128)(2,1)S(1)}, bf16[80,1792]{1,0:T(8,128)(2,1)S(1)}, u32[]{:S(2)}, u32[]{:S(2)}) collective-permute-start(bf16[80,1792]{1,0:T(8,128)(2,1)S(1)} %get-tuple-element.33.refs_0_), channel_id=1, source_target_pairs={{0,2},{2,0},{1,3},{3,1},{4,6},{6,4},{5,7},{7,5},{8,10},{10,8},{9,1... | collective-permute-start | bytes 860168 | tf_op jit(solution)/shard_map/ppermute | solution.py:24
  5.9 14.6 %collective-permute-start.4 = (bf16[80,1792]{1,0:T(8,128)(2,1)S(1)}, bf16[80,1792]{1,0:T(8,128)(2,1)S(1)}, u32[]{:S(2)}, u32[]{:S(2)}) collective-permute-start(bf16[80,1792]{1,0:T(8,128)(2,1)S(1)} %get-tuple-element.36.refs_1_.refs_0_), channel_id=1, source_target_pairs={{0,1},{1,0},{2,3},{3,2},{4,5},{5,4},{6,7},{7,6},{8,9},{9,8},{10,11... | collective-permute-start | bytes 860168 | tf_op jit(solution)/shard_map/ppermute | solution.py:24
  7.5 14.5 %collective-permute-start.1 = (bf16[80,1792]{1,0:T(8,128)(2,1)S(1)}, bf16[80,1792]{1,0:T(8,128)(2,1)S(1)}, u32[]{:S(2)}, u32[]{:S(2)}) collective-permute-start(bf16[80,1792]{1,0:T(8,128)(2,1)S(1)} %get-tuple-element.35), channel_id=1, source_target_pairs={{0,8},{8,0},{1,9},{9,1},{2,10},{10,2},{3,11},{11,3},{4,12},{12,4},... | collective-permute-start | bytes 860168 | tf_op jit(solution)/shard_map/ppermute | solution.py:24
  9.1 13.0 %collective-permute-start.3 = (bf16[80,1792]{1,0:T(8,128)(2,1)S(1)}, bf16[80,1792]{1,0:T(8,128)(2,1)S(1)}, u32[]{:S(2)}, u32[]{:S(2)}) collective-permute-start(bf16[80,1792]{1,0:T(8,128)(2,1)S(1)} %get-tuple-element.37), channel_id=1, source_target_pairs={{0,16},{16,0},{1,17},{17,1},{2,18},{18,2},{3,19},{19,3},{4,20},{20... | collective-permute-start | bytes 860168 | tf_op jit(solution)/shard_map/ppermute | solution.py:24
  19.0 8.0 %collective-permute-start.2 = (bf16[80,1792]{1,0:T(8,128)(2,1)S(1)}, bf16[80,1792]{1,0:T(8,128)(2,1)S(1)}, u32[]{:S(2)}, u32[]{:S(2)}) collective-permute-start(bf16[80,1792]{1,0:T(8,128)(2,1)S(1)} %collective-permute-done.refs_1_), channel_id=1, source_target_pairs={{0,8},{8,0},{1,9},{9,1},{2,10},{10,2},{3,11},{11,3},{4,12},{12,4},... | collective-permute-start | bytes 860168 | tf_op jit(solution)/shard_map/ppermute | solution.py:24
  20.5 7.4 %collective-permute-start.5 = (bf16[80,1792]{1,0:T(8,128)(2,1)S(1)}, bf16[80,1792]{1,0:T(8,128)(2,1)S(1)}, u32[]{:S(2)}, u32[]{:S(2)}) collective-permute-start(bf16[80,1792]{1,0:T(8,128)(2,1)S(1)} %collective-permute-done.4.refs_0_), channel_id=1, source_target_pairs={{0,16},{16,0},{1,17},{17,1},{2,18},{18,2},{3,19},{19,3},{4,20},{20... | collective-permute-start | bytes 860168 | tf_op jit(solution)/shard_map/ppermute | solution.py:24
  22.1 5.9 %collective-permute-start.6 = (bf16[160,1792]{1,0:T(8,128)(2,1)S(1)}, bf16[160,1792]{1,0:T(8,128)(2,1)S(1)}, u32[]{:S(2)}, u32[]{:S(2)}) collective-permute-start(bf16[160,1792]{1,0:T(8,128)(2,1)S(1)} %shard_map.61.refs_4_.refs_8_.refs_0_), channel_id=1, source_target_pairs={{0,4},{4,0},{1,5},{5,1},{2,6},{6,2},{3,7},{7,3},{8,12},{12,8},{9,1... | collective-permute-start | bytes 1720328 | tf_op jit(solution)/shard_map/ppermute | solution.py:24
  27.9 2.0 %collective-permute-start.7 = (bf16[160,1792]{1,0:T(8,128)(2,1)S(1)}, bf16[160,1792]{1,0:T(8,128)(2,1)S(1)}, u32[]{:S(2)}, u32[]{:S(2)}) collective-permute-start(bf16[160,1792]{1,0:T(8,128)(2,1)S(1)} %shard_map.62.refs_5_.refs_9_.refs_1_), channel_id=1, source_target_pairs={{0,4},{4,0},{1,5},{5,1},{2,6},{6,2},{3,7},{7,3},{8,12},{12,8},{9,1... | collective-permute-start | bytes 1720328 | tf_op jit(solution)/shard_map/ppermute | solution.py:24
  30.9 4.5 %collective-permute-start.8 = (bf16[320,1024]{1,0:T(8,128)(2,1)S(1)}, bf16[320,1024]{1,0:T(8,128)(2,1)S(1)}, u32[]{:S(2)}, u32[]{:S(2)}) collective-permute-start(bf16[320,1024]{1,0:T(8,128)(2,1)S(1)} %get-tuple-element.46.images), channel_id=1, source_target_pairs={{0,4},{4,0},{1,5},{5,1},{2,6},{6,2},{3,7},{7,3},{8,12},{12,8},{9,1... | collective-permute-start | bytes 1966088 | tf_op jit(solution)/shard_map/ppermute | solution.py:24
  31.1 7.2 %collective-permute-start.12 = (f32[8,8,128]{2,1,0:T(8,128)S(1)}, f32[8,8,128]{2,1,0:T(8,128)S(1)}, u32[]{:S(2)}, u32[]{:S(2)}) collective-permute-start(f32[8,8,128]{2,1,0:T(8,128)S(1)} %get-tuple-element.48.refs_2_), channel_id=1, source_target_pairs={{0,17},{1,16},{16,1},{17,0},{2,19},{3,18},{18,3},{19,2},{4,21},{5,... | collective-permute-start | bytes 98312 | tf_op jit(solution)/shard_map/ppermute | solution.py:24
  33.8 4.6 %collective-permute-start.11 = (f32[8,8,128]{2,1,0:T(8,128)S(1)}, f32[8,8,128]{2,1,0:T(8,128)S(1)}, u32[]{:S(2)}, u32[]{:S(2)}) collective-permute-start(f32[8,8,128]{2,1,0:T(8,128)S(1)} %get-tuple-element.48.refs_2_), channel_id=1, source_target_pairs={{0,16},{1,17},{16,0},{17,1},{2,18},{3,19},{18,2},{19,3},{4,20},{5,... | collective-permute-start | bytes 98312 | tf_op jit(solution)/shard_map/ppermute | solution.py:24
  34.3 4.1 %collective-permute-start.10 = (f32[8,8,128]{2,1,0:T(8,128)S(1)}, f32[8,8,128]{2,1,0:T(8,128)S(1)}, u32[]{:S(2)}, u32[]{:S(2)}) collective-permute-start(f32[8,8,128]{2,1,0:T(8,128)S(1)} %get-tuple-element.48.refs_2_), channel_id=1, source_target_pairs={{0,1},{1,0},{16,17},{17,16},{2,3},{3,2},{18,19},{19,18},{4,5},{5,4... | collective-permute-start | bytes 98312 | tf_op jit(solution)/shard_map/ppermute | solution.py:24
  34.6 3.7 %collective-permute-start.9 = (f32[4,8,128]{2,1,0:T(8,128)S(1)}, f32[4,8,128]{2,1,0:T(8,128)S(1)}, u32[]{:S(2)}, u32[]{:S(2)}) collective-permute-start(f32[4,8,128]{2,1,0:T(8,128)S(1)} %get-tuple-element.47.refs_0_), channel_id=1, source_target_pairs={{0,8},{8,0},{1,9},{9,1},{2,10},{10,2},{3,11},{11,3},{4,12},{12,4},... | collective-permute-start | bytes 49160 | tf_op jit(solution)/shard_map/ppermute | solution.py:24
  38.5 5.0 %collective-permute-start.14 = (f32[8,8,128]{2,1,0:T(8,128)S(1)}, f32[8,8,128]{2,1,0:T(8,128)S(1)}, u32[]{:S(2)}, u32[]{:S(2)}) collective-permute-start(f32[8,8,128]{2,1,0:T(8,128)S(1)} %get-tuple-element.50.refs_6_), channel_id=1, source_target_pairs={{0,4},{4,0},{1,5},{5,1},{2,6},{6,2},{3,7},{7,3},{8,12},{12,8},{9,1... | collective-permute-start | bytes 98312 | tf_op jit(solution)/shard_map/ppermute | solution.py:24
  38.6 5.0 %collective-permute-start.13 = (f32[4,8,128]{2,1,0:T(8,128)S(1)}, f32[4,8,128]{2,1,0:T(8,128)S(1)}, u32[]{:S(2)}, u32[]{:S(2)}) collective-permute-start(f32[4,8,128]{2,1,0:T(8,128)S(1)} %get-tuple-element.49.refs_4_), channel_id=1, source_target_pairs={{0,2},{2,0},{1,3},{3,1},{4,6},{6,4},{5,7},{7,5},{8,10},{10,8},{9,1... | collective-permute-start | bytes 49160 | tf_op jit(solution)/shard_map/ppermute | solution.py:24
  44.5 1.6 %collective-permute-start.15 = (bf16[320,320]{1,0:T(8,128)(2,1)S(1)}, bf16[320,320]{1,0:T(8,128)(2,1)S(1)}, u32[]{:S(2)}, u32[]{:S(2)}) collective-permute-start(bf16[320,320]{1,0:T(8,128)(2,1)S(1)} %get-tuple-element.52), channel_id=1, source_target_pairs={{0,4},{4,0},{1,5},{5,1},{2,6},{6,2},{3,7},{7,3},{8,12},{12,8},{9,1... | collective-permute-start | bytes 614408 | tf_op jit(solution)/shard_map/ppermute | solution.py:24
  44.6 6.6 %collective-permute-start.19 = (bf16[80,1024]{1,0:T(8,128)(2,1)S(1)}, bf16[80,1024]{1,0:T(8,128)(2,1)S(1)}, u32[]{:S(2)}, u32[]{:S(2)}) collective-permute-start(bf16[80,1024]{1,0:T(8,128)(2,1)S(1)} %get-tuple-element.60), channel_id=1, source_target_pairs={{0,8},{8,0},{1,9},{9,1},{2,10},{10,2},{3,11},{11,3},{4,12},{12,4},... | collective-permute-start | bytes 491528 | tf_op jit(solution)/shard_map/ppermute | solution.py:24
  46.9 9.4 %collective-permute-start.17 = (bf16[80,1024]{1,0:T(8,128)(2,1)S(1)}, bf16[80,1024]{1,0:T(8,128)(2,1)S(1)}, u32[]{:S(2)}, u32[]{:S(2)}) collective-permute-start(bf16[80,1024]{1,0:T(8,128)(2,1)S(1)} %get-tuple-element.56), channel_id=1, source_target_pairs={{0,16},{16,0},{1,17},{17,1},{2,18},{18,2},{3,19},{19,3},{4,20},{20... | collective-permute-start | bytes 491528 | tf_op jit(solution)/shard_map/ppermute | solution.py:24
  51.2 10.7 %collective-permute-start.21 = (bf16[80,1024]{1,0:T(8,128)(2,1)S(1)}, bf16[80,1024]{1,0:T(8,128)(2,1)S(1)}, u32[]{:S(2)}, u32[]{:S(2)}) collective-permute-start(bf16[80,1024]{1,0:T(8,128)(2,1)S(1)} %add_convert_fusion), channel_id=1, source_target_pairs={{0,2},{2,0},{1,3},{3,1},{4,6},{6,4},{5,7},{7,5},{8,10},{10,8},{9,1... | collective-permute-start | bytes 491528 | tf_op jit(solution)/shard_map/ppermute | solution.py:24
  54.3 5.5 %collective-permute-start.20 = (bf16[80,1024]{1,0:T(8,128)(2,1)S(1)}, bf16[80,1024]{1,0:T(8,128)(2,1)S(1)}, u32[]{:S(2)}, u32[]{:S(2)}) collective-permute-start(bf16[80,1024]{1,0:T(8,128)(2,1)S(1)} %get-tuple-element.61), channel_id=1, source_target_pairs={{0,8},{8,0},{1,9},{9,1},{2,10},{10,2},{3,11},{11,3},{4,12},{12,4},... | collective-permute-start | bytes 491528 | tf_op jit(solution)/shard_map/ppermute | solution.py:24
  54.8 7.1 %collective-permute-start.16 = (bf16[80,1024]{1,0:T(8,128)(2,1)S(1)}, bf16[80,1024]{1,0:T(8,128)(2,1)S(1)}, u32[]{:S(2)}, u32[]{:S(2)}) collective-permute-start(bf16[80,1024]{1,0:T(8,128)(2,1)S(1)} %get-tuple-element.54), channel_id=1, source_target_pairs={{0,16},{16,0},{1,17},{17,1},{2,18},{18,2},{3,19},{19,3},{4,20},{20... | collective-permute-start | bytes 491528 | tf_op jit(solution)/shard_map/ppermute | solution.py:24
  56.3 7.2 %collective-permute-start.18 = (bf16[80,1024]{1,0:T(8,128)(2,1)S(1)}, bf16[80,1024]{1,0:T(8,128)(2,1)S(1)}, u32[]{:S(2)}, u32[]{:S(2)}) collective-permute-start(bf16[80,1024]{1,0:T(8,128)(2,1)S(1)} %add_convert_fusion.1), channel_id=1, source_target_pairs={{0,1},{1,0},{2,3},{3,2},{4,5},{5,4},{6,7},{7,6},{8,9},{9,8},{10,11... | collective-permute-start | bytes 491528 | tf_op jit(solution)/shard_map/ppermute | solution.py:24

commit v13 on v9

--- a/solution.py
+++ b/solution.py
@@ -149,26 +149,27 @@
 
 
 def head_kernel(n_img, rows, width, *refs):
-    img_parts, cap_parts = refs[:n_img], refs[n_img:-4]
-    student_ref, teacher_ref, row_ref, lines_ref = refs[-4:]
+    img_parts, cap_parts = refs[:n_img], refs[n_img:-5]
+    student_ref, teacher_ref, row_ref, lines_ref, images = refs[-5:]
     count = student_ref.shape[1]
-    columns, lines = [], []
-    for part, out in ((slice(0, width), student_ref), (slice(width, None), teacher_ref)):
-        more = logits(joined(img_parts, part), window(cap_parts, 0, count, part), out)
-        columns, lines = columns + more[0], lines + more[1]
-    store_slots(row_ref, lines_of(columns), rows)
-    lines_ref[...] = stacked(lines)
-
-
-def tail_kernel(n_img, start, rows, width, head_ref, lines_ref, *refs):
-    img_parts, cap_parts = refs[:n_img], refs[n_img:-5]
-    student_ref, teacher_ref, row_ref, col_ref, images = refs[-5:]
-    stop = start + student_ref.shape[1]
     columns, lines = [], []
     for part, out in ((slice(0, width), student_ref), (slice(width, None), teacher_ref)):
         left = joined(img_parts, part)
         if out is student_ref:
             images[...] = left
+        more = logits(left, window(cap_parts, 0, count, part), out)
+        columns, lines = columns + more[0], lines + more[1]
+    store_slots(row_ref, lines_of(columns), rows)
+    lines_ref[...] = stacked(lines)
+
+
+def tail_kernel(n_img, start, rows, width, head_ref, lines_ref, images, *refs):
+    img_parts, cap_parts = refs[:n_img], refs[n_img:-4]
+    student_ref, teacher_ref, row_ref, col_ref = refs[-4:]
+    stop = start + student_ref.shape[1]
+    columns, lines = [], []
+    for part, out in ((slice(0, width), student_ref), (slice(width, None), teacher_ref)):
+        left = images[...] if out is student_ref else joined(img_parts, part)
         more = logits(left, window(cap_parts, start, stop, part), out)
         columns, lines = columns + more[0], lines + more[1]
     store_slots(row_ref, lines_of(columns), rows)
@@ -352,7 +353,7 @@
     early = [cap[h, 0] for h in range(ihi)]
     early = assemble([after(early[0], img[1, 0], img[0, 1])] + early[1:])
     late = [cap[h, c] for c in range(1, clo) for h in range(ihi)]
-    late = assemble([after(late[0], img[1, 1])] + late[1:])
+    late = assemble(late[:-1] + [after(late[-1], img[1, 1])])
     img = [img[h, c] for h in range(ilo) for c in range(chi)]
     cap = [early, late, swap(early, "core", 1), swap(late, "core", 1)]
     if not aligned:
@@ -364,20 +365,20 @@
     skipped = [part for k, part in enumerate(cap) if sum(p.shape[0] for p in cap[: k + 1]) <= head]
     needed = cap[len(skipped) :]
     start = head - sum(part.shape[0] for part in skipped)
-    student, teacher, row_head, lines = call(
+    student, teacher, row_head, lines, images = call(
         functools.partial(head_kernel, len(img), rows, width),
-        [shape((total, head), f32)] * 2 + [row_shape, shape((8, head), f32)],
+        [shape((total, head), f32)] * 2 + [row_shape, shape((8, head), f32), shape((total, width), bf16)],
         img + ready,
         2 * total * head * (width + depth),
     )
-    student_tail, teacher_tail, row_stats, col_stats, images = call(
+    student_tail, teacher_tail, row_stats, col_stats = call(
         functools.partial(tail_kernel, len(img), start, rows, width),
-        [shape((total, columns - head), f32)] * 2 + [row_shape, col_shape, shape((total, width), bf16)],
-        [row_head, lines] + img + needed,
+        [shape((total, columns - head), f32)] * 2 + [row_shape, col_shape],
+        [row_head, lines, images] + img + needed,
         2 * total * (columns - head) * (width + depth),
     )
 
-    images_other = swap(images, "core", 1)
+    images_other = swap(after(images, row_stats), "core", 1)
     stats = [row_stats, col_stats]
     for row_names, col_names in zip(ROW_STAGES, COL_STAGES):
         plan, blocks = [], []

time: 64.4 us -> 61.8 us (0.960)
  starting transfers between devices: 30 us -> 27.2 us
    ppermute x22, starting transfers between devices: 30 us -> 27.2 us  [swap(): return lax.ppermute(value, axis, [(j, j ^ mask) for j in range(size)])]
  transfers between devices with their start and end apart: 22 -> 22, of which waited for: 9 -> 10; matrix products, arithmetic and copies ran while one was open for 0% -> 0% of each run, Pallas kernels for 4% -> 4%
where the time goes in v13:
time: 61.8 us; the launch traced here: 61.7 us
  starting transfers between devices  27.2 us (44%)
  waiting for transfers between devices  26.9 us (44%)
  Pallas kernels  6.68 us (11%)
  between operations  0.75 us (1%)
    ppermute x22, starting transfers between devices, swap(): return lax.ppermute(value, axis, [(j, j ^ mask) for j in range(size)])  27.2 us
    ppermute x22, waiting for transfers between devices, swap(): return lax.ppermute(value, axis, [(j, j ^ mask) for j in range(size)])  26.9 us
    pallas_call x11, Pallas kernels, call(): pl.pallas_call(kernel, out_shape=[out_space(out.shape, out.dtype) for out...  6.68 us
  transfers between devices with their start and end apart: 22, of which 10 were waited for; matrix products, arithmetic and copies ran while one was open for 0% of the time, Pallas kernels for 4%

profile of v13, /device:TPU:0, one launch (start us, length us, event | category | flops | bytes accessed | tf_op | source)
XLA Modules:
  0.0 61.7 jit_solution(6679057121007471196)
XLA Ops:
  0.6 1.2 %shard_map.59 = (bf16[80,1792]{1,0:T(8,128)(2,1)S(1)}, bf16[80,1792]{1,0:T(8,128)(2,1)S(1)}) custom-call(bf16[80,1024]{1,0:T(8,128)(2,1)} %image_s.1, bf16[80,768]{1,0:T(8,128)(2,1)} %image_t.1, bf16[80,1024]{1,0:T(8,128)(2,1)} %caption_s.1, bf16[80,768]{1,0:T(8,128)(2,1)} %caption_t.1), custom_call_target="tpu_custom_call" | custom-call | bytes 1146880 | tf_op jit(solution)/shard_map/pallas_call | solution.py:295
  1.8 3.1 %collective-permute-start.4 = (bf16[80,1792]{1,0:T(8,128)(2,1)S(1)}, bf16[80,1792]{1,0:T(8,128)(2,1)S(1)}, u32[]{:S(2)}, u32[]{:S(2)}) collective-permute-start(bf16[80,1792]{1,0:T(8,128)(2,1)S(1)} %get-tuple-element.36.refs_1_.refs_0_), channel_id=1, source_target_pairs={{0,1},{1,0},{2,3},{3,2},{4,5},{5,4},{6,7},{7,6},{8,9},{9,8},{10,11... | collective-permute-start | bytes 860168 | tf_op jit(solution)/shard_map/ppermute | solution.py:24
  4.9 2.6 %collective-permute-start = (bf16[80,1792]{1,0:T(8,128)(2,1)S(1)}, bf16[80,1792]{1,0:T(8,128)(2,1)S(1)}, u32[]{:S(2)}, u32[]{:S(2)}) collective-permute-start(bf16[80,1792]{1,0:T(8,128)(2,1)S(1)} %get-tuple-element.33.refs_0_), channel_id=1, source_target_pairs={{0,2},{2,0},{1,3},{3,1},{4,6},{6,4},{5,7},{7,5},{8,10},{10,8},{9,1... | collective-permute-start | bytes 860168 | tf_op jit(solution)/shard_map/ppermute | solution.py:24
  7.5 1.6 %collective-permute-start.1 = (bf16[80,1792]{1,0:T(8,128)(2,1)S(1)}, bf16[80,1792]{1,0:T(8,128)(2,1)S(1)}, u32[]{:S(2)}, u32[]{:S(2)}) collective-permute-start(bf16[80,1792]{1,0:T(8,128)(2,1)S(1)} %get-tuple-element.35), channel_id=1, source_target_pairs={{0,8},{8,0},{1,9},{9,1},{2,10},{10,2},{3,11},{11,3},{4,12},{12,4},... | collective-permute-start | bytes 860168 | tf_op jit(solution)/shard_map/ppermute | solution.py:24
  9.1 1.5 %collective-permute-start.3 = (bf16[80,1792]{1,0:T(8,128)(2,1)S(1)}, bf16[80,1792]{1,0:T(8,128)(2,1)S(1)}, u32[]{:S(2)}, u32[]{:S(2)}) collective-permute-start(bf16[80,1792]{1,0:T(8,128)(2,1)S(1)} %get-tuple-element.37), channel_id=1, source_target_pairs={{0,16},{16,0},{1,17},{17,1},{2,18},{18,2},{3,19},{19,3},{4,20},{20... | collective-permute-start | bytes 860168 | tf_op jit(solution)/shard_map/ppermute | solution.py:24
  10.6 7.2 %collective-permute-done.4.refs_0_ = bf16[80,1792]{1,0:T(8,128)(2,1)S(1)} collective-permute-done((bf16[80,1792]{1,0:T(8,128)(2,1)S(1)}, bf16[80,1792]{1,0:T(8,128)(2,1)S(1)}, u32[]{:S(2)}, u32[]{:S(2)}) %collective-permute-start.4) | collective-permute-done | bytes 286752 | tf_op jit(solution)/shard_map/ppermute | solution.py:24
  17.7 1.7 %collective-permute-start.5 = (bf16[80,1792]{1,0:T(8,128)(2,1)S(1)}, bf16[80,1792]{1,0:T(8,128)(2,1)S(1)}, u32[]{:S(2)}, u32[]{:S(2)}) collective-permute-start(bf16[80,1792]{1,0:T(8,128)(2,1)S(1)} %collective-permute-done.4.refs_0_), channel_id=1, source_target_pairs={{0,16},{16,0},{1,17},{17,1},{2,18},{18,2},{3,19},{19,3},{4,20},{20... | collective-permute-start | bytes 860168 | tf_op jit(solution)/shard_map/ppermute | solution.py:24
  19.4 0.8 %collective-permute-done.refs_1_ = bf16[80,1792]{1,0:T(8,128)(2,1)S(1)} collective-permute-done((bf16[80,1792]{1,0:T(8,128)(2,1)S(1)}, bf16[80,1792]{1,0:T(8,128)(2,1)S(1)}, u32[]{:S(2)}, u32[]{:S(2)}) %collective-permute-start) | collective-permute-done | bytes 286752 | tf_op jit(solution)/shard_map/ppermute | solution.py:24
  20.3 1.5 %collective-permute-start.2 = (bf16[80,1792]{1,0:T(8,128)(2,1)S(1)}, bf16[80,1792]{1,0:T(8,128)(2,1)S(1)}, u32[]{:S(2)}, u32[]{:S(2)}) collective-permute-start(bf16[80,1792]{1,0:T(8,128)(2,1)S(1)} %collective-permute-done.refs_1_), channel_id=1, source_target_pairs={{0,8},{8,0},{1,9},{9,1},{2,10},{10,2},{3,11},{11,3},{4,12},{12,4},... | collective-permute-start | bytes 860168 | tf_op jit(solution)/shard_map/ppermute | solution.py:24
  21.9 3.9 %collective-permute-done.5.refs_1_ = bf16[80,1792]{1,0:T(8,128)(2,1)S(1)} collective-permute-done((bf16[80,1792]{1,0:T(8,128)(2,1)S(1)}, bf16[80,1792]{1,0:T(8,128)(2,1)S(1)}, u32[]{:S(2)}, u32[]{:S(2)}) %collective-permute-start.5) | collective-permute-done | bytes 286752 | tf_op jit(solution)/shard_map/ppermute | solution.py:24
  25.8 1.1 %collective-permute-done.2.refs_3_ = bf16[80,1792]{1,0:T(8,128)(2,1)S(1)} collective-permute-done((bf16[80,1792]{1,0:T(8,128)(2,1)S(1)}, bf16[80,1792]{1,0:T(8,128)(2,1)S(1)}, u32[]{:S(2)}, u32[]{:S(2)}) %collective-permute-start.2) | collective-permute-done | bytes 286752 | tf_op jit(solution)/shard_map/ppermute | solution.py:24
  27.0 1.1 %shard_map.63 = (f32[320,384]{1,0:T(8,128)S(1)}, f32[320,384]{1,0:T(8,128)S(1)}, f32[4,8,128]{2,1,0:T(8,128)S(1)}, f32[8,384]{1,0:T(8,128)S(1)}, bf16[320,1024]{1,0:T(8,128)(2,1)S(1)}) custom-call(bf16[80,1792]{1,0:T(8,128)(2,1)S(1)} %get-tuple-element.33.refs_0_, bf16[80,1792]{1,0:T(8,128)(2,1)S(1)} %collective-permute-done.refs_1_, ...), custom_call_target="tpu_custom_call" | custom-call | flops 440401920 | bytes 4534272 | tf_op jit(solution)/shard_map/pallas_call | solution.py:295
  28.2 0.8 %collective-permute-done.7.refs_5_.refs_11_.refs_3_ = bf16[160,1792]{1,0:T(8,128)(2,1)S(1)} collective-permute-done((bf16[160,1792]{1,0:T(8,128)(2,1)S(1)}, bf16[160,1792]{1,0:T(8,128)(2,1)S(1)}, u32[]{:S(2)}, u32[]{:S(2)}) %collective-permute-start.7) | collective-permute-done | bytes 573472 | tf_op jit(solution)/shard_map/ppermute | solution.py:24
  29.0 0.9 %shard_map.64 = (f32[320,256]{1,0:T(8,128)S(1)}, f32[320,256]{1,0:T(8,128)S(1)}, f32[4,8,128]{2,1,0:T(8,128)S(1)}, f32[8,8,128]{2,1,0:T(8,128)S(1)}) custom-call(f32[4,8,128]{2,1,0:T(8,128)S(1)} %get-tuple-element.40.head_ref, f32[8,384]{1,0:T(8,128)S(1)} %get-tuple-element.41.lines_ref, bf16[320,1024]{1,0:T(8,128)(2,1)S(1)} %get-tuple-element.47.images, ...), custom_call_target="tpu_custom_call" | custom-call | flops 293601280 | bytes 3682304 | tf_op jit(solution)/shard_map/pallas_call | solution.py:295
  30.1 2.4 %collective-permute-start.12 = (f32[8,8,128]{2,1,0:T(8,128)S(1)}, f32[8,8,128]{2,1,0:T(8,128)S(1)}, u32[]{:S(2)}, u32[]{:S(2)}) collective-permute-start(f32[8,8,128]{2,1,0:T(8,128)S(1)} %get-tuple-element.49.refs_2_), channel_id=1, source_target_pairs={{0,17},{1,16},{16,1},{17,0},{2,19},{3,18},{18,3},{19,2},{4,21},{5,... | collective-permute-start | bytes 98312 | tf_op jit(solution)/shard_map/ppermute | solution.py:24
  33.1 0.6 collective-permute-start.10
  33.6 1.5 %collective-permute-start.9 = (f32[4,8,128]{2,1,0:T(8,128)S(1)}, f32[4,8,128]{2,1,0:T(8,128)S(1)}, u32[]{:S(2)}, u32[]{:S(2)}) collective-permute-start(f32[4,8,128]{2,1,0:T(8,128)S(1)} %get-tuple-element.48.refs_0_), channel_id=1, source_target_pairs={{0,8},{8,0},{1,9},{9,1},{2,10},{10,2},{3,11},{11,3},{4,12},{12,4},... | collective-permute-start | bytes 49160 | tf_op jit(solution)/shard_map/ppermute | solution.py:24
  35.1 2.2 %collective-permute-done.9.refs_1_ = f32[4,8,128]{2,1,0:T(8,128)S(1)} collective-permute-done((f32[4,8,128]{2,1,0:T(8,128)S(1)}, f32[4,8,128]{2,1,0:T(8,128)S(1)}, u32[]{:S(2)}, u32[]{:S(2)}) %collective-permute-start.9) | collective-permute-done | bytes 16416 | tf_op jit(solution)/shard_map/ppermute | solution.py:24
  37.5 1.4 %collective-permute-start.13 = (f32[4,8,128]{2,1,0:T(8,128)S(1)}, f32[4,8,128]{2,1,0:T(8,128)S(1)}, u32[]{:S(2)}, u32[]{:S(2)}) collective-permute-start(f32[4,8,128]{2,1,0:T(8,128)S(1)} %get-tuple-element.50.refs_4_), channel_id=1, source_target_pairs={{0,2},{2,0},{1,3},{3,1},{4,6},{6,4},{5,7},{7,5},{8,10},{10,8},{9,1... | collective-permute-start | bytes 49160 | tf_op jit(solution)/shard_map/ppermute | solution.py:24
  39.0 3.3 %collective-permute-done.13.refs_5_ = f32[4,8,128]{2,1,0:T(8,128)S(1)} collective-permute-done((f32[4,8,128]{2,1,0:T(8,128)S(1)}, f32[4,8,128]{2,1,0:T(8,128)S(1)}, u32[]{:S(2)}, u32[]{:S(2)}) %collective-permute-start.13) | collective-permute-done | bytes 16416 | tf_op jit(solution)/shard_map/ppermute | solution.py:24
  42.3 1.0 %shard_map.66 = (bf16[320,640]{1,0:T(8,128)(2,1)S(1)}, bf16[320,320]{1,0:T(8,128)(2,1)S(1)}, bf16[80,1024]{1,0:T(8,128)(2,1)S(1)}) custom-call(f32[320,384]{1,0:T(8,128)S(1)} %get-tuple-element.39.refs_0_, f32[320,256]{1,0:T(8,128)S(1)} %get-tuple-element.43.refs_1_, f32[320,384]{1,0:T(8,128)S(1)} %get-tuple-element.44.refs_2_, ...), custom_call_target="tpu_custom_call" | custom-call | flops 104857600 | bytes 4808704 | tf_op jit(solution)/shard_map/pallas_call | solution.py:295
  43.3 1.6 %collective-permute-start.20 = (bf16[80,1024]{1,0:T(8,128)(2,1)S(1)}, bf16[80,1024]{1,0:T(8,128)(2,1)S(1)}, u32[]{:S(2)}, u32[]{:S(2)}) collective-permute-start(bf16[80,1024]{1,0:T(8,128)(2,1)S(1)} %get-tuple-element.61), channel_id=1, source_target_pairs={{0,8},{8,0},{1,9},{9,1},{2,10},{10,2},{3,11},{11,3},{4,12},{12,4},... | collective-permute-start | bytes 491528 | tf_op jit(solution)/shard_map/ppermute | solution.py:24
  44.9 0.5 shard_map.68
  45.4 0.6 collective-permute-start.19
  46.0 0.9 %shard_map.67 = (f32[80,1024]{1,0:T(8,128)S(1)}, bf16[80,1024]{1,0:T(8,128)(2,1)S(1)}, f32[80,1024]{1,0:T(8,128)S(1)}, bf16[80,1024]{1,0:T(8,128)(2,1)S(1)}) custom-call(bf16[320,640]{1,0:T(8,128)(2,1)S(1)} %get-tuple-element.52.tile_ref, bf16[320,320]{1,0:T(8,128)(2,1)S(1)} %collective-permute-done.15.tile_other, ...), custom_call_target="tpu_custom_call" | custom-call | flops 419430400 | bytes 2908160 | tf_op jit(solution)/shard_map/pallas_call | solution.py:295
  46.9 1.6 %collective-permute-start.17 = (bf16[80,1024]{1,0:T(8,128)(2,1)S(1)}, bf16[80,1024]{1,0:T(8,128)(2,1)S(1)}, u32[]{:S(2)}, u32[]{:S(2)}) collective-permute-start(bf16[80,1024]{1,0:T(8,128)(2,1)S(1)} %get-tuple-element.57), channel_id=1, source_target_pairs={{0,16},{16,0},{1,17},{17,1},{2,18},{18,2},{3,19},{19,3},{4,20},{20... | collective-permute-start | bytes 491528 | tf_op jit(solution)/shard_map/ppermute | solution.py:24
  48.5 1.9 %collective-permute-done.20 = bf16[80,1024]{1,0:T(8,128)(2,1)S(1)} collective-permute-done((bf16[80,1024]{1,0:T(8,128)(2,1)S(1)}, bf16[80,1024]{1,0:T(8,128)(2,1)S(1)}, u32[]{:S(2)}, u32[]{:S(2)}) %collective-permute-start.20) | collective-permute-done | bytes 163872 | tf_op jit(solution)/shard_map/ppermute | solution.py:24
  50.4 1.4 %collective-permute-start.21 = (bf16[80,1024]{1,0:T(8,128)(2,1)S(1)}, bf16[80,1024]{1,0:T(8,128)(2,1)S(1)}, u32[]{:S(2)}, u32[]{:S(2)}) collective-permute-start(bf16[80,1024]{1,0:T(8,128)(2,1)S(1)} %add_convert_fusion), channel_id=1, source_target_pairs={{0,2},{2,0},{1,3},{3,1},{4,6},{6,4},{5,7},{7,5},{8,10},{10,8},{9,1... | collective-permute-start | bytes 491528 | tf_op jit(solution)/shard_map/ppermute | solution.py:24
  51.8 1.5 %collective-permute-start.16 = (bf16[80,1024]{1,0:T(8,128)(2,1)S(1)}, bf16[80,1024]{1,0:T(8,128)(2,1)S(1)}, u32[]{:S(2)}, u32[]{:S(2)}) collective-permute-start(bf16[80,1024]{1,0:T(8,128)(2,1)S(1)} %get-tuple-element.55), channel_id=1, source_target_pairs={{0,16},{16,0},{1,17},{17,1},{2,18},{18,2},{3,19},{19,3},{4,20},{20... | collective-permute-start | bytes 491528 | tf_op jit(solution)/shard_map/ppermute | solution.py:24
  53.4 1.8 %collective-permute-start.18 = (bf16[80,1024]{1,0:T(8,128)(2,1)S(1)}, bf16[80,1024]{1,0:T(8,128)(2,1)S(1)}, u32[]{:S(2)}, u32[]{:S(2)}) collective-permute-start(bf16[80,1024]{1,0:T(8,128)(2,1)S(1)} %add_convert_fusion.1), channel_id=1, source_target_pairs={{0,1},{1,0},{2,3},{3,2},{4,5},{5,4},{6,7},{7,6},{8,9},{9,8},{10,11... | collective-permute-start | bytes 491528 | tf_op jit(solution)/shard_map/ppermute | solution.py:24
  55.1 5.2 %collective-permute-done.21.refs_5_ = bf16[80,1024]{1,0:T(8,128)(2,1)S(1)} collective-permute-done((bf16[80,1024]{1,0:T(8,128)(2,1)S(1)}, bf16[80,1024]{1,0:T(8,128)(2,1)S(1)}, u32[]{:S(2)}, u32[]{:S(2)}) %collective-permute-start.21) | collective-permute-done | bytes 163872 | tf_op jit(solution)/shard_map/ppermute | solution.py:24
  60.8 0.9 %shard_map.69 = (f32[80,1024]{1,0:T(8,128)}, f32[80,1024]{1,0:T(8,128)}) custom-call(f32[80,1024]{1,0:T(8,128)S(1)} %get-tuple-element.54.refs_0_, bf16[80,1024]{1,0:T(8,128)(2,1)S(1)} %collective-permute-done.16.refs_1_, bf16[80,1024]{1,0:T(8,128)(2,1)S(1)} %collective-permute-done.18.refs_2_, f32[80,1024]{1,0:T(8,128)S(1)} %get-tuple-element.58.refs_3_, ...), custom_call_target="tpu_custom_call" | custom-call | bytes 1966080 | tf_op jit(solution)/shard_map/pallas_call | solution.py:295
  (25 shorter events, 1.7 us)
Async XLA Ops:
  1.8 16.0 %collective-permute-start.4 = (bf16[80,1792]{1,0:T(8,128)(2,1)S(1)}, bf16[80,1792]{1,0:T(8,128)(2,1)S(1)}, u32[]{:S(2)}, u32[]{:S(2)}) collective-permute-start(bf16[80,1792]{1,0:T(8,128)(2,1)S(1)} %get-tuple-element.36.refs_1_.refs_0_), channel_id=1, source_target_pairs={{0,1},{1,0},{2,3},{3,2},{4,5},{5,4},{6,7},{7,6},{8,9},{9,8},{10,11... | collective-permute-start | bytes 860168 | tf_op jit(solution)/shard_map/ppermute | solution.py:24
  4.9 15.4 %collective-permute-start = (bf16[80,1792]{1,0:T(8,128)(2,1)S(1)}, bf16[80,1792]{1,0:T(8,128)(2,1)S(1)}, u32[]{:S(2)}, u32[]{:S(2)}) collective-permute-start(bf16[80,1792]{1,0:T(8,128)(2,1)S(1)} %get-tuple-element.33.refs_0_), channel_id=1, source_target_pairs={{0,2},{2,0},{1,3},{3,1},{4,6},{6,4},{5,7},{7,5},{8,10},{10,8},{9,1... | collective-permute-start | bytes 860168 | tf_op jit(solution)/shard_map/ppermute | solution.py:24
  7.5 14.2 %collective-permute-start.1 = (bf16[80,1792]{1,0:T(8,128)(2,1)S(1)}, bf16[80,1792]{1,0:T(8,128)(2,1)S(1)}, u32[]{:S(2)}, u32[]{:S(2)}) collective-permute-start(bf16[80,1792]{1,0:T(8,128)(2,1)S(1)} %get-tuple-element.35), channel_id=1, source_target_pairs={{0,8},{8,0},{1,9},{9,1},{2,10},{10,2},{3,11},{11,3},{4,12},{12,4},... | collective-permute-start | bytes 860168 | tf_op jit(solution)/shard_map/ppermute | solution.py:24
  9.1 12.7 %collective-permute-start.3 = (bf16[80,1792]{1,0:T(8,128)(2,1)S(1)}, bf16[80,1792]{1,0:T(8,128)(2,1)S(1)}, u32[]{:S(2)}, u32[]{:S(2)}) collective-permute-start(bf16[80,1792]{1,0:T(8,128)(2,1)S(1)} %get-tuple-element.37), channel_id=1, source_target_pairs={{0,16},{16,0},{1,17},{17,1},{2,18},{18,2},{3,19},{19,3},{4,20},{20... | collective-permute-start | bytes 860168 | tf_op jit(solution)/shard_map/ppermute | solution.py:24
  17.7 8.0 %collective-permute-start.5 = (bf16[80,1792]{1,0:T(8,128)(2,1)S(1)}, bf16[80,1792]{1,0:T(8,128)(2,1)S(1)}, u32[]{:S(2)}, u32[]{:S(2)}) collective-permute-start(bf16[80,1792]{1,0:T(8,128)(2,1)S(1)} %collective-permute-done.4.refs_0_), channel_id=1, source_target_pairs={{0,16},{16,0},{1,17},{17,1},{2,18},{18,2},{3,19},{19,3},{4,20},{20... | collective-permute-start | bytes 860168 | tf_op jit(solution)/shard_map/ppermute | solution.py:24
  20.3 6.6 %collective-permute-start.2 = (bf16[80,1792]{1,0:T(8,128)(2,1)S(1)}, bf16[80,1792]{1,0:T(8,128)(2,1)S(1)}, u32[]{:S(2)}, u32[]{:S(2)}) collective-permute-start(bf16[80,1792]{1,0:T(8,128)(2,1)S(1)} %collective-permute-done.refs_1_), channel_id=1, source_target_pairs={{0,8},{8,0},{1,9},{9,1},{2,10},{10,2},{3,11},{11,3},{4,12},{12,4},... | collective-permute-start | bytes 860168 | tf_op jit(solution)/shard_map/ppermute | solution.py:24
  21.8 5.2 %collective-permute-start.6 = (bf16[160,1792]{1,0:T(8,128)(2,1)S(1)}, bf16[160,1792]{1,0:T(8,128)(2,1)S(1)}, u32[]{:S(2)}, u32[]{:S(2)}) collective-permute-start(bf16[160,1792]{1,0:T(8,128)(2,1)S(1)} %shard_map.61.refs_4_.refs_8_.refs_0_), channel_id=1, source_target_pairs={{0,4},{4,0},{1,5},{5,1},{2,6},{6,2},{3,7},{7,3},{8,12},{12,8},{9,1... | collective-permute-start | bytes 1720328 | tf_op jit(solution)/shard_map/ppermute | solution.py:24
  26.9 2.0 %collective-permute-start.7 = (bf16[160,1792]{1,0:T(8,128)(2,1)S(1)}, bf16[160,1792]{1,0:T(8,128)(2,1)S(1)}, u32[]{:S(2)}, u32[]{:S(2)}) collective-permute-start(bf16[160,1792]{1,0:T(8,128)(2,1)S(1)} %shard_map.62.refs_5_.refs_9_.refs_1_), channel_id=1, source_target_pairs={{0,4},{4,0},{1,5},{5,1},{2,6},{6,2},{3,7},{7,3},{8,12},{12,8},{9,1... | collective-permute-start | bytes 1720328 | tf_op jit(solution)/shard_map/ppermute | solution.py:24
  29.9 5.2 %collective-permute-start.8 = (bf16[320,1024]{1,0:T(8,128)(2,1)S(1)}, bf16[320,1024]{1,0:T(8,128)(2,1)S(1)}, u32[]{:S(2)}, u32[]{:S(2)}) collective-permute-start(bf16[320,1024]{1,0:T(8,128)(2,1)S(1)} %get-tuple-element.47.images), channel_id=1, source_target_pairs={{0,4},{4,0},{1,5},{5,1},{2,6},{6,2},{3,7},{7,3},{8,12},{12,8},{9,1... | collective-permute-start | bytes 1966088 | tf_op jit(solution)/shard_map/ppermute | solution.py:24
  30.1 7.2 %collective-permute-start.12 = (f32[8,8,128]{2,1,0:T(8,128)S(1)}, f32[8,8,128]{2,1,0:T(8,128)S(1)}, u32[]{:S(2)}, u32[]{:S(2)}) collective-permute-start(f32[8,8,128]{2,1,0:T(8,128)S(1)} %get-tuple-element.49.refs_2_), channel_id=1, source_target_pairs={{0,17},{1,16},{16,1},{17,0},{2,19},{3,18},{18,3},{19,2},{4,21},{5,... | collective-permute-start | bytes 98312 | tf_op jit(solution)/shard_map/ppermute | solution.py:24
  32.6 4.8 %collective-permute-start.11 = (f32[8,8,128]{2,1,0:T(8,128)S(1)}, f32[8,8,128]{2,1,0:T(8,128)S(1)}, u32[]{:S(2)}, u32[]{:S(2)}) collective-permute-start(f32[8,8,128]{2,1,0:T(8,128)S(1)} %get-tuple-element.49.refs_2_), channel_id=1, source_target_pairs={{0,16},{1,17},{16,0},{17,1},{2,18},{3,19},{18,2},{19,3},{4,20},{5,... | collective-permute-start | bytes 98312 | tf_op jit(solution)/shard_map/ppermute | solution.py:24
  33.1 4.3 %collective-permute-start.10 = (f32[8,8,128]{2,1,0:T(8,128)S(1)}, f32[8,8,128]{2,1,0:T(8,128)S(1)}, u32[]{:S(2)}, u32[]{:S(2)}) collective-permute-start(f32[8,8,128]{2,1,0:T(8,128)S(1)} %get-tuple-element.49.refs_2_), channel_id=1, source_target_pairs={{0,1},{1,0},{16,17},{17,16},{2,3},{3,2},{18,19},{19,18},{4,5},{5,4... | collective-permute-start | bytes 98312 | tf_op jit(solution)/shard_map/ppermute | solution.py:24
  33.6 3.7 %collective-permute-start.9 = (f32[4,8,128]{2,1,0:T(8,128)S(1)}, f32[4,8,128]{2,1,0:T(8,128)S(1)}, u32[]{:S(2)}, u32[]{:S(2)}) collective-permute-start(f32[4,8,128]{2,1,0:T(8,128)S(1)} %get-tuple-element.48.refs_0_), channel_id=1, source_target_pairs={{0,8},{8,0},{1,9},{9,1},{2,10},{10,2},{3,11},{11,3},{4,12},{12,4},... | collective-permute-start | bytes 49160 | tf_op jit(solution)/shard_map/ppermute | solution.py:24
  37.5 4.8 %collective-permute-start.14 = (f32[8,8,128]{2,1,0:T(8,128)S(1)}, f32[8,8,128]{2,1,0:T(8,128)S(1)}, u32[]{:S(2)}, u32[]{:S(2)}) collective-permute-start(f32[8,8,128]{2,1,0:T(8,128)S(1)} %get-tuple-element.51.refs_6_), channel_id=1, source_target_pairs={{0,4},{4,0},{1,5},{5,1},{2,6},{6,2},{3,7},{7,3},{8,12},{12,8},{9,1... | collective-permute-start | bytes 98312 | tf_op jit(solution)/shard_map/ppermute | solution.py:24
  37.5 4.7 %collective-permute-start.13 = (f32[4,8,128]{2,1,0:T(8,128)S(1)}, f32[4,8,128]{2,1,0:T(8,128)S(1)}, u32[]{:S(2)}, u32[]{:S(2)}) collective-permute-start(f32[4,8,128]{2,1,0:T(8,128)S(1)} %get-tuple-element.50.refs_4_), channel_id=1, source_target_pairs={{0,2},{2,0},{1,3},{3,1},{4,6},{6,4},{5,7},{7,5},{8,10},{10,8},{9,1... | collective-permute-start | bytes 49160 | tf_op jit(solution)/shard_map/ppermute | solution.py:24
  43.2 2.8 %collective-permute-start.15 = (bf16[320,320]{1,0:T(8,128)(2,1)S(1)}, bf16[320,320]{1,0:T(8,128)(2,1)S(1)}, u32[]{:S(2)}, u32[]{:S(2)}) collective-permute-start(bf16[320,320]{1,0:T(8,128)(2,1)S(1)} %get-tuple-element.53), channel_id=1, source_target_pairs={{0,4},{4,0},{1,5},{5,1},{2,6},{6,2},{3,7},{7,3},{8,12},{12,8},{9,1... | collective-permute-start | bytes 614408 | tf_op jit(solution)/shard_map/ppermute | solution.py:24
  43.3 7.1 %collective-permute-start.20 = (bf16[80,1024]{1,0:T(8,128)(2,1)S(1)}, bf16[80,1024]{1,0:T(8,128)(2,1)S(1)}, u32[]{:S(2)}, u32[]{:S(2)}) collective-permute-start(bf16[80,1024]{1,0:T(8,128)(2,1)S(1)} %get-tuple-element.61), channel_id=1, source_target_pairs={{0,8},{8,0},{1,9},{9,1},{2,10},{10,2},{3,11},{11,3},{4,12},{12,4},... | collective-permute-start | bytes 491528 | tf_op jit(solution)/shard_map/ppermute | solution.py:24
  45.4 9.7 %collective-permute-start.19 = (bf16[80,1024]{1,0:T(8,128)(2,1)S(1)}, bf16[80,1024]{1,0:T(8,128)(2,1)S(1)}, u32[]{:S(2)}, u32[]{:S(2)}) collective-permute-start(bf16[80,1024]{1,0:T(8,128)(2,1)S(1)} %get-tuple-element.59), channel_id=1, source_target_pairs={{0,8},{8,0},{1,9},{9,1},{2,10},{10,2},{3,11},{11,3},{4,12},{12,4},... | collective-permute-start | bytes 491528 | tf_op jit(solution)/shard_map/ppermute | solution.py:24
  46.9 6.5 %collective-permute-start.17 = (bf16[80,1024]{1,0:T(8,128)(2,1)S(1)}, bf16[80,1024]{1,0:T(8,128)(2,1)S(1)}, u32[]{:S(2)}, u32[]{:S(2)}) collective-permute-start(bf16[80,1024]{1,0:T(8,128)(2,1)S(1)} %get-tuple-element.57), channel_id=1, source_target_pairs={{0,16},{16,0},{1,17},{17,1},{2,18},{18,2},{3,19},{19,3},{4,20},{20... | collective-permute-start | bytes 491528 | tf_op jit(solution)/shard_map/ppermute | solution.py:24
  50.4 9.9 %collective-permute-start.21 = (bf16[80,1024]{1,0:T(8,128)(2,1)S(1)}, bf16[80,1024]{1,0:T(8,128)(2,1)S(1)}, u32[]{:S(2)}, u32[]{:S(2)}) collective-permute-start(bf16[80,1024]{1,0:T(8,128)(2,1)S(1)} %add_convert_fusion), channel_id=1, source_target_pairs={{0,2},{2,0},{1,3},{3,1},{4,6},{6,4},{5,7},{7,5},{8,10},{10,8},{9,1... | collective-permute-start | bytes 491528 | tf_op jit(solution)/shard_map/ppermute | solution.py:24
  51.8 8.5 %collective-permute-start.16 = (bf16[80,1024]{1,0:T(8,128)(2,1)S(1)}, bf16[80,1024]{1,0:T(8,128)(2,1)S(1)}, u32[]{:S(2)}, u32[]{:S(2)}) collective-permute-start(bf16[80,1024]{1,0:T(8,128)(2,1)S(1)} %get-tuple-element.55), channel_id=1, source_target_pairs={{0,16},{16,0},{1,17},{17,1},{2,18},{18,2},{3,19},{19,3},{4,20},{20... | collective-permute-start | bytes 491528 | tf_op jit(solution)/shard_map/ppermute | solution.py:24
  53.4 7.4 %collective-permute-start.18 = (bf16[80,1024]{1,0:T(8,128)(2,1)S(1)}, bf16[80,1024]{1,0:T(8,128)(2,1)S(1)}, u32[]{:S(2)}, u32[]{:S(2)}) collective-permute-start(bf16[80,1024]{1,0:T(8,128)(2,1)S(1)} %add_convert_fusion.1), channel_id=1, source_target_pairs={{0,1},{1,0},{2,3},{3,2},{4,5},{5,4},{6,7},{7,6},{8,9},{9,8},{10,11... | collective-permute-start | bytes 491528 | tf_op jit(solution)/shard_map/ppermute | solution.py:24

commit v14 on v13

--- a/solution.py
+++ b/solution.py
@@ -16,7 +16,8 @@
 ROW_ORDER = ("ihi", "ilo", "core", "chi", "clo")
 COL_ORDER = ("chi", "clo", "ihi", "ilo", "core")
 LANES = 128
-PEAK_S, TOTAL_S, PEAK_T, TOTAL_T, INDEX = range(5)
+SLOT_LINES = 4
+LSE_S, LSE_T, INDEX = range(3)
 
 
 def swap(value, axis, mask):
@@ -60,12 +61,14 @@
 
 def store_slots(ref, lines, rows):
     ref[...] = jnp.zeros_like(ref)
-    for s in range(ref.shape[0]):
-        ref[s, :, :rows] = lines[:, s * rows : (s + 1) * rows]
+    for s in range(2 * ref.shape[0]):
+        first = s % 2 * SLOT_LINES
+        ref[s // 2, first : first + SLOT_LINES, :rows] = lines[:SLOT_LINES, s * rows : (s + 1) * rows]
 
 
 def load_slots(blocks, rows):
-    return jnp.concatenate([block[:, :rows] for block in blocks], axis=1)
+    halves = [block[first : first + SLOT_LINES, :rows] for block in blocks for first in (0, SLOT_LINES)]
+    return jnp.concatenate(halves, axis=1)
 
 
 def owners(axes, order):
@@ -174,29 +177,25 @@
         columns, lines = columns + more[0], lines + more[1]
     store_slots(row_ref, lines_of(columns), rows)
     store_slots(col_ref, jnp.concatenate([lines_ref[...], stacked(lines)], axis=1), rows)
-    row = lax.broadcasted_iota(jnp.int32, (8, LANES), 0)
-    lane = lax.broadcasted_iota(jnp.int32, (8, LANES), 1)
-    for ref, axes, order in ((row_ref, ROW_AXES, ROW_ORDER), (col_ref, COL_AXES, COL_ORDER)):
-        for s, owner in enumerate(owners(axes, order)):
-            block = merged(head_ref[s], ref[s]) if ref is row_ref else ref[s]
-            ref[s] = jnp.where(row == INDEX, (owner * rows + lane).astype(jnp.float32), block)
+    for k in range(row_ref.shape[0]):
+        row_ref[k] = merged(head_ref[k], row_ref[k])
 
 
 def merged(x, y):
-    line = lax.broadcasted_iota(jnp.int32, x.shape, 0)
-    student = line <= TOTAL_S
-    x_peak = jnp.where(student, x[PEAK_S : PEAK_S + 1], x[PEAK_T : PEAK_T + 1])
-    y_peak = jnp.where(student, y[PEAK_S : PEAK_S + 1], y[PEAK_T : PEAK_T + 1])
+    even = lax.broadcasted_iota(jnp.int32, x.shape, 0) % 2 == 0
+    x_peak, y_peak = (jnp.where(even, value, pltpu.roll(value, 1, 0)) for value in (x, y))
     peak = jnp.maximum(x_peak, y_peak)
     total = x * jnp.exp(x_peak - peak) + y * jnp.exp(y_peak - peak)
-    both = jnp.where((line == PEAK_S) | (line == PEAK_T), peak, total)
-    return jnp.where(line < INDEX, both, x)
+    return jnp.where(even, peak, total)
 
 
 def merged_blocks(mine, others, distances):
-    blocks = [mine[s] for s in range(mine.shape[0])]
+    blocks = [mine[k] for k in range(mine.shape[0])]
     for other, distance in zip(others, distances):
-        blocks = [merged(block, other[s ^ distance]) for s, block in enumerate(blocks)]
+        terms = [other[k ^ (distance // 2)] for k in range(len(blocks))]
+        if distance % 2:
+            terms = [pltpu.roll(term, SLOT_LINES, 0) for term in terms]
+        blocks = [merged(block, term) for block, term in zip(blocks, terms)]
     return blocks
 
 
@@ -225,14 +224,16 @@
     tile_ref, send_ref, first_ref = refs
     total, count = tile_ref.shape
 
-    def finish(blocks):
+    lane = lax.broadcasted_iota(jnp.int32, (8, LANES), 1)[:1, :rows]
+
+    def finish(blocks, axes, order):
         lines = load_slots(blocks, rows)
-        line = lax.broadcasted_iota(jnp.int32, lines.shape, 0)
-        lse_s = lines[PEAK_S : PEAK_S + 1] + jnp.log(lines[TOTAL_S : TOTAL_S + 1])
-        lse_t = lines[PEAK_T : PEAK_T + 1] + jnp.log(lines[TOTAL_T : TOTAL_T + 1])
-        return jnp.where(line == 0, lse_s, jnp.where(line == 1, lse_t, lines))
-
-    down, across = columns_of(finish(blocks[0])), finish(blocks[1])
+        index = jnp.concatenate([owner * rows + lane for owner in owners(axes, order)], axis=1)
+        lse_s, lse_t = lines[0:1] + jnp.log(lines[1:2]), lines[2:3] + jnp.log(lines[3:4])
+        return stacked([lse_s, lse_t, index.astype(jnp.float32)])
+
+    down = columns_of(finish(blocks[0], ROW_AXES, ROW_ORDER))
+    across = finish(blocks[1], COL_AXES, COL_ORDER)
     step = 64 if total % 64 == 0 else total
     for r in range(0, total, step):
         at = slice(r, r + step)
@@ -359,7 +360,7 @@
     if not aligned:
         img, cap = [assemble(img)], [assemble(cap)]
 
-    row_shape, col_shape = shape((n_img, 8, LANES), f32), shape((n_cap, 8, LANES), f32)
+    row_shape, col_shape = shape((n_img // 2, 8, LANES), f32), shape((n_cap // 2, 8, LANES), f32)
     head = (columns - (cap[-1].shape[0] if aligned else rows)) // LANES * LANES
     ready = cap[:-1] if aligned else cap
     skipped = [part for k, part in enumerate(cap) if sum(p.shape[0] for p in cap[: k + 1]) <= head]

time: 61.8 us -> 61.6 us (level)
  no operation moved by 1% of the time
where the time goes in v14:
time: 61.6 us; the launch traced here: 61.4 us
  starting transfers between devices  27.2 us (44%)
  waiting for transfers between devices  26.7 us (43%)
  Pallas kernels  6.63 us (11%)
  between operations  0.76 us (1%)
    ppermute x22, starting transfers between devices, swap(): return lax.ppermute(value, axis, [(j, j ^ mask) for j in range(size)])  27.2 us
    ppermute x22, waiting for transfers between devices, swap(): return lax.ppermute(value, axis, [(j, j ^ mask) for j in range(size)])  26.7 us
    pallas_call x11, Pallas kernels, call(): pl.pallas_call(kernel, out_shape=[out_space(out.shape, out.dtype) for out...  6.63 us
  transfers between devices with their start and end apart: 22, of which 10 were waited for; matrix products, arithmetic and copies ran while one was open for 0% of the time, Pallas kernels for 4%

profile of v14, /device:TPU:0, one launch (start us, length us, event | category | flops | bytes accessed | tf_op | source)
XLA Modules:
  0.0 61.4 jit_solution(1271833924732446248)
XLA Ops:
  0.6 1.2 %shard_map.59 = (bf16[80,1792]{1,0:T(8,128)(2,1)S(1)}, bf16[80,1792]{1,0:T(8,128)(2,1)S(1)}) custom-call(bf16[80,1024]{1,0:T(8,128)(2,1)} %image_s.1, bf16[80,768]{1,0:T(8,128)(2,1)} %image_t.1, bf16[80,1024]{1,0:T(8,128)(2,1)} %caption_s.1, bf16[80,768]{1,0:T(8,128)(2,1)} %caption_t.1), custom_call_target="tpu_custom_call" | custom-call | bytes 1146880 | tf_op jit(solution)/shard_map/pallas_call | solution.py:296
  1.8 3.1 %collective-permute-start.4 = (bf16[80,1792]{1,0:T(8,128)(2,1)S(1)}, bf16[80,1792]{1,0:T(8,128)(2,1)S(1)}, u32[]{:S(2)}, u32[]{:S(2)}) collective-permute-start(bf16[80,1792]{1,0:T(8,128)(2,1)S(1)} %get-tuple-element.36.refs_1_.refs_0_), channel_id=1, source_target_pairs={{0,1},{1,0},{2,3},{3,2},{4,5},{5,4},{6,7},{7,6},{8,9},{9,8},{10,11... | collective-permute-start | bytes 860168 | tf_op jit(solution)/shard_map/ppermute | solution.py:25
  4.9 2.6 %collective-permute-start = (bf16[80,1792]{1,0:T(8,128)(2,1)S(1)}, bf16[80,1792]{1,0:T(8,128)(2,1)S(1)}, u32[]{:S(2)}, u32[]{:S(2)}) collective-permute-start(bf16[80,1792]{1,0:T(8,128)(2,1)S(1)} %get-tuple-element.33.refs_0_), channel_id=1, source_target_pairs={{0,2},{2,0},{1,3},{3,1},{4,6},{6,4},{5,7},{7,5},{8,10},{10,8},{9,1... | collective-permute-start | bytes 860168 | tf_op jit(solution)/shard_map/ppermute | solution.py:25
  7.5 1.6 %collective-permute-start.1 = (bf16[80,1792]{1,0:T(8,128)(2,1)S(1)}, bf16[80,1792]{1,0:T(8,128)(2,1)S(1)}, u32[]{:S(2)}, u32[]{:S(2)}) collective-permute-start(bf16[80,1792]{1,0:T(8,128)(2,1)S(1)} %get-tuple-element.35), channel_id=1, source_target_pairs={{0,8},{8,0},{1,9},{9,1},{2,10},{10,2},{3,11},{11,3},{4,12},{12,4},... | collective-permute-start | bytes 860168 | tf_op jit(solution)/shard_map/ppermute | solution.py:25
  9.1 1.5 %collective-permute-start.3 = (bf16[80,1792]{1,0:T(8,128)(2,1)S(1)}, bf16[80,1792]{1,0:T(8,128)(2,1)S(1)}, u32[]{:S(2)}, u32[]{:S(2)}) collective-permute-start(bf16[80,1792]{1,0:T(8,128)(2,1)S(1)} %get-tuple-element.37), channel_id=1, source_target_pairs={{0,16},{16,0},{1,17},{17,1},{2,18},{18,2},{3,19},{19,3},{4,20},{20... | collective-permute-start | bytes 860168 | tf_op jit(solution)/shard_map/ppermute | solution.py:25
  10.6 7.2 %collective-permute-done.4.refs_0_ = bf16[80,1792]{1,0:T(8,128)(2,1)S(1)} collective-permute-done((bf16[80,1792]{1,0:T(8,128)(2,1)S(1)}, bf16[80,1792]{1,0:T(8,128)(2,1)S(1)}, u32[]{:S(2)}, u32[]{:S(2)}) %collective-permute-start.4) | collective-permute-done | bytes 286752 | tf_op jit(solution)/shard_map/ppermute | solution.py:25
  17.7 1.7 %collective-permute-start.5 = (bf16[80,1792]{1,0:T(8,128)(2,1)S(1)}, bf16[80,1792]{1,0:T(8,128)(2,1)S(1)}, u32[]{:S(2)}, u32[]{:S(2)}) collective-permute-start(bf16[80,1792]{1,0:T(8,128)(2,1)S(1)} %collective-permute-done.4.refs_0_), channel_id=1, source_target_pairs={{0,16},{16,0},{1,17},{17,1},{2,18},{18,2},{3,19},{19,3},{4,20},{20... | collective-permute-start | bytes 860168 | tf_op jit(solution)/shard_map/ppermute | solution.py:25
  19.4 0.8 %collective-permute-done.refs_1_ = bf16[80,1792]{1,0:T(8,128)(2,1)S(1)} collective-permute-done((bf16[80,1792]{1,0:T(8,128)(2,1)S(1)}, bf16[80,1792]{1,0:T(8,128)(2,1)S(1)}, u32[]{:S(2)}, u32[]{:S(2)}) %collective-permute-start) | collective-permute-done | bytes 286752 | tf_op jit(solution)/shard_map/ppermute | solution.py:25
  20.3 1.5 %collective-permute-start.2 = (bf16[80,1792]{1,0:T(8,128)(2,1)S(1)}, bf16[80,1792]{1,0:T(8,128)(2,1)S(1)}, u32[]{:S(2)}, u32[]{:S(2)}) collective-permute-start(bf16[80,1792]{1,0:T(8,128)(2,1)S(1)} %collective-permute-done.refs_1_), channel_id=1, source_target_pairs={{0,8},{8,0},{1,9},{9,1},{2,10},{10,2},{3,11},{11,3},{4,12},{12,4},... | collective-permute-start | bytes 860168 | tf_op jit(solution)/shard_map/ppermute | solution.py:25
  21.9 3.9 %collective-permute-done.5.refs_1_ = bf16[80,1792]{1,0:T(8,128)(2,1)S(1)} collective-permute-done((bf16[80,1792]{1,0:T(8,128)(2,1)S(1)}, bf16[80,1792]{1,0:T(8,128)(2,1)S(1)}, u32[]{:S(2)}, u32[]{:S(2)}) %collective-permute-start.5) | collective-permute-done | bytes 286752 | tf_op jit(solution)/shard_map/ppermute | solution.py:25
  25.8 1.1 %collective-permute-done.2.refs_3_ = bf16[80,1792]{1,0:T(8,128)(2,1)S(1)} collective-permute-done((bf16[80,1792]{1,0:T(8,128)(2,1)S(1)}, bf16[80,1792]{1,0:T(8,128)(2,1)S(1)}, u32[]{:S(2)}, u32[]{:S(2)}) %collective-permute-start.2) | collective-permute-done | bytes 286752 | tf_op jit(solution)/shard_map/ppermute | solution.py:25
  27.0 1.1 %shard_map.63 = (f32[320,384]{1,0:T(8,128)S(1)}, f32[320,384]{1,0:T(8,128)S(1)}, f32[2,8,128]{2,1,0:T(8,128)S(1)}, f32[8,384]{1,0:T(8,128)S(1)}, bf16[320,1024]{1,0:T(8,128)(2,1)S(1)}) custom-call(bf16[80,1792]{1,0:T(8,128)(2,1)S(1)} %get-tuple-element.33.refs_0_, bf16[80,1792]{1,0:T(8,128)(2,1)S(1)} %collective-permute-done.refs_1_, ...), custom_call_target="tpu_custom_call" | custom-call | flops 440401920 | bytes 4526080 | tf_op jit(solution)/shard_map/pallas_call | solution.py:296
  28.2 0.8 %collective-permute-done.7.refs_5_.refs_11_.refs_3_ = bf16[160,1792]{1,0:T(8,128)(2,1)S(1)} collective-permute-done((bf16[160,1792]{1,0:T(8,128)(2,1)S(1)}, bf16[160,1792]{1,0:T(8,128)(2,1)S(1)}, u32[]{:S(2)}, u32[]{:S(2)}) %collective-permute-start.7) | collective-permute-done | bytes 573472 | tf_op jit(solution)/shard_map/ppermute | solution.py:25
  29.0 0.9 %shard_map.64 = (f32[320,256]{1,0:T(8,128)S(1)}, f32[320,256]{1,0:T(8,128)S(1)}, f32[2,8,128]{2,1,0:T(8,128)S(1)}, f32[4,8,128]{2,1,0:T(8,128)S(1)}) custom-call(f32[2,8,128]{2,1,0:T(8,128)S(1)} %get-tuple-element.40.head_ref, f32[8,384]{1,0:T(8,128)S(1)} %get-tuple-element.41.lines_ref, bf16[320,1024]{1,0:T(8,128)(2,1)S(1)} %get-tuple-element.47.images, ...), custom_call_target="tpu_custom_call" | custom-call | flops 293601280 | bytes 3649536 | tf_op jit(solution)/shard_map/pallas_call | solution.py:296
  30.1 2.4 %collective-permute-start.12 = (f32[4,8,128]{2,1,0:T(8,128)S(1)}, f32[4,8,128]{2,1,0:T(8,128)S(1)}, u32[]{:S(2)}, u32[]{:S(2)}) collective-permute-start(f32[4,8,128]{2,1,0:T(8,128)S(1)} %get-tuple-element.49.refs_2_), channel_id=1, source_target_pairs={{0,17},{1,16},{16,1},{17,0},{2,19},{3,18},{18,3},{19,2},{4,21},{5,... | collective-permute-start | bytes 49160 | tf_op jit(solution)/shard_map/ppermute | solution.py:25
  33.0 0.6 collective-permute-start.10
  33.6 1.5 %collective-permute-start.9 = (f32[2,8,128]{2,1,0:T(8,128)S(1)}, f32[2,8,128]{2,1,0:T(8,128)S(1)}, u32[]{:S(2)}, u32[]{:S(2)}) collective-permute-start(f32[2,8,128]{2,1,0:T(8,128)S(1)} %get-tuple-element.48.refs_0_), channel_id=1, source_target_pairs={{0,8},{8,0},{1,9},{9,1},{2,10},{10,2},{3,11},{11,3},{4,12},{12,4},... | collective-permute-start | bytes 24584 | tf_op jit(solution)/shard_map/ppermute | solution.py:25
  35.1 2.2 %collective-permute-done.9.refs_1_ = f32[2,8,128]{2,1,0:T(8,128)S(1)} collective-permute-done((f32[2,8,128]{2,1,0:T(8,128)S(1)}, f32[2,8,128]{2,1,0:T(8,128)S(1)}, u32[]{:S(2)}, u32[]{:S(2)}) %collective-permute-start.9) | collective-permute-done | bytes 8224 | tf_op jit(solution)/shard_map/ppermute | solution.py:25
  37.4 1.4 %collective-permute-start.13 = (f32[2,8,128]{2,1,0:T(8,128)S(1)}, f32[2,8,128]{2,1,0:T(8,128)S(1)}, u32[]{:S(2)}, u32[]{:S(2)}) collective-permute-start(f32[2,8,128]{2,1,0:T(8,128)S(1)} %get-tuple-element.50.refs_4_), channel_id=1, source_target_pairs={{0,2},{2,0},{1,3},{3,1},{4,6},{6,4},{5,7},{7,5},{8,10},{10,8},{9,1... | collective-permute-start | bytes 24584 | tf_op jit(solution)/shard_map/ppermute | solution.py:25
  38.8 3.2 %collective-permute-done.13.refs_5_ = f32[2,8,128]{2,1,0:T(8,128)S(1)} collective-permute-done((f32[2,8,128]{2,1,0:T(8,128)S(1)}, f32[2,8,128]{2,1,0:T(8,128)S(1)}, u32[]{:S(2)}, u32[]{:S(2)}) %collective-permute-start.13) | collective-permute-done | bytes 8224 | tf_op jit(solution)/shard_map/ppermute | solution.py:25
  42.0 1.0 %shard_map.66 = (bf16[320,640]{1,0:T(8,128)(2,1)S(1)}, bf16[320,320]{1,0:T(8,128)(2,1)S(1)}, bf16[80,1024]{1,0:T(8,128)(2,1)S(1)}) custom-call(f32[320,384]{1,0:T(8,128)S(1)} %get-tuple-element.39.refs_0_, f32[320,256]{1,0:T(8,128)S(1)} %get-tuple-element.43.refs_1_, f32[320,384]{1,0:T(8,128)S(1)} %get-tuple-element.44.refs_2_, ...), custom_call_target="tpu_custom_call" | custom-call | flops 104857600 | bytes 4759552 | tf_op jit(solution)/shard_map/pallas_call | solution.py:296
  43.1 1.6 %collective-permute-start.20 = (bf16[80,1024]{1,0:T(8,128)(2,1)S(1)}, bf16[80,1024]{1,0:T(8,128)(2,1)S(1)}, u32[]{:S(2)}, u32[]{:S(2)}) collective-permute-start(bf16[80,1024]{1,0:T(8,128)(2,1)S(1)} %get-tuple-element.61), channel_id=1, source_target_pairs={{0,8},{8,0},{1,9},{9,1},{2,10},{10,2},{3,11},{11,3},{4,12},{12,4},... | collective-permute-start | bytes 491528 | tf_op jit(solution)/shard_map/ppermute | solution.py:25
  44.7 0.5 shard_map.68
  45.2 0.6 collective-permute-start.19
  45.8 0.9 %shard_map.67 = (f32[80,1024]{1,0:T(8,128)S(1)}, bf16[80,1024]{1,0:T(8,128)(2,1)S(1)}, f32[80,1024]{1,0:T(8,128)S(1)}, bf16[80,1024]{1,0:T(8,128)(2,1)S(1)}) custom-call(bf16[320,640]{1,0:T(8,128)(2,1)S(1)} %get-tuple-element.52.tile_ref, bf16[320,320]{1,0:T(8,128)(2,1)S(1)} %collective-permute-done.15.tile_other, ...), custom_call_target="tpu_custom_call" | custom-call | flops 419430400 | bytes 2908160 | tf_op jit(solution)/shard_map/pallas_call | solution.py:296
  46.7 1.6 %collective-permute-start.17 = (bf16[80,1024]{1,0:T(8,128)(2,1)S(1)}, bf16[80,1024]{1,0:T(8,128)(2,1)S(1)}, u32[]{:S(2)}, u32[]{:S(2)}) collective-permute-start(bf16[80,1024]{1,0:T(8,128)(2,1)S(1)} %get-tuple-element.57), channel_id=1, source_target_pairs={{0,16},{16,0},{1,17},{17,1},{2,18},{18,2},{3,19},{19,3},{4,20},{20... | collective-permute-start | bytes 491528 | tf_op jit(solution)/shard_map/ppermute | solution.py:25
  48.3 1.9 %collective-permute-done.20 = bf16[80,1024]{1,0:T(8,128)(2,1)S(1)} collective-permute-done((bf16[80,1024]{1,0:T(8,128)(2,1)S(1)}, bf16[80,1024]{1,0:T(8,128)(2,1)S(1)}, u32[]{:S(2)}, u32[]{:S(2)}) %collective-permute-start.20) | collective-permute-done | bytes 163872 | tf_op jit(solution)/shard_map/ppermute | solution.py:25
  50.2 1.4 %collective-permute-start.21 = (bf16[80,1024]{1,0:T(8,128)(2,1)S(1)}, bf16[80,1024]{1,0:T(8,128)(2,1)S(1)}, u32[]{:S(2)}, u32[]{:S(2)}) collective-permute-start(bf16[80,1024]{1,0:T(8,128)(2,1)S(1)} %add_convert_fusion), channel_id=1, source_target_pairs={{0,2},{2,0},{1,3},{3,1},{4,6},{6,4},{5,7},{7,5},{8,10},{10,8},{9,1... | collective-permute-start | bytes 491528 | tf_op jit(solution)/shard_map/ppermute | solution.py:25
  51.6 1.5 %collective-permute-start.16 = (bf16[80,1024]{1,0:T(8,128)(2,1)S(1)}, bf16[80,1024]{1,0:T(8,128)(2,1)S(1)}, u32[]{:S(2)}, u32[]{:S(2)}) collective-permute-start(bf16[80,1024]{1,0:T(8,128)(2,1)S(1)} %get-tuple-element.55), channel_id=1, source_target_pairs={{0,16},{16,0},{1,17},{17,1},{2,18},{18,2},{3,19},{19,3},{4,20},{20... | collective-permute-start | bytes 491528 | tf_op jit(solution)/shard_map/ppermute | solution.py:25
  53.2 1.8 %collective-permute-start.18 = (bf16[80,1024]{1,0:T(8,128)(2,1)S(1)}, bf16[80,1024]{1,0:T(8,128)(2,1)S(1)}, u32[]{:S(2)}, u32[]{:S(2)}) collective-permute-start(bf16[80,1024]{1,0:T(8,128)(2,1)S(1)} %add_convert_fusion.1), channel_id=1, source_target_pairs={{0,1},{1,0},{2,3},{3,2},{4,5},{5,4},{6,7},{7,6},{8,9},{9,8},{10,11... | collective-permute-start | bytes 491528 | tf_op jit(solution)/shard_map/ppermute | solution.py:25
  54.9 5.2 %collective-permute-done.21.refs_5_ = bf16[80,1024]{1,0:T(8,128)(2,1)S(1)} collective-permute-done((bf16[80,1024]{1,0:T(8,128)(2,1)S(1)}, bf16[80,1024]{1,0:T(8,128)(2,1)S(1)}, u32[]{:S(2)}, u32[]{:S(2)}) %collective-permute-start.21) | collective-permute-done | bytes 163872 | tf_op jit(solution)/shard_map/ppermute | solution.py:25
  60.5 0.9 %shard_map.69 = (f32[80,1024]{1,0:T(8,128)}, f32[80,1024]{1,0:T(8,128)}) custom-call(f32[80,1024]{1,0:T(8,128)S(1)} %get-tuple-element.54.refs_0_, bf16[80,1024]{1,0:T(8,128)(2,1)S(1)} %collective-permute-done.16.refs_1_, bf16[80,1024]{1,0:T(8,128)(2,1)S(1)} %collective-permute-done.18.refs_2_, f32[80,1024]{1,0:T(8,128)S(1)} %get-tuple-element.58.refs_3_, ...), custom_call_target="tpu_custom_call" | custom-call | bytes 1966080 | tf_op jit(solution)/shard_map/pallas_call | solution.py:296
  (25 shorter events, 1.7 us)
Async XLA Ops:
  1.8 16.0 %collective-permute-start.4 = (bf16[80,1792]{1,0:T(8,128)(2,1)S(1)}, bf16[80,1792]{1,0:T(8,128)(2,1)S(1)}, u32[]{:S(2)}, u32[]{:S(2)}) collective-permute-start(bf16[80,1792]{1,0:T(8,128)(2,1)S(1)} %get-tuple-element.36.refs_1_.refs_0_), channel_id=1, source_target_pairs={{0,1},{1,0},{2,3},{3,2},{4,5},{5,4},{6,7},{7,6},{8,9},{9,8},{10,11... | collective-permute-start | bytes 860168 | tf_op jit(solution)/shard_map/ppermute | solution.py:25
  4.9 15.4 %collective-permute-start = (bf16[80,1792]{1,0:T(8,128)(2,1)S(1)}, bf16[80,1792]{1,0:T(8,128)(2,1)S(1)}, u32[]{:S(2)}, u32[]{:S(2)}) collective-permute-start(bf16[80,1792]{1,0:T(8,128)(2,1)S(1)} %get-tuple-element.33.refs_0_), channel_id=1, source_target_pairs={{0,2},{2,0},{1,3},{3,1},{4,6},{6,4},{5,7},{7,5},{8,10},{10,8},{9,1... | collective-permute-start | bytes 860168 | tf_op jit(solution)/shard_map/ppermute | solution.py:25
  7.5 14.2 %collective-permute-start.1 = (bf16[80,1792]{1,0:T(8,128)(2,1)S(1)}, bf16[80,1792]{1,0:T(8,128)(2,1)S(1)}, u32[]{:S(2)}, u32[]{:S(2)}) collective-permute-start(bf16[80,1792]{1,0:T(8,128)(2,1)S(1)} %get-tuple-element.35), channel_id=1, source_target_pairs={{0,8},{8,0},{1,9},{9,1},{2,10},{10,2},{3,11},{11,3},{4,12},{12,4},... | collective-permute-start | bytes 860168 | tf_op jit(solution)/shard_map/ppermute | solution.py:25
  9.1 12.7 %collective-permute-start.3 = (bf16[80,1792]{1,0:T(8,128)(2,1)S(1)}, bf16[80,1792]{1,0:T(8,128)(2,1)S(1)}, u32[]{:S(2)}, u32[]{:S(2)}) collective-permute-start(bf16[80,1792]{1,0:T(8,128)(2,1)S(1)} %get-tuple-element.37), channel_id=1, source_target_pairs={{0,16},{16,0},{1,17},{17,1},{2,18},{18,2},{3,19},{19,3},{4,20},{20... | collective-permute-start | bytes 860168 | tf_op jit(solution)/shard_map/ppermute | solution.py:25
  17.7 8.0 %collective-permute-start.5 = (bf16[80,1792]{1,0:T(8,128)(2,1)S(1)}, bf16[80,1792]{1,0:T(8,128)(2,1)S(1)}, u32[]{:S(2)}, u32[]{:S(2)}) collective-permute-start(bf16[80,1792]{1,0:T(8,128)(2,1)S(1)} %collective-permute-done.4.refs_0_), channel_id=1, source_target_pairs={{0,16},{16,0},{1,17},{17,1},{2,18},{18,2},{3,19},{19,3},{4,20},{20... | collective-permute-start | bytes 860168 | tf_op jit(solution)/shard_map/ppermute | solution.py:25
  20.3 6.6 %collective-permute-start.2 = (bf16[80,1792]{1,0:T(8,128)(2,1)S(1)}, bf16[80,1792]{1,0:T(8,128)(2,1)S(1)}, u32[]{:S(2)}, u32[]{:S(2)}) collective-permute-start(bf16[80,1792]{1,0:T(8,128)(2,1)S(1)} %collective-permute-done.refs_1_), channel_id=1, source_target_pairs={{0,8},{8,0},{1,9},{9,1},{2,10},{10,2},{3,11},{11,3},{4,12},{12,4},... | collective-permute-start | bytes 860168 | tf_op jit(solution)/shard_map/ppermute | solution.py:25
  21.8 5.2 %collective-permute-start.6 = (bf16[160,1792]{1,0:T(8,128)(2,1)S(1)}, bf16[160,1792]{1,0:T(8,128)(2,1)S(1)}, u32[]{:S(2)}, u32[]{:S(2)}) collective-permute-start(bf16[160,1792]{1,0:T(8,128)(2,1)S(1)} %shard_map.61.refs_4_.refs_8_.refs_0_), channel_id=1, source_target_pairs={{0,4},{4,0},{1,5},{5,1},{2,6},{6,2},{3,7},{7,3},{8,12},{12,8},{9,1... | collective-permute-start | bytes 1720328 | tf_op jit(solution)/shard_map/ppermute | solution.py:25
  26.9 2.0 %collective-permute-start.7 = (bf16[160,1792]{1,0:T(8,128)(2,1)S(1)}, bf16[160,1792]{1,0:T(8,128)(2,1)S(1)}, u32[]{:S(2)}, u32[]{:S(2)}) collective-permute-start(bf16[160,1792]{1,0:T(8,128)(2,1)S(1)} %shard_map.62.refs_5_.refs_9_.refs_1_), channel_id=1, source_target_pairs={{0,4},{4,0},{1,5},{5,1},{2,6},{6,2},{3,7},{7,3},{8,12},{12,8},{9,1... | collective-permute-start | bytes 1720328 | tf_op jit(solution)/shard_map/ppermute | solution.py:25
  29.9 5.2 %collective-permute-start.8 = (bf16[320,1024]{1,0:T(8,128)(2,1)S(1)}, bf16[320,1024]{1,0:T(8,128)(2,1)S(1)}, u32[]{:S(2)}, u32[]{:S(2)}) collective-permute-start(bf16[320,1024]{1,0:T(8,128)(2,1)S(1)} %get-tuple-element.47.images), channel_id=1, source_target_pairs={{0,4},{4,0},{1,5},{5,1},{2,6},{6,2},{3,7},{7,3},{8,12},{12,8},{9,1... | collective-permute-start | bytes 1966088 | tf_op jit(solution)/shard_map/ppermute | solution.py:25
  30.1 7.2 %collective-permute-start.12 = (f32[4,8,128]{2,1,0:T(8,128)S(1)}, f32[4,8,128]{2,1,0:T(8,128)S(1)}, u32[]{:S(2)}, u32[]{:S(2)}) collective-permute-start(f32[4,8,128]{2,1,0:T(8,128)S(1)} %get-tuple-element.49.refs_2_), channel_id=1, source_target_pairs={{0,17},{1,16},{16,1},{17,0},{2,19},{3,18},{18,3},{19,2},{4,21},{5,... | collective-permute-start | bytes 49160 | tf_op jit(solution)/shard_map/ppermute | solution.py:25
  32.5 4.7 %collective-permute-start.11 = (f32[4,8,128]{2,1,0:T(8,128)S(1)}, f32[4,8,128]{2,1,0:T(8,128)S(1)}, u32[]{:S(2)}, u32[]{:S(2)}) collective-permute-start(f32[4,8,128]{2,1,0:T(8,128)S(1)} %get-tuple-element.49.refs_2_), channel_id=1, source_target_pairs={{0,16},{1,17},{16,0},{17,1},{2,18},{3,19},{18,2},{19,3},{4,20},{5,... | collective-permute-start | bytes 49160 | tf_op jit(solution)/shard_map/ppermute | solution.py:25
  33.0 4.2 %collective-permute-start.10 = (f32[4,8,128]{2,1,0:T(8,128)S(1)}, f32[4,8,128]{2,1,0:T(8,128)S(1)}, u32[]{:S(2)}, u32[]{:S(2)}) collective-permute-start(f32[4,8,128]{2,1,0:T(8,128)S(1)} %get-tuple-element.49.refs_2_), channel_id=1, source_target_pairs={{0,1},{1,0},{16,17},{17,16},{2,3},{3,2},{18,19},{19,18},{4,5},{5,4... | collective-permute-start | bytes 49160 | tf_op jit(solution)/shard_map/ppermute | solution.py:25
  33.6 3.7 %collective-permute-start.9 = (f32[2,8,128]{2,1,0:T(8,128)S(1)}, f32[2,8,128]{2,1,0:T(8,128)S(1)}, u32[]{:S(2)}, u32[]{:S(2)}) collective-permute-start(f32[2,8,128]{2,1,0:T(8,128)S(1)} %get-tuple-element.48.refs_0_), channel_id=1, source_target_pairs={{0,8},{8,0},{1,9},{9,1},{2,10},{10,2},{3,11},{11,3},{4,12},{12,4},... | collective-permute-start | bytes 24584 | tf_op jit(solution)/shard_map/ppermute | solution.py:25
  37.3 4.7 %collective-permute-start.14 = (f32[4,8,128]{2,1,0:T(8,128)S(1)}, f32[4,8,128]{2,1,0:T(8,128)S(1)}, u32[]{:S(2)}, u32[]{:S(2)}) collective-permute-start(f32[4,8,128]{2,1,0:T(8,128)S(1)} %get-tuple-element.51.refs_6_), channel_id=1, source_target_pairs={{0,4},{4,0},{1,5},{5,1},{2,6},{6,2},{3,7},{7,3},{8,12},{12,8},{9,1... | collective-permute-start | bytes 49160 | tf_op jit(solution)/shard_map/ppermute | solution.py:25
  37.4 4.6 %collective-permute-start.13 = (f32[2,8,128]{2,1,0:T(8,128)S(1)}, f32[2,8,128]{2,1,0:T(8,128)S(1)}, u32[]{:S(2)}, u32[]{:S(2)}) collective-permute-start(f32[2,8,128]{2,1,0:T(8,128)S(1)} %get-tuple-element.50.refs_4_), channel_id=1, source_target_pairs={{0,2},{2,0},{1,3},{3,1},{4,6},{6,4},{5,7},{7,5},{8,10},{10,8},{9,1... | collective-permute-start | bytes 24584 | tf_op jit(solution)/shard_map/ppermute | solution.py:25
  43.0 2.8 %collective-permute-start.15 = (bf16[320,320]{1,0:T(8,128)(2,1)S(1)}, bf16[320,320]{1,0:T(8,128)(2,1)S(1)}, u32[]{:S(2)}, u32[]{:S(2)}) collective-permute-start(bf16[320,320]{1,0:T(8,128)(2,1)S(1)} %get-tuple-element.53), channel_id=1, source_target_pairs={{0,4},{4,0},{1,5},{5,1},{2,6},{6,2},{3,7},{7,3},{8,12},{12,8},{9,1... | collective-permute-start | bytes 614408 | tf_op jit(solution)/shard_map/ppermute | solution.py:25
  43.1 7.1 %collective-permute-start.20 = (bf16[80,1024]{1,0:T(8,128)(2,1)S(1)}, bf16[80,1024]{1,0:T(8,128)(2,1)S(1)}, u32[]{:S(2)}, u32[]{:S(2)}) collective-permute-start(bf16[80,1024]{1,0:T(8,128)(2,1)S(1)} %get-tuple-element.61), channel_id=1, source_target_pairs={{0,8},{8,0},{1,9},{9,1},{2,10},{10,2},{3,11},{11,3},{4,12},{12,4},... | collective-permute-start | bytes 491528 | tf_op jit(solution)/shard_map/ppermute | solution.py:25
  45.2 9.7 %collective-permute-start.19 = (bf16[80,1024]{1,0:T(8,128)(2,1)S(1)}, bf16[80,1024]{1,0:T(8,128)(2,1)S(1)}, u32[]{:S(2)}, u32[]{:S(2)}) collective-permute-start(bf16[80,1024]{1,0:T(8,128)(2,1)S(1)} %get-tuple-element.59), channel_id=1, source_target_pairs={{0,8},{8,0},{1,9},{9,1},{2,10},{10,2},{3,11},{11,3},{4,12},{12,4},... | collective-permute-start | bytes 491528 | tf_op jit(solution)/shard_map/ppermute | solution.py:25
  46.7 6.4 %collective-permute-start.17 = (bf16[80,1024]{1,0:T(8,128)(2,1)S(1)}, bf16[80,1024]{1,0:T(8,128)(2,1)S(1)}, u32[]{:S(2)}, u32[]{:S(2)}) collective-permute-start(bf16[80,1024]{1,0:T(8,128)(2,1)S(1)} %get-tuple-element.57), channel_id=1, source_target_pairs={{0,16},{16,0},{1,17},{17,1},{2,18},{18,2},{3,19},{19,3},{4,20},{20... | collective-permute-start | bytes 491528 | tf_op jit(solution)/shard_map/ppermute | solution.py:25
  50.2 9.9 %collective-permute-start.21 = (bf16[80,1024]{1,0:T(8,128)(2,1)S(1)}, bf16[80,1024]{1,0:T(8,128)(2,1)S(1)}, u32[]{:S(2)}, u32[]{:S(2)}) collective-permute-start(bf16[80,1024]{1,0:T(8,128)(2,1)S(1)} %add_convert_fusion), channel_id=1, source_target_pairs={{0,2},{2,0},{1,3},{3,1},{4,6},{6,4},{5,7},{7,5},{8,10},{10,8},{9,1... | collective-permute-start | bytes 491528 | tf_op jit(solution)/shard_map/ppermute | solution.py:25
  51.6 8.5 %collective-permute-start.16 = (bf16[80,1024]{1,0:T(8,128)(2,1)S(1)}, bf16[80,1024]{1,0:T(8,128)(2,1)S(1)}, u32[]{:S(2)}, u32[]{:S(2)}) collective-permute-start(bf16[80,1024]{1,0:T(8,128)(2,1)S(1)} %get-tuple-element.55), channel_id=1, source_target_pairs={{0,16},{16,0},{1,17},{17,1},{2,18},{18,2},{3,19},{19,3},{4,20},{20... | collective-permute-start | bytes 491528 | tf_op jit(solution)/shard_map/ppermute | solution.py:25
  53.2 7.4 %collective-permute-start.18 = (bf16[80,1024]{1,0:T(8,128)(2,1)S(1)}, bf16[80,1024]{1,0:T(8,128)(2,1)S(1)}, u32[]{:S(2)}, u32[]{:S(2)}) collective-permute-start(bf16[80,1024]{1,0:T(8,128)(2,1)S(1)} %add_convert_fusion.1), channel_id=1, source_target_pairs={{0,1},{1,0},{2,3},{3,2},{4,5},{5,4},{6,7},{7,6},{8,9},{9,8},{10,11... | collective-permute-start | bytes 491528 | tf_op jit(solution)/shard_map/ppermute | solution.py:25

commit v15 on v14

--- a/solution.py
+++ b/solution.py
@@ -17,7 +17,7 @@
 COL_ORDER = ("chi", "clo", "ihi", "ilo", "core")
 LANES = 128
 SLOT_LINES = 4
-LSE_S, LSE_T, INDEX = range(3)
+SCALE_S, SCALE_T, INDEX = range(3)
 
 
 def swap(value, axis, mask):
@@ -152,8 +152,8 @@
 
 
 def head_kernel(n_img, rows, width, *refs):
-    img_parts, cap_parts = refs[:n_img], refs[n_img:-5]
-    student_ref, teacher_ref, row_ref, lines_ref, images = refs[-5:]
+    *parts, student_ref, teacher_ref, row_ref, lines_ref, images = refs
+    cap_parts, img_parts = parts[:-n_img], parts[-n_img:]
     count = student_ref.shape[1]
     columns, lines = [], []
     for part, out in ((slice(0, width), student_ref), (slice(width, None), teacher_ref)):
@@ -216,9 +216,22 @@
             out[s] = block
 
 
+def exp_kernel(rows, student, student_tail, teacher, teacher_tail, row_ref, col_ref, *outs):
+    down, across = (load_slots([ref[k] for k in range(ref.shape[0])], rows) for ref in (row_ref, col_ref))
+    down = columns_of(stacked([down[0:1], down[2:3]]))
+    total = student.shape[0]
+    step = 64 if total % 64 == 0 else total
+    for r in range(0, total, step):
+        at = slice(r, r + step)
+        for k, pair in enumerate(((student, student_tail), (teacher, teacher_tail))):
+            matrix = jnp.concatenate([ref[at] for ref in pair], axis=1)
+            outs[2 * k][at] = jnp.exp(matrix - down[at, k : k + 1])
+            outs[2 * k + 1][at] = jnp.exp(matrix - across[2 * k : 2 * k + 1])
+
+
 def tile_kernel(plan, n_cap, rows, width, *refs):
     refs = list(refs)
-    student_refs, teacher_refs = (refs.pop(0), refs.pop(0)), (refs.pop(0), refs.pop(0))
+    student_row, student_col, teacher_row, teacher_col, own_row, own_col = (refs.pop(0) for _ in range(6))
     blocks = take(refs, plan)
     captions = [refs.pop(0) for _ in range(n_cap)]
     tile_ref, send_ref, first_ref = refs
@@ -226,21 +239,22 @@
 
     lane = lax.broadcasted_iota(jnp.int32, (8, LANES), 1)[:1, :rows]
 
-    def finish(blocks, axes, order):
+    def finish(blocks, own_ref, axes, order):
         lines = load_slots(blocks, rows)
+        own = load_slots([own_ref[k] for k in range(own_ref.shape[0])], rows)
         index = jnp.concatenate([owner * rows + lane for owner in owners(axes, order)], axis=1)
         lse_s, lse_t = lines[0:1] + jnp.log(lines[1:2]), lines[2:3] + jnp.log(lines[3:4])
-        return stacked([lse_s, lse_t, index.astype(jnp.float32)])
-
-    down = columns_of(finish(blocks[0], ROW_AXES, ROW_ORDER))
-    across = finish(blocks[1], COL_AXES, COL_ORDER)
+        scale_s, scale_t = 0.5 * jnp.exp(own[0:1] - lse_s), 0.25 * jnp.exp(own[2:3] - lse_t)
+        return stacked([scale_s, scale_t, index.astype(jnp.float32)])
+
+    down = columns_of(finish(blocks[0], own_row, ROW_AXES, ROW_ORDER))
+    across = finish(blocks[1], own_col, COL_AXES, COL_ORDER)
     step = 64 if total % 64 == 0 else total
     for r in range(0, total, step):
         at = slice(r, r + step)
-        s, t = (jnp.concatenate([ref[at] for ref in pair], axis=1) for pair in (student_refs, teacher_refs))
-        grad = 0.5 * (jnp.exp(s - down[at, 0:1]) + jnp.exp(s - across[0:1]))
-        grad = grad - 0.25 * (jnp.exp(t - down[at, 1:2]) + jnp.exp(t - across[1:2]))
-        grad = grad - jnp.where(down[at, INDEX : INDEX + 1] == across[INDEX : INDEX + 1], 0.5, 0.0)
+        grad = student_row[at] * down[at, SCALE_S : SCALE_S + 1] + student_col[at] * across[SCALE_S : SCALE_S + 1]
+        less = teacher_row[at] * down[at, SCALE_T : SCALE_T + 1] + teacher_col[at] * across[SCALE_T : SCALE_T + 1]
+        grad = grad - less - jnp.where(down[at, INDEX : INDEX + 1] == across[INDEX : INDEX + 1], 0.5, 0.0)
         tile_ref[at] = grad.astype(jnp.bfloat16)
     send_ref[...] = tile_ref[:, count // 2 :]
     right = joined(captions, slice(0, width))
@@ -369,7 +383,7 @@
     student, teacher, row_head, lines, images = call(
         functools.partial(head_kernel, len(img), rows, width),
         [shape((total, head), f32)] * 2 + [row_shape, shape((8, head), f32), shape((total, width), bf16)],
-        img + ready,
+        ready + img,
         2 * total * head * (width + depth),
     )
     student_tail, teacher_tail, row_stats, col_stats = call(
@@ -380,6 +394,13 @@
     )
 
     images_other = swap(after(images, row_stats), "core", 1)
+    exps = call(
+        functools.partial(exp_kernel, rows),
+        [shape((total, columns), f32)] * 4,
+        [student, student_tail, teacher, teacher_tail, row_stats, col_stats],
+        40 * total * columns,
+    )
+    exps = list(exps)
     stats = [row_stats, col_stats]
     for row_names, col_names in zip(ROW_STAGES, COL_STAGES):
         plan, blocks = [], []
@@ -400,7 +421,7 @@
     tile, tile_send, image_first = call(
         functools.partial(tile_kernel, plan, len(cap), rows, width),
         [shape((total, columns), bf16), shape((total, columns // 2), bf16), shape((rows, width), bf16)],
-        [student, student_tail, teacher, teacher_tail] + blocks + cap,
+        exps + [row_stats, col_stats] + blocks + cap,
         2 * rows * columns * width,
     )
     tile_other = swap(tile_send, "core", 1)

time: 61.6 us -> 62.3 us (1.011)
  waiting for transfers between devices: 26.7 us -> 27.8 us
  starting transfers between devices: 27.2 us -> 26.5 us
    ppermute x22, waiting for transfers between devices: 26.7 us -> 27.8 us  [swap(): return lax.ppermute(value, axis, [(j, j ^ mask) for j in range(size)])]
    ppermute x22, starting transfers between devices: 27.2 us -> 26.5 us  [swap(): return lax.ppermute(value, axis, [(j, j ^ mask) for j in range(size)])]
    pallas_call x11 -> x12, Pallas kernels: 6.63 us -> 7.1 us  [call(): pl.pallas_call(kernel, out_shape=[out_space(out.shape, out.dtype) for out...]
  transfers between devices with their start and end apart: 22 -> 22, of which waited for: 10 -> 12; matrix products, arithmetic and copies ran while one was open for 0% -> 0% of each run, Pallas kernels for 4% -> 5%
where the time goes in v15:
time: 62.3 us; the launch traced here: 62.2 us
  waiting for transfers between devices  27.8 us (45%)
  starting transfers between devices  26.5 us (43%)
  Pallas kernels  7.1 us (11%)
  between operations  0.75 us (1%)
    ppermute x22, waiting for transfers between devices, swap(): return lax.ppermute(value, axis, [(j, j ^ mask) for j in range(size)])  27.8 us
    ppermute x22, starting transfers between devices, swap(): return lax.ppermute(value, axis, [(j, j ^ mask) for j in range(size)])  26.5 us
    pallas_call x12, Pallas kernels, call(): pl.pallas_call(kernel, out_shape=[out_space(out.shape, out.dtype) for out...  7.1 us
  transfers between devices with their start and end apart: 22, of which 12 were waited for; matrix products, arithmetic and copies ran while one was open for 0% of the time, Pallas kernels for 5%

profile of v15, /device:TPU:0, one launch (start us, length us, event | category | flops | bytes accessed | tf_op | source)
XLA Modules:
  0.0 62.2 jit_solution(16071221349699061209)
XLA Ops:
  0.6 1.2 %shard_map.59 = (bf16[80,1792]{1,0:T(8,128)(2,1)S(1)}, bf16[80,1792]{1,0:T(8,128)(2,1)S(1)}) custom-call(bf16[80,1024]{1,0:T(8,128)(2,1)} %image_s.1, bf16[80,768]{1,0:T(8,128)(2,1)} %image_t.1, bf16[80,1024]{1,0:T(8,128)(2,1)} %caption_s.1, bf16[80,768]{1,0:T(8,128)(2,1)} %caption_t.1), custom_call_target="tpu_custom_call" | custom-call | bytes 1146880 | tf_op jit(solution)/shard_map/pallas_call | solution.py:310
  1.8 3.1 %collective-permute-start.3 = (bf16[80,1792]{1,0:T(8,128)(2,1)S(1)}, bf16[80,1792]{1,0:T(8,128)(2,1)S(1)}, u32[]{:S(2)}, u32[]{:S(2)}) collective-permute-start(bf16[80,1792]{1,0:T(8,128)(2,1)S(1)} %get-tuple-element.40.refs_1_.refs_0_), channel_id=1, source_target_pairs={{0,1},{1,0},{2,3},{3,2},{4,5},{5,4},{6,7},{7,6},{8,9},{9,8},{10,11... | collective-permute-start | bytes 860168 | tf_op jit(solution)/shard_map/ppermute | solution.py:25
  4.9 2.6 %collective-permute-start.1 = (bf16[80,1792]{1,0:T(8,128)(2,1)S(1)}, bf16[80,1792]{1,0:T(8,128)(2,1)S(1)}, u32[]{:S(2)}, u32[]{:S(2)}) collective-permute-start(bf16[80,1792]{1,0:T(8,128)(2,1)S(1)} %get-tuple-element.38.refs_0_.refs_3_), channel_id=1, source_target_pairs={{0,2},{2,0},{1,3},{3,1},{4,6},{6,4},{5,7},{7,5},{8,10},{10,8},{9,1... | collective-permute-start | bytes 860168 | tf_op jit(solution)/shard_map/ppermute | solution.py:25
  7.5 1.6 %collective-permute-start = (bf16[80,1792]{1,0:T(8,128)(2,1)S(1)}, bf16[80,1792]{1,0:T(8,128)(2,1)S(1)}, u32[]{:S(2)}, u32[]{:S(2)}) collective-permute-start(bf16[80,1792]{1,0:T(8,128)(2,1)S(1)} %get-tuple-element.39), channel_id=1, source_target_pairs={{0,8},{8,0},{1,9},{9,1},{2,10},{10,2},{3,11},{11,3},{4,12},{12,4},... | collective-permute-start | bytes 860168 | tf_op jit(solution)/shard_map/ppermute | solution.py:25
  9.1 1.5 %collective-permute-start.2 = (bf16[80,1792]{1,0:T(8,128)(2,1)S(1)}, bf16[80,1792]{1,0:T(8,128)(2,1)S(1)}, u32[]{:S(2)}, u32[]{:S(2)}) collective-permute-start(bf16[80,1792]{1,0:T(8,128)(2,1)S(1)} %get-tuple-element.41), channel_id=1, source_target_pairs={{0,16},{16,0},{1,17},{17,1},{2,18},{18,2},{3,19},{19,3},{4,20},{20... | collective-permute-start | bytes 860168 | tf_op jit(solution)/shard_map/ppermute | solution.py:25
  10.6 7.2 %collective-permute-done.3.refs_0_ = bf16[80,1792]{1,0:T(8,128)(2,1)S(1)} collective-permute-done((bf16[80,1792]{1,0:T(8,128)(2,1)S(1)}, bf16[80,1792]{1,0:T(8,128)(2,1)S(1)}, u32[]{:S(2)}, u32[]{:S(2)}) %collective-permute-start.3) | collective-permute-done | bytes 286752 | tf_op jit(solution)/shard_map/ppermute | solution.py:25
  17.7 1.7 %collective-permute-start.4 = (bf16[80,1792]{1,0:T(8,128)(2,1)S(1)}, bf16[80,1792]{1,0:T(8,128)(2,1)S(1)}, u32[]{:S(2)}, u32[]{:S(2)}) collective-permute-start(bf16[80,1792]{1,0:T(8,128)(2,1)S(1)} %collective-permute-done.3.refs_0_), channel_id=1, source_target_pairs={{0,16},{16,0},{1,17},{17,1},{2,18},{18,2},{3,19},{19,3},{4,20},{20... | collective-permute-start | bytes 860168 | tf_op jit(solution)/shard_map/ppermute | solution.py:25
  19.4 0.8 %collective-permute-done.1.refs_4_.refs_1_ = bf16[80,1792]{1,0:T(8,128)(2,1)S(1)} collective-permute-done((bf16[80,1792]{1,0:T(8,128)(2,1)S(1)}, bf16[80,1792]{1,0:T(8,128)(2,1)S(1)}, u32[]{:S(2)}, u32[]{:S(2)}) %collective-permute-start.1) | collective-permute-done | bytes 286752 | tf_op jit(solution)/shard_map/ppermute | solution.py:25
  20.3 1.5 %collective-permute-start.5 = (bf16[80,1792]{1,0:T(8,128)(2,1)S(1)}, bf16[80,1792]{1,0:T(8,128)(2,1)S(1)}, u32[]{:S(2)}, u32[]{:S(2)}) collective-permute-start(bf16[80,1792]{1,0:T(8,128)(2,1)S(1)} %collective-permute-done.1.refs_4_.refs_1_), channel_id=1, source_target_pairs={{0,8},{8,0},{1,9},{9,1},{2,10},{10,2},{3,11},{11,3},{4,12},{12,4},... | collective-permute-start | bytes 860168 | tf_op jit(solution)/shard_map/ppermute | solution.py:25
  21.9 3.9 %collective-permute-done.4.refs_1_ = bf16[80,1792]{1,0:T(8,128)(2,1)S(1)} collective-permute-done((bf16[80,1792]{1,0:T(8,128)(2,1)S(1)}, bf16[80,1792]{1,0:T(8,128)(2,1)S(1)}, u32[]{:S(2)}, u32[]{:S(2)}) %collective-permute-start.4) | collective-permute-done | bytes 286752 | tf_op jit(solution)/shard_map/ppermute | solution.py:25
  25.8 1.1 %collective-permute-done.5.refs_6_.refs_3_ = bf16[80,1792]{1,0:T(8,128)(2,1)S(1)} collective-permute-done((bf16[80,1792]{1,0:T(8,128)(2,1)S(1)}, bf16[80,1792]{1,0:T(8,128)(2,1)S(1)}, u32[]{:S(2)}, u32[]{:S(2)}) %collective-permute-start.5) | collective-permute-done | bytes 286752 | tf_op jit(solution)/shard_map/ppermute | solution.py:25
  27.0 1.1 %shard_map.63 = (f32[320,384]{1,0:T(8,128)S(1)}, f32[320,384]{1,0:T(8,128)S(1)}, f32[2,8,128]{2,1,0:T(8,128)S(1)}, f32[8,384]{1,0:T(8,128)S(1)}, bf16[320,1024]{1,0:T(8,128)(2,1)S(1)}) custom-call(bf16[160,1792]{1,0:T(8,128)(2,1)S(1)} %shard_map.61.refs_0_.refs_10_, bf16[160,1792]{1,0:T(8,128)(2,1)S(1)} %shard_map.62.refs_1_.refs_11_, ...), custom_call_target="tpu_custom_call" | custom-call | flops 440401920 | bytes 4526080 | tf_op jit(solution)/shard_map/pallas_call | solution.py:310
  28.2 0.8 %collective-permute-done.7.refs_5_.refs_13_.refs_3_ = bf16[160,1792]{1,0:T(8,128)(2,1)S(1)} collective-permute-done((bf16[160,1792]{1,0:T(8,128)(2,1)S(1)}, bf16[160,1792]{1,0:T(8,128)(2,1)S(1)}, u32[]{:S(2)}, u32[]{:S(2)}) %collective-permute-start.7) | collective-permute-done | bytes 573472 | tf_op jit(solution)/shard_map/ppermute | solution.py:25
  29.0 0.9 %shard_map.64 = (f32[320,256]{1,0:T(8,128)S(1)}, f32[320,256]{1,0:T(8,128)S(1)}, f32[2,8,128]{2,1,0:T(8,128)S(1)}, f32[4,8,128]{2,1,0:T(8,128)S(1)}) custom-call(f32[2,8,128]{2,1,0:T(8,128)S(1)} %get-tuple-element.44.head_ref, f32[8,384]{1,0:T(8,128)S(1)} %get-tuple-element.45.lines_ref, bf16[320,1024]{1,0:T(8,128)(2,1)S(1)} %get-tuple-element.56.images, ...), custom_call_target="tpu_custom_call" | custom-call | flops 293601280 | bytes 3649536 | tf_op jit(solution)/shard_map/pallas_call | solution.py:310
  30.1 1.5 %collective-permute-start.10 = (f32[4,8,128]{2,1,0:T(8,128)S(1)}, f32[4,8,128]{2,1,0:T(8,128)S(1)}, u32[]{:S(2)}, u32[]{:S(2)}) collective-permute-start(f32[4,8,128]{2,1,0:T(8,128)S(1)} %get-tuple-element.51.col_ref.refs_2_.refs_5_), channel_id=1, source_target_pairs={{0,1},{1,0},{16,17},{17,16},{2,3},{3,2},{18,19},{19,18},{4,5},{5,4... | collective-permute-start | bytes 49160 | tf_op jit(solution)/shard_map/ppermute | solution.py:25
  31.6 1.5 %collective-permute-start.11 = (f32[4,8,128]{2,1,0:T(8,128)S(1)}, f32[4,8,128]{2,1,0:T(8,128)S(1)}, u32[]{:S(2)}, u32[]{:S(2)}) collective-permute-start(f32[4,8,128]{2,1,0:T(8,128)S(1)} %get-tuple-element.51.col_ref.refs_2_.refs_5_), channel_id=1, source_target_pairs={{0,16},{1,17},{16,0},{17,1},{2,18},{3,19},{18,2},{19,3},{4,20},{5,... | collective-permute-start | bytes 49160 | tf_op jit(solution)/shard_map/ppermute | solution.py:25
  33.6 1.5 %collective-permute-start.9 = (f32[2,8,128]{2,1,0:T(8,128)S(1)}, f32[2,8,128]{2,1,0:T(8,128)S(1)}, u32[]{:S(2)}, u32[]{:S(2)}) collective-permute-start(f32[2,8,128]{2,1,0:T(8,128)S(1)} %get-tuple-element.57.row_ref.refs_0_.refs_4_), channel_id=1, source_target_pairs={{0,8},{8,0},{1,9},{9,1},{2,10},{10,2},{3,11},{11,3},{4,12},{12,4},... | collective-permute-start | bytes 24584 | tf_op jit(solution)/shard_map/ppermute | solution.py:25
  35.1 2.2 %collective-permute-done.9.refs_1_ = f32[2,8,128]{2,1,0:T(8,128)S(1)} collective-permute-done((f32[2,8,128]{2,1,0:T(8,128)S(1)}, f32[2,8,128]{2,1,0:T(8,128)S(1)}, u32[]{:S(2)}, u32[]{:S(2)}) %collective-permute-start.9) | collective-permute-done | bytes 8224 | tf_op jit(solution)/shard_map/ppermute | solution.py:25
  37.9 1.6 %collective-permute-start.13 = (f32[2,8,128]{2,1,0:T(8,128)S(1)}, f32[2,8,128]{2,1,0:T(8,128)S(1)}, u32[]{:S(2)}, u32[]{:S(2)}) collective-permute-start(f32[2,8,128]{2,1,0:T(8,128)S(1)} %get-tuple-element.58.refs_6_), channel_id=1, source_target_pairs={{0,2},{2,0},{1,3},{3,1},{4,6},{6,4},{5,7},{7,5},{8,10},{10,8},{9,1... | collective-permute-start | bytes 24584 | tf_op jit(solution)/shard_map/ppermute | solution.py:25
  40.1 2.4 %collective-permute-done.13.refs_7_ = f32[2,8,128]{2,1,0:T(8,128)S(1)} collective-permute-done((f32[2,8,128]{2,1,0:T(8,128)S(1)}, f32[2,8,128]{2,1,0:T(8,128)S(1)}, u32[]{:S(2)}, u32[]{:S(2)}) %collective-permute-start.13) | collective-permute-done | bytes 8224 | tf_op jit(solution)/shard_map/ppermute | solution.py:25
  42.5 0.9 %shard_map.67 = (bf16[320,640]{1,0:T(8,128)(2,1)S(1)}, bf16[320,320]{1,0:T(8,128)(2,1)S(1)}, bf16[80,1024]{1,0:T(8,128)(2,1)S(1)}) custom-call(f32[320,640]{1,0:T(8,128)S(1)} %get-tuple-element.52.refs_0_, f32[320,640]{1,0:T(8,128)S(1)} %get-tuple-element.53.refs_1_, f32[320,640]{1,0:T(8,128)S(1)} %get-tuple-element.54.refs_2_, ...), custom_call_target="tpu_custom_call" | custom-call | flops 104857600 | bytes 6422528 | tf_op jit(solution)/shard_map/pallas_call | solution.py:310
  43.5 1.6 %collective-permute-start.20 = (bf16[80,1024]{1,0:T(8,128)(2,1)S(1)}, bf16[80,1024]{1,0:T(8,128)(2,1)S(1)}, u32[]{:S(2)}, u32[]{:S(2)}) collective-permute-start(bf16[80,1024]{1,0:T(8,128)(2,1)S(1)} %get-tuple-element.69), channel_id=1, source_target_pairs={{0,8},{8,0},{1,9},{9,1},{2,10},{10,2},{3,11},{11,3},{4,12},{12,4},... | collective-permute-start | bytes 491528 | tf_op jit(solution)/shard_map/ppermute | solution.py:25
  45.6 0.6 collective-permute-start.19
  46.2 0.9 %shard_map.68 = (f32[80,1024]{1,0:T(8,128)S(1)}, bf16[80,1024]{1,0:T(8,128)(2,1)S(1)}, f32[80,1024]{1,0:T(8,128)S(1)}, bf16[80,1024]{1,0:T(8,128)(2,1)S(1)}) custom-call(bf16[320,640]{1,0:T(8,128)(2,1)S(1)} %get-tuple-element.60.tile_ref, bf16[320,320]{1,0:T(8,128)(2,1)S(1)} %collective-permute-done.15.tile_other, ...), custom_call_target="tpu_custom_call" | custom-call | flops 419430400 | bytes 2908160 | tf_op jit(solution)/shard_map/pallas_call | solution.py:310
  47.0 1.1 %collective-permute-start.17 = (bf16[80,1024]{1,0:T(8,128)(2,1)S(1)}, bf16[80,1024]{1,0:T(8,128)(2,1)S(1)}, u32[]{:S(2)}, u32[]{:S(2)}) collective-permute-start(bf16[80,1024]{1,0:T(8,128)(2,1)S(1)} %get-tuple-element.65), channel_id=1, source_target_pairs={{0,16},{16,0},{1,17},{17,1},{2,18},{18,2},{3,19},{19,3},{4,20},{20... | collective-permute-start | bytes 491528 | tf_op jit(solution)/shard_map/ppermute | solution.py:25
  48.2 2.3 %collective-permute-done.20 = bf16[80,1024]{1,0:T(8,128)(2,1)S(1)} collective-permute-done((bf16[80,1024]{1,0:T(8,128)(2,1)S(1)}, bf16[80,1024]{1,0:T(8,128)(2,1)S(1)}, u32[]{:S(2)}, u32[]{:S(2)}) %collective-permute-start.20) | collective-permute-done | bytes 163872 | tf_op jit(solution)/shard_map/ppermute | solution.py:25
  50.6 1.6 %collective-permute-start.21 = (bf16[80,1024]{1,0:T(8,128)(2,1)S(1)}, bf16[80,1024]{1,0:T(8,128)(2,1)S(1)}, u32[]{:S(2)}, u32[]{:S(2)}) collective-permute-start(bf16[80,1024]{1,0:T(8,128)(2,1)S(1)} %add_convert_fusion), channel_id=1, source_target_pairs={{0,2},{2,0},{1,3},{3,1},{4,6},{6,4},{5,7},{7,5},{8,10},{10,8},{9,1... | collective-permute-start | bytes 491528 | tf_op jit(solution)/shard_map/ppermute | solution.py:25
  52.2 0.8 %collective-permute-start.16 = (bf16[80,1024]{1,0:T(8,128)(2,1)S(1)}, bf16[80,1024]{1,0:T(8,128)(2,1)S(1)}, u32[]{:S(2)}, u32[]{:S(2)}) collective-permute-start(bf16[80,1024]{1,0:T(8,128)(2,1)S(1)} %get-tuple-element.63), channel_id=1, source_target_pairs={{0,16},{16,0},{1,17},{17,1},{2,18},{18,2},{3,19},{19,3},{4,20},{20... | collective-permute-start | bytes 491528 | tf_op jit(solution)/shard_map/ppermute | solution.py:25
  53.1 1.7 %collective-permute-start.18 = (bf16[80,1024]{1,0:T(8,128)(2,1)S(1)}, bf16[80,1024]{1,0:T(8,128)(2,1)S(1)}, u32[]{:S(2)}, u32[]{:S(2)}) collective-permute-start(bf16[80,1024]{1,0:T(8,128)(2,1)S(1)} %add_convert_fusion.1), channel_id=1, source_target_pairs={{0,1},{1,0},{2,3},{3,2},{4,5},{5,4},{6,7},{7,6},{8,9},{9,8},{10,11... | collective-permute-start | bytes 491528 | tf_op jit(solution)/shard_map/ppermute | solution.py:25
  54.8 5.6 %collective-permute-done.21.refs_5_ = bf16[80,1024]{1,0:T(8,128)(2,1)S(1)} collective-permute-done((bf16[80,1024]{1,0:T(8,128)(2,1)S(1)}, bf16[80,1024]{1,0:T(8,128)(2,1)S(1)}, u32[]{:S(2)}, u32[]{:S(2)}) %collective-permute-start.21) | collective-permute-done | bytes 163872 | tf_op jit(solution)/shard_map/ppermute | solution.py:25
  60.5 0.8 %collective-permute-done.18.refs_2_ = bf16[80,1024]{1,0:T(8,128)(2,1)S(1)} collective-permute-done((bf16[80,1024]{1,0:T(8,128)(2,1)S(1)}, bf16[80,1024]{1,0:T(8,128)(2,1)S(1)}, u32[]{:S(2)}, u32[]{:S(2)}) %collective-permute-start.18) | collective-permute-done | bytes 163872 | tf_op jit(solution)/shard_map/ppermute | solution.py:25
  61.3 0.9 %shard_map.70 = (f32[80,1024]{1,0:T(8,128)}, f32[80,1024]{1,0:T(8,128)}) custom-call(f32[80,1024]{1,0:T(8,128)S(1)} %get-tuple-element.62.refs_0_, bf16[80,1024]{1,0:T(8,128)(2,1)S(1)} %collective-permute-done.16.refs_1_, bf16[80,1024]{1,0:T(8,128)(2,1)S(1)} %collective-permute-done.18.refs_2_, f32[80,1024]{1,0:T(8,128)S(1)} %get-tuple-element.66.refs_3_, ...), custom_call_target="tpu_custom_call" | custom-call | bytes 1966080 | tf_op jit(solution)/shard_map/pallas_call | solution.py:310
  (26 shorter events, 2.9 us)
Async XLA Ops:
  1.8 16.0 %collective-permute-start.3 = (bf16[80,1792]{1,0:T(8,128)(2,1)S(1)}, bf16[80,1792]{1,0:T(8,128)(2,1)S(1)}, u32[]{:S(2)}, u32[]{:S(2)}) collective-permute-start(bf16[80,1792]{1,0:T(8,128)(2,1)S(1)} %get-tuple-element.40.refs_1_.refs_0_), channel_id=1, source_target_pairs={{0,1},{1,0},{2,3},{3,2},{4,5},{5,4},{6,7},{7,6},{8,9},{9,8},{10,11... | collective-permute-start | bytes 860168 | tf_op jit(solution)/shard_map/ppermute | solution.py:25
  4.9 15.4 %collective-permute-start.1 = (bf16[80,1792]{1,0:T(8,128)(2,1)S(1)}, bf16[80,1792]{1,0:T(8,128)(2,1)S(1)}, u32[]{:S(2)}, u32[]{:S(2)}) collective-permute-start(bf16[80,1792]{1,0:T(8,128)(2,1)S(1)} %get-tuple-element.38.refs_0_.refs_3_), channel_id=1, source_target_pairs={{0,2},{2,0},{1,3},{3,1},{4,6},{6,4},{5,7},{7,5},{8,10},{10,8},{9,1... | collective-permute-start | bytes 860168 | tf_op jit(solution)/shard_map/ppermute | solution.py:25
  7.5 14.2 %collective-permute-start = (bf16[80,1792]{1,0:T(8,128)(2,1)S(1)}, bf16[80,1792]{1,0:T(8,128)(2,1)S(1)}, u32[]{:S(2)}, u32[]{:S(2)}) collective-permute-start(bf16[80,1792]{1,0:T(8,128)(2,1)S(1)} %get-tuple-element.39), channel_id=1, source_target_pairs={{0,8},{8,0},{1,9},{9,1},{2,10},{10,2},{3,11},{11,3},{4,12},{12,4},... | collective-permute-start | bytes 860168 | tf_op jit(solution)/shard_map/ppermute | solution.py:25
  9.1 12.7 %collective-permute-start.2 = (bf16[80,1792]{1,0:T(8,128)(2,1)S(1)}, bf16[80,1792]{1,0:T(8,128)(2,1)S(1)}, u32[]{:S(2)}, u32[]{:S(2)}) collective-permute-start(bf16[80,1792]{1,0:T(8,128)(2,1)S(1)} %get-tuple-element.41), channel_id=1, source_target_pairs={{0,16},{16,0},{1,17},{17,1},{2,18},{18,2},{3,19},{19,3},{4,20},{20... | collective-permute-start | bytes 860168 | tf_op jit(solution)/shard_map/ppermute | solution.py:25
  17.7 8.0 %collective-permute-start.4 = (bf16[80,1792]{1,0:T(8,128)(2,1)S(1)}, bf16[80,1792]{1,0:T(8,128)(2,1)S(1)}, u32[]{:S(2)}, u32[]{:S(2)}) collective-permute-start(bf16[80,1792]{1,0:T(8,128)(2,1)S(1)} %collective-permute-done.3.refs_0_), channel_id=1, source_target_pairs={{0,16},{16,0},{1,17},{17,1},{2,18},{18,2},{3,19},{19,3},{4,20},{20... | collective-permute-start | bytes 860168 | tf_op jit(solution)/shard_map/ppermute | solution.py:25
  20.3 6.6 %collective-permute-start.5 = (bf16[80,1792]{1,0:T(8,128)(2,1)S(1)}, bf16[80,1792]{1,0:T(8,128)(2,1)S(1)}, u32[]{:S(2)}, u32[]{:S(2)}) collective-permute-start(bf16[80,1792]{1,0:T(8,128)(2,1)S(1)} %collective-permute-done.1.refs_4_.refs_1_), channel_id=1, source_target_pairs={{0,8},{8,0},{1,9},{9,1},{2,10},{10,2},{3,11},{11,3},{4,12},{12,4},... | collective-permute-start | bytes 860168 | tf_op jit(solution)/shard_map/ppermute | solution.py:25
  21.8 5.2 %collective-permute-start.6 = (bf16[160,1792]{1,0:T(8,128)(2,1)S(1)}, bf16[160,1792]{1,0:T(8,128)(2,1)S(1)}, u32[]{:S(2)}, u32[]{:S(2)}) collective-permute-start(bf16[160,1792]{1,0:T(8,128)(2,1)S(1)} %shard_map.61.refs_0_.refs_10_), channel_id=1, source_target_pairs={{0,4},{4,0},{1,5},{5,1},{2,6},{6,2},{3,7},{7,3},{8,12},{12,8},{9,1... | collective-permute-start | bytes 1720328 | tf_op jit(solution)/shard_map/ppermute | solution.py:25
  26.9 2.0 %collective-permute-start.7 = (bf16[160,1792]{1,0:T(8,128)(2,1)S(1)}, bf16[160,1792]{1,0:T(8,128)(2,1)S(1)}, u32[]{:S(2)}, u32[]{:S(2)}) collective-permute-start(bf16[160,1792]{1,0:T(8,128)(2,1)S(1)} %shard_map.62.refs_1_.refs_11_), channel_id=1, source_target_pairs={{0,4},{4,0},{1,5},{5,1},{2,6},{6,2},{3,7},{7,3},{8,12},{12,8},{9,1... | collective-permute-start | bytes 1720328 | tf_op jit(solution)/shard_map/ppermute | solution.py:25
  29.9 5.2 %collective-permute-start.8 = (bf16[320,1024]{1,0:T(8,128)(2,1)S(1)}, bf16[320,1024]{1,0:T(8,128)(2,1)S(1)}, u32[]{:S(2)}, u32[]{:S(2)}) collective-permute-start(bf16[320,1024]{1,0:T(8,128)(2,1)S(1)} %get-tuple-element.56.images), channel_id=1, source_target_pairs={{0,4},{4,0},{1,5},{5,1},{2,6},{6,2},{3,7},{7,3},{8,12},{12,8},{9,1... | collective-permute-start | bytes 1966088 | tf_op jit(solution)/shard_map/ppermute | solution.py:25
  30.1 7.2 %collective-permute-start.10 = (f32[4,8,128]{2,1,0:T(8,128)S(1)}, f32[4,8,128]{2,1,0:T(8,128)S(1)}, u32[]{:S(2)}, u32[]{:S(2)}) collective-permute-start(f32[4,8,128]{2,1,0:T(8,128)S(1)} %get-tuple-element.51.col_ref.refs_2_.refs_5_), channel_id=1, source_target_pairs={{0,1},{1,0},{16,17},{17,16},{2,3},{3,2},{18,19},{19,18},{4,5},{5,4... | collective-permute-start | bytes 49160 | tf_op jit(solution)/shard_map/ppermute | solution.py:25
  31.6 5.7 %collective-permute-start.11 = (f32[4,8,128]{2,1,0:T(8,128)S(1)}, f32[4,8,128]{2,1,0:T(8,128)S(1)}, u32[]{:S(2)}, u32[]{:S(2)}) collective-permute-start(f32[4,8,128]{2,1,0:T(8,128)S(1)} %get-tuple-element.51.col_ref.refs_2_.refs_5_), channel_id=1, source_target_pairs={{0,16},{1,17},{16,0},{17,1},{2,18},{3,19},{18,2},{19,3},{4,20},{5,... | collective-permute-start | bytes 49160 | tf_op jit(solution)/shard_map/ppermute | solution.py:25
  33.1 4.6 %collective-permute-start.12 = (f32[4,8,128]{2,1,0:T(8,128)S(1)}, f32[4,8,128]{2,1,0:T(8,128)S(1)}, u32[]{:S(2)}, u32[]{:S(2)}) collective-permute-start(f32[4,8,128]{2,1,0:T(8,128)S(1)} %get-tuple-element.51.col_ref.refs_2_.refs_5_), channel_id=1, source_target_pairs={{0,17},{1,16},{16,1},{17,0},{2,19},{3,18},{18,3},{19,2},{4,21},{5,... | collective-permute-start | bytes 49160 | tf_op jit(solution)/shard_map/ppermute | solution.py:25
  33.6 3.7 %collective-permute-start.9 = (f32[2,8,128]{2,1,0:T(8,128)S(1)}, f32[2,8,128]{2,1,0:T(8,128)S(1)}, u32[]{:S(2)}, u32[]{:S(2)}) collective-permute-start(f32[2,8,128]{2,1,0:T(8,128)S(1)} %get-tuple-element.57.row_ref.refs_0_.refs_4_), channel_id=1, source_target_pairs={{0,8},{8,0},{1,9},{9,1},{2,10},{10,2},{3,11},{11,3},{4,12},{12,4},... | collective-permute-start | bytes 24584 | tf_op jit(solution)/shard_map/ppermute | solution.py:25
  37.8 4.7 %collective-permute-start.14 = (f32[4,8,128]{2,1,0:T(8,128)S(1)}, f32[4,8,128]{2,1,0:T(8,128)S(1)}, u32[]{:S(2)}, u32[]{:S(2)}) collective-permute-start(f32[4,8,128]{2,1,0:T(8,128)S(1)} %get-tuple-element.59.refs_8_), channel_id=1, source_target_pairs={{0,4},{4,0},{1,5},{5,1},{2,6},{6,2},{3,7},{7,3},{8,12},{12,8},{9,1... | collective-permute-start | bytes 49160 | tf_op jit(solution)/shard_map/ppermute | solution.py:25
  37.9 4.6 %collective-permute-start.13 = (f32[2,8,128]{2,1,0:T(8,128)S(1)}, f32[2,8,128]{2,1,0:T(8,128)S(1)}, u32[]{:S(2)}, u32[]{:S(2)}) collective-permute-start(f32[2,8,128]{2,1,0:T(8,128)S(1)} %get-tuple-element.58.refs_6_), channel_id=1, source_target_pairs={{0,2},{2,0},{1,3},{3,1},{4,6},{6,4},{5,7},{7,5},{8,10},{10,8},{9,1... | collective-permute-start | bytes 24584 | tf_op jit(solution)/shard_map/ppermute | solution.py:25
  43.4 2.8 %collective-permute-start.15 = (bf16[320,320]{1,0:T(8,128)(2,1)S(1)}, bf16[320,320]{1,0:T(8,128)(2,1)S(1)}, u32[]{:S(2)}, u32[]{:S(2)}) collective-permute-start(bf16[320,320]{1,0:T(8,128)(2,1)S(1)} %get-tuple-element.61), channel_id=1, source_target_pairs={{0,4},{4,0},{1,5},{5,1},{2,6},{6,2},{3,7},{7,3},{8,12},{12,8},{9,1... | collective-permute-start | bytes 614408 | tf_op jit(solution)/shard_map/ppermute | solution.py:25
  43.5 7.1 %collective-permute-start.20 = (bf16[80,1024]{1,0:T(8,128)(2,1)S(1)}, bf16[80,1024]{1,0:T(8,128)(2,1)S(1)}, u32[]{:S(2)}, u32[]{:S(2)}) collective-permute-start(bf16[80,1024]{1,0:T(8,128)(2,1)S(1)} %get-tuple-element.69), channel_id=1, source_target_pairs={{0,8},{8,0},{1,9},{9,1},{2,10},{10,2},{3,11},{11,3},{4,12},{12,4},... | collective-permute-start | bytes 491528 | tf_op jit(solution)/shard_map/ppermute | solution.py:25
  45.6 9.3 %collective-permute-start.19 = (bf16[80,1024]{1,0:T(8,128)(2,1)S(1)}, bf16[80,1024]{1,0:T(8,128)(2,1)S(1)}, u32[]{:S(2)}, u32[]{:S(2)}) collective-permute-start(bf16[80,1024]{1,0:T(8,128)(2,1)S(1)} %get-tuple-element.67), channel_id=1, source_target_pairs={{0,8},{8,0},{1,9},{9,1},{2,10},{10,2},{3,11},{11,3},{4,12},{12,4},... | collective-permute-start | bytes 491528 | tf_op jit(solution)/shard_map/ppermute | solution.py:25
  47.0 6.1 %collective-permute-start.17 = (bf16[80,1024]{1,0:T(8,128)(2,1)S(1)}, bf16[80,1024]{1,0:T(8,128)(2,1)S(1)}, u32[]{:S(2)}, u32[]{:S(2)}) collective-permute-start(bf16[80,1024]{1,0:T(8,128)(2,1)S(1)} %get-tuple-element.65), channel_id=1, source_target_pairs={{0,16},{16,0},{1,17},{17,1},{2,18},{18,2},{3,19},{19,3},{4,20},{20... | collective-permute-start | bytes 491528 | tf_op jit(solution)/shard_map/ppermute | solution.py:25
  50.6 9.9 %collective-permute-start.21 = (bf16[80,1024]{1,0:T(8,128)(2,1)S(1)}, bf16[80,1024]{1,0:T(8,128)(2,1)S(1)}, u32[]{:S(2)}, u32[]{:S(2)}) collective-permute-start(bf16[80,1024]{1,0:T(8,128)(2,1)S(1)} %add_convert_fusion), channel_id=1, source_target_pairs={{0,2},{2,0},{1,3},{3,1},{4,6},{6,4},{5,7},{7,5},{8,10},{10,8},{9,1... | collective-permute-start | bytes 491528 | tf_op jit(solution)/shard_map/ppermute | solution.py:25
  52.2 8.3 %collective-permute-start.16 = (bf16[80,1024]{1,0:T(8,128)(2,1)S(1)}, bf16[80,1024]{1,0:T(8,128)(2,1)S(1)}, u32[]{:S(2)}, u32[]{:S(2)}) collective-permute-start(bf16[80,1024]{1,0:T(8,128)(2,1)S(1)} %get-tuple-element.63), channel_id=1, source_target_pairs={{0,16},{16,0},{1,17},{17,1},{2,18},{18,2},{3,19},{19,3},{4,20},{20... | collective-permute-start | bytes 491528 | tf_op jit(solution)/shard_map/ppermute | solution.py:25
  53.1 8.2 %collective-permute-start.18 = (bf16[80,1024]{1,0:T(8,128)(2,1)S(1)}, bf16[80,1024]{1,0:T(8,128)(2,1)S(1)}, u32[]{:S(2)}, u32[]{:S(2)}) collective-permute-start(bf16[80,1024]{1,0:T(8,128)(2,1)S(1)} %add_convert_fusion.1), channel_id=1, source_target_pairs={{0,1},{1,0},{2,3},{3,2},{4,5},{5,4},{6,7},{7,6},{8,9},{9,8},{10,11... | collective-permute-start | bytes 491528 | tf_op jit(solution)/shard_map/ppermute | solution.py:25

commit v16 on v14

--- a/solution.py
+++ b/solution.py
@@ -189,8 +189,8 @@
     return jnp.where(even, peak, total)
 
 
-def merged_blocks(mine, others, distances):
-    blocks = [mine[k] for k in range(mine.shape[0])]
+def merged_blocks(mine, others, distances, limit):
+    blocks = [mine[k] for k in range(min(mine.shape[0], limit))]
     for other, distance in zip(others, distances):
         terms = [other[k ^ (distance // 2)] for k in range(len(blocks))]
         if distance % 2:
@@ -199,27 +199,27 @@
     return blocks
 
 
-def take(refs, plan):
+def take(refs, plan, limits):
     result = []
-    for distances in plan:
+    for distances, limit in zip(plan, limits):
         mine, others = refs[0], refs[1 : 1 + len(distances)]
         del refs[: 1 + len(distances)]
-        result.append(merged_blocks(mine, others, distances))
+        result.append(merged_blocks(mine, others, distances, limit))
     return result
 
 
 def merge_kernel(plan, *refs):
     refs = list(refs)
-    results = take(refs, plan)
+    results = take(refs, plan, [ref.shape[0] for ref in refs[-2:]])
     for out, blocks in zip(refs, results):
-        for s, block in enumerate(blocks):
-            out[s] = block
-
-
-def tile_kernel(plan, n_cap, rows, width, *refs):
+        for s in range(out.shape[0]):
+            out[s] = blocks[s] if s < len(blocks) else jnp.zeros_like(blocks[0])
+
+
+def tile_kernel(plan, limits, n_cap, rows, width, *refs):
     refs = list(refs)
     student_refs, teacher_refs = (refs.pop(0), refs.pop(0)), (refs.pop(0), refs.pop(0))
-    blocks = take(refs, plan)
+    blocks = take(refs, plan, limits)
     captions = [refs.pop(0) for _ in range(n_cap)]
     tile_ref, send_ref, first_ref = refs
     total, count = tile_ref.shape
@@ -389,7 +389,8 @@
             blocks += [block] + [swap(block, names, mask) for mask, _ in others]
         if row_names != ROW_STAGES[-1]:
             blocks[0] = after(blocks[0], images_other)
-            stats = call(functools.partial(merge_kernel, plan), [row_shape, col_shape], blocks)
+            row_wide = shape((max(n_img // 2, n_cap // 2), 8, LANES), f32)
+            stats = call(functools.partial(merge_kernel, plan), [row_wide, col_shape], blocks)
 
     image_blocks = [(h, c) for h in range(ilo) for c in range(chi)]
     caption_blocks = [(h, c) for c in range(clo) for h in range(ihi)]
@@ -398,7 +399,7 @@
         return [shape((rows, width), bf16 if h else f32) for h, _ in blocks]
 
     tile, tile_send, image_first = call(
-        functools.partial(tile_kernel, plan, len(cap), rows, width),
+        functools.partial(tile_kernel, plan, (n_img // 2, n_cap // 2), len(cap), rows, width),
         [shape((total, columns), bf16), shape((total, columns // 2), bf16), shape((rows, width), bf16)],
         [student, student_tail, teacher, teacher_tail] + blocks + cap,
         2 * rows * columns * width,

time: 61.6 us -> 61.6 us (level)
  no operation moved by 1% of the time
where the time goes in v16:
time: 61.6 us; the launch traced here: 61.4 us
  starting transfers between devices  27.2 us (44%)
  waiting for transfers between devices  26.8 us (44%)
  Pallas kernels  6.63 us (11%)
  between operations  0.75 us (1%)
    ppermute x22, starting transfers between devices, swap(): return lax.ppermute(value, axis, [(j, j ^ mask) for j in range(size)])  27.2 us
    ppermute x22, waiting for transfers between devices, swap(): return lax.ppermute(value, axis, [(j, j ^ mask) for j in range(size)])  26.8 us
    pallas_call x11, Pallas kernels, call(): pl.pallas_call(kernel, out_shape=[out_space(out.shape, out.dtype) for out...  6.63 us
  transfers between devices with their start and end apart: 22, of which 10 were waited for; matrix products, arithmetic and copies ran while one was open for 0% of the time, Pallas kernels for 4%

profile of v16, /device:TPU:0, one launch (start us, length us, event | category | flops | bytes accessed | tf_op | source)
XLA Modules:
  0.0 61.4 jit_solution(10275970019446656069)
XLA Ops:
  0.6 1.2 %shard_map.59 = (bf16[80,1792]{1,0:T(8,128)(2,1)S(1)}, bf16[80,1792]{1,0:T(8,128)(2,1)S(1)}) custom-call(bf16[80,1024]{1,0:T(8,128)(2,1)} %image_s.1, bf16[80,768]{1,0:T(8,128)(2,1)} %image_t.1, bf16[80,1024]{1,0:T(8,128)(2,1)} %caption_s.1, bf16[80,768]{1,0:T(8,128)(2,1)} %caption_t.1), custom_call_target="tpu_custom_call" | custom-call | bytes 1146880 | tf_op jit(solution)/shard_map/pallas_call | solution.py:296
  1.8 3.1 %collective-permute-start.4 = (bf16[80,1792]{1,0:T(8,128)(2,1)S(1)}, bf16[80,1792]{1,0:T(8,128)(2,1)S(1)}, u32[]{:S(2)}, u32[]{:S(2)}) collective-permute-start(bf16[80,1792]{1,0:T(8,128)(2,1)S(1)} %get-tuple-element.36.refs_1_.refs_0_), channel_id=1, source_target_pairs={{0,1},{1,0},{2,3},{3,2},{4,5},{5,4},{6,7},{7,6},{8,9},{9,8},{10,11... | collective-permute-start | bytes 860168 | tf_op jit(solution)/shard_map/ppermute | solution.py:25
  4.9 2.6 %collective-permute-start = (bf16[80,1792]{1,0:T(8,128)(2,1)S(1)}, bf16[80,1792]{1,0:T(8,128)(2,1)S(1)}, u32[]{:S(2)}, u32[]{:S(2)}) collective-permute-start(bf16[80,1792]{1,0:T(8,128)(2,1)S(1)} %get-tuple-element.33.refs_0_), channel_id=1, source_target_pairs={{0,2},{2,0},{1,3},{3,1},{4,6},{6,4},{5,7},{7,5},{8,10},{10,8},{9,1... | collective-permute-start | bytes 860168 | tf_op jit(solution)/shard_map/ppermute | solution.py:25
  7.5 1.6 %collective-permute-start.1 = (bf16[80,1792]{1,0:T(8,128)(2,1)S(1)}, bf16[80,1792]{1,0:T(8,128)(2,1)S(1)}, u32[]{:S(2)}, u32[]{:S(2)}) collective-permute-start(bf16[80,1792]{1,0:T(8,128)(2,1)S(1)} %get-tuple-element.35), channel_id=1, source_target_pairs={{0,8},{8,0},{1,9},{9,1},{2,10},{10,2},{3,11},{11,3},{4,12},{12,4},... | collective-permute-start | bytes 860168 | tf_op jit(solution)/shard_map/ppermute | solution.py:25
  9.1 1.5 %collective-permute-start.3 = (bf16[80,1792]{1,0:T(8,128)(2,1)S(1)}, bf16[80,1792]{1,0:T(8,128)(2,1)S(1)}, u32[]{:S(2)}, u32[]{:S(2)}) collective-permute-start(bf16[80,1792]{1,0:T(8,128)(2,1)S(1)} %get-tuple-element.37), channel_id=1, source_target_pairs={{0,16},{16,0},{1,17},{17,1},{2,18},{18,2},{3,19},{19,3},{4,20},{20... | collective-permute-start | bytes 860168 | tf_op jit(solution)/shard_map/ppermute | solution.py:25
  10.6 7.2 %collective-permute-done.4.refs_0_ = bf16[80,1792]{1,0:T(8,128)(2,1)S(1)} collective-permute-done((bf16[80,1792]{1,0:T(8,128)(2,1)S(1)}, bf16[80,1792]{1,0:T(8,128)(2,1)S(1)}, u32[]{:S(2)}, u32[]{:S(2)}) %collective-permute-start.4) | collective-permute-done | bytes 286752 | tf_op jit(solution)/shard_map/ppermute | solution.py:25
  17.7 1.7 %collective-permute-start.5 = (bf16[80,1792]{1,0:T(8,128)(2,1)S(1)}, bf16[80,1792]{1,0:T(8,128)(2,1)S(1)}, u32[]{:S(2)}, u32[]{:S(2)}) collective-permute-start(bf16[80,1792]{1,0:T(8,128)(2,1)S(1)} %collective-permute-done.4.refs_0_), channel_id=1, source_target_pairs={{0,16},{16,0},{1,17},{17,1},{2,18},{18,2},{3,19},{19,3},{4,20},{20... | collective-permute-start | bytes 860168 | tf_op jit(solution)/shard_map/ppermute | solution.py:25
  19.4 0.8 %collective-permute-done.refs_1_ = bf16[80,1792]{1,0:T(8,128)(2,1)S(1)} collective-permute-done((bf16[80,1792]{1,0:T(8,128)(2,1)S(1)}, bf16[80,1792]{1,0:T(8,128)(2,1)S(1)}, u32[]{:S(2)}, u32[]{:S(2)}) %collective-permute-start) | collective-permute-done | bytes 286752 | tf_op jit(solution)/shard_map/ppermute | solution.py:25
  20.3 1.5 %collective-permute-start.2 = (bf16[80,1792]{1,0:T(8,128)(2,1)S(1)}, bf16[80,1792]{1,0:T(8,128)(2,1)S(1)}, u32[]{:S(2)}, u32[]{:S(2)}) collective-permute-start(bf16[80,1792]{1,0:T(8,128)(2,1)S(1)} %collective-permute-done.refs_1_), channel_id=1, source_target_pairs={{0,8},{8,0},{1,9},{9,1},{2,10},{10,2},{3,11},{11,3},{4,12},{12,4},... | collective-permute-start | bytes 860168 | tf_op jit(solution)/shard_map/ppermute | solution.py:25
  21.9 3.9 %collective-permute-done.5.refs_1_ = bf16[80,1792]{1,0:T(8,128)(2,1)S(1)} collective-permute-done((bf16[80,1792]{1,0:T(8,128)(2,1)S(1)}, bf16[80,1792]{1,0:T(8,128)(2,1)S(1)}, u32[]{:S(2)}, u32[]{:S(2)}) %collective-permute-start.5) | collective-permute-done | bytes 286752 | tf_op jit(solution)/shard_map/ppermute | solution.py:25
  25.8 1.1 %collective-permute-done.2.refs_3_ = bf16[80,1792]{1,0:T(8,128)(2,1)S(1)} collective-permute-done((bf16[80,1792]{1,0:T(8,128)(2,1)S(1)}, bf16[80,1792]{1,0:T(8,128)(2,1)S(1)}, u32[]{:S(2)}, u32[]{:S(2)}) %collective-permute-start.2) | collective-permute-done | bytes 286752 | tf_op jit(solution)/shard_map/ppermute | solution.py:25
  27.0 1.1 %shard_map.63 = (f32[320,384]{1,0:T(8,128)S(1)}, f32[320,384]{1,0:T(8,128)S(1)}, f32[2,8,128]{2,1,0:T(8,128)S(1)}, f32[8,384]{1,0:T(8,128)S(1)}, bf16[320,1024]{1,0:T(8,128)(2,1)S(1)}) custom-call(bf16[80,1792]{1,0:T(8,128)(2,1)S(1)} %get-tuple-element.33.refs_0_, bf16[80,1792]{1,0:T(8,128)(2,1)S(1)} %collective-permute-done.refs_1_, ...), custom_call_target="tpu_custom_call" | custom-call | flops 440401920 | bytes 4526080 | tf_op jit(solution)/shard_map/pallas_call | solution.py:296
  28.2 0.8 %collective-permute-done.7.refs_5_.refs_11_.refs_3_ = bf16[160,1792]{1,0:T(8,128)(2,1)S(1)} collective-permute-done((bf16[160,1792]{1,0:T(8,128)(2,1)S(1)}, bf16[160,1792]{1,0:T(8,128)(2,1)S(1)}, u32[]{:S(2)}, u32[]{:S(2)}) %collective-permute-start.7) | collective-permute-done | bytes 573472 | tf_op jit(solution)/shard_map/ppermute | solution.py:25
  29.0 0.9 %shard_map.64 = (f32[320,256]{1,0:T(8,128)S(1)}, f32[320,256]{1,0:T(8,128)S(1)}, f32[2,8,128]{2,1,0:T(8,128)S(1)}, f32[4,8,128]{2,1,0:T(8,128)S(1)}) custom-call(f32[2,8,128]{2,1,0:T(8,128)S(1)} %get-tuple-element.40.head_ref, f32[8,384]{1,0:T(8,128)S(1)} %get-tuple-element.41.lines_ref, bf16[320,1024]{1,0:T(8,128)(2,1)S(1)} %get-tuple-element.47.images, ...), custom_call_target="tpu_custom_call" | custom-call | flops 293601280 | bytes 3649536 | tf_op jit(solution)/shard_map/pallas_call | solution.py:296
  30.1 2.4 %collective-permute-start.12 = (f32[4,8,128]{2,1,0:T(8,128)S(1)}, f32[4,8,128]{2,1,0:T(8,128)S(1)}, u32[]{:S(2)}, u32[]{:S(2)}) collective-permute-start(f32[4,8,128]{2,1,0:T(8,128)S(1)} %get-tuple-element.49.refs_2_), channel_id=1, source_target_pairs={{0,17},{1,16},{16,1},{17,0},{2,19},{3,18},{18,3},{19,2},{4,21},{5,... | collective-permute-start | bytes 49160 | tf_op jit(solution)/shard_map/ppermute | solution.py:25
  33.0 0.6 collective-permute-start.10
  33.6 1.5 %collective-permute-start.9 = (f32[2,8,128]{2,1,0:T(8,128)S(1)}, f32[2,8,128]{2,1,0:T(8,128)S(1)}, u32[]{:S(2)}, u32[]{:S(2)}) collective-permute-start(f32[2,8,128]{2,1,0:T(8,128)S(1)} %get-tuple-element.48.refs_0_), channel_id=1, source_target_pairs={{0,8},{8,0},{1,9},{9,1},{2,10},{10,2},{3,11},{11,3},{4,12},{12,4},... | collective-permute-start | bytes 24584 | tf_op jit(solution)/shard_map/ppermute | solution.py:25
  35.1 2.2 %collective-permute-done.9.refs_1_ = f32[2,8,128]{2,1,0:T(8,128)S(1)} collective-permute-done((f32[2,8,128]{2,1,0:T(8,128)S(1)}, f32[2,8,128]{2,1,0:T(8,128)S(1)}, u32[]{:S(2)}, u32[]{:S(2)}) %collective-permute-start.9) | collective-permute-done | bytes 8224 | tf_op jit(solution)/shard_map/ppermute | solution.py:25
  37.3 1.4 %collective-permute-start.13 = (f32[4,8,128]{2,1,0:T(8,128)S(1)}, f32[4,8,128]{2,1,0:T(8,128)S(1)}, u32[]{:S(2)}, u32[]{:S(2)}) collective-permute-start(f32[4,8,128]{2,1,0:T(8,128)S(1)} %get-tuple-element.50.refs_4_), channel_id=1, source_target_pairs={{0,2},{2,0},{1,3},{3,1},{4,6},{6,4},{5,7},{7,5},{8,10},{10,8},{9,1... | collective-permute-start | bytes 49160 | tf_op jit(solution)/shard_map/ppermute | solution.py:25
  38.7 3.3 %collective-permute-done.13.refs_5_ = f32[4,8,128]{2,1,0:T(8,128)S(1)} collective-permute-done((f32[4,8,128]{2,1,0:T(8,128)S(1)}, f32[4,8,128]{2,1,0:T(8,128)S(1)}, u32[]{:S(2)}, u32[]{:S(2)}) %collective-permute-start.13) | collective-permute-done | bytes 16416 | tf_op jit(solution)/shard_map/ppermute | solution.py:25
  42.0 1.0 %shard_map.66 = (bf16[320,640]{1,0:T(8,128)(2,1)S(1)}, bf16[320,320]{1,0:T(8,128)(2,1)S(1)}, bf16[80,1024]{1,0:T(8,128)(2,1)S(1)}) custom-call(f32[320,384]{1,0:T(8,128)S(1)} %get-tuple-element.39.refs_0_, f32[320,256]{1,0:T(8,128)S(1)} %get-tuple-element.43.refs_1_, f32[320,384]{1,0:T(8,128)S(1)} %get-tuple-element.44.refs_2_, ...), custom_call_target="tpu_custom_call" | custom-call | flops 104857600 | bytes 4775936 | tf_op jit(solution)/shard_map/pallas_call | solution.py:296
  43.1 1.6 %collective-permute-start.20 = (bf16[80,1024]{1,0:T(8,128)(2,1)S(1)}, bf16[80,1024]{1,0:T(8,128)(2,1)S(1)}, u32[]{:S(2)}, u32[]{:S(2)}) collective-permute-start(bf16[80,1024]{1,0:T(8,128)(2,1)S(1)} %get-tuple-element.61), channel_id=1, source_target_pairs={{0,8},{8,0},{1,9},{9,1},{2,10},{10,2},{3,11},{11,3},{4,12},{12,4},... | collective-permute-start | bytes 491528 | tf_op jit(solution)/shard_map/ppermute | solution.py:25
  44.7 0.5 shard_map.68
  45.2 0.6 collective-permute-start.19
  45.8 0.9 %shard_map.67 = (f32[80,1024]{1,0:T(8,128)S(1)}, bf16[80,1024]{1,0:T(8,128)(2,1)S(1)}, f32[80,1024]{1,0:T(8,128)S(1)}, bf16[80,1024]{1,0:T(8,128)(2,1)S(1)}) custom-call(bf16[320,640]{1,0:T(8,128)(2,1)S(1)} %get-tuple-element.52.tile_ref, bf16[320,320]{1,0:T(8,128)(2,1)S(1)} %collective-permute-done.15.tile_other, ...), custom_call_target="tpu_custom_call" | custom-call | flops 419430400 | bytes 2908160 | tf_op jit(solution)/shard_map/pallas_call | solution.py:296
  46.7 1.6 %collective-permute-start.17 = (bf16[80,1024]{1,0:T(8,128)(2,1)S(1)}, bf16[80,1024]{1,0:T(8,128)(2,1)S(1)}, u32[]{:S(2)}, u32[]{:S(2)}) collective-permute-start(bf16[80,1024]{1,0:T(8,128)(2,1)S(1)} %get-tuple-element.57), channel_id=1, source_target_pairs={{0,16},{16,0},{1,17},{17,1},{2,18},{18,2},{3,19},{19,3},{4,20},{20... | collective-permute-start | bytes 491528 | tf_op jit(solution)/shard_map/ppermute | solution.py:25
  48.3 1.9 %collective-permute-done.20 = bf16[80,1024]{1,0:T(8,128)(2,1)S(1)} collective-permute-done((bf16[80,1024]{1,0:T(8,128)(2,1)S(1)}, bf16[80,1024]{1,0:T(8,128)(2,1)S(1)}, u32[]{:S(2)}, u32[]{:S(2)}) %collective-permute-start.20) | collective-permute-done | bytes 163872 | tf_op jit(solution)/shard_map/ppermute | solution.py:25
  50.2 1.4 %collective-permute-start.21 = (bf16[80,1024]{1,0:T(8,128)(2,1)S(1)}, bf16[80,1024]{1,0:T(8,128)(2,1)S(1)}, u32[]{:S(2)}, u32[]{:S(2)}) collective-permute-start(bf16[80,1024]{1,0:T(8,128)(2,1)S(1)} %add_convert_fusion), channel_id=1, source_target_pairs={{0,2},{2,0},{1,3},{3,1},{4,6},{6,4},{5,7},{7,5},{8,10},{10,8},{9,1... | collective-permute-start | bytes 491528 | tf_op jit(solution)/shard_map/ppermute | solution.py:25
  51.6 1.5 %collective-permute-start.16 = (bf16[80,1024]{1,0:T(8,128)(2,1)S(1)}, bf16[80,1024]{1,0:T(8,128)(2,1)S(1)}, u32[]{:S(2)}, u32[]{:S(2)}) collective-permute-start(bf16[80,1024]{1,0:T(8,128)(2,1)S(1)} %get-tuple-element.55), channel_id=1, source_target_pairs={{0,16},{16,0},{1,17},{17,1},{2,18},{18,2},{3,19},{19,3},{4,20},{20... | collective-permute-start | bytes 491528 | tf_op jit(solution)/shard_map/ppermute | solution.py:25
  53.2 1.8 %collective-permute-start.18 = (bf16[80,1024]{1,0:T(8,128)(2,1)S(1)}, bf16[80,1024]{1,0:T(8,128)(2,1)S(1)}, u32[]{:S(2)}, u32[]{:S(2)}) collective-permute-start(bf16[80,1024]{1,0:T(8,128)(2,1)S(1)} %add_convert_fusion.1), channel_id=1, source_target_pairs={{0,1},{1,0},{2,3},{3,2},{4,5},{5,4},{6,7},{7,6},{8,9},{9,8},{10,11... | collective-permute-start | bytes 491528 | tf_op jit(solution)/shard_map/ppermute | solution.py:25
  54.9 5.2 %collective-permute-done.21.refs_5_ = bf16[80,1024]{1,0:T(8,128)(2,1)S(1)} collective-permute-done((bf16[80,1024]{1,0:T(8,128)(2,1)S(1)}, bf16[80,1024]{1,0:T(8,128)(2,1)S(1)}, u32[]{:S(2)}, u32[]{:S(2)}) %collective-permute-start.21) | collective-permute-done | bytes 163872 | tf_op jit(solution)/shard_map/ppermute | solution.py:25
  60.5 0.9 %shard_map.69 = (f32[80,1024]{1,0:T(8,128)}, f32[80,1024]{1,0:T(8,128)}) custom-call(f32[80,1024]{1,0:T(8,128)S(1)} %get-tuple-element.54.refs_0_, bf16[80,1024]{1,0:T(8,128)(2,1)S(1)} %collective-permute-done.16.refs_1_, bf16[80,1024]{1,0:T(8,128)(2,1)S(1)} %collective-permute-done.18.refs_2_, f32[80,1024]{1,0:T(8,128)S(1)} %get-tuple-element.58.refs_3_, ...), custom_call_target="tpu_custom_call" | custom-call | bytes 1966080 | tf_op jit(solution)/shard_map/pallas_call | solution.py:296
  (25 shorter events, 1.6 us)
Async XLA Ops:
  1.8 16.0 %collective-permute-start.4 = (bf16[80,1792]{1,0:T(8,128)(2,1)S(1)}, bf16[80,1792]{1,0:T(8,128)(2,1)S(1)}, u32[]{:S(2)}, u32[]{:S(2)}) collective-permute-start(bf16[80,1792]{1,0:T(8,128)(2,1)S(1)} %get-tuple-element.36.refs_1_.refs_0_), channel_id=1, source_target_pairs={{0,1},{1,0},{2,3},{3,2},{4,5},{5,4},{6,7},{7,6},{8,9},{9,8},{10,11... | collective-permute-start | bytes 860168 | tf_op jit(solution)/shard_map/ppermute | solution.py:25
  4.9 15.4 %collective-permute-start = (bf16[80,1792]{1,0:T(8,128)(2,1)S(1)}, bf16[80,1792]{1,0:T(8,128)(2,1)S(1)}, u32[]{:S(2)}, u32[]{:S(2)}) collective-permute-start(bf16[80,1792]{1,0:T(8,128)(2,1)S(1)} %get-tuple-element.33.refs_0_), channel_id=1, source_target_pairs={{0,2},{2,0},{1,3},{3,1},{4,6},{6,4},{5,7},{7,5},{8,10},{10,8},{9,1... | collective-permute-start | bytes 860168 | tf_op jit(solution)/shard_map/ppermute | solution.py:25
  7.5 14.2 %collective-permute-start.1 = (bf16[80,1792]{1,0:T(8,128)(2,1)S(1)}, bf16[80,1792]{1,0:T(8,128)(2,1)S(1)}, u32[]{:S(2)}, u32[]{:S(2)}) collective-permute-start(bf16[80,1792]{1,0:T(8,128)(2,1)S(1)} %get-tuple-element.35), channel_id=1, source_target_pairs={{0,8},{8,0},{1,9},{9,1},{2,10},{10,2},{3,11},{11,3},{4,12},{12,4},... | collective-permute-start | bytes 860168 | tf_op jit(solution)/shard_map/ppermute | solution.py:25
  9.1 12.7 %collective-permute-start.3 = (bf16[80,1792]{1,0:T(8,128)(2,1)S(1)}, bf16[80,1792]{1,0:T(8,128)(2,1)S(1)}, u32[]{:S(2)}, u32[]{:S(2)}) collective-permute-start(bf16[80,1792]{1,0:T(8,128)(2,1)S(1)} %get-tuple-element.37), channel_id=1, source_target_pairs={{0,16},{16,0},{1,17},{17,1},{2,18},{18,2},{3,19},{19,3},{4,20},{20... | collective-permute-start | bytes 860168 | tf_op jit(solution)/shard_map/ppermute | solution.py:25
  17.7 8.0 %collective-permute-start.5 = (bf16[80,1792]{1,0:T(8,128)(2,1)S(1)}, bf16[80,1792]{1,0:T(8,128)(2,1)S(1)}, u32[]{:S(2)}, u32[]{:S(2)}) collective-permute-start(bf16[80,1792]{1,0:T(8,128)(2,1)S(1)} %collective-permute-done.4.refs_0_), channel_id=1, source_target_pairs={{0,16},{16,0},{1,17},{17,1},{2,18},{18,2},{3,19},{19,3},{4,20},{20... | collective-permute-start | bytes 860168 | tf_op jit(solution)/shard_map/ppermute | solution.py:25
  20.3 6.6 %collective-permute-start.2 = (bf16[80,1792]{1,0:T(8,128)(2,1)S(1)}, bf16[80,1792]{1,0:T(8,128)(2,1)S(1)}, u32[]{:S(2)}, u32[]{:S(2)}) collective-permute-start(bf16[80,1792]{1,0:T(8,128)(2,1)S(1)} %collective-permute-done.refs_1_), channel_id=1, source_target_pairs={{0,8},{8,0},{1,9},{9,1},{2,10},{10,2},{3,11},{11,3},{4,12},{12,4},... | collective-permute-start | bytes 860168 | tf_op jit(solution)/shard_map/ppermute | solution.py:25
  21.8 5.2 %collective-permute-start.6 = (bf16[160,1792]{1,0:T(8,128)(2,1)S(1)}, bf16[160,1792]{1,0:T(8,128)(2,1)S(1)}, u32[]{:S(2)}, u32[]{:S(2)}) collective-permute-start(bf16[160,1792]{1,0:T(8,128)(2,1)S(1)} %shard_map.61.refs_4_.refs_8_.refs_0_), channel_id=1, source_target_pairs={{0,4},{4,0},{1,5},{5,1},{2,6},{6,2},{3,7},{7,3},{8,12},{12,8},{9,1... | collective-permute-start | bytes 1720328 | tf_op jit(solution)/shard_map/ppermute | solution.py:25
  26.9 2.0 %collective-permute-start.7 = (bf16[160,1792]{1,0:T(8,128)(2,1)S(1)}, bf16[160,1792]{1,0:T(8,128)(2,1)S(1)}, u32[]{:S(2)}, u32[]{:S(2)}) collective-permute-start(bf16[160,1792]{1,0:T(8,128)(2,1)S(1)} %shard_map.62.refs_5_.refs_9_.refs_1_), channel_id=1, source_target_pairs={{0,4},{4,0},{1,5},{5,1},{2,6},{6,2},{3,7},{7,3},{8,12},{12,8},{9,1... | collective-permute-start | bytes 1720328 | tf_op jit(solution)/shard_map/ppermute | solution.py:25
  29.9 5.2 %collective-permute-start.8 = (bf16[320,1024]{1,0:T(8,128)(2,1)S(1)}, bf16[320,1024]{1,0:T(8,128)(2,1)S(1)}, u32[]{:S(2)}, u32[]{:S(2)}) collective-permute-start(bf16[320,1024]{1,0:T(8,128)(2,1)S(1)} %get-tuple-element.47.images), channel_id=1, source_target_pairs={{0,4},{4,0},{1,5},{5,1},{2,6},{6,2},{3,7},{7,3},{8,12},{12,8},{9,1... | collective-permute-start | bytes 1966088 | tf_op jit(solution)/shard_map/ppermute | solution.py:25
  30.1 7.2 %collective-permute-start.12 = (f32[4,8,128]{2,1,0:T(8,128)S(1)}, f32[4,8,128]{2,1,0:T(8,128)S(1)}, u32[]{:S(2)}, u32[]{:S(2)}) collective-permute-start(f32[4,8,128]{2,1,0:T(8,128)S(1)} %get-tuple-element.49.refs_2_), channel_id=1, source_target_pairs={{0,17},{1,16},{16,1},{17,0},{2,19},{3,18},{18,3},{19,2},{4,21},{5,... | collective-permute-start | bytes 49160 | tf_op jit(solution)/shard_map/ppermute | solution.py:25
  32.5 4.7 %collective-permute-start.11 = (f32[4,8,128]{2,1,0:T(8,128)S(1)}, f32[4,8,128]{2,1,0:T(8,128)S(1)}, u32[]{:S(2)}, u32[]{:S(2)}) collective-permute-start(f32[4,8,128]{2,1,0:T(8,128)S(1)} %get-tuple-element.49.refs_2_), channel_id=1, source_target_pairs={{0,16},{1,17},{16,0},{17,1},{2,18},{3,19},{18,2},{19,3},{4,20},{5,... | collective-permute-start | bytes 49160 | tf_op jit(solution)/shard_map/ppermute | solution.py:25
  33.0 4.2 %collective-permute-start.10 = (f32[4,8,128]{2,1,0:T(8,128)S(1)}, f32[4,8,128]{2,1,0:T(8,128)S(1)}, u32[]{:S(2)}, u32[]{:S(2)}) collective-permute-start(f32[4,8,128]{2,1,0:T(8,128)S(1)} %get-tuple-element.49.refs_2_), channel_id=1, source_target_pairs={{0,1},{1,0},{16,17},{17,16},{2,3},{3,2},{18,19},{19,18},{4,5},{5,4... | collective-permute-start | bytes 49160 | tf_op jit(solution)/shard_map/ppermute | solution.py:25
  33.6 3.7 %collective-permute-start.9 = (f32[2,8,128]{2,1,0:T(8,128)S(1)}, f32[2,8,128]{2,1,0:T(8,128)S(1)}, u32[]{:S(2)}, u32[]{:S(2)}) collective-permute-start(f32[2,8,128]{2,1,0:T(8,128)S(1)} %get-tuple-element.48.refs_0_), channel_id=1, source_target_pairs={{0,8},{8,0},{1,9},{9,1},{2,10},{10,2},{3,11},{11,3},{4,12},{12,4},... | collective-permute-start | bytes 24584 | tf_op jit(solution)/shard_map/ppermute | solution.py:25
  37.3 4.7 %collective-permute-start.13 = (f32[4,8,128]{2,1,0:T(8,128)S(1)}, f32[4,8,128]{2,1,0:T(8,128)S(1)}, u32[]{:S(2)}, u32[]{:S(2)}) collective-permute-start(f32[4,8,128]{2,1,0:T(8,128)S(1)} %get-tuple-element.50.refs_4_), channel_id=1, source_target_pairs={{0,2},{2,0},{1,3},{3,1},{4,6},{6,4},{5,7},{7,5},{8,10},{10,8},{9,1... | collective-permute-start | bytes 49160 | tf_op jit(solution)/shard_map/ppermute | solution.py:25
  38.7 3.3 %collective-permute-start.14 = (f32[4,8,128]{2,1,0:T(8,128)S(1)}, f32[4,8,128]{2,1,0:T(8,128)S(1)}, u32[]{:S(2)}, u32[]{:S(2)}) collective-permute-start(f32[4,8,128]{2,1,0:T(8,128)S(1)} %get-tuple-element.51.refs_6_), channel_id=1, source_target_pairs={{0,4},{4,0},{1,5},{5,1},{2,6},{6,2},{3,7},{7,3},{8,12},{12,8},{9,1... | collective-permute-start | bytes 49160 | tf_op jit(solution)/shard_map/ppermute | solution.py:25
  43.0 2.8 %collective-permute-start.15 = (bf16[320,320]{1,0:T(8,128)(2,1)S(1)}, bf16[320,320]{1,0:T(8,128)(2,1)S(1)}, u32[]{:S(2)}, u32[]{:S(2)}) collective-permute-start(bf16[320,320]{1,0:T(8,128)(2,1)S(1)} %get-tuple-element.53), channel_id=1, source_target_pairs={{0,4},{4,0},{1,5},{5,1},{2,6},{6,2},{3,7},{7,3},{8,12},{12,8},{9,1... | collective-permute-start | bytes 614408 | tf_op jit(solution)/shard_map/ppermute | solution.py:25
  43.1 7.1 %collective-permute-start.20 = (bf16[80,1024]{1,0:T(8,128)(2,1)S(1)}, bf16[80,1024]{1,0:T(8,128)(2,1)S(1)}, u32[]{:S(2)}, u32[]{:S(2)}) collective-permute-start(bf16[80,1024]{1,0:T(8,128)(2,1)S(1)} %get-tuple-element.61), channel_id=1, source_target_pairs={{0,8},{8,0},{1,9},{9,1},{2,10},{10,2},{3,11},{11,3},{4,12},{12,4},... | collective-permute-start | bytes 491528 | tf_op jit(solution)/shard_map/ppermute | solution.py:25
  45.2 9.7 %collective-permute-start.19 = (bf16[80,1024]{1,0:T(8,128)(2,1)S(1)}, bf16[80,1024]{1,0:T(8,128)(2,1)S(1)}, u32[]{:S(2)}, u32[]{:S(2)}) collective-permute-start(bf16[80,1024]{1,0:T(8,128)(2,1)S(1)} %get-tuple-element.59), channel_id=1, source_target_pairs={{0,8},{8,0},{1,9},{9,1},{2,10},{10,2},{3,11},{11,3},{4,12},{12,4},... | collective-permute-start | bytes 491528 | tf_op jit(solution)/shard_map/ppermute | solution.py:25
  46.7 6.4 %collective-permute-start.17 = (bf16[80,1024]{1,0:T(8,128)(2,1)S(1)}, bf16[80,1024]{1,0:T(8,128)(2,1)S(1)}, u32[]{:S(2)}, u32[]{:S(2)}) collective-permute-start(bf16[80,1024]{1,0:T(8,128)(2,1)S(1)} %get-tuple-element.57), channel_id=1, source_target_pairs={{0,16},{16,0},{1,17},{17,1},{2,18},{18,2},{3,19},{19,3},{4,20},{20... | collective-permute-start | bytes 491528 | tf_op jit(solution)/shard_map/ppermute | solution.py:25
  50.2 9.9 %collective-permute-start.21 = (bf16[80,1024]{1,0:T(8,128)(2,1)S(1)}, bf16[80,1024]{1,0:T(8,128)(2,1)S(1)}, u32[]{:S(2)}, u32[]{:S(2)}) collective-permute-start(bf16[80,1024]{1,0:T(8,128)(2,1)S(1)} %add_convert_fusion), channel_id=1, source_target_pairs={{0,2},{2,0},{1,3},{3,1},{4,6},{6,4},{5,7},{7,5},{8,10},{10,8},{9,1... | collective-permute-start | bytes 491528 | tf_op jit(solution)/shard_map/ppermute | solution.py:25
  51.6 8.5 %collective-permute-start.16 = (bf16[80,1024]{1,0:T(8,128)(2,1)S(1)}, bf16[80,1024]{1,0:T(8,128)(2,1)S(1)}, u32[]{:S(2)}, u32[]{:S(2)}) collective-permute-start(bf16[80,1024]{1,0:T(8,128)(2,1)S(1)} %get-tuple-element.55), channel_id=1, source_target_pairs={{0,16},{16,0},{1,17},{17,1},{2,18},{18,2},{3,19},{19,3},{4,20},{20... | collective-permute-start | bytes 491528 | tf_op jit(solution)/shard_map/ppermute | solution.py:25
  53.2 7.4 %collective-permute-start.18 = (bf16[80,1024]{1,0:T(8,128)(2,1)S(1)}, bf16[80,1024]{1,0:T(8,128)(2,1)S(1)}, u32[]{:S(2)}, u32[]{:S(2)}) collective-permute-start(bf16[80,1024]{1,0:T(8,128)(2,1)S(1)} %add_convert_fusion.1), channel_id=1, source_target_pairs={{0,1},{1,0},{2,3},{3,2},{4,5},{5,4},{6,7},{7,6},{8,9},{9,8},{10,11... | collective-permute-start | bytes 491528 | tf_op jit(solution)/shard_map/ppermute | solution.py:25

commit v17 on v14

--- a/solution.py
+++ b/solution.py
@@ -221,7 +221,7 @@
     student_refs, teacher_refs = (refs.pop(0), refs.pop(0)), (refs.pop(0), refs.pop(0))
     blocks = take(refs, plan)
     captions = [refs.pop(0) for _ in range(n_cap)]
-    tile_ref, send_ref, first_ref = refs
+    tile_ref, send_ref, send_more, first_ref = refs
     total, count = tile_ref.shape
 
     lane = lax.broadcasted_iota(jnp.int32, (8, LANES), 1)[:1, :rows]
@@ -242,7 +242,8 @@
         grad = grad - 0.25 * (jnp.exp(t - down[at, 1:2]) + jnp.exp(t - across[1:2]))
         grad = grad - jnp.where(down[at, INDEX : INDEX + 1] == across[INDEX : INDEX + 1], 0.5, 0.0)
         tile_ref[at] = grad.astype(jnp.bfloat16)
-    send_ref[...] = tile_ref[:, count // 2 :]
+    send_ref[...] = tile_ref[: total // 2, count // 2 :]
+    send_more[...] = tile_ref[total // 2 :, count // 2 :]
     right = joined(captions, slice(0, width))
     part = jnp.dot(tile_ref[total - first_ref.shape[0] :], right, preferred_element_type=jnp.float32)
     first_ref[...] = part.astype(jnp.bfloat16)
@@ -263,10 +264,11 @@
     spread(jnp.dot(tile_ref[:count], right, preferred_element_type=jnp.float32), outs)
 
 
-def caption_kernel(tile_ref, tile_other, images, images_other, *outs):
-    half = tile_other.shape[1]
+def caption_kernel(tile_ref, other, more, images, images_other, *outs):
+    half = other.shape[1]
+    tile = jnp.concatenate([other[...], more[...]], axis=0)
     part = 0.0
-    for tile, rows in ((tile_ref[:, :half], images[...]), (tile_other[...], images_other[...])):
+    for tile, rows in ((tile_ref[:, :half], images[...]), (tile, images_other[...])):
         part = part + lax.dot_general(tile, rows, (((0,), (0,)), ((), ())), preferred_element_type=jnp.float32)
     spread(part, outs)
 
@@ -397,13 +399,13 @@
     def pieces(blocks):
         return [shape((rows, width), bf16 if h else f32) for h, _ in blocks]
 
-    tile, tile_send, image_first = call(
+    tile, tile_send, tile_more, image_first = call(
         functools.partial(tile_kernel, plan, len(cap), rows, width),
-        [shape((total, columns), bf16), shape((total, columns // 2), bf16), shape((rows, width), bf16)],
+        [shape((total, columns), bf16)] + [shape((total // 2, columns // 2), bf16)] * 2 + [shape((rows, width), bf16)],
         [student, student_tail, teacher, teacher_tail] + blocks + cap,
         2 * rows * columns * width,
     )
-    tile_other = swap(tile_send, "core", 1)
+    tile_other, tile_other_more = swap(tile_send, "core", 1), swap(tile_more, "core", 1)
 
     image_parts = call(
         functools.partial(image_kernel, width),
@@ -415,7 +417,7 @@
     caption_parts = call(
         caption_kernel,
         pieces(caption_blocks),
-        [tile, tile_other, images, images_other],
+        [tile, tile_other, tile_other_more, images, images_other],
         2 * total * columns * width,
     )
     caption_parts = dict(zip(caption_blocks, caption_parts))

time: 61.6 us -> 64 us (1.039)
  waiting for transfers between devices: 26.7 us -> 30 us
  starting transfers between devices: 27.2 us -> 26.4 us
    ppermute x22 -> x23, waiting for transfers between devices: 26.7 us -> 30 us  [swap(): return lax.ppermute(value, axis, [(j, j ^ mask) for j in range(size)])]
    ppermute x22 -> x23, starting transfers between devices: 27.2 us -> 26.4 us  [swap(): return lax.ppermute(value, axis, [(j, j ^ mask) for j in range(size)])]
  transfers between devices with their start and end apart: 22 -> 23, of which waited for: 10 -> 10; matrix products, arithmetic and copies ran while one was open for 0% -> 0% of each run, Pallas kernels for 4% -> 4%
where the time goes in v17:
time: 64 us; the launch traced here: 63.9 us
  waiting for transfers between devices  30 us (47%)
  starting transfers between devices  26.4 us (41%)
  Pallas kernels  6.64 us (10%)
  between operations  0.75 us (1%)
    ppermute x23, waiting for transfers between devices, swap(): return lax.ppermute(value, axis, [(j, j ^ mask) for j in range(size)])  30 us
    ppermute x23, starting transfers between devices, swap(): return lax.ppermute(value, axis, [(j, j ^ mask) for j in range(size)])  26.4 us
    pallas_call x11, Pallas kernels, call(): pl.pallas_call(kernel, out_shape=[out_space(out.shape, out.dtype) for out...  6.64 us
  transfers between devices with their start and end apart: 23, of which 10 were waited for; matrix products, arithmetic and copies ran while one was open for 0% of the time, Pallas kernels for 4%

profile of v17, /device:TPU:0, one launch (start us, length us, event | category | flops | bytes accessed | tf_op | source)
XLA Modules:
  0.0 63.9 jit_solution(14799684209926567800)
XLA Ops:
  0.6 1.2 %shard_map.59 = (bf16[80,1792]{1,0:T(8,128)(2,1)S(1)}, bf16[80,1792]{1,0:T(8,128)(2,1)S(1)}) custom-call(bf16[80,1024]{1,0:T(8,128)(2,1)} %image_s.1, bf16[80,768]{1,0:T(8,128)(2,1)} %image_t.1, bf16[80,1024]{1,0:T(8,128)(2,1)} %caption_s.1, bf16[80,768]{1,0:T(8,128)(2,1)} %caption_t.1), custom_call_target="tpu_custom_call" | custom-call | bytes 1146880 | tf_op jit(solution)/shard_map/pallas_call | solution.py:298
  1.8 3.1 %collective-permute-start.4 = (bf16[80,1792]{1,0:T(8,128)(2,1)S(1)}, bf16[80,1792]{1,0:T(8,128)(2,1)S(1)}, u32[]{:S(2)}, u32[]{:S(2)}) collective-permute-start(bf16[80,1792]{1,0:T(8,128)(2,1)S(1)} %get-tuple-element.37.refs_1_.refs_0_), channel_id=1, source_target_pairs={{0,1},{1,0},{2,3},{3,2},{4,5},{5,4},{6,7},{7,6},{8,9},{9,8},{10,11... | collective-permute-start | bytes 860168 | tf_op jit(solution)/shard_map/ppermute | solution.py:25
  4.9 2.6 %collective-permute-start = (bf16[80,1792]{1,0:T(8,128)(2,1)S(1)}, bf16[80,1792]{1,0:T(8,128)(2,1)S(1)}, u32[]{:S(2)}, u32[]{:S(2)}) collective-permute-start(bf16[80,1792]{1,0:T(8,128)(2,1)S(1)} %get-tuple-element.34.refs_0_), channel_id=1, source_target_pairs={{0,2},{2,0},{1,3},{3,1},{4,6},{6,4},{5,7},{7,5},{8,10},{10,8},{9,1... | collective-permute-start | bytes 860168 | tf_op jit(solution)/shard_map/ppermute | solution.py:25
  7.5 1.6 %collective-permute-start.1 = (bf16[80,1792]{1,0:T(8,128)(2,1)S(1)}, bf16[80,1792]{1,0:T(8,128)(2,1)S(1)}, u32[]{:S(2)}, u32[]{:S(2)}) collective-permute-start(bf16[80,1792]{1,0:T(8,128)(2,1)S(1)} %get-tuple-element.36), channel_id=1, source_target_pairs={{0,8},{8,0},{1,9},{9,1},{2,10},{10,2},{3,11},{11,3},{4,12},{12,4},... | collective-permute-start | bytes 860168 | tf_op jit(solution)/shard_map/ppermute | solution.py:25
  9.1 1.5 %collective-permute-start.3 = (bf16[80,1792]{1,0:T(8,128)(2,1)S(1)}, bf16[80,1792]{1,0:T(8,128)(2,1)S(1)}, u32[]{:S(2)}, u32[]{:S(2)}) collective-permute-start(bf16[80,1792]{1,0:T(8,128)(2,1)S(1)} %get-tuple-element.38), channel_id=1, source_target_pairs={{0,16},{16,0},{1,17},{17,1},{2,18},{18,2},{3,19},{19,3},{4,20},{20... | collective-permute-start | bytes 860168 | tf_op jit(solution)/shard_map/ppermute | solution.py:25
  10.6 7.2 %collective-permute-done.4.refs_0_ = bf16[80,1792]{1,0:T(8,128)(2,1)S(1)} collective-permute-done((bf16[80,1792]{1,0:T(8,128)(2,1)S(1)}, bf16[80,1792]{1,0:T(8,128)(2,1)S(1)}, u32[]{:S(2)}, u32[]{:S(2)}) %collective-permute-start.4) | collective-permute-done | bytes 286752 | tf_op jit(solution)/shard_map/ppermute | solution.py:25
  17.7 1.7 %collective-permute-start.5 = (bf16[80,1792]{1,0:T(8,128)(2,1)S(1)}, bf16[80,1792]{1,0:T(8,128)(2,1)S(1)}, u32[]{:S(2)}, u32[]{:S(2)}) collective-permute-start(bf16[80,1792]{1,0:T(8,128)(2,1)S(1)} %collective-permute-done.4.refs_0_), channel_id=1, source_target_pairs={{0,16},{16,0},{1,17},{17,1},{2,18},{18,2},{3,19},{19,3},{4,20},{20... | collective-permute-start | bytes 860168 | tf_op jit(solution)/shard_map/ppermute | solution.py:25
  19.4 0.8 %collective-permute-done.refs_1_ = bf16[80,1792]{1,0:T(8,128)(2,1)S(1)} collective-permute-done((bf16[80,1792]{1,0:T(8,128)(2,1)S(1)}, bf16[80,1792]{1,0:T(8,128)(2,1)S(1)}, u32[]{:S(2)}, u32[]{:S(2)}) %collective-permute-start) | collective-permute-done | bytes 286752 | tf_op jit(solution)/shard_map/ppermute | solution.py:25
  20.3 1.5 %collective-permute-start.2 = (bf16[80,1792]{1,0:T(8,128)(2,1)S(1)}, bf16[80,1792]{1,0:T(8,128)(2,1)S(1)}, u32[]{:S(2)}, u32[]{:S(2)}) collective-permute-start(bf16[80,1792]{1,0:T(8,128)(2,1)S(1)} %collective-permute-done.refs_1_), channel_id=1, source_target_pairs={{0,8},{8,0},{1,9},{9,1},{2,10},{10,2},{3,11},{11,3},{4,12},{12,4},... | collective-permute-start | bytes 860168 | tf_op jit(solution)/shard_map/ppermute | solution.py:25
  21.9 3.9 %collective-permute-done.5.refs_1_ = bf16[80,1792]{1,0:T(8,128)(2,1)S(1)} collective-permute-done((bf16[80,1792]{1,0:T(8,128)(2,1)S(1)}, bf16[80,1792]{1,0:T(8,128)(2,1)S(1)}, u32[]{:S(2)}, u32[]{:S(2)}) %collective-permute-start.5) | collective-permute-done | bytes 286752 | tf_op jit(solution)/shard_map/ppermute | solution.py:25
  25.8 1.1 %collective-permute-done.2.refs_3_ = bf16[80,1792]{1,0:T(8,128)(2,1)S(1)} collective-permute-done((bf16[80,1792]{1,0:T(8,128)(2,1)S(1)}, bf16[80,1792]{1,0:T(8,128)(2,1)S(1)}, u32[]{:S(2)}, u32[]{:S(2)}) %collective-permute-start.2) | collective-permute-done | bytes 286752 | tf_op jit(solution)/shard_map/ppermute | solution.py:25
  27.0 1.1 %shard_map.63 = (f32[320,384]{1,0:T(8,128)S(1)}, f32[320,384]{1,0:T(8,128)S(1)}, f32[2,8,128]{2,1,0:T(8,128)S(1)}, f32[8,384]{1,0:T(8,128)S(1)}, bf16[320,1024]{1,0:T(8,128)(2,1)S(1)}) custom-call(bf16[80,1792]{1,0:T(8,128)(2,1)S(1)} %get-tuple-element.34.refs_0_, bf16[80,1792]{1,0:T(8,128)(2,1)S(1)} %collective-permute-done.refs_1_, ...), custom_call_target="tpu_custom_call" | custom-call | flops 440401920 | bytes 4526080 | tf_op jit(solution)/shard_map/pallas_call | solution.py:298
  28.2 0.8 %collective-permute-done.7.refs_5_.refs_11_.refs_3_ = bf16[160,1792]{1,0:T(8,128)(2,1)S(1)} collective-permute-done((bf16[160,1792]{1,0:T(8,128)(2,1)S(1)}, bf16[160,1792]{1,0:T(8,128)(2,1)S(1)}, u32[]{:S(2)}, u32[]{:S(2)}) %collective-permute-start.7) | collective-permute-done | bytes 573472 | tf_op jit(solution)/shard_map/ppermute | solution.py:25
  29.0 0.9 %shard_map.64 = (f32[320,256]{1,0:T(8,128)S(1)}, f32[320,256]{1,0:T(8,128)S(1)}, f32[2,8,128]{2,1,0:T(8,128)S(1)}, f32[4,8,128]{2,1,0:T(8,128)S(1)}) custom-call(f32[2,8,128]{2,1,0:T(8,128)S(1)} %get-tuple-element.41.head_ref, f32[8,384]{1,0:T(8,128)S(1)} %get-tuple-element.42.lines_ref, bf16[320,1024]{1,0:T(8,128)(2,1)S(1)} %get-tuple-element.48.images, ...), custom_call_target="tpu_custom_call" | custom-call | flops 293601280 | bytes 3649536 | tf_op jit(solution)/shard_map/pallas_call | solution.py:298
  30.1 2.4 %collective-permute-start.12 = (f32[4,8,128]{2,1,0:T(8,128)S(1)}, f32[4,8,128]{2,1,0:T(8,128)S(1)}, u32[]{:S(2)}, u32[]{:S(2)}) collective-permute-start(f32[4,8,128]{2,1,0:T(8,128)S(1)} %get-tuple-element.50.refs_2_), channel_id=1, source_target_pairs={{0,17},{1,16},{16,1},{17,0},{2,19},{3,18},{18,3},{19,2},{4,21},{5,... | collective-permute-start | bytes 49160 | tf_op jit(solution)/shard_map/ppermute | solution.py:25
  33.0 0.6 collective-permute-start.10
  33.6 1.5 %collective-permute-start.9 = (f32[2,8,128]{2,1,0:T(8,128)S(1)}, f32[2,8,128]{2,1,0:T(8,128)S(1)}, u32[]{:S(2)}, u32[]{:S(2)}) collective-permute-start(f32[2,8,128]{2,1,0:T(8,128)S(1)} %get-tuple-element.49.refs_0_), channel_id=1, source_target_pairs={{0,8},{8,0},{1,9},{9,1},{2,10},{10,2},{3,11},{11,3},{4,12},{12,4},... | collective-permute-start | bytes 24584 | tf_op jit(solution)/shard_map/ppermute | solution.py:25
  35.1 2.2 %collective-permute-done.9.refs_1_ = f32[2,8,128]{2,1,0:T(8,128)S(1)} collective-permute-done((f32[2,8,128]{2,1,0:T(8,128)S(1)}, f32[2,8,128]{2,1,0:T(8,128)S(1)}, u32[]{:S(2)}, u32[]{:S(2)}) %collective-permute-start.9) | collective-permute-done | bytes 8224 | tf_op jit(solution)/shard_map/ppermute | solution.py:25
  37.4 1.4 %collective-permute-start.13 = (f32[2,8,128]{2,1,0:T(8,128)S(1)}, f32[2,8,128]{2,1,0:T(8,128)S(1)}, u32[]{:S(2)}, u32[]{:S(2)}) collective-permute-start(f32[2,8,128]{2,1,0:T(8,128)S(1)} %get-tuple-element.51.refs_4_), channel_id=1, source_target_pairs={{0,2},{2,0},{1,3},{3,1},{4,6},{6,4},{5,7},{7,5},{8,10},{10,8},{9,1... | collective-permute-start | bytes 24584 | tf_op jit(solution)/shard_map/ppermute | solution.py:25
  38.8 3.2 %collective-permute-done.13.refs_5_ = f32[2,8,128]{2,1,0:T(8,128)S(1)} collective-permute-done((f32[2,8,128]{2,1,0:T(8,128)S(1)}, f32[2,8,128]{2,1,0:T(8,128)S(1)}, u32[]{:S(2)}, u32[]{:S(2)}) %collective-permute-start.13) | collective-permute-done | bytes 8224 | tf_op jit(solution)/shard_map/ppermute | solution.py:25
  42.0 1.0 %shard_map.66 = (bf16[320,640]{1,0:T(8,128)(2,1)S(1)}, bf16[160,320]{1,0:T(8,128)(2,1)S(1)}, bf16[160,320]{1,0:T(8,128)(2,1)S(1)}, bf16[80,1024]{1,0:T(8,128)(2,1)S(1)}) custom-call(f32[320,384]{1,0:T(8,128)S(1)} %get-tuple-element.40.refs_0_, f32[320,256]{1,0:T(8,128)S(1)} %get-tuple-element.44.refs_1_, f32[320,384]{1,0:T(8,128)S(1)} %get-tuple-element.45.refs_2_, ...), custom_call_target="tpu_custom_call" | custom-call | flops 104857600 | bytes 4759552 | tf_op jit(solution)/shard_map/pallas_call | solution.py:298
  43.0 1.6 %collective-permute-start.21 = (bf16[80,1024]{1,0:T(8,128)(2,1)S(1)}, bf16[80,1024]{1,0:T(8,128)(2,1)S(1)}, u32[]{:S(2)}, u32[]{:S(2)}) collective-permute-start(bf16[80,1024]{1,0:T(8,128)(2,1)S(1)} %get-tuple-element.63), channel_id=1, source_target_pairs={{0,8},{8,0},{1,9},{9,1},{2,10},{10,2},{3,11},{11,3},{4,12},{12,4},... | collective-permute-start | bytes 491528 | tf_op jit(solution)/shard_map/ppermute | solution.py:25
  45.1 0.5 shard_map.68
  45.6 0.6 collective-permute-start.20
  46.2 0.9 %shard_map.67 = (f32[80,1024]{1,0:T(8,128)S(1)}, bf16[80,1024]{1,0:T(8,128)(2,1)S(1)}, f32[80,1024]{1,0:T(8,128)S(1)}, bf16[80,1024]{1,0:T(8,128)(2,1)S(1)}) custom-call(bf16[320,640]{1,0:T(8,128)(2,1)S(1)} %get-tuple-element.53.tile_ref, bf16[160,320]{1,0:T(8,128)(2,1)S(1)} %collective-permute-done.15.other, ...), custom_call_target="tpu_custom_call" | custom-call | flops 419430400 | bytes 2908160 | tf_op jit(solution)/shard_map/pallas_call | solution.py:298
  47.1 1.6 %collective-permute-start.17 = (bf16[80,1024]{1,0:T(8,128)(2,1)S(1)}, bf16[80,1024]{1,0:T(8,128)(2,1)S(1)}, u32[]{:S(2)}, u32[]{:S(2)}) collective-permute-start(bf16[80,1024]{1,0:T(8,128)(2,1)S(1)} %get-tuple-element.57), channel_id=1, source_target_pairs={{0,16},{16,0},{1,17},{17,1},{2,18},{18,2},{3,19},{19,3},{4,20},{20... | collective-permute-start | bytes 491528 | tf_op jit(solution)/shard_map/ppermute | solution.py:25
  49.2 1.4 %collective-permute-start.22 = (bf16[80,1024]{1,0:T(8,128)(2,1)S(1)}, bf16[80,1024]{1,0:T(8,128)(2,1)S(1)}, u32[]{:S(2)}, u32[]{:S(2)}) collective-permute-start(bf16[80,1024]{1,0:T(8,128)(2,1)S(1)} %add_convert_fusion), channel_id=1, source_target_pairs={{0,2},{2,0},{1,3},{3,1},{4,6},{6,4},{5,7},{7,5},{8,10},{10,8},{9,1... | collective-permute-start | bytes 491528 | tf_op jit(solution)/shard_map/ppermute | solution.py:25
  50.7 6.3 %collective-permute-done.18 = bf16[80,1024]{1,0:T(8,128)(2,1)S(1)} collective-permute-done((bf16[80,1024]{1,0:T(8,128)(2,1)S(1)}, bf16[80,1024]{1,0:T(8,128)(2,1)S(1)}, u32[]{:S(2)}, u32[]{:S(2)}) %collective-permute-start.18) | collective-permute-done | bytes 163872 | tf_op jit(solution)/shard_map/ppermute | solution.py:25
  57.0 1.5 %collective-permute-start.19 = (bf16[80,1024]{1,0:T(8,128)(2,1)S(1)}, bf16[80,1024]{1,0:T(8,128)(2,1)S(1)}, u32[]{:S(2)}, u32[]{:S(2)}) collective-permute-start(bf16[80,1024]{1,0:T(8,128)(2,1)S(1)} %add_convert_fusion.1), channel_id=1, source_target_pairs={{0,1},{1,0},{2,3},{3,2},{4,5},{5,4},{6,7},{7,6},{8,9},{9,8},{10,11... | collective-permute-start | bytes 491528 | tf_op jit(solution)/shard_map/ppermute | solution.py:25
  58.5 1.0 %collective-permute-done.22.refs_5_ = bf16[80,1024]{1,0:T(8,128)(2,1)S(1)} collective-permute-done((bf16[80,1024]{1,0:T(8,128)(2,1)S(1)}, bf16[80,1024]{1,0:T(8,128)(2,1)S(1)}, u32[]{:S(2)}, u32[]{:S(2)}) %collective-permute-start.22) | collective-permute-done | bytes 163872 | tf_op jit(solution)/shard_map/ppermute | solution.py:25
  59.5 3.5 %collective-permute-done.19.refs_2_ = bf16[80,1024]{1,0:T(8,128)(2,1)S(1)} collective-permute-done((bf16[80,1024]{1,0:T(8,128)(2,1)S(1)}, bf16[80,1024]{1,0:T(8,128)(2,1)S(1)}, u32[]{:S(2)}, u32[]{:S(2)}) %collective-permute-start.19) | collective-permute-done | bytes 163872 | tf_op jit(solution)/shard_map/ppermute | solution.py:25
  63.0 0.9 %shard_map.69 = (f32[80,1024]{1,0:T(8,128)}, f32[80,1024]{1,0:T(8,128)}) custom-call(f32[80,1024]{1,0:T(8,128)S(1)} %get-tuple-element.56.refs_0_, bf16[80,1024]{1,0:T(8,128)(2,1)S(1)} %collective-permute-done.17.refs_1_, bf16[80,1024]{1,0:T(8,128)(2,1)S(1)} %collective-permute-done.19.refs_2_, f32[80,1024]{1,0:T(8,128)S(1)} %get-tuple-element.60.refs_3_, ...), custom_call_target="tpu_custom_call" | custom-call | bytes 1966080 | tf_op jit(solution)/shard_map/pallas_call | solution.py:298
  (27 shorter events, 2.2 us)
Async XLA Ops:
  1.8 16.0 %collective-permute-start.4 = (bf16[80,1792]{1,0:T(8,128)(2,1)S(1)}, bf16[80,1792]{1,0:T(8,128)(2,1)S(1)}, u32[]{:S(2)}, u32[]{:S(2)}) collective-permute-start(bf16[80,1792]{1,0:T(8,128)(2,1)S(1)} %get-tuple-element.37.refs_1_.refs_0_), channel_id=1, source_target_pairs={{0,1},{1,0},{2,3},{3,2},{4,5},{5,4},{6,7},{7,6},{8,9},{9,8},{10,11... | collective-permute-start | bytes 860168 | tf_op jit(solution)/shard_map/ppermute | solution.py:25
  4.9 15.4 %collective-permute-start = (bf16[80,1792]{1,0:T(8,128)(2,1)S(1)}, bf16[80,1792]{1,0:T(8,128)(2,1)S(1)}, u32[]{:S(2)}, u32[]{:S(2)}) collective-permute-start(bf16[80,1792]{1,0:T(8,128)(2,1)S(1)} %get-tuple-element.34.refs_0_), channel_id=1, source_target_pairs={{0,2},{2,0},{1,3},{3,1},{4,6},{6,4},{5,7},{7,5},{8,10},{10,8},{9,1... | collective-permute-start | bytes 860168 | tf_op jit(solution)/shard_map/ppermute | solution.py:25
  7.5 14.2 %collective-permute-start.1 = (bf16[80,1792]{1,0:T(8,128)(2,1)S(1)}, bf16[80,1792]{1,0:T(8,128)(2,1)S(1)}, u32[]{:S(2)}, u32[]{:S(2)}) collective-permute-start(bf16[80,1792]{1,0:T(8,128)(2,1)S(1)} %get-tuple-element.36), channel_id=1, source_target_pairs={{0,8},{8,0},{1,9},{9,1},{2,10},{10,2},{3,11},{11,3},{4,12},{12,4},... | collective-permute-start | bytes 860168 | tf_op jit(solution)/shard_map/ppermute | solution.py:25
  9.1 12.7 %collective-permute-start.3 = (bf16[80,1792]{1,0:T(8,128)(2,1)S(1)}, bf16[80,1792]{1,0:T(8,128)(2,1)S(1)}, u32[]{:S(2)}, u32[]{:S(2)}) collective-permute-start(bf16[80,1792]{1,0:T(8,128)(2,1)S(1)} %get-tuple-element.38), channel_id=1, source_target_pairs={{0,16},{16,0},{1,17},{17,1},{2,18},{18,2},{3,19},{19,3},{4,20},{20... | collective-permute-start | bytes 860168 | tf_op jit(solution)/shard_map/ppermute | solution.py:25
  17.7 8.0 %collective-permute-start.5 = (bf16[80,1792]{1,0:T(8,128)(2,1)S(1)}, bf16[80,1792]{1,0:T(8,128)(2,1)S(1)}, u32[]{:S(2)}, u32[]{:S(2)}) collective-permute-start(bf16[80,1792]{1,0:T(8,128)(2,1)S(1)} %collective-permute-done.4.refs_0_), channel_id=1, source_target_pairs={{0,16},{16,0},{1,17},{17,1},{2,18},{18,2},{3,19},{19,3},{4,20},{20... | collective-permute-start | bytes 860168 | tf_op jit(solution)/shard_map/ppermute | solution.py:25
  20.3 6.6 %collective-permute-start.2 = (bf16[80,1792]{1,0:T(8,128)(2,1)S(1)}, bf16[80,1792]{1,0:T(8,128)(2,1)S(1)}, u32[]{:S(2)}, u32[]{:S(2)}) collective-permute-start(bf16[80,1792]{1,0:T(8,128)(2,1)S(1)} %collective-permute-done.refs_1_), channel_id=1, source_target_pairs={{0,8},{8,0},{1,9},{9,1},{2,10},{10,2},{3,11},{11,3},{4,12},{12,4},... | collective-permute-start | bytes 860168 | tf_op jit(solution)/shard_map/ppermute | solution.py:25
  21.8 5.2 %collective-permute-start.6 = (bf16[160,1792]{1,0:T(8,128)(2,1)S(1)}, bf16[160,1792]{1,0:T(8,128)(2,1)S(1)}, u32[]{:S(2)}, u32[]{:S(2)}) collective-permute-start(bf16[160,1792]{1,0:T(8,128)(2,1)S(1)} %shard_map.61.refs_4_.refs_8_.refs_0_), channel_id=1, source_target_pairs={{0,4},{4,0},{1,5},{5,1},{2,6},{6,2},{3,7},{7,3},{8,12},{12,8},{9,1... | collective-permute-start | bytes 1720328 | tf_op jit(solution)/shard_map/ppermute | solution.py:25
  26.9 2.0 %collective-permute-start.7 = (bf16[160,1792]{1,0:T(8,128)(2,1)S(1)}, bf16[160,1792]{1,0:T(8,128)(2,1)S(1)}, u32[]{:S(2)}, u32[]{:S(2)}) collective-permute-start(bf16[160,1792]{1,0:T(8,128)(2,1)S(1)} %shard_map.62.refs_5_.refs_9_.refs_1_), channel_id=1, source_target_pairs={{0,4},{4,0},{1,5},{5,1},{2,6},{6,2},{3,7},{7,3},{8,12},{12,8},{9,1... | collective-permute-start | bytes 1720328 | tf_op jit(solution)/shard_map/ppermute | solution.py:25
  29.9 5.2 %collective-permute-start.8 = (bf16[320,1024]{1,0:T(8,128)(2,1)S(1)}, bf16[320,1024]{1,0:T(8,128)(2,1)S(1)}, u32[]{:S(2)}, u32[]{:S(2)}) collective-permute-start(bf16[320,1024]{1,0:T(8,128)(2,1)S(1)} %get-tuple-element.48.images), channel_id=1, source_target_pairs={{0,4},{4,0},{1,5},{5,1},{2,6},{6,2},{3,7},{7,3},{8,12},{12,8},{9,1... | collective-permute-start | bytes 1966088 | tf_op jit(solution)/shard_map/ppermute | solution.py:25
  30.1 7.2 %collective-permute-start.12 = (f32[4,8,128]{2,1,0:T(8,128)S(1)}, f32[4,8,128]{2,1,0:T(8,128)S(1)}, u32[]{:S(2)}, u32[]{:S(2)}) collective-permute-start(f32[4,8,128]{2,1,0:T(8,128)S(1)} %get-tuple-element.50.refs_2_), channel_id=1, source_target_pairs={{0,17},{1,16},{16,1},{17,0},{2,19},{3,18},{18,3},{19,2},{4,21},{5,... | collective-permute-start | bytes 49160 | tf_op jit(solution)/shard_map/ppermute | solution.py:25
  32.5 4.7 %collective-permute-start.11 = (f32[4,8,128]{2,1,0:T(8,128)S(1)}, f32[4,8,128]{2,1,0:T(8,128)S(1)}, u32[]{:S(2)}, u32[]{:S(2)}) collective-permute-start(f32[4,8,128]{2,1,0:T(8,128)S(1)} %get-tuple-element.50.refs_2_), channel_id=1, source_target_pairs={{0,16},{1,17},{16,0},{17,1},{2,18},{3,19},{18,2},{19,3},{4,20},{5,... | collective-permute-start | bytes 49160 | tf_op jit(solution)/shard_map/ppermute | solution.py:25
  33.0 4.2 %collective-permute-start.10 = (f32[4,8,128]{2,1,0:T(8,128)S(1)}, f32[4,8,128]{2,1,0:T(8,128)S(1)}, u32[]{:S(2)}, u32[]{:S(2)}) collective-permute-start(f32[4,8,128]{2,1,0:T(8,128)S(1)} %get-tuple-element.50.refs_2_), channel_id=1, source_target_pairs={{0,1},{1,0},{16,17},{17,16},{2,3},{3,2},{18,19},{19,18},{4,5},{5,4... | collective-permute-start | bytes 49160 | tf_op jit(solution)/shard_map/ppermute | solution.py:25
  33.6 3.7 %collective-permute-start.9 = (f32[2,8,128]{2,1,0:T(8,128)S(1)}, f32[2,8,128]{2,1,0:T(8,128)S(1)}, u32[]{:S(2)}, u32[]{:S(2)}) collective-permute-start(f32[2,8,128]{2,1,0:T(8,128)S(1)} %get-tuple-element.49.refs_0_), channel_id=1, source_target_pairs={{0,8},{8,0},{1,9},{9,1},{2,10},{10,2},{3,11},{11,3},{4,12},{12,4},... | collective-permute-start | bytes 24584 | tf_op jit(solution)/shard_map/ppermute | solution.py:25
  37.3 4.7 %collective-permute-start.14 = (f32[4,8,128]{2,1,0:T(8,128)S(1)}, f32[4,8,128]{2,1,0:T(8,128)S(1)}, u32[]{:S(2)}, u32[]{:S(2)}) collective-permute-start(f32[4,8,128]{2,1,0:T(8,128)S(1)} %get-tuple-element.52.refs_6_), channel_id=1, source_target_pairs={{0,4},{4,0},{1,5},{5,1},{2,6},{6,2},{3,7},{7,3},{8,12},{12,8},{9,1... | collective-permute-start | bytes 49160 | tf_op jit(solution)/shard_map/ppermute | solution.py:25
  37.4 4.6 %collective-permute-start.13 = (f32[2,8,128]{2,1,0:T(8,128)S(1)}, f32[2,8,128]{2,1,0:T(8,128)S(1)}, u32[]{:S(2)}, u32[]{:S(2)}) collective-permute-start(f32[2,8,128]{2,1,0:T(8,128)S(1)} %get-tuple-element.51.refs_4_), channel_id=1, source_target_pairs={{0,2},{2,0},{1,3},{3,1},{4,6},{6,4},{5,7},{7,5},{8,10},{10,8},{9,1... | collective-permute-start | bytes 24584 | tf_op jit(solution)/shard_map/ppermute | solution.py:25
  43.0 6.2 %collective-permute-start.21 = (bf16[80,1024]{1,0:T(8,128)(2,1)S(1)}, bf16[80,1024]{1,0:T(8,128)(2,1)S(1)}, u32[]{:S(2)}, u32[]{:S(2)}) collective-permute-start(bf16[80,1024]{1,0:T(8,128)(2,1)S(1)} %get-tuple-element.63), channel_id=1, source_target_pairs={{0,8},{8,0},{1,9},{9,1},{2,10},{10,2},{3,11},{11,3},{4,12},{12,4},... | collective-permute-start | bytes 491528 | tf_op jit(solution)/shard_map/ppermute | solution.py:25
  44.6 1.7 %collective-permute-start.15 = (bf16[160,320]{1,0:T(8,128)(2,1)S(1)}, bf16[160,320]{1,0:T(8,128)(2,1)S(1)}, u32[]{:S(2)}, u32[]{:S(2)}) collective-permute-start(bf16[160,320]{1,0:T(8,128)(2,1)S(1)} %get-tuple-element.54), channel_id=1, source_target_pairs={{0,4},{4,0},{1,5},{5,1},{2,6},{6,2},{3,7},{7,3},{8,12},{12,8},{9,1... | collective-permute-start | bytes 307208 | tf_op jit(solution)/shard_map/ppermute | solution.py:25
  44.6 1.7 %collective-permute-start.16 = (bf16[160,320]{1,0:T(8,128)(2,1)S(1)}, bf16[160,320]{1,0:T(8,128)(2,1)S(1)}, u32[]{:S(2)}, u32[]{:S(2)}) collective-permute-start(bf16[160,320]{1,0:T(8,128)(2,1)S(1)} %get-tuple-element.55), channel_id=1, source_target_pairs={{0,4},{4,0},{1,5},{5,1},{2,6},{6,2},{3,7},{7,3},{8,12},{12,8},{9,1... | collective-permute-start | bytes 307208 | tf_op jit(solution)/shard_map/ppermute | solution.py:25
  45.6 12.9 %collective-permute-start.20 = (bf16[80,1024]{1,0:T(8,128)(2,1)S(1)}, bf16[80,1024]{1,0:T(8,128)(2,1)S(1)}, u32[]{:S(2)}, u32[]{:S(2)}) collective-permute-start(bf16[80,1024]{1,0:T(8,128)(2,1)S(1)} %get-tuple-element.61), channel_id=1, source_target_pairs={{0,8},{8,0},{1,9},{9,1},{2,10},{10,2},{3,11},{11,3},{4,12},{12,4},... | collective-permute-start | bytes 491528 | tf_op jit(solution)/shard_map/ppermute | solution.py:25
  47.1 11.4 %collective-permute-start.17 = (bf16[80,1024]{1,0:T(8,128)(2,1)S(1)}, bf16[80,1024]{1,0:T(8,128)(2,1)S(1)}, u32[]{:S(2)}, u32[]{:S(2)}) collective-permute-start(bf16[80,1024]{1,0:T(8,128)(2,1)S(1)} %get-tuple-element.57), channel_id=1, source_target_pairs={{0,16},{16,0},{1,17},{17,1},{2,18},{18,2},{3,19},{19,3},{4,20},{20... | collective-permute-start | bytes 491528 | tf_op jit(solution)/shard_map/ppermute | solution.py:25
  48.7 8.3 %collective-permute-start.18 = (bf16[80,1024]{1,0:T(8,128)(2,1)S(1)}, bf16[80,1024]{1,0:T(8,128)(2,1)S(1)}, u32[]{:S(2)}, u32[]{:S(2)}) collective-permute-start(bf16[80,1024]{1,0:T(8,128)(2,1)S(1)} %get-tuple-element.59), channel_id=1, source_target_pairs={{0,16},{16,0},{1,17},{17,1},{2,18},{18,2},{3,19},{19,3},{4,20},{20... | collective-permute-start | bytes 491528 | tf_op jit(solution)/shard_map/ppermute | solution.py:25
  49.2 10.3 %collective-permute-start.22 = (bf16[80,1024]{1,0:T(8,128)(2,1)S(1)}, bf16[80,1024]{1,0:T(8,128)(2,1)S(1)}, u32[]{:S(2)}, u32[]{:S(2)}) collective-permute-start(bf16[80,1024]{1,0:T(8,128)(2,1)S(1)} %add_convert_fusion), channel_id=1, source_target_pairs={{0,2},{2,0},{1,3},{3,1},{4,6},{6,4},{5,7},{7,5},{8,10},{10,8},{9,1... | collective-permute-start | bytes 491528 | tf_op jit(solution)/shard_map/ppermute | solution.py:25
  57.0 6.0 %collective-permute-start.19 = (bf16[80,1024]{1,0:T(8,128)(2,1)S(1)}, bf16[80,1024]{1,0:T(8,128)(2,1)S(1)}, u32[]{:S(2)}, u32[]{:S(2)}) collective-permute-start(bf16[80,1024]{1,0:T(8,128)(2,1)S(1)} %add_convert_fusion.1), channel_id=1, source_target_pairs={{0,1},{1,0},{2,3},{3,2},{4,5},{5,4},{6,7},{7,6},{8,9},{9,8},{10,11... | collective-permute-start | bytes 491528 | tf_op jit(solution)/shard_map/ppermute | solution.py:25
